TPU v7x, 32 devices: a whole 2x2x4 slice. The times are simulated.
32 devices in a mesh: gx: 8 (over z, x), gy: 4 (over y, core).
Axes of the slice: x: 2, y: 2, z: 4, core: 2. Of those that a mesh axis runs over, the one named last changes fastest.
Arguments:
- field: bfloat16 [20, 16, 16, 512], P(None, 'gx', 'gy'), may hold values from -6 to 6
- cotangent: bfloat16 [20, 16, 16, 512], P(None, 'gx', 'gy'), may hold values from -6 to 6
- spectral_weight: float32 [64, 2, 20, 20, 16, 16], P('gx', None, None, None, 'gy'), may hold values from -3 to 3
- pointwise_weight: bfloat16 [20, 20], replicated, may hold values from -1.25 to 1.25
- channel_bias: float32 [20], replicated, may hold values from -3 to 3
Outputs:
- layer_out: bfloat16 [20, 16, 16, 512], P(None, 'gx', 'gy')
- grad_field: bfloat16 [20, 16, 16, 512], P(None, 'gx', 'gy')
- grad_spectral: float32 [64, 2, 20, 20, 16, 16], P('gx', None, None, None, 'gy')
All inputs are finite; a program needn't handle non-finite values.
Results may differ from a plain program's by a relative error of at most 0.0061.
Values sent between devices are 32-bit elements; how exact they have to be, the bound alone decides.
No kernel may reach another device: no remote copies, remote signals or barrier semaphores. Data moves between devices by JAX's collectives and lax.ppermute only.
A program may use at most 128 MiB of HBM per device.

v0:
```python
import math

import jax
import jax.numpy as jnp
import ml_dtypes
import numpy as np
from jax import lax
from jax.experimental import pallas as pl
from jax.experimental.pallas import tpu as pltpu
from jax.sharding import PartitionSpec as P

KZ = 16
KT = 4
NT = 16
LANES = 128
EXACT = lax.Precision.HIGHEST
F32 = jnp.float32
BF16 = jnp.bfloat16


def round_up(value, step):
    return -(-value // step) * step


def frequencies(kept):
    index = np.arange(kept)
    return np.where(index < kept // 2, index, index - kept)


def depth_time_table(cells):
    depth_cells = cells // NT
    depth = np.arange(depth_cells)[:, None, None, None] * frequencies(KZ)[None, None, :, None] * NT
    time = np.arange(NT)[None, :, None, None] * np.arange(KT)[None, None, None, :] * depth_cells
    phase = np.mod(depth + time, cells).reshape(cells, KZ * KT)
    angles = phase.astype(np.float32) * np.float32(2.0 * math.pi / cells)
    factor = np.float32(1.0 / math.sqrt(cells))
    return np.stack([np.cos(angles) * factor, -np.sin(angles) * factor], axis=1).astype(np.float32)


def plane_table(nx, ny, cells_x, cells_y, kept_x, kept_y, half):
    length_x, length_y = nx * cells_x, ny * cells_y
    phase_x = np.arange(length_x)[:, None] * frequencies(kept_x)[None, :]
    phase_y = np.arange(length_y)[:, None] * frequencies(kept_y)[None, :]
    angle = (
        np.mod(phase_x, length_x)[:, None, :, None] / length_x
        + np.mod(phase_y, length_y)[None, :, None, :] / length_y
    )
    factor = 1.0 / math.sqrt(length_x * length_y)
    cosine = np.cos(2.0 * math.pi * angle) * factor
    sine = np.sin(2.0 * math.pi * angle) * factor
    table = np.stack([np.stack([cosine, -sine]), np.stack([sine, cosine])])
    local = kept_x // ny
    table = table.reshape(2, 2, nx, cells_x, ny // 2, 2, cells_y, ny, local * kept_y)
    table = table.transpose(7, 5, 2, 4, 3, 6, 0, 1, 8)
    padded = np.zeros(table.shape[:-1] + (half,), np.float32)
    padded[..., : local * kept_y] = table
    out = np.stack([padded[j][[j % 2, 1 - j % 2]] for j in range(ny)])
    return out.reshape(ny, nx * cells_x * ny * cells_y, 4 * half)


class Sizes:
    def __init__(self, field, weight):
        self.nx, self.ny = lax.axis_size("gx"), lax.axis_size("gy")
        self.channels, self.cells_x, self.cells_y, self.depth = field.shape
        self.modes = weight.shape[0]
        self.local_x, self.kept_y = weight.shape[4:]
        self.kept_x = self.local_x * self.ny
        self.cells = self.cells_x * self.cells_y
        self.chips = self.nx * self.ny // 2
        self.kept = self.local_x * self.kept_y
        self.half = round_up(self.kept, LANES // 2)
        self.flat = 2 * self.channels * self.modes
        self.width = round_up(self.flat, LANES)
        self.all_modes = 2 * self.modes * self.nx
        self.rows = round_up(self.channels, 8)


def gather_cells(source, scratch, sizes):
    for w in range(sizes.channels):
        for x in range(sizes.cells_x):
            first = (w * sizes.cells_x + x) * sizes.cells_y
            scratch[first : first + sizes.cells_y, :] = source[w, x].astype(F32)
    return scratch[...]


def scatter_cells(values, target, sizes):
    for w in range(sizes.channels):
        for x in range(sizes.cells_x):
            first = (w * sizes.cells_x + x) * sizes.cells_y
            target[w, x] = values[first : first + sizes.cells_y, :].astype(target.dtype)


def lane_group(sizes):
    return lax.broadcasted_iota(jnp.int32, (sizes.cells, LANES), 1) // sizes.modes


def send_modes(values, target, sizes):
    group = lane_group(sizes)
    tiles = [values[w * sizes.cells : (w + 1) * sizes.cells, :] for w in range(sizes.channels)]
    for i in range(sizes.nx):
        out = [jnp.zeros((sizes.cells, LANES), F32) for _ in range(sizes.width // LANES)]
        for s in range(2):
            have = (i * 2 + s) * sizes.modes
            for w in range(sizes.channels):
                tile, want = divmod((s * sizes.channels + w) * sizes.modes, LANES)
                moved = tiles[w]
                if want != have:
                    moved = pltpu.roll(moved, (want - have) % LANES, 1)
                out[tile] = jnp.where(group == want // sizes.modes, moved, out[tile])
        for t, value in enumerate(out):
            for y in range(sizes.ny // 2):
                target[i * (sizes.ny // 2) + y, :, t * LANES : (t + 1) * LANES] = value


def receive_modes(source, scratch, sizes):
    group = lane_group(sizes)
    tiles = []
    for i in range(sizes.nx):
        row = []
        for t in range(sizes.width // LANES):
            value = None
            for y in range(sizes.ny // 2):
                part = source[i * (sizes.ny // 2) + y, :, t * LANES : (t + 1) * LANES]
                value = part if value is None else value + part
            row.append(value)
        tiles.append(row)
    for w in range(sizes.channels):
        out = jnp.zeros((sizes.cells, LANES), F32)
        for i in range(sizes.nx):
            for s in range(2):
                want = (i * 2 + s) * sizes.modes
                tile, have = divmod((s * sizes.channels + w) * sizes.modes, LANES)
                moved = tiles[i][tile]
                if want != have:
                    moved = pltpu.roll(moved, (want - have) % LANES, 1)
                out = jnp.where(group == want // sizes.modes, moved, out)
        scratch[w * sizes.cells : (w + 1) * sizes.cells, :] = out
    return scratch[...]


def dot(left, right, **kwargs):
    return jnp.dot(left, right, preferred_element_type=F32, **kwargs)


def depth_forward(sizes, field, table, out, cells):
    values = gather_cells(field, cells, sizes).astype(BF16)
    send_modes(dot(values, table[...]), out, sizes)


def turn_weights(sizes, source, target):
    pad = jnp.zeros((sizes.rows - sizes.channels, 2 * sizes.half), F32) if sizes.rows > sizes.channels else None
    for w in range(sizes.channels):
        if sizes.half > sizes.kept:
            target[0, w] = jnp.zeros((sizes.rows, 2 * sizes.half), F32)
        elif pad is not None:
            target[0, w, sizes.channels :, :] = pad
        if sizes.half == sizes.kept:
            block = jnp.concatenate([source[0, s, w].reshape(sizes.kept, sizes.channels) for s in range(2)], 0)
            target[0, w, : sizes.channels, :] = block.T
        else:
            for s in range(2):
                block = source[0, s, w].reshape(sizes.kept, sizes.channels).T
                target[0, w, : sizes.channels, s * sizes.half : s * sizes.half + sizes.kept] = block


def plane_spectra(sizes, own, other, table, target):
    received = jnp.concatenate(
        [ref[...].reshape(sizes.chips * sizes.cells, sizes.width) for ref in (own, other)], 0
    )
    both = dot(received.T, table[...], precision=EXACT)
    count = sizes.channels * sizes.modes
    target[:count, :] = both[:count, : 2 * sizes.half] + both[count : 2 * count, 2 * sizes.half :]


def plane_cells(sizes, mixed, spread, table, own, other):
    rows, lanes = mixed.shape
    spread[...] = jnp.zeros_like(spread)
    for s in range(2):
        spread[s * rows : (s + 1) * rows, s * lanes : (s + 1) * lanes] = mixed[...]
    cells = lax.dot_general(
        table[...], spread[...], (((1,), (1,)), ((), ())), precision=EXACT, preferred_element_type=F32
    )
    count = sizes.chips * sizes.cells
    for at, ref in enumerate((own, other)):
        ref[...] = cells[at * count : (at + 1) * count, :].reshape(ref.shape)


def swap_parts(values, sizes):
    return pltpu.roll(values, sizes.half, 1)


def mode_rows(first, sizes):
    return pl.ds(first, sizes.channels, stride=sizes.modes)


def first_lanes(rows, sizes):
    return lax.broadcasted_iota(jnp.int32, (rows, 2 * sizes.half), 1) < sizes.half


def mix_forward(sizes, own, other, table, weight, spectra, out_own, out_other, mixed, spread):
    plane_spectra(sizes, own, other, table, spectra)
    real = first_lanes(sizes.rows, sizes)
    for m in range(sizes.modes):
        straight = jnp.zeros((sizes.rows, 2 * sizes.half), F32)
        crossed = jnp.zeros((sizes.rows, 2 * sizes.half), F32)
        for w in range(sizes.channels):
            row = spectra[w * sizes.modes + m : w * sizes.modes + m + 1, :]
            block = weight[m, w]
            straight = straight + row * block
            crossed = crossed + swap_parts(row, sizes) * block
        real_part = straight - swap_parts(straight, sizes)
        imag_part = crossed + swap_parts(crossed, sizes)
        result = jnp.where(real, real_part, imag_part)
        mixed[mode_rows(m, sizes), :] = result[: sizes.channels]
    plane_cells(sizes, mixed, spread, table, out_own, out_other)


def mix_back(sizes, own, other, table, weight, back, out_own, out_other, mixed, spread, spectra):
    plane_spectra(sizes, own, other, table, spectra)
    real = first_lanes(sizes.channels, sizes)
    for m in range(sizes.modes):
        rows = spectra[mode_rows(m, sizes), :]
        if sizes.rows > sizes.channels:
            rows = jnp.concatenate([rows, jnp.zeros((sizes.rows - sizes.channels, 2 * sizes.half), F32)], 0)
        back[m] = rows
        turned = swap_parts(rows, sizes)
        straight, crossed = [], []
        for w in range(sizes.channels):
            block = weight[m, w]
            straight.append(jnp.sum(block * rows, axis=0, keepdims=True))
            crossed.append(jnp.sum(block * turned, axis=0, keepdims=True))
        straight = jnp.concatenate(straight, 0)
        crossed = jnp.concatenate(crossed, 0)
        real_part = straight + swap_parts(straight, sizes)
        imag_part = swap_parts(crossed, sizes) - crossed
        mixed[mode_rows(m, sizes), :] = jnp.where(real, real_part, imag_part)
    plane_cells(sizes, mixed, spread, table, out_own, out_other)


def grad_weights(sizes, spectra, back, target):
    mode = pl.program_id(0)
    rows = back[0]
    turned = swap_parts(rows, sizes)
    real = first_lanes(1, sizes)
    for w in range(sizes.channels):
        row = spectra[pl.ds(w * sizes.modes + mode, 1), :]
        swapped = swap_parts(row, sizes)
        real_part = jnp.where(real, row, swapped)
        imag_part = jnp.where(real, swapped, -row)
        block = (real_part * rows + imag_part * turned)[: sizes.channels]
        for s in range(2):
            part = block[:, s * sizes.half : s * sizes.half + sizes.kept].T
            target[0, s, w] = part.reshape(sizes.local_x, sizes.kept_y, sizes.channels)


def activate(sizes, received, field, cotangent, inverse, forward, mixer, bias, layer_out, signal_out, out, cells, spectrum):
    spatial = dot(receive_modes(received, spectrum, sizes), inverse[...], precision=EXACT)
    values = gather_cells(field, cells, sizes).astype(BF16)
    pre = spatial + dot(mixer[...], values) + bias[...]
    slope = math.sqrt(2.0 / math.pi)
    squared = pre * pre
    bend = jnp.tanh(slope * (pre + 0.044715 * (squared * pre)))
    scatter_cells(0.5 * pre * (1.0 + bend), layer_out, sizes)
    derivative = 0.5 * (1.0 + bend) + 0.5 * pre * (1.0 - bend * bend) * (slope * (1.0 + 3.0 * 0.044715 * squared))
    signal = (gather_cells(cotangent, cells, sizes) * derivative).astype(BF16)
    signal_out[...] = signal
    send_modes(dot(signal, forward[...]), out, sizes)


def finish(sizes, received, signal, inverse, mixer, grad_field, spectrum):
    spatial = dot(receive_modes(received, spectrum, sizes), inverse[...], precision=EXACT)
    scatter_cells(spatial + dot(mixer[...], signal[...]), grad_field, sizes)


def shape_of(shape, dtype=F32):
    return jax.ShapeDtypeStruct(shape, dtype)


def whole_call(body, sizes, out_shape, scratch, *args):
    def kernel(*refs):
        body(sizes, *refs)

    vmem = pl.BlockSpec(memory_space=pltpu.VMEM)
    return pl.pallas_call(
        kernel,
        out_shape=out_shape,
        in_specs=[vmem] * len(args),
        out_specs=jax.tree.map(lambda _: vmem, out_shape),
        scratch_shapes=scratch,
        name=body.__name__,
        compiler_params=pltpu.CompilerParams(vmem_limit_bytes=32 * 1024 * 1024),
    )(*args)


def on_device(field, cotangent, spectral_weight, pointwise_weight, channel_bias):
    z = Sizes(field, spectral_weight)
    depth_table = depth_time_table(z.depth)
    modes = depth_table.shape[2]
    kappa = np.where(np.arange(modes) % KT == 0, 1.0, 2.0).astype(np.float32)
    ordered = depth_table.reshape(z.depth, 2, z.nx, z.modes).transpose(0, 2, 1, 3).reshape(z.depth, z.all_modes)
    doubled = np.repeat(kappa.reshape(z.nx, 1, z.modes), 2, axis=1).reshape(z.all_modes)
    forward_first = jnp.asarray(ordered.astype(ml_dtypes.bfloat16))
    forward_back = jnp.asarray((ordered.astype(ml_dtypes.bfloat16).astype(np.float32) * doubled).astype(ml_dtypes.bfloat16))
    inverse_back = jnp.asarray(np.ascontiguousarray(ordered.T))
    inverse_first = jnp.asarray(np.ascontiguousarray((ordered * doubled).T))
    tables = jnp.asarray(plane_table(z.nx, z.ny, z.cells_x, z.cells_y, z.kept_x, z.kept_y, z.half))
    plane = lax.dynamic_index_in_dim(tables, lax.axis_index("gy"), 0, keepdims=False)

    groups = [[gx * z.ny + 2 * y + c for gx in range(z.nx) for y in range(z.ny // 2)] for c in range(2)]
    pairs = [(s, s ^ 1) for s in range(z.ny)]

    def exchange(payload):
        return lax.all_to_all(
            payload, ("gx", "gy"), split_axis=0, concat_axis=0, tiled=True, axis_index_groups=groups
        )

    def other_core(payload):
        return lax.ppermute(payload, "gy", pairs)

    payload = shape_of((z.chips, z.cells, z.width))
    cell_rows = z.channels * z.cells
    cells_scratch = pltpu.VMEM((cell_rows, z.depth), F32)
    spectrum_scratch = pltpu.VMEM((cell_rows, z.all_modes), F32)
    mode_rows_count = z.channels * z.modes
    spectra_shape = (mode_rows_count, 2 * z.half)
    mixed_scratch = [pltpu.VMEM(spectra_shape, F32), pltpu.VMEM((z.width, 4 * z.half), F32)]

    native = jnp.transpose(spectral_weight, (0, 1, 2, 4, 5, 3))
    block_in = (1, 2, z.channels, z.local_x, z.kept_y, z.channels)
    block_turned = (1, z.channels, z.rows, 2 * z.half)
    turned = pl.pallas_call(
        lambda source, target: turn_weights(z, source, target),
        grid=(z.modes,),
        out_shape=shape_of((z.modes,) + block_turned[1:]),
        in_specs=[pl.BlockSpec(block_in, lambda m: (m, 0, 0, 0, 0, 0))],
        out_specs=pl.BlockSpec(block_turned, lambda m: (m, 0, 0, 0)),
        name="turn_weights",
        compiler_params=pltpu.CompilerParams(vmem_limit_bytes=32 * 1024 * 1024),
    )(native)

    identity = jnp.eye(z.cells, dtype=BF16)
    mixer_back = jnp.kron(pointwise_weight, identity)
    mixer_first = jnp.kron(pointwise_weight.T, identity)
    bias = jnp.repeat(channel_bias, z.cells)[:, None]

    sent = whole_call(depth_forward, z, payload, [cells_scratch], field, forward_first)
    own = exchange(sent)
    spectra, part_own, part_other = whole_call(
        mix_forward, z, (shape_of(spectra_shape), payload, payload), mixed_scratch,
        own, other_core(own), plane, turned,
    )
    returned = exchange(part_own + other_core(part_other))
    layer_out, signal, sent = whole_call(
        activate, z,
        (shape_of(field.shape, BF16), shape_of((cell_rows, z.depth), BF16), payload),
        [cells_scratch, spectrum_scratch],
        returned, field, cotangent, inverse_first, forward_back, mixer_first, bias,
    )
    own = exchange(sent)
    back, part_own, part_other = whole_call(
        mix_back, z, (shape_of((z.modes, z.rows, 2 * z.half)), payload, payload),
        mixed_scratch + [pltpu.VMEM(spectra_shape, F32)],
        own, other_core(own), plane, turned,
    )
    returned = exchange(part_own + other_core(part_other))
    gradient = pl.pallas_call(
        lambda spectra_ref, back_ref, target: grad_weights(z, spectra_ref, back_ref, target),
        grid=(z.modes,),
        out_shape=shape_of(native.shape),
        in_specs=[
            pl.BlockSpec(spectra_shape, lambda m: (0, 0)),
            pl.BlockSpec((1, z.rows, 2 * z.half), lambda m: (m, 0, 0)),
        ],
        out_specs=pl.BlockSpec(block_in, lambda m: (m, 0, 0, 0, 0, 0)),
        name="grad_weights",
        compiler_params=pltpu.CompilerParams(vmem_limit_bytes=32 * 1024 * 1024),
    )(spectra, back)
    grad_field = whole_call(
        finish, z, shape_of(field.shape, BF16), [spectrum_scratch], returned, signal, inverse_back, mixer_back
    )
    return (layer_out, grad_field, jnp.transpose(gradient, (0, 1, 2, 5, 3, 4)))


def solution(mesh):
    return jax.shard_map(
        on_device,
        mesh=mesh,
        in_specs=(
            P(None, "gx", "gy", None),
            P(None, "gx", "gy", None),
            P("gx", None, None, None, "gy", None),
            P(),
            P(),
        ),
        out_specs=(
            P(None, "gx", "gy", None),
            P(None, "gx", "gy", None),
            P("gx", None, None, None, "gy", None),
        ),
        check_vma=False,
    )
```

profile of v0, /device:TPU:0, one launch (start us, length us, event | category | flops | bytes accessed | tf_op | source)
XLA Modules:
  0.0 88.8 jit_solution(1319322390987264535)
XLA Ops:
  0.6 0.0 copy-start.1
  0.6 0.9 %copy-done.1 = bf16[20,2,4,512]{3,2,1,0:T(4,128)(2,1)S(1)} copy-done((bf16[20,2,4,512]{3,2,1,0:T(4,128)(2,1)S(1)}, bf16[20,2,4,512]{3,2,1,0:T(4,128)(2,1)}, u32[]{:S(2)}) %copy-start.1) | copy-done | bytes 163864
  1.5 0.0 copy-start.7
  1.5 0.9 %copy-done.7 = bf16[512,128]{1,0:T(8,128)(2,1)S(1)} copy-done((bf16[512,128]{1,0:T(8,128)(2,1)S(1)}, bf16[512,128]{1,0:T(8,128)(2,1)}, u32[]{:S(2)}) %copy-start.7) | copy-done | bytes 131096
  2.5 0.0 copy-start.8
  2.5 0.0 copy-start.9
  2.5 0.0 copy-start.2
  2.5 0.0 copy-start.4
  2.5 0.5 depth_forward.1
  3.0 16.8 %all_to_all.20.refs_0_ = f32[16,8,384]{2,1,0:T(8,128)S(1)} all-to-all(f32[16,8,384]{2,1,0:T(8,128)S(1)} %depth_forward.1), channel_id=1, replica_groups={{0,2,4,6,8,10,12,14,16,18,20,22,24,26,28,30},{1,3,5,7,9,11,13,15,17,19,..., dimensions={0} | all-to-all | bytes 393216 | tf_op jit(solution)/shard_map/all_to_all | solution.py:313
  19.8 0.0 collective-permute-start
  19.8 0.0 copy-start
  19.8 4.0 %copy-done = f32[8,2,20,20,4,16]{3,5,4,2,1,0:T(8,128)S(1)} copy-done((f32[8,2,20,20,4,16]{3,5,4,2,1,0:T(8,128)S(1)}, f32[8,2,20,20,4,16]{3,5,4,2,1,0:T(8,128)}, u32[]{:S(2)}) %copy-start) | copy-done | bytes 1638424
  23.7 3.0 %turn_weights.1.refs_3_ = f32[8,20,24,128]{3,2,1,0:T(8,128)S(1)} custom-call(f32[8,2,20,4,16,20]{5,4,3,2,1,0:T(8,128)S(1)} %bitcast.5), custom_call_target="tpu_custom_call" | custom-call | tf_op jit(solution)/shard_map/turn_weights/pallas_call | solution.py:331
  26.7 1.0 %dynamic-slice_bitcast_fusion.refs_2_ = f32[256,256]{1,0:T(8,128)S(1)} fusion(f32[4,256,256]{2,1,0:T(8,128)} %constant.24.clone, s32[]{:T(128)S(6)} %select_n.4), kind=kLoop, calls=%fused_computation.2 | loop fusion | bytes 524292 | tf_op jit(solution)/shard_map/jit(dynamic_index_in_dim)/squeeze | solution.py:307
  27.7 0.0 collective-permute-done.refs_1_
  27.7 2.7 %mix_forward.1 = (f32[160,128]{1,0:T(8,128)S(1)}, f32[16,8,384]{2,1,0:T(8,128)S(1)}, f32[16,8,384]{2,1,0:T(8,128)}) custom-call(f32[16,8,384]{2,1,0:T(8,128)S(1)} %all_to_all.20.refs_0_, f32[16,8,384]{2,1,0:T(8,128)S(1)} %collective-permute-done.refs_1_, f32[256,256]{1,0:T(8,128)S(1)} %dynamic-slice_bitcast_fusion.refs_2_, ...), custom_call_target="tpu_custom_call" | custom-call | tf_op jit(solution)/shard_map/mix_forward/pallas_call | solution.py:284
  30.4 0.5 collective-permute-start.1
  30.9 0.0 copy-done.8
  31.0 0.0 copy-start.3
  31.0 0.1 copy.14
  31.1 0.0 copy-done.9
  31.1 0.1 broadcast_in_dim.9
  31.1 0.1 broadcast_in_dim_reshape.4.refs_6_
  31.2 1.1 %collective-permute-done.1 = f32[16,8,384]{2,1,0:T(8,128)} collective-permute-done((f32[16,8,384]{2,1,0:T(8,128)}, f32[16,8,384]{2,1,0:T(8,128)}, u32[]{:S(2)}, u32[]{:S(2)}) %collective-permute-start.1) | collective-permute-done | bytes 196640 | tf_op jit(solution)/shard_map/ppermute | solution.py:318
  32.4 1.6 %add.11 = f32[16,8,384]{2,1,0:T(8,128)} add(f32[16,8,384]{2,1,0:T(8,128)S(1)} %get-tuple-element.12, f32[16,8,384]{2,1,0:T(8,128)} %collective-permute-done.1) | non-fusion elementwise | flops 49152 | bytes 589824 | tf_op jit(solution)/shard_map/add | solution.py:352
  34.0 3.5 %all-to-all-start.1 = ((f32[16,8,384]{2,1,0:T(8,128)}), f32[16,8,384]{2,1,0:T(8,128)S(1)}, u32[]{:S(2)}, u32[]{:S(2)}) async-start(f32[16,8,384]{2,1,0:T(8,128)} %add.11), calls=%async_computation.1 | async-start | bytes 393216 | tf_op jit(solution)/shard_map/all_to_all | solution.py:313
  37.5 1.5 %broadcast_multiply_fusion = (bf16[20,8,20,8]{3,2,1,0:T(8,128)(2,1)}, bf16[20,8,20,8]{3,2,1,0:T(8,128)(2,1)}) fusion(bf16[20,20]{1,0:T(8,128)(2,1)S(1)} %copy-done.8, bf16[8,8]{1,0:T(8,128)(2,1)S(1)} %fusion, bf16[20,20]{1,0:T(8,128)(2,1)S(1)} %copy.14), kind=kLoop, calls=%fused_computation | loop fusion | flops 51200 | bytes 104128 | tf_op jit(solution)/shard_map/jit(kron)/mul | solution.py:342
  39.0 1.8 %mul.44.refs_5_ = bf16[160,160]{1,0:T(8,128)(2,1)S(1)} reshape(bf16[20,8,20,8]{3,2,1,0:T(8,128)(2,1)} %get-tuple-element.22) | data formatting | bytes 102400 | tf_op jit(solution)/shard_map/jit(kron)/mul | solution.py:343
  40.8 5.7 %all-to-all-done.1.refs_0_ = f32[16,8,384]{2,1,0:T(8,128)S(1)} async-done(((f32[16,8,384]{2,1,0:T(8,128)}), f32[16,8,384]{2,1,0:T(8,128)S(1)}, u32[]{:S(2)}, u32[]{:S(2)}) %all-to-all-start.1) | async-done | bytes 196640 | tf_op jit(solution)/shard_map/all_to_all | solution.py:313
  46.5 0.0 copy-done.2
  46.5 0.0 copy-done.4
  46.5 0.0 copy-start.5
  46.5 0.9 %copy-done.5 = bf16[20,2,4,512]{3,2,1,0:T(4,128)(2,1)S(1)} copy-done((bf16[20,2,4,512]{3,2,1,0:T(4,128)(2,1)S(1)}, bf16[20,2,4,512]{3,2,1,0:T(4,128)(2,1)}, u32[]{:S(2)}) %copy-start.5) | copy-done | bytes 163864
  47.4 0.0 copy-start.6
  47.4 0.9 %copy-done.6 = bf16[512,128]{1,0:T(8,128)(2,1)S(1)} copy-done((bf16[512,128]{1,0:T(8,128)(2,1)S(1)}, bf16[512,128]{1,0:T(8,128)(2,1)}, u32[]{:S(2)}) %copy-start.6) | copy-done | bytes 131096
  48.3 2.0 %activate.1 = (bf16[20,2,4,512]{3,2,1,0:T(4,128)(2,1)}, bf16[160,512]{1,0:T(8,128)(2,1)S(1)}, f32[16,8,384]{2,1,0:T(8,128)S(1)}) custom-call(f32[16,8,384]{2,1,0:T(8,128)S(1)} %all-to-all-done.1.refs_0_, bf16[20,2,4,512]{3,2,1,0:T(4,128)(2,1)S(1)} %copy-done.2, bf16[20,2,4,512]{3,2,1,0:T(4,128)(2,1)S(1)} %copy-done.5, f32[128,512]{1,0:T(8,128)S(1)} %copy-done.4, ...), custom_call_target="tpu_custom_call" | custom-call | tf_op jit(solution)/shard_map/activate/pallas_call | solution.py:284
  50.3 11.6 %all_to_all.21.refs_0_ = f32[16,8,384]{2,1,0:T(8,128)S(1)} all-to-all(f32[16,8,384]{2,1,0:T(8,128)S(1)} %get-tuple-element.15), channel_id=1, replica_groups={{0,2,4,6,8,10,12,14,16,18,20,22,24,26,28,30},{1,3,5,7,9,11,13,15,17,19,..., dimensions={0} | all-to-all | bytes 393216 | tf_op jit(solution)/shard_map/all_to_all | solution.py:313
  61.9 0.0 collective-permute-start.2
  62.0 1.4 %collective-permute-done.2.refs_1_ = f32[16,8,384]{2,1,0:T(8,128)S(1)} collective-permute-done((f32[16,8,384]{2,1,0:T(8,128)S(1)}, f32[16,8,384]{2,1,0:T(8,128)S(1)}, u32[]{:S(2)}, u32[]{:S(2)}) %collective-permute-start.2) | collective-permute-done | bytes 196640 | tf_op jit(solution)/shard_map/ppermute | solution.py:318
  63.4 2.2 %mix_back.1 = (f32[8,24,128]{2,1,0:T(8,128)S(1)}, f32[16,8,384]{2,1,0:T(8,128)S(1)}, f32[16,8,384]{2,1,0:T(8,128)S(1)}) custom-call(f32[16,8,384]{2,1,0:T(8,128)S(1)} %all_to_all.21.refs_0_, f32[16,8,384]{2,1,0:T(8,128)S(1)} %collective-permute-done.2.refs_1_, f32[256,256]{1,0:T(8,128)S(1)} %dynamic-slice_bitcast_fusion.refs_2_, ...), custom_call_target="tpu_custom_call" | custom-call | tf_op jit(solution)/shard_map/mix_back/pallas_call | solution.py:284
  65.6 0.2 collective-permute-start.3
  65.8 1.3 %collective-permute-done.3 = f32[16,8,384]{2,1,0:T(8,128)S(1)} collective-permute-done((f32[16,8,384]{2,1,0:T(8,128)S(1)}, f32[16,8,384]{2,1,0:T(8,128)S(1)}, u32[]{:S(2)}, u32[]{:S(2)}) %collective-permute-start.3) | collective-permute-done | bytes 196640 | tf_op jit(solution)/shard_map/ppermute | solution.py:318
  67.1 0.7 add.12
  67.8 3.6 %all-to-all-start.3 = ((f32[16,8,384]{2,1,0:T(8,128)}), f32[16,8,384]{2,1,0:T(8,128)S(1)}, u32[]{:S(2)}, u32[]{:S(2)}) async-start(f32[16,8,384]{2,1,0:T(8,128)} %add.12), calls=%async_computation.3 | async-start | bytes 393216 | tf_op jit(solution)/shard_map/all_to_all | solution.py:313
  71.4 1.8 %mul.47.refs_3_ = bf16[160,160]{1,0:T(8,128)(2,1)S(1)} reshape(bf16[20,8,20,8]{3,2,1,0:T(8,128)(2,1)} %get-tuple-element.21) | data formatting | bytes 102400 | tf_op jit(solution)/shard_map/jit(kron)/mul | solution.py:342
  73.2 14.2 %grad_weights.1 = f32[8,2,20,4,16,20]{5,4,3,2,1,0:T(8,128)} custom-call(f32[160,128]{1,0:T(8,128)S(1)} %get-tuple-element.19.spectra_ref, f32[8,24,128]{2,1,0:T(8,128)S(1)} %get-tuple-element.20.back_ref), custom_call_target="tpu_custom_call" | custom-call | tf_op jit(solution)/shard_map/grad_weights/pallas_call | solution.py:366
  87.4 0.0 all-to-all-done.3.refs_0_
  87.4 0.0 copy-done.3
  87.4 1.4 %finish.1 = bf16[20,2,4,512]{3,2,1,0:T(4,128)(2,1)} custom-call(f32[16,8,384]{2,1,0:T(8,128)S(1)} %all-to-all-done.3.refs_0_, bf16[160,512]{1,0:T(8,128)(2,1)S(1)} %get-tuple-element.18.refs_1_, f32[128,512]{1,0:T(8,128)S(1)} %copy-done.3, bf16[160,160]{1,0:T(8,128)(2,1)S(1)} %mul.47.refs_3_), custom_call_target="tpu_custom_call" | custom-call | tf_op jit(solution)/shard_map/finish/pallas_call | solution.py:284
  (1 shorter events, 0.0 us)
Async XLA Ops:
  0.6 0.9 %copy-start.1 = (bf16[20,2,4,512]{3,2,1,0:T(4,128)(2,1)S(1)}, bf16[20,2,4,512]{3,2,1,0:T(4,128)(2,1)}, u32[]{:S(2)}) copy-start(bf16[20,2,4,512]{3,2,1,0:T(4,128)(2,1)} %refs_1_.2) | copy-start | bytes 491524
  1.5 0.9 %copy-start.7 = (bf16[512,128]{1,0:T(8,128)(2,1)S(1)}, bf16[512,128]{1,0:T(8,128)(2,1)}, u32[]{:S(2)}) copy-start(bf16[512,128]{1,0:T(8,128)(2,1)} %constant.20.clone.refs_1_) | copy-start | bytes 393220
  2.5 28.5 %copy-start.8 = (bf16[20,20]{1,0:T(8,128)(2,1)S(1)}, bf16[20,20]{1,0:T(8,128)(2,1)}, u32[]{:S(2)}) copy-start(bf16[20,20]{1,0:T(8,128)(2,1)} %param.13) | copy-start | bytes 2404
  2.5 28.6 %copy-start.9 = (f32[20]{0:T(128)S(1)}, f32[20]{0:T(128)}, u32[]{:S(2)}) copy-start(f32[20]{0:T(128)} %param.14) | copy-start | bytes 244
  2.5 44.0 %copy-start.2 = (bf16[20,2,4,512]{3,2,1,0:T(4,128)(2,1)S(1)}, bf16[20,2,4,512]{3,2,1,0:T(4,128)(2,1)}, u32[]{:S(2)}) copy-start(bf16[20,2,4,512]{3,2,1,0:T(4,128)(2,1)} %refs_1_.2) | copy-start | bytes 491524
  2.5 44.0 %copy-start.4 = (f32[128,512]{1,0:T(8,128)S(1)}, f32[128,512]{1,0:T(8,128)}, u32[]{:S(2)}) copy-start(f32[128,512]{1,0:T(8,128)} %constant.23.clone.refs_3_) | copy-start | bytes 786436
  19.8 8.0 %collective-permute-start = (f32[16,8,384]{2,1,0:T(8,128)S(1)}, f32[16,8,384]{2,1,0:T(8,128)S(1)}, u32[]{:S(2)}, u32[]{:S(2)}) collective-permute-start(f32[16,8,384]{2,1,0:T(8,128)S(1)} %all_to_all.20.refs_0_), channel_id=1, source_target_pairs={{0,1},{1,0},{2,3},{3,2},{4,5},{5,4},{6,7},{7,6},{8,9},{9,8},{10,11... | collective-permute-start | bytes 589832 | tf_op jit(solution)/shard_map/ppermute | solution.py:318
  19.8 4.0 %copy-start = (f32[8,2,20,20,4,16]{3,5,4,2,1,0:T(8,128)S(1)}, f32[8,2,20,20,4,16]{3,5,4,2,1,0:T(8,128)}, u32[]{:S(2)}) copy-start(f32[8,2,20,20,4,16]{3,5,4,2,1,0:T(8,128)} %param.12) | copy-start | bytes 4915204
  30.4 1.9 %collective-permute-start.1 = (f32[16,8,384]{2,1,0:T(8,128)}, f32[16,8,384]{2,1,0:T(8,128)}, u32[]{:S(2)}, u32[]{:S(2)}) collective-permute-start(f32[16,8,384]{2,1,0:T(8,128)} %get-tuple-element.13), channel_id=1, source_target_pairs={{0,1},{1,0},{2,3},{3,2},{4,5},{5,4},{6,7},{7,6},{8,9},{9,8},{10,11... | collective-permute-start | bytes 589832 | tf_op jit(solution)/shard_map/ppermute | solution.py:318
  31.0 56.4 %copy-start.3 = (f32[128,512]{1,0:T(8,128)S(1)}, f32[128,512]{1,0:T(8,128)}, u32[]{:S(2)}) copy-start(f32[128,512]{1,0:T(8,128)} %constant.22.clone.refs_2_) | copy-start | bytes 786436
  34.0 12.5 %all-to-all-start.1 = ((f32[16,8,384]{2,1,0:T(8,128)}), f32[16,8,384]{2,1,0:T(8,128)S(1)}, u32[]{:S(2)}, u32[]{:S(2)}) async-start(f32[16,8,384]{2,1,0:T(8,128)} %add.11), calls=%async_computation.1 | async-start | bytes 393216 | tf_op jit(solution)/shard_map/all_to_all | solution.py:313
  46.5 0.9 %copy-start.5 = (bf16[20,2,4,512]{3,2,1,0:T(4,128)(2,1)S(1)}, bf16[20,2,4,512]{3,2,1,0:T(4,128)(2,1)}, u32[]{:S(2)}) copy-start(bf16[20,2,4,512]{3,2,1,0:T(4,128)(2,1)} %refs_2_.2) | copy-start | bytes 491524
  47.4 0.9 %copy-start.6 = (bf16[512,128]{1,0:T(8,128)(2,1)S(1)}, bf16[512,128]{1,0:T(8,128)(2,1)}, u32[]{:S(2)}) copy-start(bf16[512,128]{1,0:T(8,128)(2,1)} %constant.21.clone.refs_4_) | copy-start | bytes 393220
  61.9 1.4 %collective-permute-start.2 = (f32[16,8,384]{2,1,0:T(8,128)S(1)}, f32[16,8,384]{2,1,0:T(8,128)S(1)}, u32[]{:S(2)}, u32[]{:S(2)}) collective-permute-start(f32[16,8,384]{2,1,0:T(8,128)S(1)} %all_to_all.21.refs_0_), channel_id=1, source_target_pairs={{0,1},{1,0},{2,3},{3,2},{4,5},{5,4},{6,7},{7,6},{8,9},{9,8},{10,11... | collective-permute-start | bytes 589832 | tf_op jit(solution)/shard_map/ppermute | solution.py:318
  65.6 1.5 %collective-permute-start.3 = (f32[16,8,384]{2,1,0:T(8,128)S(1)}, f32[16,8,384]{2,1,0:T(8,128)S(1)}, u32[]{:S(2)}, u32[]{:S(2)}) collective-permute-start(f32[16,8,384]{2,1,0:T(8,128)S(1)} %get-tuple-element.17), channel_id=1, source_target_pairs={{0,1},{1,0},{2,3},{3,2},{4,5},{5,4},{6,7},{7,6},{8,9},{9,8},{10,11... | collective-permute-start | bytes 589832 | tf_op jit(solution)/shard_map/ppermute | solution.py:318
  67.8 19.6 %all-to-all-start.3 = ((f32[16,8,384]{2,1,0:T(8,128)}), f32[16,8,384]{2,1,0:T(8,128)S(1)}, u32[]{:S(2)}, u32[]{:S(2)}) async-start(f32[16,8,384]{2,1,0:T(8,128)} %add.12), calls=%async_computation.3 | async-start | bytes 393216 | tf_op jit(solution)/shard_map/all_to_all | solution.py:313
where the time goes:
time: 89.5 us; the launch traced here: 88.8 us
  blocking collectives  28.4 us (32%)
  Pallas kernels  26.1 us (29%)
  local copies, waits for them, and re-layouts  12.5 us (14%)
  waiting for transfers between devices  9.56 us (11%)
  starting transfers between devices  7.83 us (9%)
  other arithmetic  3.79 us (4%)
    all_to_all x2, blocking collectives, exchange(): lax.all_to_all(payload, ('gx', 'gy'), split_axis=0, concat_axis=0, tiled=...  28.4 us
    pallas_call x1, Pallas kernels, on_device(): pl.pallas_call(lambda spectra_ref, back_ref, target: grad_weights(z, spec...  14.2 us
    pallas_call x5, Pallas kernels, whole_call(): pl.pallas_call(kernel, out_shape=out_shape, in_specs=[vmem] * len(args),...  8.88 us
    unnamed x20, local copies, waits for them, and re-layouts  7.63 us
    all_to_all x2, starting transfers between devices, exchange(): lax.all_to_all(payload, ('gx', 'gy'), split_axis=0, concat_axis=0, tiled=...  7.12 us
    all_to_all x2, waiting for transfers between devices, exchange(): lax.all_to_all(payload, ('gx', 'gy'), split_axis=0, concat_axis=0, tiled=...  5.68 us
    ppermute x4, waiting for transfers between devices, other_core(): return lax.ppermute(payload, 'gy', pairs)  3.88 us
    pallas_call x1, Pallas kernels, on_device(): pl.pallas_call(lambda source, target: turn_weights(z, source, target), gr...  3 us
  transfers between devices with their start and end apart: 6, of which 4 were waited for; matrix products, arithmetic and copies ran while one was open for 7% of the time, Pallas kernels for 19%

commit v1 on v0

--- a/solution.py
+++ b/solution.py
@@ -37,25 +37,26 @@
     return np.stack([np.cos(angles) * factor, -np.sin(angles) * factor], axis=1).astype(np.float32)
 
 
-def plane_table(nx, ny, cells_x, cells_y, kept_x, kept_y, half):
-    length_x, length_y = nx * cells_x, ny * cells_y
-    phase_x = np.arange(length_x)[:, None] * frequencies(kept_x)[None, :]
-    phase_y = np.arange(length_y)[:, None] * frequencies(kept_y)[None, :]
-    angle = (
-        np.mod(phase_x, length_x)[:, None, :, None] / length_x
-        + np.mod(phase_y, length_y)[None, :, None, :] / length_y
-    )
-    factor = 1.0 / math.sqrt(length_x * length_y)
-    cosine = np.cos(2.0 * math.pi * angle) * factor
-    sine = np.sin(2.0 * math.pi * angle) * factor
-    table = np.stack([np.stack([cosine, -sine]), np.stack([sine, cosine])])
-    local = kept_x // ny
-    table = table.reshape(2, 2, nx, cells_x, ny // 2, 2, cells_y, ny, local * kept_y)
-    table = table.transpose(7, 5, 2, 4, 3, 6, 0, 1, 8)
-    padded = np.zeros(table.shape[:-1] + (half,), np.float32)
-    padded[..., : local * kept_y] = table
-    out = np.stack([padded[j][[j % 2, 1 - j % 2]] for j in range(ny)])
-    return out.reshape(ny, nx * cells_x * ny * cells_y, 4 * half)
+def plane_table(sizes, place, cores, owners):
+    shape = (cores * sizes.chips * sizes.cells, owners * 4 * sizes.half)
+    row = lax.broadcasted_iota(jnp.int32, shape, 0)
+    lane = lax.broadcasted_iota(jnp.int32, shape, 1)
+    chip = row // sizes.cells % sizes.chips
+    core = (place + row // (sizes.cells * sizes.chips)) % 2
+    x = chip // (sizes.ny // 2) * sizes.cells_x + row // sizes.cells_y % sizes.cells_x
+    y = (chip % (sizes.ny // 2) * 2 + core) * sizes.cells_y + row % sizes.cells_y
+    mode = lane % sizes.half
+    quarter = lane // sizes.half % 2 - lane // (2 * sizes.half) % 2
+    owner = place // 2 * 2 + (place + lane // (4 * sizes.half)) % 2
+    kx = owner * sizes.local_x + mode // sizes.kept_y
+    ky = mode % sizes.kept_y
+    kx = jnp.where(kx < sizes.kept_x // 2, kx, kx - sizes.kept_x)
+    ky = jnp.where(ky < sizes.kept_y // 2, ky, ky - sizes.kept_y)
+    length_x, length_y = sizes.nx * sizes.cells_x, sizes.ny * sizes.cells_y
+    turn = math.lcm(length_x, length_y, 4)
+    phase = jnp.mod(x * kx * (turn // length_x) + y * ky * (turn // length_y) + quarter * (turn // 4), turn)
+    values = jnp.cos(phase.astype(F32) * (2.0 * math.pi / turn)) * (1.0 / math.sqrt(length_x * length_y))
+    return jnp.where(mode < sizes.kept, values, 0.0)
 
 
 class Sizes:
@@ -142,9 +143,51 @@
     return jnp.dot(left, right, preferred_element_type=F32, **kwargs)
 
 
-def depth_forward(sizes, field, table, out, cells):
-    values = gather_cells(field, cells, sizes).astype(BF16)
-    send_modes(dot(values, table[...]), out, sizes)
+def fetch(sources, targets, semaphores):
+    copies = [pltpu.make_async_copy(*pair, semaphores.at[at]) for at, pair in enumerate(zip(sources, targets))]
+    for copy in copies:
+        copy.start()
+    for copy in copies:
+        copy.wait()
+
+
+def depth_forward(sizes, field, table, out, cells, field_here, table_here, semaphores):
+    fetch((field, table), (field_here, table_here), semaphores)
+    values = gather_cells(field_here, cells, sizes).astype(BF16)
+    send_modes(dot(values, table_here[...]), out, sizes)
+
+
+def one_hot(rows, columns, step, along_rows):
+    row = lax.broadcasted_iota(jnp.int32, (rows, columns), 0)
+    column = lax.broadcasted_iota(jnp.int32, (rows, columns), 1)
+    same = row // step == column if along_rows else row == column // step
+    return jnp.where(same, 1.0, 0.0).astype(BF16)
+
+
+def cell_mixer(weights, sizes):
+    count = sizes.channels * sizes.cells
+    left = one_hot(count, sizes.channels, sizes.cells, True)
+    right = one_hot(sizes.channels, count, sizes.cells, False)
+    wide = dot(dot(left, weights).astype(BF16), right)
+    row = lax.broadcasted_iota(jnp.int32, (count, count), 0)
+    column = lax.broadcasted_iota(jnp.int32, (count, count), 1)
+    same = lax.rem(row, sizes.cells) == lax.rem(column, sizes.cells)
+    return jnp.where(same, wide, 0.0).astype(BF16)
+
+
+def prepare(sizes, field, cotangent, turned_weight, bias, inverse, forward, local, cot_cells, inverse_out, forward_out, cells, field_here, cot_here, semaphores):
+    fetch((field, cotangent, inverse, forward), (field_here, cot_here, inverse_out, forward_out), semaphores)
+    values = gather_cells(field_here, cells, sizes).astype(BF16)
+    bypass = dot(cell_mixer(turned_weight[...], sizes), values)
+    for o in range(sizes.channels):
+        rows = slice(o * sizes.cells, (o + 1) * sizes.cells)
+        local[rows, :] = bypass[rows, :] + bias[o]
+    gather_cells(cot_here, cot_cells, sizes)
+
+
+def emit(sizes, pre, signal, weight, layer_out, local):
+    scatter_cells(gelu_parts(pre[...])[0], layer_out, sizes)
+    local[...] = dot(cell_mixer(weight[...], sizes), signal[...])
 
 
 def turn_weights(sizes, source, target):
@@ -172,17 +215,17 @@
     target[:count, :] = both[:count, : 2 * sizes.half] + both[count : 2 * count, 2 * sizes.half :]
 
 
-def plane_cells(sizes, mixed, spread, table, own, other):
-    rows, lanes = mixed.shape
+def plane_cells(sizes, own, other, table, out, spread):
+    rows, lanes = own.shape
     spread[...] = jnp.zeros_like(spread)
-    for s in range(2):
-        spread[s * rows : (s + 1) * rows, s * lanes : (s + 1) * lanes] = mixed[...]
+    for at, ref in enumerate((own, other)):
+        for s in range(2):
+            first = (at * 2 + s) * lanes
+            spread[s * rows : (s + 1) * rows, first : first + lanes] = ref[...]
     cells = lax.dot_general(
         table[...], spread[...], (((1,), (1,)), ((), ())), precision=EXACT, preferred_element_type=F32
     )
-    count = sizes.chips * sizes.cells
-    for at, ref in enumerate((own, other)):
-        ref[...] = cells[at * count : (at + 1) * count, :].reshape(ref.shape)
+    out[...] = cells.reshape(out.shape)
 
 
 def swap_parts(values, sizes):
@@ -197,7 +240,7 @@
     return lax.broadcasted_iota(jnp.int32, (rows, 2 * sizes.half), 1) < sizes.half
 
 
-def mix_forward(sizes, own, other, table, weight, spectra, out_own, out_other, mixed, spread):
+def mix_forward(sizes, own, other, table, weight, spectra, mixed):
     plane_spectra(sizes, own, other, table, spectra)
     real = first_lanes(sizes.rows, sizes)
     for m in range(sizes.modes):
@@ -212,10 +255,9 @@
         imag_part = crossed + swap_parts(crossed, sizes)
         result = jnp.where(real, real_part, imag_part)
         mixed[mode_rows(m, sizes), :] = result[: sizes.channels]
-    plane_cells(sizes, mixed, spread, table, out_own, out_other)
-
-
-def mix_back(sizes, own, other, table, weight, back, out_own, out_other, mixed, spread, spectra):
+
+
+def mix_back(sizes, own, other, table, weight, back, mixed, spectra):
     plane_spectra(sizes, own, other, table, spectra)
     real = first_lanes(sizes.channels, sizes)
     for m in range(sizes.modes):
@@ -234,7 +276,6 @@
         real_part = straight + swap_parts(straight, sizes)
         imag_part = swap_parts(crossed, sizes) - crossed
         mixed[mode_rows(m, sizes), :] = jnp.where(real, real_part, imag_part)
-    plane_cells(sizes, mixed, spread, table, out_own, out_other)
 
 
 def grad_weights(sizes, spectra, back, target):
@@ -247,48 +288,64 @@
         swapped = swap_parts(row, sizes)
         real_part = jnp.where(real, row, swapped)
         imag_part = jnp.where(real, swapped, -row)
-        block = (real_part * rows + imag_part * turned)[: sizes.channels]
+        block = (real_part * rows + imag_part * turned).T
         for s in range(2):
-            part = block[:, s * sizes.half : s * sizes.half + sizes.kept].T
+            part = block[s * sizes.half : s * sizes.half + sizes.kept, : sizes.channels]
             target[0, s, w] = part.reshape(sizes.local_x, sizes.kept_y, sizes.channels)
 
 
-def activate(sizes, received, field, cotangent, inverse, forward, mixer, bias, layer_out, signal_out, out, cells, spectrum):
-    spatial = dot(receive_modes(received, spectrum, sizes), inverse[...], precision=EXACT)
-    values = gather_cells(field, cells, sizes).astype(BF16)
-    pre = spatial + dot(mixer[...], values) + bias[...]
+def gelu_parts(pre):
     slope = math.sqrt(2.0 / math.pi)
     squared = pre * pre
     bend = jnp.tanh(slope * (pre + 0.044715 * (squared * pre)))
-    scatter_cells(0.5 * pre * (1.0 + bend), layer_out, sizes)
+    value = 0.5 * pre * (1.0 + bend)
     derivative = 0.5 * (1.0 + bend) + 0.5 * pre * (1.0 - bend * bend) * (slope * (1.0 + 3.0 * 0.044715 * squared))
-    signal = (gather_cells(cotangent, cells, sizes) * derivative).astype(BF16)
+    return value, derivative
+
+
+def activate(sizes, received, local, cotangent, inverse, forward, pre_out, signal_out, out, spectrum):
+    pre = dot(receive_modes(received, spectrum, sizes), inverse[...], precision=EXACT) + local[...]
+    pre_out[...] = pre
+    signal = (cotangent[...] * gelu_parts(pre)[1]).astype(BF16)
     signal_out[...] = signal
     send_modes(dot(signal, forward[...]), out, sizes)
 
 
-def finish(sizes, received, signal, inverse, mixer, grad_field, spectrum):
+def finish(sizes, received, local, inverse, grad_field, spectrum):
     spatial = dot(receive_modes(received, spectrum, sizes), inverse[...], precision=EXACT)
-    scatter_cells(spatial + dot(mixer[...], signal[...]), grad_field, sizes)
+    scatter_cells(spatial + local[...], grad_field, sizes)
 
 
 def shape_of(shape, dtype=F32):
     return jax.ShapeDtypeStruct(shape, dtype)
 
 
-def whole_call(body, sizes, out_shape, scratch, *args):
+VMEM = pl.BlockSpec(memory_space=pltpu.VMEM)
+SMEM = pl.BlockSpec(memory_space=pltpu.SMEM)
+REMOTE = pl.BlockSpec(memory_space=pl.ANY)
+
+
+def settings(mebibytes):
+    return pltpu.CompilerParams(vmem_limit_bytes=mebibytes * 1024 * 1024)
+
+
+def cost(nanoseconds):
+    return pl.CostEstimate(flops=0, bytes_accessed=3000 * nanoseconds, transcendentals=0)
+
+
+def whole_call(body, sizes, nanoseconds, out_shape, scratch, *args, specs=None):
     def kernel(*refs):
         body(sizes, *refs)
 
-    vmem = pl.BlockSpec(memory_space=pltpu.VMEM)
     return pl.pallas_call(
         kernel,
         out_shape=out_shape,
-        in_specs=[vmem] * len(args),
-        out_specs=jax.tree.map(lambda _: vmem, out_shape),
+        in_specs=specs or [VMEM] * len(args),
+        out_specs=jax.tree.map(lambda _: VMEM, out_shape),
         scratch_shapes=scratch,
         name=body.__name__,
-        compiler_params=pltpu.CompilerParams(vmem_limit_bytes=32 * 1024 * 1024),
+        cost_estimate=cost(nanoseconds),
+        compiler_params=settings(16),
     )(*args)
 
 
@@ -303,9 +360,6 @@
     forward_back = jnp.asarray((ordered.astype(ml_dtypes.bfloat16).astype(np.float32) * doubled).astype(ml_dtypes.bfloat16))
     inverse_back = jnp.asarray(np.ascontiguousarray(ordered.T))
     inverse_first = jnp.asarray(np.ascontiguousarray((ordered * doubled).T))
-    tables = jnp.asarray(plane_table(z.nx, z.ny, z.cells_x, z.cells_y, z.kept_x, z.kept_y, z.half))
-    plane = lax.dynamic_index_in_dim(tables, lax.axis_index("gy"), 0, keepdims=False)
-
     groups = [[gx * z.ny + 2 * y + c for gx in range(z.nx) for y in range(z.ny // 2)] for c in range(2)]
     pairs = [(s, s ^ 1) for s in range(z.ny)]
 
@@ -319,12 +373,24 @@
 
     payload = shape_of((z.chips, z.cells, z.width))
     cell_rows = z.channels * z.cells
-    cells_scratch = pltpu.VMEM((cell_rows, z.depth), F32)
+    cells_shape = (cell_rows, z.depth)
+    cells_scratch = pltpu.VMEM(cells_shape, F32)
     spectrum_scratch = pltpu.VMEM((cell_rows, z.all_modes), F32)
-    mode_rows_count = z.channels * z.modes
-    spectra_shape = (mode_rows_count, 2 * z.half)
-    mixed_scratch = [pltpu.VMEM(spectra_shape, F32), pltpu.VMEM((z.width, 4 * z.half), F32)]
-
+    spectra_shape = (z.channels * z.modes, 2 * z.half)
+    spectra_scratch = pltpu.VMEM(spectra_shape, F32)
+    spread_scratch = pltpu.VMEM((z.width, 8 * z.half), F32)
+    field_scratch = pltpu.VMEM(field.shape, BF16)
+
+    sent = whole_call(
+        depth_forward, z, 1500, payload,
+        [cells_scratch, field_scratch, pltpu.VMEM(forward_first.shape, BF16), pltpu.SemaphoreType.DMA((2,))],
+        field, forward_first, specs=[REMOTE] * 2,
+    )
+
+    sent, field, cotangent, spectral_weight, place = lax.optimization_barrier(
+        (sent, field, cotangent, spectral_weight, lax.axis_index("gy"))
+    )
+    own = exchange(sent)
     native = jnp.transpose(spectral_weight, (0, 1, 2, 4, 5, 3))
     block_in = (1, 2, z.channels, z.local_x, z.kept_y, z.channels)
     block_turned = (1, z.channels, z.rows, 2 * z.half)
@@ -335,34 +401,46 @@
         in_specs=[pl.BlockSpec(block_in, lambda m: (m, 0, 0, 0, 0, 0))],
         out_specs=pl.BlockSpec(block_turned, lambda m: (m, 0, 0, 0)),
         name="turn_weights",
-        compiler_params=pltpu.CompilerParams(vmem_limit_bytes=32 * 1024 * 1024),
+        cost_estimate=cost(5000),
+        compiler_params=settings(56),
     )(native)
-
-    identity = jnp.eye(z.cells, dtype=BF16)
-    mixer_back = jnp.kron(pointwise_weight, identity)
-    mixer_first = jnp.kron(pointwise_weight.T, identity)
-    bias = jnp.repeat(channel_bias, z.cells)[:, None]
-
-    sent = whole_call(depth_forward, z, payload, [cells_scratch], field, forward_first)
+    local, cot_cells, inverse_here, forward_here = whole_call(
+        prepare, z, 2000,
+        (shape_of(cells_shape), shape_of(cells_shape), shape_of(inverse_first.shape), shape_of(forward_back.shape, BF16)),
+        [cells_scratch, field_scratch, field_scratch, pltpu.SemaphoreType.DMA((4,))],
+        field, cotangent, pointwise_weight.T, channel_bias, inverse_first, forward_back,
+        specs=[REMOTE, REMOTE, VMEM, SMEM, REMOTE, REMOTE],
+    )
+    plane = plane_table(z, place, 2, 1)
+    plane_back = plane_table(z, place, 1, 2)
+    own, turned, local, cot_cells, inverse_here, forward_here, plane, plane_back = lax.optimization_barrier(
+        (own, turned, local, cot_cells, inverse_here, forward_here, plane, plane_back)
+    )
+
+    spectra, mixed = whole_call(
+        mix_forward, z, 2000, (shape_of(spectra_shape), shape_of(spectra_shape)), [],
+        own, other_core(own), plane, turned,
+    )
+    sent = whole_call(plane_cells, z, 1000, payload, [spread_scratch], mixed, other_core(mixed), plane_back)
+    returned = exchange(sent)
+    pre, signal, sent = whole_call(
+        activate, z, 2000,
+        (shape_of(cells_shape), shape_of(cells_shape, BF16), payload), [spectrum_scratch],
+        returned, local, cot_cells, inverse_here, forward_here,
+    )
+    sent, pre, signal = lax.optimization_barrier((sent, pre, signal))
     own = exchange(sent)
-    spectra, part_own, part_other = whole_call(
-        mix_forward, z, (shape_of(spectra_shape), payload, payload), mixed_scratch,
+    layer_out, local = whole_call(
+        emit, z, 2000, (shape_of(field.shape, BF16), shape_of(cells_shape)), [], pre, signal, pointwise_weight
+    )
+    own, layer_out, local = lax.optimization_barrier((own, layer_out, local))
+    back, mixed = whole_call(
+        mix_back, z, 2000, (shape_of((z.modes, z.rows, 2 * z.half)), shape_of(spectra_shape)), [spectra_scratch],
         own, other_core(own), plane, turned,
     )
-    returned = exchange(part_own + other_core(part_other))
-    layer_out, signal, sent = whole_call(
-        activate, z,
-        (shape_of(field.shape, BF16), shape_of((cell_rows, z.depth), BF16), payload),
-        [cells_scratch, spectrum_scratch],
-        returned, field, cotangent, inverse_first, forward_back, mixer_first, bias,
-    )
-    own = exchange(sent)
-    back, part_own, part_other = whole_call(
-        mix_back, z, (shape_of((z.modes, z.rows, 2 * z.half)), payload, payload),
-        mixed_scratch + [pltpu.VMEM(spectra_shape, F32)],
-        own, other_core(own), plane, turned,
-    )
-    returned = exchange(part_own + other_core(part_other))
+    sent = whole_call(plane_cells, z, 1000, payload, [spread_scratch], mixed, other_core(mixed), plane_back)
+    sent, back, spectra = lax.optimization_barrier((sent, back, spectra))
+    returned = exchange(sent)
     gradient = pl.pallas_call(
         lambda spectra_ref, back_ref, target: grad_weights(z, spectra_ref, back_ref, target),
         grid=(z.modes,),
@@ -373,10 +451,12 @@
         ],
         out_specs=pl.BlockSpec(block_in, lambda m: (m, 0, 0, 0, 0, 0)),
         name="grad_weights",
-        compiler_params=pltpu.CompilerParams(vmem_limit_bytes=32 * 1024 * 1024),
+        cost_estimate=cost(5000),
+        compiler_params=settings(56),
     )(spectra, back)
+    returned, gradient = lax.optimization_barrier((returned, gradient))
     grad_field = whole_call(
-        finish, z, shape_of(field.shape, BF16), [spectrum_scratch], returned, signal, inverse_back, mixer_back
+        finish, z, 1000, shape_of(field.shape, BF16), [spectrum_scratch], returned, local, inverse_back
     )
     return (layer_out, grad_field, jnp.transpose(gradient, (0, 1, 2, 5, 3, 4)))
 

time: 89.5 us -> 84 us (0.939)
  blocking collectives: 28.4 us -> 15.7 us
  starting transfers between devices: 7.83 us -> 15.8 us
  local copies, waits for them, and re-layouts: 12.5 us -> 5.74 us
  Pallas kernels: 26.1 us -> 30.2 us
  waiting for transfers between devices: 9.56 us -> 12 us
  other arithmetic: 3.79 us -> 2.82 us
    all_to_all x2 -> x1, blocking collectives: 28.4 us -> 15.7 us  [exchange(): lax.all_to_all(payload, ('gx', 'gy'), split_axis=0, concat_axis=0, tiled=...]
    all_to_all x2 -> x3, starting transfers between devices: 7.12 us -> 15.4 us  [exchange(): lax.all_to_all(payload, ('gx', 'gy'), split_axis=0, concat_axis=0, tiled=...]
    pallas_call x1, Pallas kernels: 3 us -> 8.66 us  [on_device(): pl.pallas_call(lambda source, target: turn_weights(z, source, target), gr...]
    pallas_call x1, Pallas kernels: 14.2 us -> 9.53 us  [on_device(): pl.pallas_call(lambda spectra_ref, back_ref, target: grad_weights(z, spec...]
    mul x2 -> x0, local copies, waits for them, and re-layouts: 3.61 us -> none  [the longest x1 1.81 us: on_device(): mixer_back = jnp.kron(pointwise_weight, identity)]
    pallas_call x5 -> x9, Pallas kernels: 8.88 us -> 12 us  [whole_call(): pl.pallas_call(kernel, out_shape=out_shape, in_specs=specs or [VMEM] * le...]
    select_n x0 -> x2, other arithmetic: none -> 2.69 us  [plane_table(): return jnp.where(mode < sizes.kept, values, 0.0)]
    add x2 -> x3, other arithmetic: 2.32 us -> 0.01 us  [the longest x2 0.01 us: plane_table(): row % sizes.cells_y]
  transfers between devices with their start and end apart: 6 -> 7, of which waited for: 4 -> 5; matrix products, arithmetic and copies ran while one was open for 7% -> 4% of each run, Pallas kernels for 19% -> 25%
where the time goes in v1:
time: 84 us; the launch traced here: 83.3 us
  Pallas kernels  30.2 us (36%)
  starting transfers between devices  15.8 us (19%)
  blocking collectives  15.7 us (19%)
  waiting for transfers between devices  12 us (14%)
  local copies, waits for them, and re-layouts  5.74 us (7%)
  other arithmetic  2.82 us (3%)
  between operations  0.97 us (1%)
    all_to_all x1, blocking collectives, exchange(): lax.all_to_all(payload, ('gx', 'gy'), split_axis=0, concat_axis=0, tiled=...  15.7 us
    all_to_all x3, starting transfers between devices, exchange(): lax.all_to_all(payload, ('gx', 'gy'), split_axis=0, concat_axis=0, tiled=...  15.4 us
    pallas_call x9, Pallas kernels, whole_call(): pl.pallas_call(kernel, out_shape=out_shape, in_specs=specs or [VMEM] * le...  12 us
    pallas_call x1, Pallas kernels, on_device(): pl.pallas_call(lambda spectra_ref, back_ref, target: grad_weights(z, spec...  9.53 us
    pallas_call x1, Pallas kernels, on_device(): pl.pallas_call(lambda source, target: turn_weights(z, source, target), gr...  8.66 us
    all_to_all x3, waiting for transfers between devices, exchange(): lax.all_to_all(payload, ('gx', 'gy'), split_axis=0, concat_axis=0, tiled=...  6.87 us
    unnamed x27, local copies, waits for them, and re-layouts  5.74 us
    ppermute x4, waiting for transfers between devices, other_core(): return lax.ppermute(payload, 'gy', pairs)  5.14 us
  transfers between devices with their start and end apart: 7, of which 5 were waited for; matrix products, arithmetic and copies ran while one was open for 4% of the time, Pallas kernels for 25%

profile of v1, /device:TPU:0, one launch (start us, length us, event | category | flops | bytes accessed | tf_op | source)
XLA Modules:
  0.0 83.3 jit_solution(16033801055022808780)
XLA Ops:
  0.6 0.0 copy-start.12
  0.6 0.0 copy-start.2
  0.7 0.9 %copy-done.2 = bf16[20,2,4,512]{3,2,1,0:T(4,128)(2,1)S(1)} copy-done((bf16[20,2,4,512]{3,2,1,0:T(4,128)(2,1)S(1)}, bf16[20,2,4,512]{3,2,1,0:T(4,128)(2,1)}, u32[]{:S(2)}) %copy-start.2) | copy-done | bytes 163864
  1.6 0.0 copy-start.8
  1.6 0.9 %copy-done.8 = bf16[512,128]{1,0:T(8,128)(2,1)S(1)} copy-done((bf16[512,128]{1,0:T(8,128)(2,1)S(1)}, bf16[512,128]{1,0:T(8,128)(2,1)}, u32[]{:S(2)}) %copy-start.8) | copy-done | bytes 131096
  2.5 0.0 copy-start.3
  2.5 0.0 copy-start.4
  2.5 0.0 copy-start.6
  2.5 0.0 copy-start.7
  2.5 0.0 copy-start.11
  2.5 1.6 %depth_forward.1 = f32[16,8,384]{2,1,0:T(8,128)} custom-call(bf16[20,2,4,512]{3,2,1,0:T(4,128)(2,1)S(1)} %copy-done.2, bf16[512,128]{1,0:T(8,128)(2,1)S(1)} %copy-done.8), custom_call_target="tpu_custom_call" | custom-call | bytes 4500000 | tf_op jit(solution)/shard_map/depth_forward/pallas_call | solution.py:340
  4.1 8.3 %all-to-all-start = ((f32[16,8,384]{2,1,0:T(8,128)}), f32[16,8,384]{2,1,0:T(8,128)S(1)}, u32[]{:S(2)}, u32[]{:S(2)}) async-start(f32[16,8,384]{2,1,0:T(8,128)} %depth_forward.1), calls=%async_computation | async-start | bytes 393216 | tf_op jit(solution)/shard_map/all_to_all | solution.py:367
  12.7 0.8 copy.12
  13.5 8.7 %turn_weights.1.refs_3_ = f32[8,20,24,128]{3,2,1,0:T(8,128)} custom-call(f32[8,2,20,4,16,20]{5,4,3,2,1,0:T(8,128)} %bitcast.4), custom_call_target="tpu_custom_call" | custom-call | bytes 15000000 | tf_op jit(solution)/shard_map/turn_weights/pallas_call | solution.py:397
  22.2 0.0 copy-done.12
  22.2 0.0 copy-done.3
  22.2 0.0 copy-done.4
  22.2 0.0 copy-done.6
  22.2 0.0 copy-done.7
  22.2 1.6 %prepare.1 = (f32[160,512]{1,0:T(8,128)S(1)}, f32[160,512]{1,0:T(8,128)S(1)}, f32[128,512]{1,0:T(8,128)S(1)}, bf16[512,128]{1,0:T(8,128)(2,1)S(1)}) custom-call(bf16[20,2,4,512]{3,2,1,0:T(4,128)(2,1)S(1)} %copy-done.3, bf16[20,2,4,512]{3,2,1,0:T(4,128)(2,1)S(1)} %copy-done.6, bf16[20,20]{1,0:T(8,128)(2,1)S(1)} %bitcast.3, f32[20]{0:T(128)S(1)} %copy-done.12, ...), custom_call_target="tpu_custom_call" | custom-call | bytes 6000000 | tf_op jit(solution)/shard_map/prepare/pallas_call | solution.py:340
  23.9 0.0 copy-start.5
  23.9 1.3 %fusion.45.refs_2_ = f32[128,512]{1,0:T(8,128)S(1)} fusion(s32[512]{0:T(512)S(1)} %get-tuple-element.97, s32[512]{0:T(512)S(1)} %get-tuple-element.102, s32[512]{0:T(512)S(1)} %get-tuple-element.98, s32[512]{0:T(512)S(1)} %get-tuple-element.115, s32[128]{0:T(128)S(1)} %get-tuple-element.112, s32[128]{0:T(128)S(1)} %get-tuple-element.117, ...), kind=kLoop, calls=%fused_computation.135 | loop fusion | flops 9895936 | bytes 285192 | tf_op jit(solution)/shard_map/jit(_where)/select_n | solution.py:59
  25.2 1.4 %fusion.22.refs_2_ = f32[256,256]{1,0:T(8,128)S(1)} fusion(s32[256]{0:T(256)S(1)} %get-tuple-element.80, s32[256]{0:T(256)S(1)} %get-tuple-element.93, s32[256]{0:T(256)S(1)} %get-tuple-element.88, s32[256]{0:T(256)S(1)} %get-tuple-element.92, s32[256]{0:T(256)S(1)} %get-tuple-element.78, s32[256]{0:T(256)S(1)} %get-tuple-element.91, ...), kind=kLoop, calls=%fused_computation.112 | loop fusion | flops 9895936 | bytes 278280 | tf_op jit(solution)/shard_map/jit(_where)/select_n | solution.py:59
  26.6 0.0 all-to-all-done.refs_0_
  26.6 0.1 collective-permute-start
  26.7 1.4 %collective-permute-done.refs_1_ = f32[16,8,384]{2,1,0:T(8,128)S(1)} collective-permute-done((f32[16,8,384]{2,1,0:T(8,128)S(1)}, f32[16,8,384]{2,1,0:T(8,128)S(1)}, u32[]{:S(2)}, u32[]{:S(2)}) %collective-permute-start) | collective-permute-done | bytes 196640 | tf_op jit(solution)/shard_map/ppermute | solution.py:372
  28.1 0.0 copy-start
  28.1 1.5 %copy-done = f32[8,20,24,128]{3,2,1,0:T(8,128)S(1)} copy-done((f32[8,20,24,128]{3,2,1,0:T(8,128)S(1)}, f32[8,20,24,128]{3,2,1,0:T(8,128)}, u32[]{:S(2)}) %copy-start) | copy-done | bytes 1966104
  29.7 0.9 %mix_forward.1 = (f32[160,128]{1,0:T(8,128)S(1)}, f32[160,128]{1,0:T(8,128)S(1)}) custom-call(f32[16,8,384]{2,1,0:T(8,128)S(1)} %all-to-all-done.refs_0_, f32[16,8,384]{2,1,0:T(8,128)S(1)} %collective-permute-done.refs_1_, f32[256,256]{1,0:T(8,128)S(1)} %fusion.22.refs_2_, f32[8,20,24,128]{3,2,1,0:T(8,128)S(1)} %copy-done), custom_call_target="tpu_custom_call" | custom-call | bytes 6000000 | tf_op jit(solution)/shard_map/mix_forward/pallas_call | solution.py:340
  30.5 0.0 copy-start.10
  30.5 0.2 collective-permute-start.1
  30.7 1.1 %collective-permute-done.1.refs_1_ = f32[160,128]{1,0:T(8,128)S(1)} collective-permute-done((f32[160,128]{1,0:T(8,128)S(1)}, f32[160,128]{1,0:T(8,128)S(1)}, u32[]{:S(2)}, u32[]{:S(2)}) %collective-permute-start.1) | collective-permute-done | bytes 81952 | tf_op jit(solution)/shard_map/ppermute | solution.py:372
  31.9 0.8 plane_cells.2
  32.7 0.0 copy-done.10
  32.7 15.7 %all_to_all.20.refs_0_ = f32[16,8,384]{2,1,0:T(8,128)S(1)} all-to-all(f32[16,8,384]{2,1,0:T(8,128)S(1)} %plane_cells.2), channel_id=1, replica_groups={{0,2,4,6,8,10,12,14,16,18,20,22,24,26,28,30},{1,3,5,7,9,11,13,15,17,19,..., dimensions={0} | all-to-all | bytes 393216 | tf_op jit(solution)/shard_map/all_to_all | solution.py:367
  48.4 2.0 %activate.1 = (f32[160,512]{1,0:T(8,128)S(1)}, bf16[160,512]{1,0:T(8,128)(2,1)S(1)}, f32[16,8,384]{2,1,0:T(8,128)}) custom-call(f32[16,8,384]{2,1,0:T(8,128)S(1)} %all_to_all.20.refs_0_, f32[160,512]{1,0:T(8,128)S(1)} %get-tuple-element.54.refs_1_, f32[160,512]{1,0:T(8,128)S(1)} %get-tuple-element.55.refs_2_, f32[128,512]{1,0:T(8,128)S(1)} %get-tuple-element.56.refs_3_, ...), custom_call_target="tpu_custom_call" | custom-call | bytes 6000000 | tf_op jit(solution)/shard_map/activate/pallas_call | solution.py:340
  50.3 3.5 %all-to-all-start.2 = ((f32[16,8,384]{2,1,0:T(8,128)}), f32[16,8,384]{2,1,0:T(8,128)S(1)}, u32[]{:S(2)}, u32[]{:S(2)}) async-start(f32[16,8,384]{2,1,0:T(8,128)} %get-tuple-element.61), calls=%async_computation.2 | async-start | bytes 393216 | tf_op jit(solution)/shard_map/all_to_all | solution.py:367
  53.9 0.0 copy-done.11
  53.9 1.2 %emit.1 = (bf16[20,2,4,512]{3,2,1,0:T(4,128)(2,1)}, f32[160,512]{1,0:T(8,128)S(1)}) custom-call(f32[160,512]{1,0:T(8,128)S(1)} %get-tuple-element.62.refs_0_, bf16[160,512]{1,0:T(8,128)(2,1)S(1)} %get-tuple-element.63.refs_1_, bf16[20,20]{1,0:T(8,128)(2,1)S(1)} %copy-done.11), custom_call_target="tpu_custom_call" | custom-call | bytes 6000000 | tf_op jit(solution)/shard_map/emit/pallas_call | solution.py:340
  55.0 6.9 %all-to-all-done.2.refs_0_ = f32[16,8,384]{2,1,0:T(8,128)S(1)} async-done(((f32[16,8,384]{2,1,0:T(8,128)}), f32[16,8,384]{2,1,0:T(8,128)S(1)}, u32[]{:S(2)}, u32[]{:S(2)}) %all-to-all-start.2) | async-done | bytes 196640 | tf_op jit(solution)/shard_map/all_to_all | solution.py:367
  61.9 0.0 collective-permute-start.2
  61.9 1.4 %collective-permute-done.2.refs_1_ = f32[16,8,384]{2,1,0:T(8,128)S(1)} collective-permute-done((f32[16,8,384]{2,1,0:T(8,128)S(1)}, f32[16,8,384]{2,1,0:T(8,128)S(1)}, u32[]{:S(2)}, u32[]{:S(2)}) %collective-permute-start.2) | collective-permute-done | bytes 196640 | tf_op jit(solution)/shard_map/ppermute | solution.py:372
  63.3 0.0 copy-start.1
  63.3 1.5 %copy-done.1 = f32[8,20,24,128]{3,2,1,0:T(8,128)S(1)} copy-done((f32[8,20,24,128]{3,2,1,0:T(8,128)S(1)}, f32[8,20,24,128]{3,2,1,0:T(8,128)}, u32[]{:S(2)}) %copy-start.1) | copy-done | bytes 1966104
  64.9 1.1 %mix_back.1 = (f32[8,24,128]{2,1,0:T(8,128)S(1)}, f32[160,128]{1,0:T(8,128)S(1)}) custom-call(f32[16,8,384]{2,1,0:T(8,128)S(1)} %all-to-all-done.2.refs_0_, f32[16,8,384]{2,1,0:T(8,128)S(1)} %collective-permute-done.2.refs_1_, f32[256,256]{1,0:T(8,128)S(1)} %fusion.22.refs_2_, f32[8,20,24,128]{3,2,1,0:T(8,128)S(1)} %copy-done.1), custom_call_target="tpu_custom_call" | custom-call | bytes 6000000 | tf_op jit(solution)/shard_map/mix_back/pallas_call | solution.py:340
  66.0 0.0 copy-start.9
  66.0 0.2 collective-permute-start.3
  66.1 1.1 %collective-permute-done.3.refs_1_ = f32[160,128]{1,0:T(8,128)S(1)} collective-permute-done((f32[160,128]{1,0:T(8,128)S(1)}, f32[160,128]{1,0:T(8,128)S(1)}, u32[]{:S(2)}, u32[]{:S(2)}) %collective-permute-start.3) | collective-permute-done | bytes 81952 | tf_op jit(solution)/shard_map/ppermute | solution.py:372
  67.3 1.5 %plane_cells.3 = f32[16,8,384]{2,1,0:T(8,128)} custom-call(f32[160,128]{1,0:T(8,128)S(1)} %get-tuple-element.68.refs_0_, f32[160,128]{1,0:T(8,128)S(1)} %collective-permute-done.3.refs_1_, f32[128,512]{1,0:T(8,128)S(1)} %fusion.45.refs_2_), custom_call_target="tpu_custom_call" | custom-call | bytes 3000000 | tf_op jit(solution)/shard_map/plane_cells/pallas_call | solution.py:340
  68.8 3.5 %all-to-all-start.3 = ((f32[16,8,384]{2,1,0:T(8,128)}), f32[16,8,384]{2,1,0:T(8,128)S(1)}, u32[]{:S(2)}, u32[]{:S(2)}) async-start(f32[16,8,384]{2,1,0:T(8,128)} %plane_cells.3), calls=%async_computation.3 | async-start | bytes 393216 | tf_op jit(solution)/shard_map/all_to_all | solution.py:367
  72.3 0.0 copy-done.9
  72.3 9.5 %grad_weights.1 = f32[8,2,20,4,16,20]{5,4,3,2,1,0:T(8,128)} custom-call(f32[160,128]{1,0:T(8,128)} %copy-done.10, f32[8,24,128]{2,1,0:T(8,128)} %copy-done.9), custom_call_target="tpu_custom_call" | custom-call | bytes 15000000 | tf_op jit(solution)/shard_map/grad_weights/pallas_call | solution.py:444
  81.9 0.0 all-to-all-done.3.refs_0_
  81.9 0.0 copy-done.5
  81.9 1.4 %finish.1 = bf16[20,2,4,512]{3,2,1,0:T(4,128)(2,1)} custom-call(f32[16,8,384]{2,1,0:T(8,128)S(1)} %all-to-all-done.3.refs_0_, f32[160,512]{1,0:T(8,128)S(1)} %get-tuple-element.75.refs_1_, f32[128,512]{1,0:T(8,128)S(1)} %copy-done.5), custom_call_target="tpu_custom_call" | custom-call | bytes 3000000 | tf_op jit(solution)/shard_map/finish/pallas_call | solution.py:340
  (23 shorter events, 0.1 us)
Async XLA Ops:
  0.6 21.6 %copy-start.12 = (f32[20]{0:T(128)S(1)}, f32[20]{0:T(128)}, u32[]{:S(2)}) copy-start(f32[20]{0:T(128)} %refs_3_.1) | copy-start | bytes 244
  0.6 0.9 %copy-start.2 = (bf16[20,2,4,512]{3,2,1,0:T(4,128)(2,1)S(1)}, bf16[20,2,4,512]{3,2,1,0:T(4,128)(2,1)}, u32[]{:S(2)}) copy-start(bf16[20,2,4,512]{3,2,1,0:T(4,128)(2,1)} %refs_0_.2) | copy-start | bytes 491524
  1.6 0.9 %copy-start.8 = (bf16[512,128]{1,0:T(8,128)(2,1)S(1)}, bf16[512,128]{1,0:T(8,128)(2,1)}, u32[]{:S(2)}) copy-start(bf16[512,128]{1,0:T(8,128)(2,1)} %constant.351.clone.refs_1_) | copy-start | bytes 393220
  2.5 19.7 %copy-start.3 = (bf16[20,2,4,512]{3,2,1,0:T(4,128)(2,1)S(1)}, bf16[20,2,4,512]{3,2,1,0:T(4,128)(2,1)}, u32[]{:S(2)}) copy-start(bf16[20,2,4,512]{3,2,1,0:T(4,128)(2,1)} %refs_0_.2) | copy-start | bytes 491524
  2.5 19.7 %copy-start.4 = (f32[128,512]{1,0:T(8,128)S(1)}, f32[128,512]{1,0:T(8,128)}, u32[]{:S(2)}) copy-start(f32[128,512]{1,0:T(8,128)} %constant.354.clone.refs_4_) | copy-start | bytes 786436
  2.5 19.7 %copy-start.6 = (bf16[20,2,4,512]{3,2,1,0:T(4,128)(2,1)S(1)}, bf16[20,2,4,512]{3,2,1,0:T(4,128)(2,1)}, u32[]{:S(2)}) copy-start(bf16[20,2,4,512]{3,2,1,0:T(4,128)(2,1)} %refs_1_.1) | copy-start | bytes 491524
  2.5 19.7 %copy-start.7 = (bf16[512,128]{1,0:T(8,128)(2,1)S(1)}, bf16[512,128]{1,0:T(8,128)(2,1)}, u32[]{:S(2)}) copy-start(bf16[512,128]{1,0:T(8,128)(2,1)} %constant.352.clone.refs_5_) | copy-start | bytes 393220
  2.5 51.4 %copy-start.11 = (bf16[20,20]{1,0:T(8,128)(2,1)S(1)}, bf16[20,20]{1,0:T(8,128)(2,1)}, u32[]{:S(2)}) copy-start(bf16[20,20]{1,0:T(8,128)(2,1)} %refs_2_.2) | copy-start | bytes 2404
  4.1 22.5 %all-to-all-start = ((f32[16,8,384]{2,1,0:T(8,128)}), f32[16,8,384]{2,1,0:T(8,128)S(1)}, u32[]{:S(2)}, u32[]{:S(2)}) async-start(f32[16,8,384]{2,1,0:T(8,128)} %depth_forward.1), calls=%async_computation | async-start | bytes 393216 | tf_op jit(solution)/shard_map/all_to_all | solution.py:367
  23.9 58.0 %copy-start.5 = (f32[128,512]{1,0:T(8,128)S(1)}, f32[128,512]{1,0:T(8,128)}, u32[]{:S(2)}) copy-start(f32[128,512]{1,0:T(8,128)} %constant.353.clone.refs_2_) | copy-start | bytes 786436
  26.6 1.5 %collective-permute-start = (f32[16,8,384]{2,1,0:T(8,128)S(1)}, f32[16,8,384]{2,1,0:T(8,128)S(1)}, u32[]{:S(2)}, u32[]{:S(2)}) collective-permute-start(f32[16,8,384]{2,1,0:T(8,128)S(1)} %all-to-all-done.refs_0_), channel_id=1, source_target_pairs={{0,1},{1,0},{2,3},{3,2},{4,5},{5,4},{6,7},{7,6},{8,9},{9,8},{10,11... | collective-permute-start | bytes 589832 | tf_op jit(solution)/shard_map/ppermute | solution.py:372
  28.1 1.5 %copy-start = (f32[8,20,24,128]{3,2,1,0:T(8,128)S(1)}, f32[8,20,24,128]{3,2,1,0:T(8,128)}, u32[]{:S(2)}) copy-start(f32[8,20,24,128]{3,2,1,0:T(8,128)} %turn_weights.1.refs_3_) | copy-start | bytes 5898244
  30.5 2.2 %copy-start.10 = (f32[160,128]{1,0:T(8,128)}, f32[160,128]{1,0:T(8,128)S(1)}, u32[]{:S(2)}) copy-start(f32[160,128]{1,0:T(8,128)S(1)} %get-tuple-element.72.spectra_ref) | copy-start | bytes 245764
  30.5 1.3 %collective-permute-start.1 = (f32[160,128]{1,0:T(8,128)S(1)}, f32[160,128]{1,0:T(8,128)S(1)}, u32[]{:S(2)}, u32[]{:S(2)}) collective-permute-start(f32[160,128]{1,0:T(8,128)S(1)} %get-tuple-element.52.refs_0_), channel_id=1, source_target_pairs={{0,1},{1,0},{2,3},{3,2},{4,5},{5,4},{6,7},{7,6},{8,9},{9,8},{10,11... | collective-permute-start | bytes 245768 | tf_op jit(solution)/shard_map/ppermute | solution.py:372
  50.3 11.6 %all-to-all-start.2 = ((f32[16,8,384]{2,1,0:T(8,128)}), f32[16,8,384]{2,1,0:T(8,128)S(1)}, u32[]{:S(2)}, u32[]{:S(2)}) async-start(f32[16,8,384]{2,1,0:T(8,128)} %get-tuple-element.61), calls=%async_computation.2 | async-start | bytes 393216 | tf_op jit(solution)/shard_map/all_to_all | solution.py:367
  61.9 1.4 %collective-permute-start.2 = (f32[16,8,384]{2,1,0:T(8,128)S(1)}, f32[16,8,384]{2,1,0:T(8,128)S(1)}, u32[]{:S(2)}, u32[]{:S(2)}) collective-permute-start(f32[16,8,384]{2,1,0:T(8,128)S(1)} %all-to-all-done.2.refs_0_), channel_id=1, source_target_pairs={{0,1},{1,0},{2,3},{3,2},{4,5},{5,4},{6,7},{7,6},{8,9},{9,8},{10,11... | collective-permute-start | bytes 589832 | tf_op jit(solution)/shard_map/ppermute | solution.py:372
  63.3 1.5 %copy-start.1 = (f32[8,20,24,128]{3,2,1,0:T(8,128)S(1)}, f32[8,20,24,128]{3,2,1,0:T(8,128)}, u32[]{:S(2)}) copy-start(f32[8,20,24,128]{3,2,1,0:T(8,128)} %turn_weights.1.refs_3_) | copy-start | bytes 5898244
  66.0 6.4 %copy-start.9 = (f32[8,24,128]{2,1,0:T(8,128)}, f32[8,24,128]{2,1,0:T(8,128)S(1)}, u32[]{:S(2)}) copy-start(f32[8,24,128]{2,1,0:T(8,128)S(1)} %get-tuple-element.73.back_ref) | copy-start | bytes 294916
  66.0 1.3 %collective-permute-start.3 = (f32[160,128]{1,0:T(8,128)S(1)}, f32[160,128]{1,0:T(8,128)S(1)}, u32[]{:S(2)}, u32[]{:S(2)}) collective-permute-start(f32[160,128]{1,0:T(8,128)S(1)} %get-tuple-element.68.refs_0_), channel_id=1, source_target_pairs={{0,1},{1,0},{2,3},{3,2},{4,5},{5,4},{6,7},{7,6},{8,9},{9,8},{10,11... | collective-permute-start | bytes 245768 | tf_op jit(solution)/shard_map/ppermute | solution.py:372
  68.8 13.1 %all-to-all-start.3 = ((f32[16,8,384]{2,1,0:T(8,128)}), f32[16,8,384]{2,1,0:T(8,128)S(1)}, u32[]{:S(2)}, u32[]{:S(2)}) async-start(f32[16,8,384]{2,1,0:T(8,128)} %plane_cells.3), calls=%async_computation.3 | async-start | bytes 393216 | tf_op jit(solution)/shard_map/all_to_all | solution.py:367

commit v2 on v1

--- a/solution.py
+++ b/solution.py
@@ -164,21 +164,22 @@
     return jnp.where(same, 1.0, 0.0).astype(BF16)
 
 
-def cell_mixer(weights, sizes):
+def cell_mixer(weights, across, sizes):
     count = sizes.channels * sizes.cells
     left = one_hot(count, sizes.channels, sizes.cells, True)
     right = one_hot(sizes.channels, count, sizes.cells, False)
-    wide = dot(dot(left, weights).astype(BF16), right)
+    tall = lax.dot_general(left, weights, (((1,), (1 if across else 0,)), ((), ())), preferred_element_type=F32)
+    wide = dot(tall.astype(BF16), right)
     row = lax.broadcasted_iota(jnp.int32, (count, count), 0)
     column = lax.broadcasted_iota(jnp.int32, (count, count), 1)
     same = lax.rem(row, sizes.cells) == lax.rem(column, sizes.cells)
     return jnp.where(same, wide, 0.0).astype(BF16)
 
 
-def prepare(sizes, field, cotangent, turned_weight, bias, inverse, forward, local, cot_cells, inverse_out, forward_out, cells, field_here, cot_here, semaphores):
+def prepare(sizes, field, cotangent, weight, bias, inverse, forward, local, cot_cells, inverse_out, forward_out, cells, field_here, cot_here, semaphores):
     fetch((field, cotangent, inverse, forward), (field_here, cot_here, inverse_out, forward_out), semaphores)
     values = gather_cells(field_here, cells, sizes).astype(BF16)
-    bypass = dot(cell_mixer(turned_weight[...], sizes), values)
+    bypass = dot(cell_mixer(weight[...], True, sizes), values)
     for o in range(sizes.channels):
         rows = slice(o * sizes.cells, (o + 1) * sizes.cells)
         local[rows, :] = bypass[rows, :] + bias[o]
@@ -187,23 +188,35 @@
 
 def emit(sizes, pre, signal, weight, layer_out, local):
     scatter_cells(gelu_parts(pre[...])[0], layer_out, sizes)
-    local[...] = dot(cell_mixer(weight[...], sizes), signal[...])
-
-
-def turn_weights(sizes, source, target):
-    pad = jnp.zeros((sizes.rows - sizes.channels, 2 * sizes.half), F32) if sizes.rows > sizes.channels else None
-    for w in range(sizes.channels):
-        if sizes.half > sizes.kept:
-            target[0, w] = jnp.zeros((sizes.rows, 2 * sizes.half), F32)
-        elif pad is not None:
-            target[0, w, sizes.channels :, :] = pad
-        if sizes.half == sizes.kept:
-            block = jnp.concatenate([source[0, s, w].reshape(sizes.kept, sizes.channels) for s in range(2)], 0)
-            target[0, w, : sizes.channels, :] = block.T
-        else:
-            for s in range(2):
-                block = source[0, s, w].reshape(sizes.kept, sizes.channels).T
-                target[0, w, : sizes.channels, s * sizes.half : s * sizes.half + sizes.kept] = block
+    local[...] = dot(cell_mixer(weight[...], False, sizes), signal[...])
+
+
+def turn_weights(sizes, source, after, target, here, semaphores):
+    del after
+    copies = [pltpu.make_async_copy(source.at[at], here.at[at], semaphores.at[at]) for at in range(2 * sizes.modes)]
+    for copy in copies:
+        copy.start()
+    if sizes.half > sizes.kept:
+        target[...] = jnp.zeros_like(target)
+    elif sizes.rows > sizes.channels:
+        target[:, :, sizes.channels :, :] = jnp.zeros(
+            (sizes.modes, sizes.channels, sizes.rows - sizes.channels, 2 * sizes.half), F32
+        )
+
+    def turn(mode, carry):
+        for s in range(2):
+            at = 2 * mode + s
+            pltpu.make_async_copy(source.at[at], here.at[at], semaphores.at[at]).wait()
+        for w in range(sizes.channels):
+            blocks = [here[2 * mode + s, w].reshape(sizes.kept, sizes.channels) for s in range(2)]
+            if sizes.half == sizes.kept:
+                target[mode, w, : sizes.channels, :] = jnp.concatenate(blocks, 0).T
+            else:
+                for s, block in enumerate(blocks):
+                    target[mode, w, : sizes.channels, s * sizes.half : s * sizes.half + sizes.kept] = block.T
+        return carry
+
+    lax.fori_loop(0, sizes.modes, turn, 0)
 
 
 def plane_spectra(sizes, own, other, table, target):
@@ -278,20 +291,31 @@
         mixed[mode_rows(m, sizes), :] = jnp.where(real, real_part, imag_part)
 
 
-def grad_weights(sizes, spectra, back, target):
-    mode = pl.program_id(0)
-    rows = back[0]
-    turned = swap_parts(rows, sizes)
+def grad_weights(sizes, spectra, back, target, here, semaphores):
     real = first_lanes(1, sizes)
-    for w in range(sizes.channels):
-        row = spectra[pl.ds(w * sizes.modes + mode, 1), :]
-        swapped = swap_parts(row, sizes)
-        real_part = jnp.where(real, row, swapped)
-        imag_part = jnp.where(real, swapped, -row)
-        block = (real_part * rows + imag_part * turned).T
+
+    def copy(at):
+        return pltpu.make_async_copy(here.at[at], target.at[at], semaphores.at[at])
+
+    def one_mode(mode, carry):
+        rows = back[mode]
+        turned = swap_parts(rows, sizes)
+        for w in range(sizes.channels):
+            row = spectra[pl.ds(w * sizes.modes + mode, 1), :]
+            swapped = swap_parts(row, sizes)
+            real_part = jnp.where(real, row, swapped)
+            imag_part = jnp.where(real, swapped, -row)
+            block = (real_part * rows + imag_part * turned).T
+            for s in range(2):
+                part = block[s * sizes.half : s * sizes.half + sizes.kept, : sizes.channels]
+                here[2 * mode + s, w] = part.reshape(sizes.local_x, sizes.kept_y, sizes.channels)
         for s in range(2):
-            part = block[s * sizes.half : s * sizes.half + sizes.kept, : sizes.channels]
-            target[0, s, w] = part.reshape(sizes.local_x, sizes.kept_y, sizes.channels)
+            copy(2 * mode + s).start()
+        return carry
+
+    lax.fori_loop(0, sizes.modes, one_mode, 0)
+    for at in range(2 * sizes.modes):
+        copy(at).wait()
 
 
 def gelu_parts(pre):
@@ -333,7 +357,7 @@
     return pl.CostEstimate(flops=0, bytes_accessed=3000 * nanoseconds, transcendentals=0)
 
 
-def whole_call(body, sizes, nanoseconds, out_shape, scratch, *args, specs=None):
+def whole_call(body, sizes, nanoseconds, out_shape, scratch, *args, specs=None, out_specs=None, room=16):
     def kernel(*refs):
         body(sizes, *refs)
 
@@ -341,11 +365,11 @@
         kernel,
         out_shape=out_shape,
         in_specs=specs or [VMEM] * len(args),
-        out_specs=jax.tree.map(lambda _: VMEM, out_shape),
+        out_specs=out_specs or jax.tree.map(lambda _: VMEM, out_shape),
         scratch_shapes=scratch,
         name=body.__name__,
         cost_estimate=cost(nanoseconds),
-        compiler_params=settings(16),
+        compiler_params=settings(room),
     )(*args)
 
 
@@ -381,48 +405,42 @@
     spread_scratch = pltpu.VMEM((z.width, 8 * z.half), F32)
     field_scratch = pltpu.VMEM(field.shape, BF16)
 
+    native = jnp.transpose(spectral_weight, (0, 1, 2, 4, 5, 3))
+    weight_shape = (2 * z.modes,) + native.shape[2:]
+    weight_scratch = [pltpu.VMEM(weight_shape, F32), pltpu.SemaphoreType.DMA((2 * z.modes,))]
+
     sent = whole_call(
         depth_forward, z, 1500, payload,
         [cells_scratch, field_scratch, pltpu.VMEM(forward_first.shape, BF16), pltpu.SemaphoreType.DMA((2,))],
-        field, forward_first, specs=[REMOTE] * 2,
-    )
-
-    sent, field, cotangent, spectral_weight, place = lax.optimization_barrier(
-        (sent, field, cotangent, spectral_weight, lax.axis_index("gy"))
+        field, forward_first, specs=[REMOTE] * 2, room=50,
     )
     own = exchange(sent)
-    native = jnp.transpose(spectral_weight, (0, 1, 2, 4, 5, 3))
-    block_in = (1, 2, z.channels, z.local_x, z.kept_y, z.channels)
-    block_turned = (1, z.channels, z.rows, 2 * z.half)
-    turned = pl.pallas_call(
-        lambda source, target: turn_weights(z, source, target),
-        grid=(z.modes,),
-        out_shape=shape_of((z.modes,) + block_turned[1:]),
-        in_specs=[pl.BlockSpec(block_in, lambda m: (m, 0, 0, 0, 0, 0))],
-        out_specs=pl.BlockSpec(block_turned, lambda m: (m, 0, 0, 0)),
-        name="turn_weights",
-        cost_estimate=cost(5000),
-        compiler_params=settings(56),
-    )(native)
+    turned = whole_call(
+        turn_weights, z, 5000, shape_of((z.modes, z.channels, z.rows, 2 * z.half)), weight_scratch,
+        native.reshape(weight_shape), sent, specs=[REMOTE] * 2, room=50,
+    )
+    own, turned, place = lax.optimization_barrier((own, turned, lax.axis_index("gy")))
+
+    plane = plane_table(z, place, 2, 1)
+    spectra, mixed = whole_call(
+        mix_forward, z, 2000, (shape_of(spectra_shape), shape_of(spectra_shape)), [],
+        own, other_core(own), plane, turned,
+    )
+    mixed, spectra, place = lax.optimization_barrier((mixed, spectra, place))
+    plane_back = plane_table(z, place, 1, 2)
+    sent = whole_call(plane_cells, z, 1000, payload, [spread_scratch], mixed, other_core(mixed), plane_back)
+    sent, field, cotangent = lax.optimization_barrier((sent, field, cotangent))
+    returned = exchange(sent)
     local, cot_cells, inverse_here, forward_here = whole_call(
         prepare, z, 2000,
         (shape_of(cells_shape), shape_of(cells_shape), shape_of(inverse_first.shape), shape_of(forward_back.shape, BF16)),
         [cells_scratch, field_scratch, field_scratch, pltpu.SemaphoreType.DMA((4,))],
-        field, cotangent, pointwise_weight.T, channel_bias, inverse_first, forward_back,
-        specs=[REMOTE, REMOTE, VMEM, SMEM, REMOTE, REMOTE],
-    )
-    plane = plane_table(z, place, 2, 1)
-    plane_back = plane_table(z, place, 1, 2)
-    own, turned, local, cot_cells, inverse_here, forward_here, plane, plane_back = lax.optimization_barrier(
-        (own, turned, local, cot_cells, inverse_here, forward_here, plane, plane_back)
-    )
-
-    spectra, mixed = whole_call(
-        mix_forward, z, 2000, (shape_of(spectra_shape), shape_of(spectra_shape)), [],
-        own, other_core(own), plane, turned,
-    )
-    sent = whole_call(plane_cells, z, 1000, payload, [spread_scratch], mixed, other_core(mixed), plane_back)
-    returned = exchange(sent)
+        field, cotangent, pointwise_weight, channel_bias, inverse_first, forward_back,
+        specs=[REMOTE, REMOTE, VMEM, SMEM, REMOTE, REMOTE], room=50,
+    )
+    returned, local, cot_cells, inverse_here, forward_here = lax.optimization_barrier(
+        (returned, local, cot_cells, inverse_here, forward_here)
+    )
     pre, signal, sent = whole_call(
         activate, z, 2000,
         (shape_of(cells_shape), shape_of(cells_shape, BF16), payload), [spectrum_scratch],
@@ -441,24 +459,14 @@
     sent = whole_call(plane_cells, z, 1000, payload, [spread_scratch], mixed, other_core(mixed), plane_back)
     sent, back, spectra = lax.optimization_barrier((sent, back, spectra))
     returned = exchange(sent)
-    gradient = pl.pallas_call(
-        lambda spectra_ref, back_ref, target: grad_weights(z, spectra_ref, back_ref, target),
-        grid=(z.modes,),
-        out_shape=shape_of(native.shape),
-        in_specs=[
-            pl.BlockSpec(spectra_shape, lambda m: (0, 0)),
-            pl.BlockSpec((1, z.rows, 2 * z.half), lambda m: (m, 0, 0)),
-        ],
-        out_specs=pl.BlockSpec(block_in, lambda m: (m, 0, 0, 0, 0, 0)),
-        name="grad_weights",
-        cost_estimate=cost(5000),
-        compiler_params=settings(56),
-    )(spectra, back)
+    gradient = whole_call(
+        grad_weights, z, 5000, shape_of(weight_shape), weight_scratch, spectra, back, out_specs=REMOTE, room=50
+    )
     returned, gradient = lax.optimization_barrier((returned, gradient))
     grad_field = whole_call(
         finish, z, 1000, shape_of(field.shape, BF16), [spectrum_scratch], returned, local, inverse_back
     )
-    return (layer_out, grad_field, jnp.transpose(gradient, (0, 1, 2, 5, 3, 4)))
+    return (layer_out, grad_field, jnp.transpose(gradient.reshape(native.shape), (0, 1, 2, 5, 3, 4)))
 
 
 def solution(mesh):

time: 84 us -> 76.5 us (0.911)
  blocking collectives: 15.7 us -> 0 us
  waiting for transfers between devices: 12 us -> 17.3 us
  Pallas kernels: 30.2 us -> 25.4 us
  starting transfers between devices: 15.8 us -> 19.9 us
  local copies, waits for them, and re-layouts: 5.74 us -> 9.5 us
    pallas_call x2 -> x0, Pallas kernels: 18.2 us -> none  [the longest x1 9.53 us: on_device(): pl.pallas_call(lambda spectra_ref, back_ref, target: grad_weights(z, spec...]
    all_to_all x1 -> x0, blocking collectives: 15.7 us -> none  [exchange(): lax.all_to_all(payload, ('gx', 'gy'), split_axis=0, concat_axis=0, tiled=...]
    pallas_call x9 -> x11, Pallas kernels: 12 us -> 25.4 us  [whole_call(): pl.pallas_call(kernel, out_shape=out_shape, in_specs=specs or [VMEM] * le...]
    all_to_all x3 -> x4, waiting for transfers between devices: 6.87 us -> 14.7 us  [exchange(): lax.all_to_all(payload, ('gx', 'gy'), split_axis=0, concat_axis=0, tiled=...]
    all_to_all x3 -> x4, starting transfers between devices: 15.4 us -> 19.1 us  [exchange(): lax.all_to_all(payload, ('gx', 'gy'), split_axis=0, concat_axis=0, tiled=...]
    unnamed x27 -> x34, local copies, waits for them, and re-layouts: 5.74 us -> 9.5 us
    ppermute x4, waiting for transfers between devices: 5.14 us -> 2.6 us  [other_core(): return lax.ppermute(payload, 'gy', pairs)]
  transfers between devices with their start and end apart: 7 -> 8, of which waited for: 5 -> 5; matrix products, arithmetic and copies ran while one was open for 4% -> 4% of each run, Pallas kernels for 25% -> 20%
where the time goes in v2:
time: 76.5 us; the launch traced here: 75.8 us
  Pallas kernels  25.4 us (33%)
  starting transfers between devices  19.9 us (26%)
  waiting for transfers between devices  17.3 us (23%)
  local copies, waits for them, and re-layouts  9.5 us (12%)
  other arithmetic  2.8 us (4%)
  between operations  1.01 us (1%)
    pallas_call x11, Pallas kernels, whole_call(): pl.pallas_call(kernel, out_shape=out_shape, in_specs=specs or [VMEM] * le...  25.4 us
    all_to_all x4, starting transfers between devices, exchange(): lax.all_to_all(payload, ('gx', 'gy'), split_axis=0, concat_axis=0, tiled=...  19.1 us
    all_to_all x4, waiting for transfers between devices, exchange(): lax.all_to_all(payload, ('gx', 'gy'), split_axis=0, concat_axis=0, tiled=...  14.7 us
    unnamed x34, local copies, waits for them, and re-layouts  9.5 us
    select_n x2, other arithmetic, plane_table(): return jnp.where(mode < sizes.kept, values, 0.0)  2.67 us
    ppermute x4, waiting for transfers between devices, other_core(): return lax.ppermute(payload, 'gy', pairs)  2.6 us
  transfers between devices with their start and end apart: 8, of which 5 were waited for; matrix products, arithmetic and copies ran while one was open for 4% of the time, Pallas kernels for 20%

profile of v2, /device:TPU:0, one launch (start us, length us, event | category | flops | bytes accessed | tf_op | source)
XLA Modules:
  0.0 75.8 jit_solution(11479606593585501425)
XLA Ops:
  0.6 0.0 copy-start
  0.6 0.9 %copy-done = bf16[20,2,4,512]{3,2,1,0:T(4,128)(2,1)S(1)} copy-done((bf16[20,2,4,512]{3,2,1,0:T(4,128)(2,1)S(1)}, bf16[20,2,4,512]{3,2,1,0:T(4,128)(2,1)}, u32[]{:S(2)}) %copy-start) | copy-done | bytes 163864
  1.5 0.0 copy-start.12
  1.6 0.9 %copy-done.12 = bf16[512,128]{1,0:T(8,128)(2,1)S(1)} copy-done((bf16[512,128]{1,0:T(8,128)(2,1)S(1)}, bf16[512,128]{1,0:T(8,128)(2,1)}, u32[]{:S(2)}) %copy-start.12) | copy-done | bytes 131096
  2.5 0.0 copy-start.1
  2.5 0.0 copy-start.8
  2.5 0.0 copy-start.9
  2.5 0.0 copy-start.15
  2.5 0.0 copy-start.16
  2.5 1.6 %depth_forward.1.refs_1_ = f32[16,8,384]{2,1,0:T(8,128)} custom-call(bf16[20,2,4,512]{3,2,1,0:T(4,128)(2,1)S(1)} %copy-done, bf16[512,128]{1,0:T(8,128)(2,1)S(1)} %copy-done.12), custom_call_target="tpu_custom_call" | custom-call | bytes 4500000 | tf_op jit(solution)/shard_map/depth_forward/pallas_call | solution.py:364
  4.1 8.3 %all-to-all-start = ((f32[16,8,384]{2,1,0:T(8,128)}), f32[16,8,384]{2,1,0:T(8,128)S(1)}, u32[]{:S(2)}, u32[]{:S(2)}) async-start(f32[16,8,384]{2,1,0:T(8,128)} %depth_forward.1.refs_1_), calls=%async_computation | async-start | bytes 393216 | tf_op jit(solution)/shard_map/all_to_all | solution.py:391
  12.7 4.5 %turn_weights.1.refs_3_ = f32[8,20,24,128]{3,2,1,0:T(8,128)S(1)} custom-call(f32[16,20,4,16,20]{4,3,2,1,0:T(8,128)} %bitcast.6, f32[16,8,384]{2,1,0:T(8,128)} %depth_forward.1.refs_1_), custom_call_target="tpu_custom_call" | custom-call | bytes 15000000 | tf_op jit(solution)/shard_map/turn_weights/pallas_call | solution.py:364
  17.2 3.8 %all-to-all-done.refs_0_ = f32[16,8,384]{2,1,0:T(8,128)S(1)} async-done(((f32[16,8,384]{2,1,0:T(8,128)}), f32[16,8,384]{2,1,0:T(8,128)S(1)}, u32[]{:S(2)}, u32[]{:S(2)}) %all-to-all-start) | async-done | bytes 196640 | tf_op jit(solution)/shard_map/all_to_all | solution.py:391
  21.1 0.0 collective-permute-start
  21.1 1.4 %fusion.22.refs_2_ = f32[256,256]{1,0:T(8,128)S(1)} fusion(s32[256]{0:T(256)S(1)} %get-tuple-element.82, s32[256]{0:T(256)S(1)} %get-tuple-element.95, s32[256]{0:T(256)S(1)} %get-tuple-element.90, s32[256]{0:T(256)S(1)} %get-tuple-element.94, s32[256]{0:T(256)S(1)} %get-tuple-element.80, s32[256]{0:T(256)S(1)} %get-tuple-element.93, ...), kind=kLoop, calls=%fused_computation.112 | loop fusion | flops 9895936 | bytes 278280 | tf_op jit(solution)/shard_map/jit(_where)/select_n | solution.py:59
  22.5 0.0 collective-permute-done.refs_1_
  22.5 0.9 %mix_forward.1 = (f32[160,128]{1,0:T(8,128)S(1)}, f32[160,128]{1,0:T(8,128)S(1)}) custom-call(f32[16,8,384]{2,1,0:T(8,128)S(1)} %all-to-all-done.refs_0_, f32[16,8,384]{2,1,0:T(8,128)S(1)} %collective-permute-done.refs_1_, f32[256,256]{1,0:T(8,128)S(1)} %fusion.22.refs_2_, f32[8,20,24,128]{3,2,1,0:T(8,128)S(1)} %turn_weights.1.refs_3_), custom_call_target="tpu_custom_call" | custom-call | bytes 6000000 | tf_op jit(solution)/shard_map/mix_forward/pallas_call | solution.py:364
  23.4 0.0 copy-start.13
  23.4 0.6 collective-permute-start.1
  24.0 1.2 %fusion.45.refs_2_ = f32[128,512]{1,0:T(8,128)S(1)} fusion(s32[512]{0:T(512)S(1)} %get-tuple-element.99, s32[512]{0:T(512)S(1)} %get-tuple-element.104, s32[512]{0:T(512)S(1)} %get-tuple-element.100, s32[512]{0:T(512)S(1)} %get-tuple-element.117, s32[128]{0:T(128)S(1)} %get-tuple-element.114, s32[128]{0:T(128)S(1)} %get-tuple-element.119, ...), kind=kLoop, calls=%fused_computation.135 | loop fusion | flops 9895936 | bytes 285192 | tf_op jit(solution)/shard_map/jit(_where)/select_n | solution.py:59
  25.2 0.0 collective-permute-done.1.refs_1_
  25.2 1.5 %plane_cells.2 = f32[16,8,384]{2,1,0:T(8,128)} custom-call(f32[160,128]{1,0:T(8,128)S(1)} %get-tuple-element.46.refs_0_, f32[160,128]{1,0:T(8,128)S(1)} %collective-permute-done.1.refs_1_, f32[128,512]{1,0:T(8,128)S(1)} %fusion.45.refs_2_), custom_call_target="tpu_custom_call" | custom-call | bytes 3000000 | tf_op jit(solution)/shard_map/plane_cells/pallas_call | solution.py:364
  26.7 0.0 copy-done.13
  26.7 3.5 %all-to-all-start.1 = ((f32[16,8,384]{2,1,0:T(8,128)}), f32[16,8,384]{2,1,0:T(8,128)S(1)}, u32[]{:S(2)}, u32[]{:S(2)}) async-start(f32[16,8,384]{2,1,0:T(8,128)} %plane_cells.2), calls=%async_computation.1 | async-start | bytes 393216 | tf_op jit(solution)/shard_map/all_to_all | solution.py:391
  30.3 0.0 copy-done.1
  30.3 0.0 copy-done.8
  30.3 0.0 copy-done.9
  30.3 0.0 copy-done.15
  30.3 0.0 copy-done.16
  30.3 0.0 copy-start.6
  30.3 0.9 %copy-done.6 = f32[128,512]{1,0:T(8,128)S(1)} copy-done((f32[128,512]{1,0:T(8,128)S(1)}, f32[128,512]{1,0:T(8,128)}, u32[]{:S(2)}) %copy-start.6) | copy-done | bytes 262168
  31.3 1.7 %prepare.1 = (f32[160,512]{1,0:T(8,128)S(1)}, f32[160,512]{1,0:T(8,128)S(1)}, f32[128,512]{1,0:T(8,128)S(1)}, bf16[512,128]{1,0:T(8,128)(2,1)S(1)}) custom-call(bf16[20,2,4,512]{3,2,1,0:T(4,128)(2,1)S(1)} %copy-done.1, bf16[20,2,4,512]{3,2,1,0:T(4,128)(2,1)S(1)} %copy-done.8, bf16[20,20]{1,0:T(8,128)(2,1)S(1)} %copy-done.15, f32[20]{0:T(128)S(1)} %copy-done.16, ...), custom_call_target="tpu_custom_call" | custom-call | bytes 6000000 | tf_op jit(solution)/shard_map/prepare/pallas_call | solution.py:364
  32.9 0.0 copy-start.2
  32.9 0.7 copy-done.2
  33.7 0.0 copy-start.4
  33.7 0.7 copy-done.4
  34.3 0.0 copy-start.10
  34.3 0.7 copy-done.10
  35.0 3.9 %all-to-all-done.1.refs_0_ = f32[16,8,384]{2,1,0:T(8,128)S(1)} async-done(((f32[16,8,384]{2,1,0:T(8,128)}), f32[16,8,384]{2,1,0:T(8,128)S(1)}, u32[]{:S(2)}, u32[]{:S(2)}) %all-to-all-start.1) | async-done | bytes 196640 | tf_op jit(solution)/shard_map/all_to_all | solution.py:391
  38.9 0.0 copy-start.3
  38.9 1.0 %copy-done.3 = f32[160,512]{1,0:T(8,128)S(1)} copy-done((f32[160,512]{1,0:T(8,128)S(1)}, f32[160,512]{1,0:T(8,128)}, u32[]{:S(2)}) %copy-start.3) | copy-done | bytes 327704
  39.9 0.0 copy-start.5
  39.9 0.9 %copy-done.5 = f32[128,512]{1,0:T(8,128)S(1)} copy-done((f32[128,512]{1,0:T(8,128)S(1)}, f32[128,512]{1,0:T(8,128)}, u32[]{:S(2)}) %copy-start.5) | copy-done | bytes 262168
  40.8 0.0 copy-start.11
  40.8 0.9 %copy-done.11 = bf16[512,128]{1,0:T(8,128)(2,1)S(1)} copy-done((bf16[512,128]{1,0:T(8,128)(2,1)S(1)}, bf16[512,128]{1,0:T(8,128)(2,1)}, u32[]{:S(2)}) %copy-start.11) | copy-done | bytes 131096
  41.8 2.0 %activate.1 = (f32[160,512]{1,0:T(8,128)S(1)}, bf16[160,512]{1,0:T(8,128)(2,1)S(1)}, f32[16,8,384]{2,1,0:T(8,128)}) custom-call(f32[16,8,384]{2,1,0:T(8,128)S(1)} %all-to-all-done.1.refs_0_, f32[160,512]{1,0:T(8,128)S(1)} %get-tuple-element.56.refs_1_, f32[160,512]{1,0:T(8,128)S(1)} %copy-done.3, f32[128,512]{1,0:T(8,128)S(1)} %copy-done.5, ...), custom_call_target="tpu_custom_call" | custom-call | bytes 6000000 | tf_op jit(solution)/shard_map/activate/pallas_call | solution.py:364
  43.7 3.7 %all-to-all-start.2 = ((f32[16,8,384]{2,1,0:T(8,128)}), f32[16,8,384]{2,1,0:T(8,128)S(1)}, u32[]{:S(2)}, u32[]{:S(2)}) async-start(f32[16,8,384]{2,1,0:T(8,128)} %get-tuple-element.63), calls=%async_computation.2 | async-start | bytes 393216 | tf_op jit(solution)/shard_map/all_to_all | solution.py:391
  47.5 1.2 %emit.1 = (bf16[20,2,4,512]{3,2,1,0:T(4,128)(2,1)}, f32[160,512]{1,0:T(8,128)S(1)}) custom-call(f32[160,512]{1,0:T(8,128)S(1)} %get-tuple-element.64.refs_0_, bf16[160,512]{1,0:T(8,128)(2,1)S(1)} %get-tuple-element.65.refs_1_, bf16[20,20]{1,0:T(8,128)(2,1)S(1)} %copy-done.15), custom_call_target="tpu_custom_call" | custom-call | bytes 6000000 | tf_op jit(solution)/shard_map/emit/pallas_call | solution.py:364
  48.6 6.9 %all-to-all-done.2.refs_0_ = f32[16,8,384]{2,1,0:T(8,128)S(1)} async-done(((f32[16,8,384]{2,1,0:T(8,128)}), f32[16,8,384]{2,1,0:T(8,128)S(1)}, u32[]{:S(2)}, u32[]{:S(2)}) %all-to-all-start.2) | async-done | bytes 196640 | tf_op jit(solution)/shard_map/all_to_all | solution.py:391
  55.5 0.0 collective-permute-start.2
  55.5 1.4 %collective-permute-done.2.refs_1_ = f32[16,8,384]{2,1,0:T(8,128)S(1)} collective-permute-done((f32[16,8,384]{2,1,0:T(8,128)S(1)}, f32[16,8,384]{2,1,0:T(8,128)S(1)}, u32[]{:S(2)}, u32[]{:S(2)}) %collective-permute-start.2) | collective-permute-done | bytes 196640 | tf_op jit(solution)/shard_map/ppermute | solution.py:396
  57.0 1.1 %mix_back.1 = (f32[8,24,128]{2,1,0:T(8,128)S(1)}, f32[160,128]{1,0:T(8,128)S(1)}) custom-call(f32[16,8,384]{2,1,0:T(8,128)S(1)} %all-to-all-done.2.refs_0_, f32[16,8,384]{2,1,0:T(8,128)S(1)} %collective-permute-done.2.refs_1_, f32[256,256]{1,0:T(8,128)S(1)} %fusion.22.refs_2_, f32[8,20,24,128]{3,2,1,0:T(8,128)S(1)} %turn_weights.1.refs_3_), custom_call_target="tpu_custom_call" | custom-call | bytes 6000000 | tf_op jit(solution)/shard_map/mix_back/pallas_call | solution.py:364
  58.0 0.2 collective-permute-start.3
  58.2 1.1 %collective-permute-done.3.refs_1_ = f32[160,128]{1,0:T(8,128)S(1)} collective-permute-done((f32[160,128]{1,0:T(8,128)S(1)}, f32[160,128]{1,0:T(8,128)S(1)}, u32[]{:S(2)}, u32[]{:S(2)}) %collective-permute-start.3) | collective-permute-done | bytes 81952 | tf_op jit(solution)/shard_map/ppermute | solution.py:396
  59.4 1.5 %plane_cells.3 = f32[16,8,384]{2,1,0:T(8,128)} custom-call(f32[160,128]{1,0:T(8,128)S(1)} %get-tuple-element.70.refs_0_, f32[160,128]{1,0:T(8,128)S(1)} %collective-permute-done.3.refs_1_, f32[128,512]{1,0:T(8,128)S(1)} %fusion.45.refs_2_), custom_call_target="tpu_custom_call" | custom-call | bytes 3000000 | tf_op jit(solution)/shard_map/plane_cells/pallas_call | solution.py:364
  60.9 3.6 %all-to-all-start.3 = ((f32[16,8,384]{2,1,0:T(8,128)}), f32[16,8,384]{2,1,0:T(8,128)S(1)}, u32[]{:S(2)}, u32[]{:S(2)}) async-start(f32[16,8,384]{2,1,0:T(8,128)} %plane_cells.3), calls=%async_computation.3 | async-start | bytes 393216 | tf_op jit(solution)/shard_map/all_to_all | solution.py:391
  64.4 0.0 copy-start.14
  64.4 0.9 %copy-done.14 = f32[160,128]{1,0:T(8,128)S(1)} copy-done((f32[160,128]{1,0:T(8,128)S(1)}, f32[160,128]{1,0:T(8,128)}, u32[]{:S(2)}) %copy-start.14) | copy-done | bytes 81944
  65.3 8.2 %grad_weights.1 = f32[16,20,4,16,20]{4,3,2,1,0:T(8,128)} custom-call(f32[160,128]{1,0:T(8,128)S(1)} %copy-done.14, f32[8,24,128]{2,1,0:T(8,128)S(1)} %get-tuple-element.75.refs_1_), custom_call_target="tpu_custom_call" | custom-call | bytes 15000000 | tf_op jit(solution)/shard_map/grad_weights/pallas_call | solution.py:364
  73.5 0.0 all-to-all-done.3.refs_0_
  73.5 0.0 copy-start.7
  73.5 0.9 %copy-done.7 = f32[128,512]{1,0:T(8,128)S(1)} copy-done((f32[128,512]{1,0:T(8,128)S(1)}, f32[128,512]{1,0:T(8,128)}, u32[]{:S(2)}) %copy-start.7) | copy-done | bytes 262168
  74.5 1.4 %finish.1 = bf16[20,2,4,512]{3,2,1,0:T(4,128)(2,1)} custom-call(f32[16,8,384]{2,1,0:T(8,128)S(1)} %all-to-all-done.3.refs_0_, f32[160,512]{1,0:T(8,128)S(1)} %get-tuple-element.77.refs_1_, f32[128,512]{1,0:T(8,128)S(1)} %copy-done.7), custom_call_target="tpu_custom_call" | custom-call | bytes 3000000 | tf_op jit(solution)/shard_map/finish/pallas_call | solution.py:364
  (23 shorter events, 0.1 us)
Async XLA Ops:
  0.6 0.9 %copy-start = (bf16[20,2,4,512]{3,2,1,0:T(4,128)(2,1)S(1)}, bf16[20,2,4,512]{3,2,1,0:T(4,128)(2,1)}, u32[]{:S(2)}) copy-start(bf16[20,2,4,512]{3,2,1,0:T(4,128)(2,1)} %refs_0_.2) | copy-start | bytes 491524
  1.5 0.9 %copy-start.12 = (bf16[512,128]{1,0:T(8,128)(2,1)S(1)}, bf16[512,128]{1,0:T(8,128)(2,1)}, u32[]{:S(2)}) copy-start(bf16[512,128]{1,0:T(8,128)(2,1)} %constant.356.clone.refs_1_) | copy-start | bytes 393220
  2.5 27.8 %copy-start.1 = (bf16[20,2,4,512]{3,2,1,0:T(4,128)(2,1)S(1)}, bf16[20,2,4,512]{3,2,1,0:T(4,128)(2,1)}, u32[]{:S(2)}) copy-start(bf16[20,2,4,512]{3,2,1,0:T(4,128)(2,1)} %refs_0_.2) | copy-start | bytes 491524
  2.5 27.8 %copy-start.8 = (bf16[20,2,4,512]{3,2,1,0:T(4,128)(2,1)S(1)}, bf16[20,2,4,512]{3,2,1,0:T(4,128)(2,1)}, u32[]{:S(2)}) copy-start(bf16[20,2,4,512]{3,2,1,0:T(4,128)(2,1)} %refs_1_.1) | copy-start | bytes 491524
  2.5 27.8 %copy-start.9 = (bf16[512,128]{1,0:T(8,128)(2,1)S(1)}, bf16[512,128]{1,0:T(8,128)(2,1)}, u32[]{:S(2)}) copy-start(bf16[512,128]{1,0:T(8,128)(2,1)} %constant.357.clone.refs_5_) | copy-start | bytes 393220
  2.5 27.8 %copy-start.15 = (bf16[20,20]{1,0:T(8,128)(2,1)S(1)}, bf16[20,20]{1,0:T(8,128)(2,1)}, u32[]{:S(2)}) copy-start(bf16[20,20]{1,0:T(8,128)(2,1)} %refs_2_.4) | copy-start | bytes 2404
  2.5 27.8 %copy-start.16 = (f32[20]{0:T(128)S(1)}, f32[20]{0:T(128)}, u32[]{:S(2)}) copy-start(f32[20]{0:T(128)} %refs_3_.1) | copy-start | bytes 244
  4.1 17.0 %all-to-all-start = ((f32[16,8,384]{2,1,0:T(8,128)}), f32[16,8,384]{2,1,0:T(8,128)S(1)}, u32[]{:S(2)}, u32[]{:S(2)}) async-start(f32[16,8,384]{2,1,0:T(8,128)} %depth_forward.1.refs_1_), calls=%async_computation | async-start | bytes 393216 | tf_op jit(solution)/shard_map/all_to_all | solution.py:391
  21.1 1.4 %collective-permute-start = (f32[16,8,384]{2,1,0:T(8,128)S(1)}, f32[16,8,384]{2,1,0:T(8,128)S(1)}, u32[]{:S(2)}, u32[]{:S(2)}) collective-permute-start(f32[16,8,384]{2,1,0:T(8,128)S(1)} %all-to-all-done.refs_0_), channel_id=1, source_target_pairs={{0,1},{1,0},{2,3},{3,2},{4,5},{5,4},{6,7},{7,6},{8,9},{9,8},{10,11... | collective-permute-start | bytes 589832 | tf_op jit(solution)/shard_map/ppermute | solution.py:396
  23.4 3.4 %copy-start.13 = (f32[160,128]{1,0:T(8,128)}, f32[160,128]{1,0:T(8,128)S(1)}, u32[]{:S(2)}) copy-start(f32[160,128]{1,0:T(8,128)S(1)} %get-tuple-element.74.refs_0_) | copy-start | bytes 245764
  23.4 1.8 %collective-permute-start.1 = (f32[160,128]{1,0:T(8,128)S(1)}, f32[160,128]{1,0:T(8,128)S(1)}, u32[]{:S(2)}, u32[]{:S(2)}) collective-permute-start(f32[160,128]{1,0:T(8,128)S(1)} %get-tuple-element.46.refs_0_), channel_id=1, source_target_pairs={{0,1},{1,0},{2,3},{3,2},{4,5},{5,4},{6,7},{7,6},{8,9},{9,8},{10,11... | collective-permute-start | bytes 245768 | tf_op jit(solution)/shard_map/ppermute | solution.py:396
  26.7 12.2 %all-to-all-start.1 = ((f32[16,8,384]{2,1,0:T(8,128)}), f32[16,8,384]{2,1,0:T(8,128)S(1)}, u32[]{:S(2)}, u32[]{:S(2)}) async-start(f32[16,8,384]{2,1,0:T(8,128)} %plane_cells.2), calls=%async_computation.1 | async-start | bytes 393216 | tf_op jit(solution)/shard_map/all_to_all | solution.py:391
  30.3 1.0 %copy-start.6 = (f32[128,512]{1,0:T(8,128)S(1)}, f32[128,512]{1,0:T(8,128)}, u32[]{:S(2)}) copy-start(f32[128,512]{1,0:T(8,128)} %constant.359.clone.refs_4_) | copy-start | bytes 786436
  32.9 0.7 copy-start.2
  33.7 0.7 copy-start.4
  34.3 0.7 copy-start.10
  38.9 1.0 %copy-start.3 = (f32[160,512]{1,0:T(8,128)S(1)}, f32[160,512]{1,0:T(8,128)}, u32[]{:S(2)}) copy-start(f32[160,512]{1,0:T(8,128)} %copy-done.2) | copy-start | bytes 983044
  39.9 0.9 %copy-start.5 = (f32[128,512]{1,0:T(8,128)S(1)}, f32[128,512]{1,0:T(8,128)}, u32[]{:S(2)}) copy-start(f32[128,512]{1,0:T(8,128)} %copy-done.4) | copy-start | bytes 786436
  40.8 0.9 %copy-start.11 = (bf16[512,128]{1,0:T(8,128)(2,1)S(1)}, bf16[512,128]{1,0:T(8,128)(2,1)}, u32[]{:S(2)}) copy-start(bf16[512,128]{1,0:T(8,128)(2,1)} %copy-done.10) | copy-start | bytes 393220
  43.7 11.8 %all-to-all-start.2 = ((f32[16,8,384]{2,1,0:T(8,128)}), f32[16,8,384]{2,1,0:T(8,128)S(1)}, u32[]{:S(2)}, u32[]{:S(2)}) async-start(f32[16,8,384]{2,1,0:T(8,128)} %get-tuple-element.63), calls=%async_computation.2 | async-start | bytes 393216 | tf_op jit(solution)/shard_map/all_to_all | solution.py:391
  55.5 1.4 %collective-permute-start.2 = (f32[16,8,384]{2,1,0:T(8,128)S(1)}, f32[16,8,384]{2,1,0:T(8,128)S(1)}, u32[]{:S(2)}, u32[]{:S(2)}) collective-permute-start(f32[16,8,384]{2,1,0:T(8,128)S(1)} %all-to-all-done.2.refs_0_), channel_id=1, source_target_pairs={{0,1},{1,0},{2,3},{3,2},{4,5},{5,4},{6,7},{7,6},{8,9},{9,8},{10,11... | collective-permute-start | bytes 589832 | tf_op jit(solution)/shard_map/ppermute | solution.py:396
  58.0 1.3 %collective-permute-start.3 = (f32[160,128]{1,0:T(8,128)S(1)}, f32[160,128]{1,0:T(8,128)S(1)}, u32[]{:S(2)}, u32[]{:S(2)}) collective-permute-start(f32[160,128]{1,0:T(8,128)S(1)} %get-tuple-element.70.refs_0_), channel_id=1, source_target_pairs={{0,1},{1,0},{2,3},{3,2},{4,5},{5,4},{6,7},{7,6},{8,9},{9,8},{10,11... | collective-permute-start | bytes 245768 | tf_op jit(solution)/shard_map/ppermute | solution.py:396
  60.9 12.6 %all-to-all-start.3 = ((f32[16,8,384]{2,1,0:T(8,128)}), f32[16,8,384]{2,1,0:T(8,128)S(1)}, u32[]{:S(2)}, u32[]{:S(2)}) async-start(f32[16,8,384]{2,1,0:T(8,128)} %plane_cells.3), calls=%async_computation.3 | async-start | bytes 393216 | tf_op jit(solution)/shard_map/all_to_all | solution.py:391
  64.4 0.9 %copy-start.14 = (f32[160,128]{1,0:T(8,128)S(1)}, f32[160,128]{1,0:T(8,128)}, u32[]{:S(2)}) copy-start(f32[160,128]{1,0:T(8,128)} %copy-done.13) | copy-start | bytes 245764
  73.5 1.0 %copy-start.7 = (f32[128,512]{1,0:T(8,128)S(1)}, f32[128,512]{1,0:T(8,128)}, u32[]{:S(2)}) copy-start(f32[128,512]{1,0:T(8,128)} %constant.358.clone.refs_2_) | copy-start | bytes 786436

commit v3 on v2

--- a/solution.py
+++ b/solution.py
@@ -37,26 +37,20 @@
     return np.stack([np.cos(angles) * factor, -np.sin(angles) * factor], axis=1).astype(np.float32)
 
 
-def plane_table(sizes, place, cores, owners):
-    shape = (cores * sizes.chips * sizes.cells, owners * 4 * sizes.half)
-    row = lax.broadcasted_iota(jnp.int32, shape, 0)
-    lane = lax.broadcasted_iota(jnp.int32, shape, 1)
-    chip = row // sizes.cells % sizes.chips
-    core = (place + row // (sizes.cells * sizes.chips)) % 2
-    x = chip // (sizes.ny // 2) * sizes.cells_x + row // sizes.cells_y % sizes.cells_x
-    y = (chip % (sizes.ny // 2) * 2 + core) * sizes.cells_y + row % sizes.cells_y
+def plane_factors(sizes):
+    length_x, length_y = sizes.nx * sizes.cells_x, sizes.ny * sizes.cells_y
+    lane = np.arange(4 * sizes.half)
     mode = lane % sizes.half
-    quarter = lane // sizes.half % 2 - lane // (2 * sizes.half) % 2
-    owner = place // 2 * 2 + (place + lane // (4 * sizes.half)) % 2
-    kx = owner * sizes.local_x + mode // sizes.kept_y
-    ky = mode % sizes.kept_y
-    kx = jnp.where(kx < sizes.kept_x // 2, kx, kx - sizes.kept_x)
-    ky = jnp.where(ky < sizes.kept_y // 2, ky, ky - sizes.kept_y)
-    length_x, length_y = sizes.nx * sizes.cells_x, sizes.ny * sizes.cells_y
-    turn = math.lcm(length_x, length_y, 4)
-    phase = jnp.mod(x * kx * (turn // length_x) + y * ky * (turn // length_y) + quarter * (turn // 4), turn)
-    values = jnp.cos(phase.astype(F32) * (2.0 * math.pi / turn)) * (1.0 / math.sqrt(length_x * length_y))
-    return jnp.where(mode < sizes.kept, values, 0.0)
+    quarter = lane // sizes.half % 2 - lane // (2 * sizes.half)
+    inside = mode < sizes.kept
+    kx = np.arange(sizes.ny)[:, None] * sizes.local_x + np.where(inside, mode // sizes.kept_y, 0)
+    turn_x = np.mod(np.arange(length_x)[:, None] * frequencies(sizes.kept_x)[kx][:, None, :], length_x) / length_x
+    turn_y = np.mod(np.arange(length_y)[:, None] * frequencies(sizes.kept_y)[mode % sizes.kept_y], length_y) / length_y
+    angle_x, angle_y = 2.0 * math.pi * turn_x, 2.0 * math.pi * (turn_y + quarter / 4.0)
+    scale = inside / math.sqrt(length_x * length_y)
+    factors_x = np.concatenate([np.cos(angle_x), -np.sin(angle_x)], -1)
+    factors_y = np.concatenate([np.cos(angle_y) * scale, np.sin(angle_y) * scale], -1)
+    return factors_x.astype(np.float32), factors_y.astype(np.float32)
 
 
 class Sizes:
@@ -186,16 +180,54 @@
     gather_cells(cot_here, cot_cells, sizes)
 
 
-def emit(sizes, pre, signal, weight, layer_out, local):
+def emit(sizes, pre, signal, weight, inverse, layer_out, local, inverse_out, semaphore):
+    copy = pltpu.make_async_copy(inverse, inverse_out, semaphore.at[0])
+    copy.start()
     scatter_cells(gelu_parts(pre[...])[0], layer_out, sizes)
     local[...] = dot(cell_mixer(weight[...], False, sizes), signal[...])
-
-
-def turn_weights(sizes, source, after, target, here, semaphores):
+    copy.wait()
+
+
+def plane_tables(sizes, place, mine, other, factors_y, table, back):
+    half_rows = sizes.chips * sizes.cells
+    lanes = 4 * sizes.half
+
+    def chosen(rows, length, index):
+        column = lax.broadcasted_iota(jnp.int32, (rows, length), 1)
+        return jnp.where(column == index(lax.broadcasted_iota(jnp.int32, (rows, length), 0)), 1.0, 0.0)
+
+    def at_x(row):
+        chip = lax.rem(row // sizes.cells, sizes.chips)
+        return chip // (sizes.ny // 2) * sizes.cells_x + lax.rem(row // sizes.cells_y, sizes.cells_x)
+
+    def at_y(row):
+        chip = lax.rem(row // sizes.cells, sizes.chips)
+        core = lax.rem(place + row // half_rows, 2)
+        return (lax.rem(chip, sizes.ny // 2) * 2 + core) * sizes.cells_y + lax.rem(row, sizes.cells_y)
+
+    def product(left, right):
+        return left[:, :lanes] * right[:, :lanes] + left[:, lanes:] * right[:, lanes:]
+
+    pick_x = chosen(2 * half_rows, sizes.nx * sizes.cells_x, at_x)
+    pick_y = chosen(2 * half_rows, sizes.ny * sizes.cells_y, at_y)
+    spread_y = dot(pick_y, factors_y[...], precision=EXACT)
+    table[...] = product(dot(pick_x, mine[...], precision=EXACT), spread_y)
+    back[:, :lanes] = table[:half_rows, :]
+    back[:, lanes:] = product(dot(pick_x[:half_rows], other[...], precision=EXACT), spread_y[:half_rows])
+
+
+def turn_weights(sizes, source, after, place, factors_x, factors_y, target, table, back, here, mine, other, mine_y, semaphores, small):
     del after
+    place = place[0]
+    pair = place + 1 - 2 * lax.rem(place, 2)
+    moves = ((factors_x.at[place], mine), (factors_x.at[pair], other), (factors_y, mine_y))
+    tables = [pltpu.make_async_copy(*move, small.at[at]) for at, move in enumerate(moves)]
     copies = [pltpu.make_async_copy(source.at[at], here.at[at], semaphores.at[at]) for at in range(2 * sizes.modes)]
-    for copy in copies:
+    for copy in tables + copies:
         copy.start()
+    for copy in tables:
+        copy.wait()
+    plane_tables(sizes, place, mine, other, mine_y, table, back)
     if sizes.half > sizes.kept:
         target[...] = jnp.zeros_like(target)
     elif sizes.rows > sizes.channels:
@@ -346,7 +378,7 @@
 
 VMEM = pl.BlockSpec(memory_space=pltpu.VMEM)
 SMEM = pl.BlockSpec(memory_space=pltpu.SMEM)
-REMOTE = pl.BlockSpec(memory_space=pl.ANY)
+HBM = pl.BlockSpec(memory_space=pltpu.HBM)
 
 
 def settings(mebibytes):
@@ -409,62 +441,75 @@
     weight_shape = (2 * z.modes,) + native.shape[2:]
     weight_scratch = [pltpu.VMEM(weight_shape, F32), pltpu.SemaphoreType.DMA((2 * z.modes,))]
 
+    factors_x, factors_y = plane_factors(z)
+    half_rows = z.chips * z.cells
+
     sent = whole_call(
         depth_forward, z, 1500, payload,
         [cells_scratch, field_scratch, pltpu.VMEM(forward_first.shape, BF16), pltpu.SemaphoreType.DMA((2,))],
-        field, forward_first, specs=[REMOTE] * 2, room=50,
+        field, forward_first, specs=[HBM] * 2,
     )
     own = exchange(sent)
-    turned = whole_call(
-        turn_weights, z, 5000, shape_of((z.modes, z.channels, z.rows, 2 * z.half)), weight_scratch,
-        native.reshape(weight_shape), sent, specs=[REMOTE] * 2, room=50,
-    )
-    own, turned, place = lax.optimization_barrier((own, turned, lax.axis_index("gy")))
-
-    plane = plane_table(z, place, 2, 1)
-    spectra, mixed = whole_call(
-        mix_forward, z, 2000, (shape_of(spectra_shape), shape_of(spectra_shape)), [],
-        own, other_core(own), plane, turned,
-    )
-    mixed, spectra, place = lax.optimization_barrier((mixed, spectra, place))
-    plane_back = plane_table(z, place, 1, 2)
-    sent = whole_call(plane_cells, z, 1000, payload, [spread_scratch], mixed, other_core(mixed), plane_back)
-    sent, field, cotangent = lax.optimization_barrier((sent, field, cotangent))
-    returned = exchange(sent)
+    factor_scratch = pltpu.VMEM(factors_x.shape[1:], F32)
+    turned, plane, plane_back = whole_call(
+        turn_weights, z, 5000,
+        (
+            shape_of((z.modes, z.channels, z.rows, 2 * z.half)),
+            shape_of((2 * half_rows, 4 * z.half)),
+            shape_of((half_rows, 8 * z.half)),
+        ),
+        [
+            weight_scratch[0], factor_scratch, factor_scratch, pltpu.VMEM(factors_y.shape, F32),
+            weight_scratch[1], pltpu.SemaphoreType.DMA((3,)),
+        ],
+        native.reshape(weight_shape), sent, lax.axis_index("gy").reshape(1), jnp.asarray(factors_x), jnp.asarray(factors_y),
+        specs=[HBM, HBM, SMEM, HBM, HBM], room=28,
+    )
+    own, turned, plane, plane_back, field, cotangent = lax.optimization_barrier(
+        (own, turned, plane, plane_back, field, cotangent)
+    )
+    other = other_core(own)
     local, cot_cells, inverse_here, forward_here = whole_call(
-        prepare, z, 2000,
+        prepare, z, 1500,
         (shape_of(cells_shape), shape_of(cells_shape), shape_of(inverse_first.shape), shape_of(forward_back.shape, BF16)),
         [cells_scratch, field_scratch, field_scratch, pltpu.SemaphoreType.DMA((4,))],
         field, cotangent, pointwise_weight, channel_bias, inverse_first, forward_back,
-        specs=[REMOTE, REMOTE, VMEM, SMEM, REMOTE, REMOTE], room=50,
-    )
-    returned, local, cot_cells, inverse_here, forward_here = lax.optimization_barrier(
-        (returned, local, cot_cells, inverse_here, forward_here)
-    )
+        specs=[HBM, HBM, VMEM, SMEM, HBM, HBM],
+    )
+    other, local, cot_cells, inverse_here, forward_here = lax.optimization_barrier(
+        (other, local, cot_cells, inverse_here, forward_here)
+    )
+    spectra, mixed = whole_call(
+        mix_forward, z, 1000, (shape_of(spectra_shape), shape_of(spectra_shape)), [], own, other, plane, turned
+    )
+    sent = whole_call(plane_cells, z, 1000, payload, [spread_scratch], mixed, other_core(mixed), plane_back)
     pre, signal, sent = whole_call(
         activate, z, 2000,
         (shape_of(cells_shape), shape_of(cells_shape, BF16), payload), [spectrum_scratch],
-        returned, local, cot_cells, inverse_here, forward_here,
-    )
-    sent, pre, signal = lax.optimization_barrier((sent, pre, signal))
-    own = exchange(sent)
-    layer_out, local = whole_call(
-        emit, z, 2000, (shape_of(field.shape, BF16), shape_of(cells_shape)), [], pre, signal, pointwise_weight
-    )
-    own, layer_out, local = lax.optimization_barrier((own, layer_out, local))
+        exchange(sent), local, cot_cells, inverse_here, forward_here,
+    )
+    own, pre, signal = lax.optimization_barrier((exchange(sent), pre, signal))
+    other = other_core(own)
+    layer_out, local, inverse_here = whole_call(
+        emit, z, 1200,
+        (shape_of(field.shape, BF16), shape_of(cells_shape), shape_of(inverse_back.shape)),
+        [pltpu.SemaphoreType.DMA((1,))],
+        pre, signal, pointwise_weight, inverse_back, specs=[VMEM, VMEM, VMEM, HBM],
+    )
+    other, layer_out, local, inverse_here = lax.optimization_barrier((other, layer_out, local, inverse_here))
     back, mixed = whole_call(
-        mix_back, z, 2000, (shape_of((z.modes, z.rows, 2 * z.half)), shape_of(spectra_shape)), [spectra_scratch],
-        own, other_core(own), plane, turned,
+        mix_back, z, 1000, (shape_of((z.modes, z.rows, 2 * z.half)), shape_of(spectra_shape)), [spectra_scratch],
+        own, other, plane, turned,
     )
     sent = whole_call(plane_cells, z, 1000, payload, [spread_scratch], mixed, other_core(mixed), plane_back)
     sent, back, spectra = lax.optimization_barrier((sent, back, spectra))
     returned = exchange(sent)
     gradient = whole_call(
-        grad_weights, z, 5000, shape_of(weight_shape), weight_scratch, spectra, back, out_specs=REMOTE, room=50
+        grad_weights, z, 5000, shape_of(weight_shape), weight_scratch, spectra, back, out_specs=HBM, room=28
     )
     returned, gradient = lax.optimization_barrier((returned, gradient))
     grad_field = whole_call(
-        finish, z, 1000, shape_of(field.shape, BF16), [spectrum_scratch], returned, local, inverse_back
+        finish, z, 1000, shape_of(field.shape, BF16), [spectrum_scratch], returned, local, inverse_here
     )
     return (layer_out, grad_field, jnp.transpose(gradient.reshape(native.shape), (0, 1, 2, 5, 3, 4)))
 

time: 76.5 us -> 79.8 us (1.043)
  blocking collectives: 0 us -> 27.1 us
  waiting for transfers between devices: 17.3 us -> 2.62 us
  starting transfers between devices: 19.9 us -> 12.9 us
  other arithmetic: 2.8 us -> 0 us
  Pallas kernels: 25.4 us -> 27.4 us
  local copies, waits for them, and re-layouts: 9.5 us -> 8.37 us
    all_to_all x0 -> x2, blocking collectives: none -> 27.1 us  [exchange(): lax.all_to_all(payload, ('gx', 'gy'), split_axis=0, concat_axis=0, tiled=...]
    all_to_all x4 -> x2, waiting for transfers between devices: 14.7 us -> 0.63 us  [exchange(): lax.all_to_all(payload, ('gx', 'gy'), split_axis=0, concat_axis=0, tiled=...]
    all_to_all x4 -> x2, starting transfers between devices: 19.1 us -> 11.9 us  [exchange(): lax.all_to_all(payload, ('gx', 'gy'), split_axis=0, concat_axis=0, tiled=...]
    select_n x2 -> x0, other arithmetic: 2.67 us -> none  [plane_table(): return jnp.where(mode < sizes.kept, values, 0.0)]
    pallas_call x11, Pallas kernels: 25.4 us -> 27.4 us  [whole_call(): pl.pallas_call(kernel, out_shape=out_shape, in_specs=specs or [VMEM] * le...]
    unnamed x34 -> x24, local copies, waits for them, and re-layouts: 9.5 us -> 8.37 us
  transfers between devices with their start and end apart: 8 -> 6, of which waited for: 5 -> 4; matrix products, arithmetic and copies ran while one was open for 4% -> 0% of each run, Pallas kernels for 20% -> 24%
where the time goes in v3:
time: 79.8 us; the launch traced here: 79.3 us
  Pallas kernels  27.4 us (34%)
  blocking collectives  27.1 us (34%)
  starting transfers between devices  12.9 us (16%)
  local copies, waits for them, and re-layouts  8.37 us (10%)
  waiting for transfers between devices  2.62 us (3%)
  between operations  0.83 us (1%)
    pallas_call x11, Pallas kernels, whole_call(): pl.pallas_call(kernel, out_shape=out_shape, in_specs=specs or [VMEM] * le...  27.4 us
    all_to_all x2, blocking collectives, exchange(): lax.all_to_all(payload, ('gx', 'gy'), split_axis=0, concat_axis=0, tiled=...  27.1 us
    all_to_all x2, starting transfers between devices, exchange(): lax.all_to_all(payload, ('gx', 'gy'), split_axis=0, concat_axis=0, tiled=...  11.9 us
    unnamed x24, local copies, waits for them, and re-layouts  8.37 us
    ppermute x4, waiting for transfers between devices, other_core(): return lax.ppermute(payload, 'gy', pairs)  1.98 us
  transfers between devices with their start and end apart: 6, of which 4 were waited for; matrix products, arithmetic and copies ran while one was open for 0% of the time, Pallas kernels for 24%

profile of v3, /device:TPU:0, one launch (start us, length us, event | category | flops | bytes accessed | tf_op | source)
XLA Modules:
  0.0 79.3 jit_solution(16573832190766625000)
XLA Ops:
  0.6 0.0 copy-start.1
  0.6 0.9 %copy-done.1 = bf16[20,2,4,512]{3,2,1,0:T(4,128)(2,1)S(1)} copy-done((bf16[20,2,4,512]{3,2,1,0:T(4,128)(2,1)S(1)}, bf16[20,2,4,512]{3,2,1,0:T(4,128)(2,1)}, u32[]{:S(2)}) %copy-start.1) | copy-done | bytes 163864
  1.5 0.0 copy-start.8
  1.6 0.9 %copy-done.8 = bf16[512,128]{1,0:T(8,128)(2,1)S(1)} copy-done((bf16[512,128]{1,0:T(8,128)(2,1)S(1)}, bf16[512,128]{1,0:T(8,128)(2,1)}, u32[]{:S(2)}) %copy-start.8) | copy-done | bytes 131096
  2.5 0.0 copy-start.2
  2.5 0.0 copy-start.4
  2.5 0.0 copy-start.5
  2.5 0.0 copy-start.10
  2.5 0.0 copy-start.11
  2.5 0.0 copy-start.3
  2.5 1.6 %depth_forward.1.refs_1_ = f32[16,8,384]{2,1,0:T(8,128)} custom-call(bf16[20,2,4,512]{3,2,1,0:T(4,128)(2,1)S(1)} %copy-done.1, bf16[512,128]{1,0:T(8,128)(2,1)S(1)} %copy-done.8), custom_call_target="tpu_custom_call" | custom-call | bytes 4500000 | tf_op jit(solution)/shard_map/depth_forward/pallas_call | solution.py:396
  4.1 8.3 %all-to-all-start = ((f32[16,8,384]{2,1,0:T(8,128)}), f32[16,8,384]{2,1,0:T(8,128)S(1)}, u32[]{:S(2)}, u32[]{:S(2)}) async-start(f32[16,8,384]{2,1,0:T(8,128)} %depth_forward.1.refs_1_), calls=%async_computation | async-start | bytes 393216 | tf_op jit(solution)/shard_map/all_to_all | solution.py:423
  12.4 0.0 copy-start
  12.5 4.0 %copy-done = f32[8,2,20,20,4,16]{3,5,4,2,1,0:T(8,128)S(1)} copy-done((f32[8,2,20,20,4,16]{3,5,4,2,1,0:T(8,128)S(1)}, f32[8,2,20,20,4,16]{3,5,4,2,1,0:T(8,128)}, u32[]{:S(2)}) %copy-start) | copy-done | bytes 1638424
  16.4 0.0 copy-start.6
  16.4 0.9 %copy-done.6 = f32[4,16,512]{2,1,0:T(8,128)S(1)} copy-done((f32[4,16,512]{2,1,0:T(8,128)S(1)}, f32[4,16,512]{2,1,0:T(8,128)}, u32[]{:S(2)}) %copy-start.6) | copy-done | bytes 131096
  17.3 0.0 copy-start.9
  17.3 0.8 copy-done.9
  18.1 7.8 %turn_weights.1 = (f32[8,20,24,128]{3,2,1,0:T(8,128)S(1)}, f32[256,256]{1,0:T(8,128)S(1)}, f32[128,512]{1,0:T(8,128)S(1)}) custom-call(f32[16,20,4,16,20]{4,3,2,1,0:T(8,128)S(1)} %bitcast.7, f32[16,8,384]{2,1,0:T(8,128)} %depth_forward.1.refs_1_, s32[1]{0:T(128)} %bitcast.2.refs_2_, f32[4,16,512]{2,1,0:T(8,128)S(1)} %copy-done.6, f32[16,512]{1,0:T(8,128)S(1)} %copy-done.9), custom_call_target="tpu_custom_call" | custom-call | bytes 15000000 | tf_op jit(solution)/shard_map/turn_weights/pallas_call | solution.py:396
  25.9 0.0 all-to-all-done.refs_0_
  25.9 0.1 collective-permute-start
  26.0 0.0 copy-done.2
  26.0 0.0 copy-done.4
  26.0 0.0 copy-done.5
  26.0 0.0 copy-done.10
  26.0 0.0 copy-done.11
  26.0 0.0 copy-start.7
  26.0 0.9 %copy-done.7 = bf16[512,128]{1,0:T(8,128)(2,1)S(1)} copy-done((bf16[512,128]{1,0:T(8,128)(2,1)S(1)}, bf16[512,128]{1,0:T(8,128)(2,1)}, u32[]{:S(2)}) %copy-start.7) | copy-done | bytes 131096
  26.9 1.7 %prepare.1 = (f32[160,512]{1,0:T(8,128)S(1)}, f32[160,512]{1,0:T(8,128)S(1)}, f32[128,512]{1,0:T(8,128)S(1)}, bf16[512,128]{1,0:T(8,128)(2,1)S(1)}) custom-call(bf16[20,2,4,512]{3,2,1,0:T(4,128)(2,1)S(1)} %copy-done.2, bf16[20,2,4,512]{3,2,1,0:T(4,128)(2,1)S(1)} %copy-done.5, bf16[20,20]{1,0:T(8,128)(2,1)S(1)} %copy-done.10, f32[20]{0:T(128)S(1)} %copy-done.11, ...), custom_call_target="tpu_custom_call" | custom-call | bytes 4500000 | tf_op jit(solution)/shard_map/prepare/pallas_call | solution.py:396
  28.6 0.0 collective-permute-done.refs_1_
  28.6 0.9 %mix_forward.1 = (f32[160,128]{1,0:T(8,128)S(1)}, f32[160,128]{1,0:T(8,128)S(1)}) custom-call(f32[16,8,384]{2,1,0:T(8,128)S(1)} %all-to-all-done.refs_0_, f32[16,8,384]{2,1,0:T(8,128)S(1)} %collective-permute-done.refs_1_, f32[256,256]{1,0:T(8,128)S(1)} %get-tuple-element.54.refs_2_, f32[8,20,24,128]{3,2,1,0:T(8,128)S(1)} %get-tuple-element.55.refs_3_), custom_call_target="tpu_custom_call" | custom-call | bytes 3000000 | tf_op jit(solution)/shard_map/mix_forward/pallas_call | solution.py:396
  29.5 0.5 collective-permute-start.1
  30.0 0.9 %collective-permute-done.1.refs_1_ = f32[160,128]{1,0:T(8,128)S(1)} collective-permute-done((f32[160,128]{1,0:T(8,128)S(1)}, f32[160,128]{1,0:T(8,128)S(1)}, u32[]{:S(2)}, u32[]{:S(2)}) %collective-permute-start.1) | collective-permute-done | bytes 81952 | tf_op jit(solution)/shard_map/ppermute | solution.py:428
  30.9 0.8 %plane_cells.2 = f32[16,8,384]{2,1,0:T(8,128)S(1)} custom-call(f32[160,128]{1,0:T(8,128)S(1)} %get-tuple-element.56.refs_0_, f32[160,128]{1,0:T(8,128)S(1)} %collective-permute-done.1.refs_1_, f32[128,512]{1,0:T(8,128)S(1)} %get-tuple-element.57.refs_2_), custom_call_target="tpu_custom_call" | custom-call | bytes 3000000 | tf_op jit(solution)/shard_map/plane_cells/pallas_call | solution.py:396
  31.7 15.9 %all_to_all.20.refs_0_ = f32[16,8,384]{2,1,0:T(8,128)S(1)} all-to-all(f32[16,8,384]{2,1,0:T(8,128)S(1)} %plane_cells.2), channel_id=1, replica_groups={{0,2,4,6,8,10,12,14,16,18,20,22,24,26,28,30},{1,3,5,7,9,11,13,15,17,19,..., dimensions={0} | all-to-all | bytes 393216 | tf_op jit(solution)/shard_map/all_to_all | solution.py:423
  47.6 1.3 %activate.1 = (f32[160,512]{1,0:T(8,128)S(1)}, bf16[160,512]{1,0:T(8,128)(2,1)S(1)}, f32[16,8,384]{2,1,0:T(8,128)S(1)}) custom-call(f32[16,8,384]{2,1,0:T(8,128)S(1)} %all_to_all.20.refs_0_, f32[160,512]{1,0:T(8,128)S(1)} %get-tuple-element.58.refs_1_, f32[160,512]{1,0:T(8,128)S(1)} %get-tuple-element.59.refs_2_, f32[128,512]{1,0:T(8,128)S(1)} %get-tuple-element.60.refs_3_, ...), custom_call_target="tpu_custom_call" | custom-call | bytes 6000000 | tf_op jit(solution)/shard_map/activate/pallas_call | solution.py:396
  48.9 11.2 %all_to_all.21.refs_0_ = f32[16,8,384]{2,1,0:T(8,128)S(1)} all-to-all(f32[16,8,384]{2,1,0:T(8,128)S(1)} %get-tuple-element.62), channel_id=1, replica_groups={{0,2,4,6,8,10,12,14,16,18,20,22,24,26,28,30},{1,3,5,7,9,11,13,15,17,19,..., dimensions={0} | all-to-all | bytes 393216 | tf_op jit(solution)/shard_map/all_to_all | solution.py:423
  60.1 0.0 collective-permute-start.2
  60.1 0.0 copy-done.3
  60.1 1.3 %emit.1 = (bf16[20,2,4,512]{3,2,1,0:T(4,128)(2,1)}, f32[160,512]{1,0:T(8,128)S(1)}, f32[128,512]{1,0:T(8,128)S(1)}) custom-call(f32[160,512]{1,0:T(8,128)S(1)} %get-tuple-element.66.refs_0_, bf16[160,512]{1,0:T(8,128)(2,1)S(1)} %get-tuple-element.67.refs_1_, bf16[20,20]{1,0:T(8,128)(2,1)S(1)} %copy-done.10, f32[128,512]{1,0:T(8,128)S(1)} %copy-done.3), custom_call_target="tpu_custom_call" | custom-call | bytes 3600000 | tf_op jit(solution)/shard_map/emit/pallas_call | solution.py:396
  61.4 0.1 collective-permute-done.2.refs_1_
  61.6 1.1 %mix_back.1 = (f32[8,24,128]{2,1,0:T(8,128)S(1)}, f32[160,128]{1,0:T(8,128)S(1)}) custom-call(f32[16,8,384]{2,1,0:T(8,128)S(1)} %all_to_all.21.refs_0_, f32[16,8,384]{2,1,0:T(8,128)S(1)} %collective-permute-done.2.refs_1_, f32[256,256]{1,0:T(8,128)S(1)} %get-tuple-element.54.refs_2_, f32[8,20,24,128]{3,2,1,0:T(8,128)S(1)} %get-tuple-element.55.refs_3_), custom_call_target="tpu_custom_call" | custom-call | bytes 3000000 | tf_op jit(solution)/shard_map/mix_back/pallas_call | solution.py:396
  62.7 0.4 collective-permute-start.3
  63.1 0.9 %collective-permute-done.3.refs_1_ = f32[160,128]{1,0:T(8,128)S(1)} collective-permute-done((f32[160,128]{1,0:T(8,128)S(1)}, f32[160,128]{1,0:T(8,128)S(1)}, u32[]{:S(2)}, u32[]{:S(2)}) %collective-permute-start.3) | collective-permute-done | bytes 81952 | tf_op jit(solution)/shard_map/ppermute | solution.py:428
  64.0 1.5 %plane_cells.3 = f32[16,8,384]{2,1,0:T(8,128)} custom-call(f32[160,128]{1,0:T(8,128)S(1)} %get-tuple-element.73.refs_0_, f32[160,128]{1,0:T(8,128)S(1)} %collective-permute-done.3.refs_1_, f32[128,512]{1,0:T(8,128)S(1)} %get-tuple-element.57.refs_2_), custom_call_target="tpu_custom_call" | custom-call | bytes 3000000 | tf_op jit(solution)/shard_map/plane_cells/pallas_call | solution.py:396
  65.5 3.6 %all-to-all-start.3 = ((f32[16,8,384]{2,1,0:T(8,128)}), f32[16,8,384]{2,1,0:T(8,128)S(1)}, u32[]{:S(2)}, u32[]{:S(2)}) async-start(f32[16,8,384]{2,1,0:T(8,128)} %plane_cells.3), calls=%async_computation.3 | async-start | bytes 393216 | tf_op jit(solution)/shard_map/all_to_all | solution.py:423
  69.1 8.2 %grad_weights.1 = f32[16,20,4,16,20]{4,3,2,1,0:T(8,128)} custom-call(f32[160,128]{1,0:T(8,128)S(1)} %get-tuple-element.77.refs_0_, f32[8,24,128]{2,1,0:T(8,128)S(1)} %get-tuple-element.78.refs_1_), custom_call_target="tpu_custom_call" | custom-call | bytes 15000000 | tf_op jit(solution)/shard_map/grad_weights/pallas_call | solution.py:396
  77.3 0.6 all-to-all-done.3.refs_0_
  77.9 1.4 %finish.1 = bf16[20,2,4,512]{3,2,1,0:T(4,128)(2,1)} custom-call(f32[16,8,384]{2,1,0:T(8,128)S(1)} %all-to-all-done.3.refs_0_, f32[160,512]{1,0:T(8,128)S(1)} %get-tuple-element.80.refs_1_, f32[128,512]{1,0:T(8,128)S(1)} %get-tuple-element.81.refs_2_), custom_call_target="tpu_custom_call" | custom-call | bytes 3000000 | tf_op jit(solution)/shard_map/finish/pallas_call | solution.py:396
Async XLA Ops:
  0.6 0.9 %copy-start.1 = (bf16[20,2,4,512]{3,2,1,0:T(4,128)(2,1)S(1)}, bf16[20,2,4,512]{3,2,1,0:T(4,128)(2,1)}, u32[]{:S(2)}) copy-start(bf16[20,2,4,512]{3,2,1,0:T(4,128)(2,1)} %refs_0_.2) | copy-start | bytes 491524
  1.5 0.9 %copy-start.8 = (bf16[512,128]{1,0:T(8,128)(2,1)S(1)}, bf16[512,128]{1,0:T(8,128)(2,1)}, u32[]{:S(2)}) copy-start(bf16[512,128]{1,0:T(8,128)(2,1)} %constant.16.clone.refs_1_) | copy-start | bytes 393220
  2.5 23.5 %copy-start.2 = (bf16[20,2,4,512]{3,2,1,0:T(4,128)(2,1)S(1)}, bf16[20,2,4,512]{3,2,1,0:T(4,128)(2,1)}, u32[]{:S(2)}) copy-start(bf16[20,2,4,512]{3,2,1,0:T(4,128)(2,1)} %refs_0_.2) | copy-start | bytes 491524
  2.5 23.5 %copy-start.4 = (f32[128,512]{1,0:T(8,128)S(1)}, f32[128,512]{1,0:T(8,128)}, u32[]{:S(2)}) copy-start(f32[128,512]{1,0:T(8,128)} %constant.19.clone.refs_4_) | copy-start | bytes 786436
  2.5 23.5 %copy-start.5 = (bf16[20,2,4,512]{3,2,1,0:T(4,128)(2,1)S(1)}, bf16[20,2,4,512]{3,2,1,0:T(4,128)(2,1)}, u32[]{:S(2)}) copy-start(bf16[20,2,4,512]{3,2,1,0:T(4,128)(2,1)} %refs_1_.1) | copy-start | bytes 491524
  2.5 23.5 %copy-start.10 = (bf16[20,20]{1,0:T(8,128)(2,1)S(1)}, bf16[20,20]{1,0:T(8,128)(2,1)}, u32[]{:S(2)}) copy-start(bf16[20,20]{1,0:T(8,128)(2,1)} %refs_2_.3) | copy-start | bytes 2404
  2.5 23.5 %copy-start.11 = (f32[20]{0:T(128)S(1)}, f32[20]{0:T(128)}, u32[]{:S(2)}) copy-start(f32[20]{0:T(128)} %refs_3_.3) | copy-start | bytes 244
  2.5 57.7 %copy-start.3 = (f32[128,512]{1,0:T(8,128)S(1)}, f32[128,512]{1,0:T(8,128)}, u32[]{:S(2)}) copy-start(f32[128,512]{1,0:T(8,128)} %constant.18.clone.refs_3_) | copy-start | bytes 786436
  4.1 21.8 %all-to-all-start = ((f32[16,8,384]{2,1,0:T(8,128)}), f32[16,8,384]{2,1,0:T(8,128)S(1)}, u32[]{:S(2)}, u32[]{:S(2)}) async-start(f32[16,8,384]{2,1,0:T(8,128)} %depth_forward.1.refs_1_), calls=%async_computation | async-start | bytes 393216 | tf_op jit(solution)/shard_map/all_to_all | solution.py:423
  12.4 4.0 %copy-start = (f32[8,2,20,20,4,16]{3,5,4,2,1,0:T(8,128)S(1)}, f32[8,2,20,20,4,16]{3,5,4,2,1,0:T(8,128)}, u32[]{:S(2)}) copy-start(f32[8,2,20,20,4,16]{3,5,4,2,1,0:T(8,128)} %param.13) | copy-start | bytes 4915204
  16.4 0.9 %copy-start.6 = (f32[4,16,512]{2,1,0:T(8,128)S(1)}, f32[4,16,512]{2,1,0:T(8,128)}, u32[]{:S(2)}) copy-start(f32[4,16,512]{2,1,0:T(8,128)} %constant.20.clone.refs_3_) | copy-start | bytes 393220
  17.3 0.8 copy-start.9
  25.9 2.7 %collective-permute-start = (f32[16,8,384]{2,1,0:T(8,128)S(1)}, f32[16,8,384]{2,1,0:T(8,128)S(1)}, u32[]{:S(2)}, u32[]{:S(2)}) collective-permute-start(f32[16,8,384]{2,1,0:T(8,128)S(1)} %all-to-all-done.refs_0_), channel_id=1, source_target_pairs={{0,1},{1,0},{2,3},{3,2},{4,5},{5,4},{6,7},{7,6},{8,9},{9,8},{10,11... | collective-permute-start | bytes 589832 | tf_op jit(solution)/shard_map/ppermute | solution.py:428
  26.0 0.9 %copy-start.7 = (bf16[512,128]{1,0:T(8,128)(2,1)S(1)}, bf16[512,128]{1,0:T(8,128)(2,1)}, u32[]{:S(2)}) copy-start(bf16[512,128]{1,0:T(8,128)(2,1)} %constant.17.clone.refs_5_) | copy-start | bytes 393220
  29.5 1.5 %collective-permute-start.1 = (f32[160,128]{1,0:T(8,128)S(1)}, f32[160,128]{1,0:T(8,128)S(1)}, u32[]{:S(2)}, u32[]{:S(2)}) collective-permute-start(f32[160,128]{1,0:T(8,128)S(1)} %get-tuple-element.56.refs_0_), channel_id=1, source_target_pairs={{0,1},{1,0},{2,3},{3,2},{4,5},{5,4},{6,7},{7,6},{8,9},{9,8},{10,11... | collective-permute-start | bytes 245768 | tf_op jit(solution)/shard_map/ppermute | solution.py:428
  60.1 1.4 %collective-permute-start.2 = (f32[16,8,384]{2,1,0:T(8,128)S(1)}, f32[16,8,384]{2,1,0:T(8,128)S(1)}, u32[]{:S(2)}, u32[]{:S(2)}) collective-permute-start(f32[16,8,384]{2,1,0:T(8,128)S(1)} %all_to_all.21.refs_0_), channel_id=1, source_target_pairs={{0,1},{1,0},{2,3},{3,2},{4,5},{5,4},{6,7},{7,6},{8,9},{9,8},{10,11... | collective-permute-start | bytes 589832 | tf_op jit(solution)/shard_map/ppermute | solution.py:428
  62.7 1.3 %collective-permute-start.3 = (f32[160,128]{1,0:T(8,128)S(1)}, f32[160,128]{1,0:T(8,128)S(1)}, u32[]{:S(2)}, u32[]{:S(2)}) collective-permute-start(f32[160,128]{1,0:T(8,128)S(1)} %get-tuple-element.73.refs_0_), channel_id=1, source_target_pairs={{0,1},{1,0},{2,3},{3,2},{4,5},{5,4},{6,7},{7,6},{8,9},{9,8},{10,11... | collective-permute-start | bytes 245768 | tf_op jit(solution)/shard_map/ppermute | solution.py:428
  65.5 12.4 %all-to-all-start.3 = ((f32[16,8,384]{2,1,0:T(8,128)}), f32[16,8,384]{2,1,0:T(8,128)S(1)}, u32[]{:S(2)}, u32[]{:S(2)}) async-start(f32[16,8,384]{2,1,0:T(8,128)} %plane_cells.3), calls=%async_computation.3 | async-start | bytes 393216 | tf_op jit(solution)/shard_map/all_to_all | solution.py:423

commit v4 on v3

--- a/solution.py
+++ b/solution.py
@@ -379,6 +379,7 @@
 VMEM = pl.BlockSpec(memory_space=pltpu.VMEM)
 SMEM = pl.BlockSpec(memory_space=pltpu.SMEM)
 HBM = pl.BlockSpec(memory_space=pltpu.HBM)
+ANYWHERE = pl.BlockSpec(memory_space=pl.ANY)
 
 
 def settings(mebibytes):
@@ -393,6 +394,10 @@
     def kernel(*refs):
         body(sizes, *refs)
 
+    if specs:
+        args = [
+            pltpu.with_memory_space_constraint(arg, pltpu.HBM) if spec is HBM else arg for arg, spec in zip(args, specs)
+        ]
     return pl.pallas_call(
         kernel,
         out_shape=out_shape,
@@ -463,7 +468,7 @@
             weight_scratch[1], pltpu.SemaphoreType.DMA((3,)),
         ],
         native.reshape(weight_shape), sent, lax.axis_index("gy").reshape(1), jnp.asarray(factors_x), jnp.asarray(factors_y),
-        specs=[HBM, HBM, SMEM, HBM, HBM], room=28,
+        specs=[HBM, ANYWHERE, SMEM, HBM, HBM], room=28,
     )
     own, turned, plane, plane_back, field, cotangent = lax.optimization_barrier(
         (own, turned, plane, plane_back, field, cotangent)

time: 79.8 us -> 73.2 us (0.917)
  local copies, waits for them, and re-layouts: 8.37 us -> 0.01 us
  Pallas kernels: 27.4 us -> 29.3 us
    unnamed x24 -> x4, local copies, waits for them, and re-layouts: 8.37 us -> 0.01 us
    pallas_call x11, Pallas kernels: 27.4 us -> 29.3 us  [whole_call(): pl.pallas_call(kernel, out_shape=out_shape, in_specs=specs or [VMEM] * le...]
  transfers between devices with their start and end apart: 6 -> 6, of which waited for: 4 -> 4; matrix products, arithmetic and copies ran while one was open for 0% -> 0% of each run, Pallas kernels for 24% -> 28%
where the time goes in v4:
time: 73.2 us; the launch traced here: 72.7 us
  Pallas kernels  29.3 us (40%)
  blocking collectives  26.6 us (36%)
  starting transfers between devices  13 us (18%)
  waiting for transfers between devices  3.03 us (4%)
  between operations  0.75 us (1%)
    pallas_call x11, Pallas kernels, whole_call(): pl.pallas_call(kernel, out_shape=out_shape, in_specs=specs or [VMEM] * le...  29.3 us
    all_to_all x2, blocking collectives, exchange(): lax.all_to_all(payload, ('gx', 'gy'), split_axis=0, concat_axis=0, tiled=...  26.6 us
    all_to_all x2, starting transfers between devices, exchange(): lax.all_to_all(payload, ('gx', 'gy'), split_axis=0, concat_axis=0, tiled=...  11.9 us
    ppermute x4, waiting for transfers between devices, other_core(): return lax.ppermute(payload, 'gy', pairs)  1.85 us
  transfers between devices with their start and end apart: 6, of which 4 were waited for; matrix products, arithmetic and copies ran while one was open for 0% of the time, Pallas kernels for 28%

profile of v4, /device:TPU:0, one launch (start us, length us, event | category | flops | bytes accessed | tf_op | source)
XLA Modules:
  0.0 72.7 jit_solution(1730299021336444410)
XLA Ops:
  0.6 0.0 copy-start
  0.6 0.0 copy-start.1
  0.7 2.2 %depth_forward.1.refs_1_ = f32[16,8,384]{2,1,0:T(8,128)} custom-call(bf16[20,2,4,512]{3,2,1,0:T(4,128)(2,1)} %refs_0_.2, bf16[512,128]{1,0:T(8,128)(2,1)} %constant.16.clone.refs_1_), custom_call_target="tpu_custom_call" | custom-call | bytes 4500000 | tf_op jit(solution)/shard_map/depth_forward/pallas_call | solution.py:401
  2.9 8.3 %all-to-all-start = ((f32[16,8,384]{2,1,0:T(8,128)}), f32[16,8,384]{2,1,0:T(8,128)S(1)}, u32[]{:S(2)}, u32[]{:S(2)}) async-start(f32[16,8,384]{2,1,0:T(8,128)} %depth_forward.1.refs_1_), calls=%async_computation | async-start | bytes 393216 | tf_op jit(solution)/shard_map/all_to_all | solution.py:428
  11.2 8.1 %turn_weights.1 = (f32[8,20,24,128]{3,2,1,0:T(8,128)S(1)}, f32[256,256]{1,0:T(8,128)S(1)}, f32[128,512]{1,0:T(8,128)S(1)}) custom-call(f32[16,20,4,16,20]{4,3,2,1,0:T(8,128)} %bitcast.7, f32[16,8,384]{2,1,0:T(8,128)} %depth_forward.1.refs_1_, s32[1]{0:T(128)} %bitcast.2.refs_2_, f32[4,16,512]{2,1,0:T(8,128)} %constant.20.clone.refs_3_, ...), custom_call_target="tpu_custom_call" | custom-call | bytes 15000000 | tf_op jit(solution)/shard_map/turn_weights/pallas_call | solution.py:401
  19.3 0.5 all-to-all-done.refs_0_
  19.9 0.0 collective-permute-start
  19.9 0.0 copy-done
  19.9 0.0 copy-done.1
  19.9 2.2 %prepare.1 = (f32[160,512]{1,0:T(8,128)S(1)}, f32[160,512]{1,0:T(8,128)S(1)}, f32[128,512]{1,0:T(8,128)S(1)}, bf16[512,128]{1,0:T(8,128)(2,1)S(1)}) custom-call(bf16[20,2,4,512]{3,2,1,0:T(4,128)(2,1)} %refs_0_.2, bf16[20,2,4,512]{3,2,1,0:T(4,128)(2,1)} %refs_1_.1, bf16[20,20]{1,0:T(8,128)(2,1)S(1)} %copy-done, f32[20]{0:T(128)S(1)} %copy-done.1, ...), custom_call_target="tpu_custom_call" | custom-call | bytes 4500000 | tf_op jit(solution)/shard_map/prepare/pallas_call | solution.py:401
  22.1 0.0 collective-permute-done.refs_1_
  22.1 0.9 %mix_forward.1 = (f32[160,128]{1,0:T(8,128)S(1)}, f32[160,128]{1,0:T(8,128)S(1)}) custom-call(f32[16,8,384]{2,1,0:T(8,128)S(1)} %all-to-all-done.refs_0_, f32[16,8,384]{2,1,0:T(8,128)S(1)} %collective-permute-done.refs_1_, f32[256,256]{1,0:T(8,128)S(1)} %get-tuple-element.54.refs_2_, f32[8,20,24,128]{3,2,1,0:T(8,128)S(1)} %get-tuple-element.55.refs_3_), custom_call_target="tpu_custom_call" | custom-call | bytes 3000000 | tf_op jit(solution)/shard_map/mix_forward/pallas_call | solution.py:401
  22.9 0.6 collective-permute-start.1
  23.5 0.9 %collective-permute-done.1.refs_1_ = f32[160,128]{1,0:T(8,128)S(1)} collective-permute-done((f32[160,128]{1,0:T(8,128)S(1)}, f32[160,128]{1,0:T(8,128)S(1)}, u32[]{:S(2)}, u32[]{:S(2)}) %collective-permute-start.1) | collective-permute-done | bytes 81952 | tf_op jit(solution)/shard_map/ppermute | solution.py:433
  24.4 0.8 %plane_cells.2 = f32[16,8,384]{2,1,0:T(8,128)S(1)} custom-call(f32[160,128]{1,0:T(8,128)S(1)} %get-tuple-element.56.refs_0_, f32[160,128]{1,0:T(8,128)S(1)} %collective-permute-done.1.refs_1_, f32[128,512]{1,0:T(8,128)S(1)} %get-tuple-element.57.refs_2_), custom_call_target="tpu_custom_call" | custom-call | bytes 3000000 | tf_op jit(solution)/shard_map/plane_cells/pallas_call | solution.py:401
  25.3 15.4 %all_to_all.20.refs_0_ = f32[16,8,384]{2,1,0:T(8,128)S(1)} all-to-all(f32[16,8,384]{2,1,0:T(8,128)S(1)} %plane_cells.2), channel_id=1, replica_groups={{0,2,4,6,8,10,12,14,16,18,20,22,24,26,28,30},{1,3,5,7,9,11,13,15,17,19,..., dimensions={0} | all-to-all | bytes 393216 | tf_op jit(solution)/shard_map/all_to_all | solution.py:428
  40.6 1.3 %activate.1 = (f32[160,512]{1,0:T(8,128)S(1)}, bf16[160,512]{1,0:T(8,128)(2,1)S(1)}, f32[16,8,384]{2,1,0:T(8,128)S(1)}) custom-call(f32[16,8,384]{2,1,0:T(8,128)S(1)} %all_to_all.20.refs_0_, f32[160,512]{1,0:T(8,128)S(1)} %get-tuple-element.58.refs_1_, f32[160,512]{1,0:T(8,128)S(1)} %get-tuple-element.59.refs_2_, f32[128,512]{1,0:T(8,128)S(1)} %get-tuple-element.60.refs_3_, ...), custom_call_target="tpu_custom_call" | custom-call | bytes 6000000 | tf_op jit(solution)/shard_map/activate/pallas_call | solution.py:401
  41.9 11.2 %all_to_all.21.refs_0_ = f32[16,8,384]{2,1,0:T(8,128)S(1)} all-to-all(f32[16,8,384]{2,1,0:T(8,128)S(1)} %get-tuple-element.62), channel_id=1, replica_groups={{0,2,4,6,8,10,12,14,16,18,20,22,24,26,28,30},{1,3,5,7,9,11,13,15,17,19,..., dimensions={0} | all-to-all | bytes 393216 | tf_op jit(solution)/shard_map/all_to_all | solution.py:428
  53.2 0.0 collective-permute-start.2
  53.2 1.7 %emit.1 = (bf16[20,2,4,512]{3,2,1,0:T(4,128)(2,1)}, f32[160,512]{1,0:T(8,128)S(1)}, f32[128,512]{1,0:T(8,128)S(1)}) custom-call(f32[160,512]{1,0:T(8,128)S(1)} %get-tuple-element.66.refs_0_, bf16[160,512]{1,0:T(8,128)(2,1)S(1)} %get-tuple-element.67.refs_1_, bf16[20,20]{1,0:T(8,128)(2,1)S(1)} %copy-done, f32[128,512]{1,0:T(8,128)} %constant.18.clone.refs_3_), custom_call_target="tpu_custom_call" | custom-call | bytes 3600000 | tf_op jit(solution)/shard_map/emit/pallas_call | solution.py:401
  54.8 0.0 collective-permute-done.2.refs_1_
  54.8 1.1 %mix_back.1 = (f32[8,24,128]{2,1,0:T(8,128)S(1)}, f32[160,128]{1,0:T(8,128)S(1)}) custom-call(f32[16,8,384]{2,1,0:T(8,128)S(1)} %all_to_all.21.refs_0_, f32[16,8,384]{2,1,0:T(8,128)S(1)} %collective-permute-done.2.refs_1_, f32[256,256]{1,0:T(8,128)S(1)} %get-tuple-element.54.refs_2_, f32[8,20,24,128]{3,2,1,0:T(8,128)S(1)} %get-tuple-element.55.refs_3_), custom_call_target="tpu_custom_call" | custom-call | bytes 3000000 | tf_op jit(solution)/shard_map/mix_back/pallas_call | solution.py:401
  55.9 0.5 collective-permute-start.3
  56.5 0.9 %collective-permute-done.3.refs_1_ = f32[160,128]{1,0:T(8,128)S(1)} collective-permute-done((f32[160,128]{1,0:T(8,128)S(1)}, f32[160,128]{1,0:T(8,128)S(1)}, u32[]{:S(2)}, u32[]{:S(2)}) %collective-permute-start.3) | collective-permute-done | bytes 81952 | tf_op jit(solution)/shard_map/ppermute | solution.py:433
  57.4 1.5 %plane_cells.3 = f32[16,8,384]{2,1,0:T(8,128)} custom-call(f32[160,128]{1,0:T(8,128)S(1)} %get-tuple-element.73.refs_0_, f32[160,128]{1,0:T(8,128)S(1)} %collective-permute-done.3.refs_1_, f32[128,512]{1,0:T(8,128)S(1)} %get-tuple-element.57.refs_2_), custom_call_target="tpu_custom_call" | custom-call | bytes 3000000 | tf_op jit(solution)/shard_map/plane_cells/pallas_call | solution.py:401
  58.9 3.6 %all-to-all-start.3 = ((f32[16,8,384]{2,1,0:T(8,128)}), f32[16,8,384]{2,1,0:T(8,128)S(1)}, u32[]{:S(2)}, u32[]{:S(2)}) async-start(f32[16,8,384]{2,1,0:T(8,128)} %plane_cells.3), calls=%async_computation.3 | async-start | bytes 393216 | tf_op jit(solution)/shard_map/all_to_all | solution.py:428
  62.5 8.2 %grad_weights.1 = f32[16,20,4,16,20]{4,3,2,1,0:T(8,128)} custom-call(f32[160,128]{1,0:T(8,128)S(1)} %get-tuple-element.77.refs_0_, f32[8,24,128]{2,1,0:T(8,128)S(1)} %get-tuple-element.78.refs_1_), custom_call_target="tpu_custom_call" | custom-call | bytes 15000000 | tf_op jit(solution)/shard_map/grad_weights/pallas_call | solution.py:401
  70.7 0.6 all-to-all-done.3.refs_0_
  71.3 1.4 %finish.1 = bf16[20,2,4,512]{3,2,1,0:T(4,128)(2,1)} custom-call(f32[16,8,384]{2,1,0:T(8,128)S(1)} %all-to-all-done.3.refs_0_, f32[160,512]{1,0:T(8,128)S(1)} %get-tuple-element.80.refs_1_, f32[128,512]{1,0:T(8,128)S(1)} %get-tuple-element.81.refs_2_), custom_call_target="tpu_custom_call" | custom-call | bytes 3000000 | tf_op jit(solution)/shard_map/finish/pallas_call | solution.py:401
Async XLA Ops:
  0.6 19.2 %copy-start = (bf16[20,20]{1,0:T(8,128)(2,1)S(1)}, bf16[20,20]{1,0:T(8,128)(2,1)}, u32[]{:S(2)}) copy-start(bf16[20,20]{1,0:T(8,128)(2,1)} %refs_2_.3) | copy-start | bytes 2404
  0.6 19.2 %copy-start.1 = (f32[20]{0:T(128)S(1)}, f32[20]{0:T(128)}, u32[]{:S(2)}) copy-start(f32[20]{0:T(128)} %refs_3_.3) | copy-start | bytes 244
  2.9 17.0 %all-to-all-start = ((f32[16,8,384]{2,1,0:T(8,128)}), f32[16,8,384]{2,1,0:T(8,128)S(1)}, u32[]{:S(2)}, u32[]{:S(2)}) async-start(f32[16,8,384]{2,1,0:T(8,128)} %depth_forward.1.refs_1_), calls=%async_computation | async-start | bytes 393216 | tf_op jit(solution)/shard_map/all_to_all | solution.py:428
  19.9 2.2 %collective-permute-start = (f32[16,8,384]{2,1,0:T(8,128)S(1)}, f32[16,8,384]{2,1,0:T(8,128)S(1)}, u32[]{:S(2)}, u32[]{:S(2)}) collective-permute-start(f32[16,8,384]{2,1,0:T(8,128)S(1)} %all-to-all-done.refs_0_), channel_id=1, source_target_pairs={{0,1},{1,0},{2,3},{3,2},{4,5},{5,4},{6,7},{7,6},{8,9},{9,8},{10,11... | collective-permute-start | bytes 589832 | tf_op jit(solution)/shard_map/ppermute | solution.py:433
  22.9 1.5 %collective-permute-start.1 = (f32[160,128]{1,0:T(8,128)S(1)}, f32[160,128]{1,0:T(8,128)S(1)}, u32[]{:S(2)}, u32[]{:S(2)}) collective-permute-start(f32[160,128]{1,0:T(8,128)S(1)} %get-tuple-element.56.refs_0_), channel_id=1, source_target_pairs={{0,1},{1,0},{2,3},{3,2},{4,5},{5,4},{6,7},{7,6},{8,9},{9,8},{10,11... | collective-permute-start | bytes 245768 | tf_op jit(solution)/shard_map/ppermute | solution.py:433
  53.2 1.7 %collective-permute-start.2 = (f32[16,8,384]{2,1,0:T(8,128)S(1)}, f32[16,8,384]{2,1,0:T(8,128)S(1)}, u32[]{:S(2)}, u32[]{:S(2)}) collective-permute-start(f32[16,8,384]{2,1,0:T(8,128)S(1)} %all_to_all.21.refs_0_), channel_id=1, source_target_pairs={{0,1},{1,0},{2,3},{3,2},{4,5},{5,4},{6,7},{7,6},{8,9},{9,8},{10,11... | collective-permute-start | bytes 589832 | tf_op jit(solution)/shard_map/ppermute | solution.py:433
  55.9 1.5 %collective-permute-start.3 = (f32[160,128]{1,0:T(8,128)S(1)}, f32[160,128]{1,0:T(8,128)S(1)}, u32[]{:S(2)}, u32[]{:S(2)}) collective-permute-start(f32[160,128]{1,0:T(8,128)S(1)} %get-tuple-element.73.refs_0_), channel_id=1, source_target_pairs={{0,1},{1,0},{2,3},{3,2},{4,5},{5,4},{6,7},{7,6},{8,9},{9,8},{10,11... | collective-permute-start | bytes 245768 | tf_op jit(solution)/shard_map/ppermute | solution.py:433
  58.9 12.4 %all-to-all-start.3 = ((f32[16,8,384]{2,1,0:T(8,128)}), f32[16,8,384]{2,1,0:T(8,128)S(1)}, u32[]{:S(2)}, u32[]{:S(2)}) async-start(f32[16,8,384]{2,1,0:T(8,128)} %plane_cells.3), calls=%async_computation.3 | async-start | bytes 393216 | tf_op jit(solution)/shard_map/all_to_all | solution.py:428

commit v5 on v4

--- a/solution.py
+++ b/solution.py
@@ -37,20 +37,21 @@
     return np.stack([np.cos(angles) * factor, -np.sin(angles) * factor], axis=1).astype(np.float32)
 
 
-def plane_factors(sizes):
+def plane_tables(sizes):
     length_x, length_y = sizes.nx * sizes.cells_x, sizes.ny * sizes.cells_y
-    lane = np.arange(4 * sizes.half)
-    mode = lane % sizes.half
-    quarter = lane // sizes.half % 2 - lane // (2 * sizes.half)
-    inside = mode < sizes.kept
-    kx = np.arange(sizes.ny)[:, None] * sizes.local_x + np.where(inside, mode // sizes.kept_y, 0)
-    turn_x = np.mod(np.arange(length_x)[:, None] * frequencies(sizes.kept_x)[kx][:, None, :], length_x) / length_x
-    turn_y = np.mod(np.arange(length_y)[:, None] * frequencies(sizes.kept_y)[mode % sizes.kept_y], length_y) / length_y
-    angle_x, angle_y = 2.0 * math.pi * turn_x, 2.0 * math.pi * (turn_y + quarter / 4.0)
-    scale = inside / math.sqrt(length_x * length_y)
-    factors_x = np.concatenate([np.cos(angle_x), -np.sin(angle_x)], -1)
-    factors_y = np.concatenate([np.cos(angle_y) * scale, np.sin(angle_y) * scale], -1)
-    return factors_x.astype(np.float32), factors_y.astype(np.float32)
+    phase_x = np.mod(np.arange(length_x)[:, None] * frequencies(sizes.kept_x), length_x) / length_x
+    phase_y = np.mod(np.arange(length_y)[:, None] * frequencies(sizes.kept_y), length_y) / length_y
+    angle = 2.0 * math.pi * (phase_x[:, None, :, None] + phase_y[None, :, None, :])
+    scale = 1.0 / math.sqrt(length_x * length_y)
+    cosine, sine = np.cos(angle) * scale, np.sin(angle) * scale
+    parts = np.stack([np.stack([cosine, -sine]), np.stack([sine, cosine])])
+    parts = parts.reshape(
+        2, 2, sizes.nx, sizes.cells_x, sizes.ny // 2, 2, sizes.cells_y, sizes.ny, sizes.kept
+    ).transpose(7, 5, 2, 4, 3, 6, 0, 1, 8)
+    padded = np.zeros(parts.shape[:-1] + (sizes.half,), np.float32)
+    padded[..., : sizes.kept] = parts
+    ordered = np.stack([padded[j][[j % 2, 1 - j % 2]] for j in range(sizes.ny)])
+    return ordered.reshape(sizes.ny, 2 * sizes.chips * sizes.cells, 4 * sizes.half)
 
 
 class Sizes:
@@ -170,16 +171,6 @@
     return jnp.where(same, wide, 0.0).astype(BF16)
 
 
-def prepare(sizes, field, cotangent, weight, bias, inverse, forward, local, cot_cells, inverse_out, forward_out, cells, field_here, cot_here, semaphores):
-    fetch((field, cotangent, inverse, forward), (field_here, cot_here, inverse_out, forward_out), semaphores)
-    values = gather_cells(field_here, cells, sizes).astype(BF16)
-    bypass = dot(cell_mixer(weight[...], True, sizes), values)
-    for o in range(sizes.channels):
-        rows = slice(o * sizes.cells, (o + 1) * sizes.cells)
-        local[rows, :] = bypass[rows, :] + bias[o]
-    gather_cells(cot_here, cot_cells, sizes)
-
-
 def emit(sizes, pre, signal, weight, inverse, layer_out, local, inverse_out, semaphore):
     copy = pltpu.make_async_copy(inverse, inverse_out, semaphore.at[0])
     copy.start()
@@ -188,46 +179,36 @@
     copy.wait()
 
 
-def plane_tables(sizes, place, mine, other, factors_y, table, back):
-    half_rows = sizes.chips * sizes.cells
-    lanes = 4 * sizes.half
-
-    def chosen(rows, length, index):
-        column = lax.broadcasted_iota(jnp.int32, (rows, length), 1)
-        return jnp.where(column == index(lax.broadcasted_iota(jnp.int32, (rows, length), 0)), 1.0, 0.0)
-
-    def at_x(row):
-        chip = lax.rem(row // sizes.cells, sizes.chips)
-        return chip // (sizes.ny // 2) * sizes.cells_x + lax.rem(row // sizes.cells_y, sizes.cells_x)
-
-    def at_y(row):
-        chip = lax.rem(row // sizes.cells, sizes.chips)
-        core = lax.rem(place + row // half_rows, 2)
-        return (lax.rem(chip, sizes.ny // 2) * 2 + core) * sizes.cells_y + lax.rem(row, sizes.cells_y)
-
-    def product(left, right):
-        return left[:, :lanes] * right[:, :lanes] + left[:, lanes:] * right[:, lanes:]
-
-    pick_x = chosen(2 * half_rows, sizes.nx * sizes.cells_x, at_x)
-    pick_y = chosen(2 * half_rows, sizes.ny * sizes.cells_y, at_y)
-    spread_y = dot(pick_y, factors_y[...], precision=EXACT)
-    table[...] = product(dot(pick_x, mine[...], precision=EXACT), spread_y)
-    back[:, :lanes] = table[:half_rows, :]
-    back[:, lanes:] = product(dot(pick_x[:half_rows], other[...], precision=EXACT), spread_y[:half_rows])
-
-
-def turn_weights(sizes, source, after, place, factors_x, factors_y, target, table, back, here, mine, other, mine_y, semaphores, small):
+def prepare(
+    sizes, source, after, place, tables, field, cotangent, weight, bias, inverse, forward,
+    target, table, back, local, cot_cells, inverse_out, forward_out,
+    here, cells, field_here, cot_here, semaphores, small,
+):
     del after
     place = place[0]
     pair = place + 1 - 2 * lax.rem(place, 2)
-    moves = ((factors_x.at[place], mine), (factors_x.at[pair], other), (factors_y, mine_y))
-    tables = [pltpu.make_async_copy(*move, small.at[at]) for at, move in enumerate(moves)]
+    half_rows, lanes = back.shape[0], table.shape[1]
+    moves = (
+        (field, field_here),
+        (cotangent, cot_here),
+        (tables.at[place], table),
+        (tables.at[place, pl.ds(0, half_rows)], back.at[:, pl.ds(0, lanes)]),
+        (tables.at[pair, pl.ds(half_rows, half_rows)], back.at[:, pl.ds(lanes, lanes)]),
+        (inverse, inverse_out),
+        (forward, forward_out),
+    )
+    few = [pltpu.make_async_copy(*move, small.at[at]) for at, move in enumerate(moves)]
     copies = [pltpu.make_async_copy(source.at[at], here.at[at], semaphores.at[at]) for at in range(2 * sizes.modes)]
-    for copy in tables + copies:
+    for copy in few + copies:
         copy.start()
-    for copy in tables:
-        copy.wait()
-    plane_tables(sizes, place, mine, other, mine_y, table, back)
+    few[0].wait()
+    values = gather_cells(field_here, cells, sizes).astype(BF16)
+    bypass = dot(cell_mixer(weight[...], True, sizes), values)
+    for o in range(sizes.channels):
+        rows = slice(o * sizes.cells, (o + 1) * sizes.cells)
+        local[rows, :] = bypass[rows, :] + bias[o]
+    few[1].wait()
+    gather_cells(cot_here, cot_cells, sizes)
     if sizes.half > sizes.kept:
         target[...] = jnp.zeros_like(target)
     elif sizes.rows > sizes.channels:
@@ -249,6 +230,8 @@
         return carry
 
     lax.fori_loop(0, sizes.modes, turn, 0)
+    for copy in few[2:]:
+        copy.wait()
 
 
 def plane_spectra(sizes, own, other, table, target):
@@ -323,31 +306,26 @@
         mixed[mode_rows(m, sizes), :] = jnp.where(real, real_part, imag_part)
 
 
-def grad_weights(sizes, spectra, back, target, here, semaphores):
-    real = first_lanes(1, sizes)
-
-    def copy(at):
-        return pltpu.make_async_copy(here.at[at], target.at[at], semaphores.at[at])
-
-    def one_mode(mode, carry):
+def grad_weights(sizes, spectra, back, target, here, straight, crossed, semaphores):
+    values = spectra[...]
+    turned = swap_parts(values, sizes)
+    real = first_lanes(values.shape[0], sizes)
+    straight[...] = jnp.where(real, values, turned)
+    crossed[...] = jnp.where(real, turned, -values)
+    copies = [pltpu.make_async_copy(here.at[at], target.at[at], semaphores.at[at]) for at in range(2 * sizes.modes)]
+    for mode in range(sizes.modes):
         rows = back[mode]
         turned = swap_parts(rows, sizes)
         for w in range(sizes.channels):
-            row = spectra[pl.ds(w * sizes.modes + mode, 1), :]
-            swapped = swap_parts(row, sizes)
-            real_part = jnp.where(real, row, swapped)
-            imag_part = jnp.where(real, swapped, -row)
-            block = (real_part * rows + imag_part * turned).T
+            at = slice(w * sizes.modes + mode, w * sizes.modes + mode + 1)
+            block = (straight[at, :] * rows + crossed[at, :] * turned).T
             for s in range(2):
                 part = block[s * sizes.half : s * sizes.half + sizes.kept, : sizes.channels]
                 here[2 * mode + s, w] = part.reshape(sizes.local_x, sizes.kept_y, sizes.channels)
         for s in range(2):
-            copy(2 * mode + s).start()
-        return carry
-
-    lax.fori_loop(0, sizes.modes, one_mode, 0)
-    for at in range(2 * sizes.modes):
-        copy(at).wait()
+            copies[2 * mode + s].start()
+    for copy in copies:
+        copy.wait()
 
 
 def gelu_parts(pre):
@@ -446,7 +424,6 @@
     weight_shape = (2 * z.modes,) + native.shape[2:]
     weight_scratch = [pltpu.VMEM(weight_shape, F32), pltpu.SemaphoreType.DMA((2 * z.modes,))]
 
-    factors_x, factors_y = plane_factors(z)
     half_rows = z.chips * z.cells
 
     sent = whole_call(
@@ -455,35 +432,26 @@
         field, forward_first, specs=[HBM] * 2,
     )
     own = exchange(sent)
-    factor_scratch = pltpu.VMEM(factors_x.shape[1:], F32)
-    turned, plane, plane_back = whole_call(
-        turn_weights, z, 5000,
+    turned, plane, plane_back, local, cot_cells, inverse_here, forward_here = whole_call(
+        prepare, z, 5000,
         (
             shape_of((z.modes, z.channels, z.rows, 2 * z.half)),
             shape_of((2 * half_rows, 4 * z.half)),
             shape_of((half_rows, 8 * z.half)),
+            shape_of(cells_shape),
+            shape_of(cells_shape),
+            shape_of(inverse_first.shape),
+            shape_of(forward_back.shape, BF16),
         ),
-        [
-            weight_scratch[0], factor_scratch, factor_scratch, pltpu.VMEM(factors_y.shape, F32),
-            weight_scratch[1], pltpu.SemaphoreType.DMA((3,)),
-        ],
-        native.reshape(weight_shape), sent, lax.axis_index("gy").reshape(1), jnp.asarray(factors_x), jnp.asarray(factors_y),
-        specs=[HBM, ANYWHERE, SMEM, HBM, HBM], room=28,
-    )
-    own, turned, plane, plane_back, field, cotangent = lax.optimization_barrier(
-        (own, turned, plane, plane_back, field, cotangent)
+        [weight_scratch[0], cells_scratch, field_scratch, field_scratch, weight_scratch[1], pltpu.SemaphoreType.DMA((7,))],
+        native.reshape(weight_shape), sent, lax.axis_index("gy").reshape(1), jnp.asarray(plane_tables(z)),
+        field, cotangent, pointwise_weight, channel_bias, inverse_first, forward_back,
+        specs=[HBM, ANYWHERE, SMEM, HBM, HBM, HBM, VMEM, SMEM, HBM, HBM], room=28,
+    )
+    own, turned, plane, plane_back, local, cot_cells, inverse_here, forward_here = lax.optimization_barrier(
+        (own, turned, plane, plane_back, local, cot_cells, inverse_here, forward_here)
     )
     other = other_core(own)
-    local, cot_cells, inverse_here, forward_here = whole_call(
-        prepare, z, 1500,
-        (shape_of(cells_shape), shape_of(cells_shape), shape_of(inverse_first.shape), shape_of(forward_back.shape, BF16)),
-        [cells_scratch, field_scratch, field_scratch, pltpu.SemaphoreType.DMA((4,))],
-        field, cotangent, pointwise_weight, channel_bias, inverse_first, forward_back,
-        specs=[HBM, HBM, VMEM, SMEM, HBM, HBM],
-    )
-    other, local, cot_cells, inverse_here, forward_here = lax.optimization_barrier(
-        (other, local, cot_cells, inverse_here, forward_here)
-    )
     spectra, mixed = whole_call(
         mix_forward, z, 1000, (shape_of(spectra_shape), shape_of(spectra_shape)), [], own, other, plane, turned
     )
@@ -510,7 +478,9 @@
     sent, back, spectra = lax.optimization_barrier((sent, back, spectra))
     returned = exchange(sent)
     gradient = whole_call(
-        grad_weights, z, 5000, shape_of(weight_shape), weight_scratch, spectra, back, out_specs=HBM, room=28
+        grad_weights, z, 5000, shape_of(weight_shape),
+        [weight_scratch[0], spectra_scratch, spectra_scratch, weight_scratch[1]],
+        spectra, back, out_specs=HBM, room=28,
     )
     returned, gradient = lax.optimization_barrier((returned, gradient))
     grad_field = whole_call(

time: 73.2 us -> 74.6 us (1.019)
  Pallas kernels: 29.3 us -> 22.3 us
  waiting for transfers between devices: 3.03 us -> 7.78 us
  local copies, waits for them, and re-layouts: 0.01 us -> 3.68 us
    pallas_call x11 -> x10, Pallas kernels: 29.3 us -> 22.3 us  [whole_call(): pl.pallas_call(kernel, out_shape=out_shape, in_specs=specs or [VMEM] * le...]
    unnamed x4 -> x10, local copies, waits for them, and re-layouts: 0.01 us -> 3.68 us
    all_to_all x2, waiting for transfers between devices: 1.17 us -> 4.27 us  [exchange(): lax.all_to_all(payload, ('gx', 'gy'), split_axis=0, concat_axis=0, tiled=...]
    ppermute x4, waiting for transfers between devices: 1.85 us -> 3.5 us  [other_core(): return lax.ppermute(payload, 'gy', pairs)]
  transfers between devices with their start and end apart: 6 -> 6, of which waited for: 4 -> 4; matrix products, arithmetic and copies ran while one was open for 0% -> 0% of each run, Pallas kernels for 28% -> 18%
where the time goes in v5:
time: 74.6 us; the launch traced here: 74.1 us
  blocking collectives  26.9 us (36%)
  Pallas kernels  22.3 us (30%)
  starting transfers between devices  12.6 us (17%)
  waiting for transfers between devices  7.78 us (10%)
  local copies, waits for them, and re-layouts  3.68 us (5%)
    all_to_all x2, blocking collectives, exchange(): lax.all_to_all(payload, ('gx', 'gy'), split_axis=0, concat_axis=0, tiled=...  26.9 us
    pallas_call x10, Pallas kernels, whole_call(): pl.pallas_call(kernel, out_shape=out_shape, in_specs=specs or [VMEM] * le...  22.3 us
    all_to_all x2, starting transfers between devices, exchange(): lax.all_to_all(payload, ('gx', 'gy'), split_axis=0, concat_axis=0, tiled=...  11.9 us
    all_to_all x2, waiting for transfers between devices, exchange(): lax.all_to_all(payload, ('gx', 'gy'), split_axis=0, concat_axis=0, tiled=...  4.27 us
    unnamed x10, local copies, waits for them, and re-layouts  3.68 us
    ppermute x4, waiting for transfers between devices, other_core(): return lax.ppermute(payload, 'gy', pairs)  3.5 us
  transfers between devices with their start and end apart: 6, of which 4 were waited for; matrix products, arithmetic and copies ran while one was open for 0% of the time, Pallas kernels for 18%

profile of v5, /device:TPU:0, one launch (start us, length us, event | category | flops | bytes accessed | tf_op | source)
XLA Modules:
  0.0 74.1 jit_solution(3227697088570406591)
XLA Ops:
  0.6 2.2 %depth_forward.1.refs_1_ = f32[16,8,384]{2,1,0:T(8,128)} custom-call(bf16[20,2,4,512]{3,2,1,0:T(4,128)(2,1)} %refs_4_.1, bf16[512,128]{1,0:T(8,128)(2,1)} %constant.14.clone.refs_1_), custom_call_target="tpu_custom_call" | custom-call | bytes 4500000 | tf_op jit(solution)/shard_map/depth_forward/pallas_call | solution.py:379
  2.9 8.3 %all-to-all-start = ((f32[16,8,384]{2,1,0:T(8,128)}), f32[16,8,384]{2,1,0:T(8,128)S(1)}, u32[]{:S(2)}, u32[]{:S(2)}) async-start(f32[16,8,384]{2,1,0:T(8,128)} %depth_forward.1.refs_1_), calls=%async_computation | async-start | bytes 393216 | tf_op jit(solution)/shard_map/all_to_all | solution.py:406
  11.2 0.0 copy-start.2
  11.2 0.7 copy-done.2
  11.9 0.0 copy-start.4
  11.9 0.7 copy-done.4
  12.5 7.0 %prepare.1 = (f32[8,20,24,128]{3,2,1,0:T(8,128)S(1)}, f32[256,256]{1,0:T(8,128)S(1)}, f32[128,512]{1,0:T(8,128)S(1)}, f32[160,512]{1,0:T(8,128)S(1)}, f32[160,51...) custom-call(f32[16,20,4,16,20]{4,3,2,1,0:T(8,128)} %bitcast.7, ...), custom_call_target="tpu_custom_call" | custom-call | bytes 15000000 | tf_op jit(solution)/shard_map/prepare/pallas_call | solution.py:379
  19.5 0.0 copy-start
  19.5 0.7 copy-done
  20.2 0.0 all-to-all-done.refs_0_
  20.2 0.0 collective-permute-start
  20.2 1.4 %collective-permute-done.refs_1_ = f32[16,8,384]{2,1,0:T(8,128)S(1)} collective-permute-done((f32[16,8,384]{2,1,0:T(8,128)S(1)}, f32[16,8,384]{2,1,0:T(8,128)S(1)}, u32[]{:S(2)}, u32[]{:S(2)}) %collective-permute-start) | collective-permute-done | bytes 196640 | tf_op jit(solution)/shard_map/ppermute | solution.py:411
  21.7 0.9 %mix_forward.1 = (f32[160,128]{1,0:T(8,128)S(1)}, f32[160,128]{1,0:T(8,128)S(1)}) custom-call(f32[16,8,384]{2,1,0:T(8,128)S(1)} %all-to-all-done.refs_0_, f32[16,8,384]{2,1,0:T(8,128)S(1)} %collective-permute-done.refs_1_, f32[256,256]{1,0:T(8,128)S(1)} %get-tuple-element.48.refs_2_, f32[8,20,24,128]{3,2,1,0:T(8,128)S(1)} %get-tuple-element.49.refs_3_), custom_call_target="tpu_custom_call" | custom-call | bytes 3000000 | tf_op jit(solution)/shard_map/mix_forward/pallas_call | solution.py:379
  22.5 0.2 collective-permute-start.1
  22.7 1.1 %collective-permute-done.1.refs_1_ = f32[160,128]{1,0:T(8,128)S(1)} collective-permute-done((f32[160,128]{1,0:T(8,128)S(1)}, f32[160,128]{1,0:T(8,128)S(1)}, u32[]{:S(2)}, u32[]{:S(2)}) %collective-permute-start.1) | collective-permute-done | bytes 81952 | tf_op jit(solution)/shard_map/ppermute | solution.py:411
  23.9 0.8 %plane_cells.2 = f32[16,8,384]{2,1,0:T(8,128)S(1)} custom-call(f32[160,128]{1,0:T(8,128)S(1)} %get-tuple-element.50.refs_0_, f32[160,128]{1,0:T(8,128)S(1)} %collective-permute-done.1.refs_1_, f32[128,512]{1,0:T(8,128)S(1)} %get-tuple-element.51.refs_2_), custom_call_target="tpu_custom_call" | custom-call | bytes 3000000 | tf_op jit(solution)/shard_map/plane_cells/pallas_call | solution.py:379
  24.7 15.7 %all_to_all.20.refs_0_ = f32[16,8,384]{2,1,0:T(8,128)S(1)} all-to-all(f32[16,8,384]{2,1,0:T(8,128)S(1)} %plane_cells.2), channel_id=1, replica_groups={{0,2,4,6,8,10,12,14,16,18,20,22,24,26,28,30},{1,3,5,7,9,11,13,15,17,19,..., dimensions={0} | all-to-all | bytes 393216 | tf_op jit(solution)/shard_map/all_to_all | solution.py:406
  40.4 0.0 copy-start.1
  40.4 0.9 %copy-done.1 = f32[128,512]{1,0:T(8,128)S(1)} copy-done((f32[128,512]{1,0:T(8,128)S(1)}, f32[128,512]{1,0:T(8,128)}, u32[]{:S(2)}) %copy-start.1) | copy-done | bytes 262168
  41.3 1.3 %activate.1 = (f32[160,512]{1,0:T(8,128)S(1)}, bf16[160,512]{1,0:T(8,128)(2,1)S(1)}, f32[16,8,384]{2,1,0:T(8,128)S(1)}) custom-call(f32[16,8,384]{2,1,0:T(8,128)S(1)} %all_to_all.20.refs_0_, f32[160,512]{1,0:T(8,128)S(1)} %get-tuple-element.52.refs_1_, f32[160,512]{1,0:T(8,128)S(1)} %get-tuple-element.53.refs_2_, f32[128,512]{1,0:T(8,128)S(1)} %copy-done.1, ...), custom_call_target="tpu_custom_call" | custom-call | bytes 6000000 | tf_op jit(solution)/shard_map/activate/pallas_call | solution.py:379
  42.6 11.2 %all_to_all.21.refs_0_ = f32[16,8,384]{2,1,0:T(8,128)S(1)} all-to-all(f32[16,8,384]{2,1,0:T(8,128)S(1)} %get-tuple-element.56), channel_id=1, replica_groups={{0,2,4,6,8,10,12,14,16,18,20,22,24,26,28,30},{1,3,5,7,9,11,13,15,17,19,..., dimensions={0} | all-to-all | bytes 393216 | tf_op jit(solution)/shard_map/all_to_all | solution.py:406
  53.8 0.0 collective-permute-start.2
  53.9 0.0 copy-start.3
  53.9 0.7 copy-done.3
  54.5 1.7 %emit.1 = (bf16[20,2,4,512]{3,2,1,0:T(4,128)(2,1)}, f32[160,512]{1,0:T(8,128)S(1)}, f32[128,512]{1,0:T(8,128)S(1)}) custom-call(f32[160,512]{1,0:T(8,128)S(1)} %get-tuple-element.60.refs_0_, bf16[160,512]{1,0:T(8,128)(2,1)S(1)} %get-tuple-element.61.refs_1_, bf16[20,20]{1,0:T(8,128)(2,1)S(1)} %copy-done.3, f32[128,512]{1,0:T(8,128)} %constant.16.clone.refs_3_), custom_call_target="tpu_custom_call" | custom-call | bytes 3600000 | tf_op jit(solution)/shard_map/emit/pallas_call | solution.py:379
  56.2 0.0 collective-permute-done.2.refs_1_
  56.2 1.1 %mix_back.1 = (f32[8,24,128]{2,1,0:T(8,128)S(1)}, f32[160,128]{1,0:T(8,128)S(1)}) custom-call(f32[16,8,384]{2,1,0:T(8,128)S(1)} %all_to_all.21.refs_0_, f32[16,8,384]{2,1,0:T(8,128)S(1)} %collective-permute-done.2.refs_1_, f32[256,256]{1,0:T(8,128)S(1)} %get-tuple-element.48.refs_2_, f32[8,20,24,128]{3,2,1,0:T(8,128)S(1)} %get-tuple-element.49.refs_3_), custom_call_target="tpu_custom_call" | custom-call | bytes 3000000 | tf_op jit(solution)/shard_map/mix_back/pallas_call | solution.py:379
  57.3 0.5 collective-permute-start.3
  57.9 0.9 %collective-permute-done.3.refs_1_ = f32[160,128]{1,0:T(8,128)S(1)} collective-permute-done((f32[160,128]{1,0:T(8,128)S(1)}, f32[160,128]{1,0:T(8,128)S(1)}, u32[]{:S(2)}, u32[]{:S(2)}) %collective-permute-start.3) | collective-permute-done | bytes 81952 | tf_op jit(solution)/shard_map/ppermute | solution.py:411
  58.8 1.5 %plane_cells.3 = f32[16,8,384]{2,1,0:T(8,128)} custom-call(f32[160,128]{1,0:T(8,128)S(1)} %get-tuple-element.67.refs_0_, f32[160,128]{1,0:T(8,128)S(1)} %collective-permute-done.3.refs_1_, f32[128,512]{1,0:T(8,128)S(1)} %get-tuple-element.51.refs_2_), custom_call_target="tpu_custom_call" | custom-call | bytes 3000000 | tf_op jit(solution)/shard_map/plane_cells/pallas_call | solution.py:379
  60.3 3.6 %all-to-all-start.3 = ((f32[16,8,384]{2,1,0:T(8,128)}), f32[16,8,384]{2,1,0:T(8,128)S(1)}, u32[]{:S(2)}, u32[]{:S(2)}) async-start(f32[16,8,384]{2,1,0:T(8,128)} %plane_cells.3), calls=%async_computation.3 | async-start | bytes 393216 | tf_op jit(solution)/shard_map/all_to_all | solution.py:406
  63.8 4.6 %grad_weights.1 = f32[16,20,4,16,20]{4,3,2,1,0:T(8,128)} custom-call(f32[160,128]{1,0:T(8,128)S(1)} %get-tuple-element.71.refs_0_, f32[8,24,128]{2,1,0:T(8,128)S(1)} %get-tuple-element.72.refs_1_), custom_call_target="tpu_custom_call" | custom-call | bytes 15000000 | tf_op jit(solution)/shard_map/grad_weights/pallas_call | solution.py:379
  68.4 4.3 %all-to-all-done.3.refs_0_ = f32[16,8,384]{2,1,0:T(8,128)S(1)} async-done(((f32[16,8,384]{2,1,0:T(8,128)}), f32[16,8,384]{2,1,0:T(8,128)S(1)}, u32[]{:S(2)}, u32[]{:S(2)}) %all-to-all-start.3) | async-done | bytes 196640 | tf_op jit(solution)/shard_map/all_to_all | solution.py:406
  72.7 1.4 %finish.1 = bf16[20,2,4,512]{3,2,1,0:T(4,128)(2,1)} custom-call(f32[16,8,384]{2,1,0:T(8,128)S(1)} %all-to-all-done.3.refs_0_, f32[160,512]{1,0:T(8,128)S(1)} %get-tuple-element.74.refs_1_, f32[128,512]{1,0:T(8,128)S(1)} %get-tuple-element.75.refs_2_), custom_call_target="tpu_custom_call" | custom-call | bytes 3000000 | tf_op jit(solution)/shard_map/finish/pallas_call | solution.py:379
Async XLA Ops:
  2.9 17.4 %all-to-all-start = ((f32[16,8,384]{2,1,0:T(8,128)}), f32[16,8,384]{2,1,0:T(8,128)S(1)}, u32[]{:S(2)}, u32[]{:S(2)}) async-start(f32[16,8,384]{2,1,0:T(8,128)} %depth_forward.1.refs_1_), calls=%async_computation | async-start | bytes 393216 | tf_op jit(solution)/shard_map/all_to_all | solution.py:406
  11.2 0.7 copy-start.2
  11.9 0.7 copy-start.4
  19.5 0.7 copy-start
  20.2 1.4 %collective-permute-start = (f32[16,8,384]{2,1,0:T(8,128)S(1)}, f32[16,8,384]{2,1,0:T(8,128)S(1)}, u32[]{:S(2)}, u32[]{:S(2)}) collective-permute-start(f32[16,8,384]{2,1,0:T(8,128)S(1)} %all-to-all-done.refs_0_), channel_id=1, source_target_pairs={{0,1},{1,0},{2,3},{3,2},{4,5},{5,4},{6,7},{7,6},{8,9},{9,8},{10,11... | collective-permute-start | bytes 589832 | tf_op jit(solution)/shard_map/ppermute | solution.py:411
  22.5 1.3 %collective-permute-start.1 = (f32[160,128]{1,0:T(8,128)S(1)}, f32[160,128]{1,0:T(8,128)S(1)}, u32[]{:S(2)}, u32[]{:S(2)}) collective-permute-start(f32[160,128]{1,0:T(8,128)S(1)} %get-tuple-element.50.refs_0_), channel_id=1, source_target_pairs={{0,1},{1,0},{2,3},{3,2},{4,5},{5,4},{6,7},{7,6},{8,9},{9,8},{10,11... | collective-permute-start | bytes 245768 | tf_op jit(solution)/shard_map/ppermute | solution.py:411
  40.4 1.0 %copy-start.1 = (f32[128,512]{1,0:T(8,128)S(1)}, f32[128,512]{1,0:T(8,128)}, u32[]{:S(2)}) copy-start(f32[128,512]{1,0:T(8,128)} %copy-done) | copy-start | bytes 786436
  53.8 2.4 %collective-permute-start.2 = (f32[16,8,384]{2,1,0:T(8,128)S(1)}, f32[16,8,384]{2,1,0:T(8,128)S(1)}, u32[]{:S(2)}, u32[]{:S(2)}) collective-permute-start(f32[16,8,384]{2,1,0:T(8,128)S(1)} %all_to_all.21.refs_0_), channel_id=1, source_target_pairs={{0,1},{1,0},{2,3},{3,2},{4,5},{5,4},{6,7},{7,6},{8,9},{9,8},{10,11... | collective-permute-start | bytes 589832 | tf_op jit(solution)/shard_map/ppermute | solution.py:411
  53.9 0.7 copy-start.3
  57.3 1.5 %collective-permute-start.3 = (f32[160,128]{1,0:T(8,128)S(1)}, f32[160,128]{1,0:T(8,128)S(1)}, u32[]{:S(2)}, u32[]{:S(2)}) collective-permute-start(f32[160,128]{1,0:T(8,128)S(1)} %get-tuple-element.67.refs_0_), channel_id=1, source_target_pairs={{0,1},{1,0},{2,3},{3,2},{4,5},{5,4},{6,7},{7,6},{8,9},{9,8},{10,11... | collective-permute-start | bytes 245768 | tf_op jit(solution)/shard_map/ppermute | solution.py:411
  60.3 12.4 %all-to-all-start.3 = ((f32[16,8,384]{2,1,0:T(8,128)}), f32[16,8,384]{2,1,0:T(8,128)S(1)}, u32[]{:S(2)}, u32[]{:S(2)}) async-start(f32[16,8,384]{2,1,0:T(8,128)} %plane_cells.3), calls=%async_computation.3 | async-start | bytes 393216 | tf_op jit(solution)/shard_map/all_to_all | solution.py:406

commit v6 on v5

--- a/solution.py
+++ b/solution.py
@@ -171,55 +171,55 @@
     return jnp.where(same, wide, 0.0).astype(BF16)
 
 
-def emit(sizes, pre, signal, weight, inverse, layer_out, local, inverse_out, semaphore):
-    copy = pltpu.make_async_copy(inverse, inverse_out, semaphore.at[0])
-    copy.start()
+def emit(sizes, pre, signal, weight, inverse, layer_out, local, inverse_out, weight_here, semaphores):
+    copies = [
+        pltpu.make_async_copy(weight, weight_here, semaphores.at[0]),
+        pltpu.make_async_copy(inverse, inverse_out, semaphores.at[1]),
+    ]
+    for copy in copies:
+        copy.start()
     scatter_cells(gelu_parts(pre[...])[0], layer_out, sizes)
-    local[...] = dot(cell_mixer(weight[...], False, sizes), signal[...])
-    copy.wait()
+    copies[0].wait()
+    local[...] = dot(cell_mixer(weight_here[...], False, sizes), signal[...])
+    copies[1].wait()
+
+
+def fetch_tables(sizes, inverse, forward, after, inverse_out, forward_out, semaphores):
+    del after
+    fetch((inverse, forward), (inverse_out, forward_out), semaphores)
 
 
 def prepare(
-    sizes, source, after, place, tables, field, cotangent, weight, bias, inverse, forward,
-    target, table, back, local, cot_cells, inverse_out, forward_out,
-    here, cells, field_here, cot_here, semaphores, small,
+    sizes, source, after, tables, field, cotangent, weight, bias,
+    target, table, back, local, cot_cells,
+    here, cells, field_here, cot_here, weight_here, bias_here, semaphores, small,
 ):
     del after
-    place = place[0]
+    place = lax.axis_index("gy")
     pair = place + 1 - 2 * lax.rem(place, 2)
     half_rows, lanes = back.shape[0], table.shape[1]
     moves = (
         (field, field_here),
         (cotangent, cot_here),
+        (weight, weight_here),
+        (bias, bias_here),
         (tables.at[place], table),
         (tables.at[place, pl.ds(0, half_rows)], back.at[:, pl.ds(0, lanes)]),
         (tables.at[pair, pl.ds(half_rows, half_rows)], back.at[:, pl.ds(lanes, lanes)]),
-        (inverse, inverse_out),
-        (forward, forward_out),
     )
     few = [pltpu.make_async_copy(*move, small.at[at]) for at, move in enumerate(moves)]
     copies = [pltpu.make_async_copy(source.at[at], here.at[at], semaphores.at[at]) for at in range(2 * sizes.modes)]
     for copy in few + copies:
         copy.start()
-    few[0].wait()
-    values = gather_cells(field_here, cells, sizes).astype(BF16)
-    bypass = dot(cell_mixer(weight[...], True, sizes), values)
-    for o in range(sizes.channels):
-        rows = slice(o * sizes.cells, (o + 1) * sizes.cells)
-        local[rows, :] = bypass[rows, :] + bias[o]
-    few[1].wait()
-    gather_cells(cot_here, cot_cells, sizes)
     if sizes.half > sizes.kept:
         target[...] = jnp.zeros_like(target)
     elif sizes.rows > sizes.channels:
         target[:, :, sizes.channels :, :] = jnp.zeros(
             (sizes.modes, sizes.channels, sizes.rows - sizes.channels, 2 * sizes.half), F32
         )
-
-    def turn(mode, carry):
+    for mode in range(sizes.modes):
         for s in range(2):
-            at = 2 * mode + s
-            pltpu.make_async_copy(source.at[at], here.at[at], semaphores.at[at]).wait()
+            copies[2 * mode + s].wait()
         for w in range(sizes.channels):
             blocks = [here[2 * mode + s, w].reshape(sizes.kept, sizes.channels) for s in range(2)]
             if sizes.half == sizes.kept:
@@ -227,11 +227,14 @@
             else:
                 for s, block in enumerate(blocks):
                     target[mode, w, : sizes.channels, s * sizes.half : s * sizes.half + sizes.kept] = block.T
-        return carry
-
-    lax.fori_loop(0, sizes.modes, turn, 0)
-    for copy in few[2:]:
-        copy.wait()
+        if mode == 1:
+            for copy in few:
+                copy.wait()
+            values = gather_cells(field_here, cells, sizes).astype(BF16)
+            spread = one_hot(sizes.channels * sizes.cells, sizes.channels, sizes.cells, True).astype(F32)
+            offset = jnp.sum(spread * bias_here[...].reshape(1, sizes.channels), axis=1, keepdims=True)
+            local[...] = dot(cell_mixer(weight_here[...], True, sizes), values) + offset
+            gather_cells(cot_here, cot_cells, sizes)
 
 
 def plane_spectra(sizes, own, other, table, target):
@@ -355,7 +358,6 @@
 
 
 VMEM = pl.BlockSpec(memory_space=pltpu.VMEM)
-SMEM = pl.BlockSpec(memory_space=pltpu.SMEM)
 HBM = pl.BlockSpec(memory_space=pltpu.HBM)
 ANYWHERE = pl.BlockSpec(memory_space=pl.ANY)
 
@@ -432,7 +434,8 @@
         field, forward_first, specs=[HBM] * 2,
     )
     own = exchange(sent)
-    turned, plane, plane_back, local, cot_cells, inverse_here, forward_here = whole_call(
+    weight_here = pltpu.VMEM(pointwise_weight.shape, BF16)
+    turned, plane, plane_back, local, cot_cells = whole_call(
         prepare, z, 5000,
         (
             shape_of((z.modes, z.channels, z.rows, 2 * z.half)),
@@ -440,18 +443,24 @@
             shape_of((half_rows, 8 * z.half)),
             shape_of(cells_shape),
             shape_of(cells_shape),
-            shape_of(inverse_first.shape),
-            shape_of(forward_back.shape, BF16),
         ),
-        [weight_scratch[0], cells_scratch, field_scratch, field_scratch, weight_scratch[1], pltpu.SemaphoreType.DMA((7,))],
-        native.reshape(weight_shape), sent, lax.axis_index("gy").reshape(1), jnp.asarray(plane_tables(z)),
-        field, cotangent, pointwise_weight, channel_bias, inverse_first, forward_back,
-        specs=[HBM, ANYWHERE, SMEM, HBM, HBM, HBM, VMEM, SMEM, HBM, HBM], room=28,
-    )
-    own, turned, plane, plane_back, local, cot_cells, inverse_here, forward_here = lax.optimization_barrier(
-        (own, turned, plane, plane_back, local, cot_cells, inverse_here, forward_here)
+        [
+            weight_scratch[0], cells_scratch, field_scratch, field_scratch, weight_here,
+            pltpu.VMEM(channel_bias.shape, F32), weight_scratch[1], pltpu.SemaphoreType.DMA((7,)),
+        ],
+        native.reshape(weight_shape), sent, jnp.asarray(plane_tables(z)), field, cotangent, pointwise_weight, channel_bias,
+        specs=[HBM, ANYWHERE] + [HBM] * 5, room=24,
+    )
+    own, turned, plane, plane_back, local, cot_cells = lax.optimization_barrier(
+        (own, turned, plane, plane_back, local, cot_cells)
     )
     other = other_core(own)
+    inverse_here, forward_here = whole_call(
+        fetch_tables, z, 1000, (shape_of(inverse_first.shape), shape_of(forward_back.shape, BF16)),
+        [pltpu.SemaphoreType.DMA((2,))],
+        inverse_first, forward_back, own, specs=[HBM, HBM, ANYWHERE],
+    )
+    other, inverse_here, forward_here = lax.optimization_barrier((other, inverse_here, forward_here))
     spectra, mixed = whole_call(
         mix_forward, z, 1000, (shape_of(spectra_shape), shape_of(spectra_shape)), [], own, other, plane, turned
     )
@@ -461,28 +470,28 @@
         (shape_of(cells_shape), shape_of(cells_shape, BF16), payload), [spectrum_scratch],
         exchange(sent), local, cot_cells, inverse_here, forward_here,
     )
-    own, pre, signal = lax.optimization_barrier((exchange(sent), pre, signal))
-    other = other_core(own)
-    layer_out, local, inverse_here = whole_call(
-        emit, z, 1200,
-        (shape_of(field.shape, BF16), shape_of(cells_shape), shape_of(inverse_back.shape)),
-        [pltpu.SemaphoreType.DMA((1,))],
-        pre, signal, pointwise_weight, inverse_back, specs=[VMEM, VMEM, VMEM, HBM],
-    )
-    other, layer_out, local, inverse_here = lax.optimization_barrier((other, layer_out, local, inverse_here))
+    own = exchange(sent)
     back, mixed = whole_call(
         mix_back, z, 1000, (shape_of((z.modes, z.rows, 2 * z.half)), shape_of(spectra_shape)), [spectra_scratch],
-        own, other, plane, turned,
+        own, other_core(own), plane, turned,
     )
     sent = whole_call(plane_cells, z, 1000, payload, [spread_scratch], mixed, other_core(mixed), plane_back)
-    sent, back, spectra = lax.optimization_barrier((sent, back, spectra))
+    sent, back, spectra, pre, signal = lax.optimization_barrier((sent, back, spectra, pre, signal))
     returned = exchange(sent)
     gradient = whole_call(
         grad_weights, z, 5000, shape_of(weight_shape),
         [weight_scratch[0], spectra_scratch, spectra_scratch, weight_scratch[1]],
         spectra, back, out_specs=HBM, room=28,
     )
-    returned, gradient = lax.optimization_barrier((returned, gradient))
+    layer_out, local, inverse_here = whole_call(
+        emit, z, 1500,
+        (shape_of(field.shape, BF16), shape_of(cells_shape), shape_of(inverse_back.shape)),
+        [weight_here, pltpu.SemaphoreType.DMA((2,))],
+        pre, signal, pointwise_weight, inverse_back, specs=[VMEM, VMEM, HBM, HBM],
+    )
+    returned, gradient, layer_out, local, inverse_here = lax.optimization_barrier(
+        (returned, gradient, layer_out, local, inverse_here)
+    )
     grad_field = whole_call(
         finish, z, 1000, shape_of(field.shape, BF16), [spectrum_scratch], returned, local, inverse_here
     )

time: 74.6 us -> 71.6 us (0.960)
  local copies, waits for them, and re-layouts: 3.68 us -> 1.87 us
  blocking collectives: 26.9 us -> 25.5 us
  Pallas kernels: 22.3 us -> 23.6 us
    unnamed x10 -> x8, local copies, waits for them, and re-layouts: 3.68 us -> 1.87 us
    all_to_all x2, blocking collectives: 26.9 us -> 25.5 us  [exchange(): lax.all_to_all(payload, ('gx', 'gy'), split_axis=0, concat_axis=0, tiled=...]
    pallas_call x10 -> x11, Pallas kernels: 22.3 us -> 23.6 us  [whole_call(): pl.pallas_call(kernel, out_shape=out_shape, in_specs=specs or [VMEM] * le...]
    all_to_all x2, waiting for transfers between devices: 4.27 us -> 2.99 us  [exchange(): lax.all_to_all(payload, ('gx', 'gy'), split_axis=0, concat_axis=0, tiled=...]
  transfers between devices with their start and end apart: 6 -> 6, of which waited for: 4 -> 6; matrix products, arithmetic and copies ran while one was open for 0% -> 0% of each run, Pallas kernels for 18% -> 20%
where the time goes in v6:
time: 71.6 us; the launch traced here: 71.1 us
  blocking collectives  25.5 us (36%)
  Pallas kernels  23.6 us (33%)
  starting transfers between devices  12.3 us (17%)
  waiting for transfers between devices  7.14 us (10%)
  local copies, waits for them, and re-layouts  1.87 us (3%)
  between operations  0.75 us (1%)
    all_to_all x2, blocking collectives, exchange(): lax.all_to_all(payload, ('gx', 'gy'), split_axis=0, concat_axis=0, tiled=...  25.5 us
    pallas_call x11, Pallas kernels, whole_call(): pl.pallas_call(kernel, out_shape=out_shape, in_specs=specs or [VMEM] * le...  23.6 us
    all_to_all x2, starting transfers between devices, exchange(): lax.all_to_all(payload, ('gx', 'gy'), split_axis=0, concat_axis=0, tiled=...  11.9 us
    ppermute x4, waiting for transfers between devices, other_core(): return lax.ppermute(payload, 'gy', pairs)  4.15 us
    all_to_all x2, waiting for transfers between devices, exchange(): lax.all_to_all(payload, ('gx', 'gy'), split_axis=0, concat_axis=0, tiled=...  2.99 us
    unnamed x8, local copies, waits for them, and re-layouts  1.87 us
  transfers between devices with their start and end apart: 6, of which 6 were waited for; matrix products, arithmetic and copies ran while one was open for 0% of the time, Pallas kernels for 20%

profile of v6, /device:TPU:0, one launch (start us, length us, event | category | flops | bytes accessed | tf_op | source)
XLA Modules:
  0.0 71.1 jit_solution(4144872929180893284)
XLA Ops:
  0.6 2.2 %depth_forward.1.refs_1_ = f32[16,8,384]{2,1,0:T(8,128)} custom-call(bf16[20,2,4,512]{3,2,1,0:T(4,128)(2,1)} %refs_3_.2, bf16[512,128]{1,0:T(8,128)(2,1)} %constant.10.clone.refs_1_), custom_call_target="tpu_custom_call" | custom-call | bytes 4500000 | tf_op jit(solution)/shard_map/depth_forward/pallas_call | solution.py:381
  2.9 8.3 %all-to-all-start = ((f32[16,8,384]{2,1,0:T(8,128)}), f32[16,8,384]{2,1,0:T(8,128)S(1)}, u32[]{:S(2)}, u32[]{:S(2)}) async-start(f32[16,8,384]{2,1,0:T(8,128)} %depth_forward.1.refs_1_), calls=%async_computation | async-start | bytes 393216 | tf_op jit(solution)/shard_map/all_to_all | solution.py:408
  11.2 7.1 %prepare.1 = (f32[8,20,24,128]{3,2,1,0:T(8,128)S(1)}, f32[256,256]{1,0:T(8,128)S(1)}, f32[128,512]{1,0:T(8,128)S(1)}, f32[160,512]{1,0:T(8,128)S(1)}, f32[160,512]{1,0:T(8,128)S(1)}) custom-call(f32[16,20,4,16,20]{4,3,2,1,0:T(8,128)} %bitcast.6, f32[16,8,384]{2,1,0:T(8,128)} %depth_forward.1.refs_1_, f32[4,256,256]{2,1,0:T(8,128)} %constant.14.clone.refs_2_, ...), custom_call_target="tpu_custom_call" | custom-call | bytes 15000000 | tf_op jit(solution)/shard_map/prepare/pallas_call | solution.py:381
  18.3 0.0 copy-start
  18.3 1.5 %all-to-all-done.refs_2_.refs_0_ = f32[16,8,384]{2,1,0:T(8,128)S(1)} async-done(((f32[16,8,384]{2,1,0:T(8,128)}), f32[16,8,384]{2,1,0:T(8,128)S(1)}, u32[]{:S(2)}, u32[]{:S(2)}) %all-to-all-start) | async-done | bytes 196640 | tf_op jit(solution)/shard_map/all_to_all | solution.py:408
  19.8 0.0 collective-permute-start
  19.8 1.0 %fetch_tables.1 = (f32[128,512]{1,0:T(8,128)S(1)}, bf16[512,128]{1,0:T(8,128)(2,1)S(1)}) custom-call(f32[128,512]{1,0:T(8,128)} %constant.13.clone.refs_0_, bf16[512,128]{1,0:T(8,128)(2,1)} %constant.11.clone.refs_1_, f32[16,8,384]{2,1,0:T(8,128)S(1)} %all-to-all-done.refs_2_.refs_0_), custom_call_target="tpu_custom_call" | custom-call | bytes 3000000 | tf_op jit(solution)/shard_map/fetch_tables/pallas_call | solution.py:381
  20.8 0.4 collective-permute-done.refs_1_
  21.3 0.9 %mix_forward.1 = (f32[160,128]{1,0:T(8,128)S(1)}, f32[160,128]{1,0:T(8,128)S(1)}) custom-call(f32[16,8,384]{2,1,0:T(8,128)S(1)} %all-to-all-done.refs_2_.refs_0_, f32[16,8,384]{2,1,0:T(8,128)S(1)} %collective-permute-done.refs_1_, f32[256,256]{1,0:T(8,128)S(1)} %get-tuple-element.48.refs_2_, f32[8,20,24,128]{3,2,1,0:T(8,128)S(1)} %get-tuple-element.49.refs_3_), custom_call_target="tpu_custom_call" | custom-call | bytes 3000000 | tf_op jit(solution)/shard_map/mix_forward/pallas_call | solution.py:381
  22.1 0.0 copy-start.2
  22.1 0.2 collective-permute-start.1
  22.3 1.1 %collective-permute-done.1.refs_1_ = f32[160,128]{1,0:T(8,128)S(1)} collective-permute-done((f32[160,128]{1,0:T(8,128)S(1)}, f32[160,128]{1,0:T(8,128)S(1)}, u32[]{:S(2)}, u32[]{:S(2)}) %collective-permute-start.1) | collective-permute-done | bytes 81952 | tf_op jit(solution)/shard_map/ppermute | solution.py:413
  23.5 0.8 %plane_cells.2 = f32[16,8,384]{2,1,0:T(8,128)S(1)} custom-call(f32[160,128]{1,0:T(8,128)S(1)} %get-tuple-element.50.refs_0_, f32[160,128]{1,0:T(8,128)S(1)} %collective-permute-done.1.refs_1_, f32[128,512]{1,0:T(8,128)S(1)} %get-tuple-element.51.refs_2_), custom_call_target="tpu_custom_call" | custom-call | bytes 3000000 | tf_op jit(solution)/shard_map/plane_cells/pallas_call | solution.py:381
  24.3 0.0 copy-done
  24.3 14.3 %all_to_all.20.refs_0_ = f32[16,8,384]{2,1,0:T(8,128)S(1)} all-to-all(f32[16,8,384]{2,1,0:T(8,128)S(1)} %plane_cells.2), channel_id=1, replica_groups={{0,2,4,6,8,10,12,14,16,18,20,22,24,26,28,30},{1,3,5,7,9,11,13,15,17,19,..., dimensions={0} | all-to-all | bytes 393216 | tf_op jit(solution)/shard_map/all_to_all | solution.py:408
  38.6 0.0 copy-start.1
  38.6 1.0 %copy-done.1 = f32[160,512]{1,0:T(8,128)S(1)} copy-done((f32[160,512]{1,0:T(8,128)S(1)}, f32[160,512]{1,0:T(8,128)}, u32[]{:S(2)}) %copy-start.1) | copy-done | bytes 327704
  39.5 1.3 %activate.1 = (f32[160,512]{1,0:T(8,128)S(1)}, bf16[160,512]{1,0:T(8,128)(2,1)S(1)}, f32[16,8,384]{2,1,0:T(8,128)S(1)}) custom-call(f32[16,8,384]{2,1,0:T(8,128)S(1)} %all_to_all.20.refs_0_, f32[160,512]{1,0:T(8,128)S(1)} %get-tuple-element.52.refs_1_, f32[160,512]{1,0:T(8,128)S(1)} %copy-done.1, f32[128,512]{1,0:T(8,128)S(1)} %get-tuple-element.54.refs_3_, ...), custom_call_target="tpu_custom_call" | custom-call | bytes 6000000 | tf_op jit(solution)/shard_map/activate/pallas_call | solution.py:381
  40.8 11.2 %all_to_all.21.refs_0_ = f32[16,8,384]{2,1,0:T(8,128)S(1)} all-to-all(f32[16,8,384]{2,1,0:T(8,128)S(1)} %get-tuple-element.56), channel_id=1, replica_groups={{0,2,4,6,8,10,12,14,16,18,20,22,24,26,28,30},{1,3,5,7,9,11,13,15,17,19,..., dimensions={0} | all-to-all | bytes 393216 | tf_op jit(solution)/shard_map/all_to_all | solution.py:408
  52.1 0.0 collective-permute-start.2
  52.1 1.4 %collective-permute-done.2.refs_1_ = f32[16,8,384]{2,1,0:T(8,128)S(1)} collective-permute-done((f32[16,8,384]{2,1,0:T(8,128)S(1)}, f32[16,8,384]{2,1,0:T(8,128)S(1)}, u32[]{:S(2)}, u32[]{:S(2)}) %collective-permute-start.2) | collective-permute-done | bytes 196640 | tf_op jit(solution)/shard_map/ppermute | solution.py:413
  53.5 1.1 %mix_back.1 = (f32[8,24,128]{2,1,0:T(8,128)S(1)}, f32[160,128]{1,0:T(8,128)S(1)}) custom-call(f32[16,8,384]{2,1,0:T(8,128)S(1)} %all_to_all.21.refs_0_, f32[16,8,384]{2,1,0:T(8,128)S(1)} %collective-permute-done.2.refs_1_, f32[256,256]{1,0:T(8,128)S(1)} %get-tuple-element.48.refs_2_, f32[8,20,24,128]{3,2,1,0:T(8,128)S(1)} %get-tuple-element.49.refs_3_), custom_call_target="tpu_custom_call" | custom-call | bytes 3000000 | tf_op jit(solution)/shard_map/mix_back/pallas_call | solution.py:381
  54.6 0.2 collective-permute-start.3
  54.8 1.1 %collective-permute-done.3.refs_1_ = f32[160,128]{1,0:T(8,128)S(1)} collective-permute-done((f32[160,128]{1,0:T(8,128)S(1)}, f32[160,128]{1,0:T(8,128)S(1)}, u32[]{:S(2)}, u32[]{:S(2)}) %collective-permute-start.3) | collective-permute-done | bytes 81952 | tf_op jit(solution)/shard_map/ppermute | solution.py:413
  55.9 1.5 %plane_cells.3 = f32[16,8,384]{2,1,0:T(8,128)} custom-call(f32[160,128]{1,0:T(8,128)S(1)} %get-tuple-element.57.refs_0_, f32[160,128]{1,0:T(8,128)S(1)} %collective-permute-done.3.refs_1_, f32[128,512]{1,0:T(8,128)S(1)} %get-tuple-element.51.refs_2_), custom_call_target="tpu_custom_call" | custom-call | bytes 3000000 | tf_op jit(solution)/shard_map/plane_cells/pallas_call | solution.py:381
  57.4 0.0 copy-done.2
  57.4 3.5 %all-to-all-start.3 = ((f32[16,8,384]{2,1,0:T(8,128)}), f32[16,8,384]{2,1,0:T(8,128)S(1)}, u32[]{:S(2)}, u32[]{:S(2)}) async-start(f32[16,8,384]{2,1,0:T(8,128)} %plane_cells.3), calls=%async_computation.3 | async-start | bytes 393216 | tf_op jit(solution)/shard_map/all_to_all | solution.py:408
  61.0 0.0 copy-start.3
  61.0 0.9 %copy-done.3 = f32[160,128]{1,0:T(8,128)S(1)} copy-done((f32[160,128]{1,0:T(8,128)S(1)}, f32[160,128]{1,0:T(8,128)}, u32[]{:S(2)}) %copy-start.3) | copy-done | bytes 81944
  61.9 4.6 %grad_weights.1 = f32[16,20,4,16,20]{4,3,2,1,0:T(8,128)} custom-call(f32[160,128]{1,0:T(8,128)S(1)} %copy-done.3, f32[8,24,128]{2,1,0:T(8,128)S(1)} %get-tuple-element.64.refs_1_), custom_call_target="tpu_custom_call" | custom-call | bytes 15000000 | tf_op jit(solution)/shard_map/grad_weights/pallas_call | solution.py:381
  66.4 1.8 %emit.1 = (bf16[20,2,4,512]{3,2,1,0:T(4,128)(2,1)}, f32[160,512]{1,0:T(8,128)S(1)}, f32[128,512]{1,0:T(8,128)S(1)}) custom-call(f32[160,512]{1,0:T(8,128)S(1)} %get-tuple-element.65.refs_0_, bf16[160,512]{1,0:T(8,128)(2,1)S(1)} %get-tuple-element.66.refs_1_, bf16[20,20]{1,0:T(8,128)(2,1)} %refs_2_.2, f32[128,512]{1,0:T(8,128)} %constant.12.clone.refs_3_), custom_call_target="tpu_custom_call" | custom-call | bytes 4500000 | tf_op jit(solution)/shard_map/emit/pallas_call | solution.py:381
  68.2 1.5 %all-to-all-done.3.refs_0_ = f32[16,8,384]{2,1,0:T(8,128)S(1)} async-done(((f32[16,8,384]{2,1,0:T(8,128)}), f32[16,8,384]{2,1,0:T(8,128)S(1)}, u32[]{:S(2)}, u32[]{:S(2)}) %all-to-all-start.3) | async-done | bytes 196640 | tf_op jit(solution)/shard_map/all_to_all | solution.py:408
  69.7 1.4 %finish.1 = bf16[20,2,4,512]{3,2,1,0:T(4,128)(2,1)} custom-call(f32[16,8,384]{2,1,0:T(8,128)S(1)} %all-to-all-done.3.refs_0_, f32[160,512]{1,0:T(8,128)S(1)} %get-tuple-element.72.refs_1_, f32[128,512]{1,0:T(8,128)S(1)} %get-tuple-element.73.refs_2_), custom_call_target="tpu_custom_call" | custom-call | bytes 3000000 | tf_op jit(solution)/shard_map/finish/pallas_call | solution.py:381
Async XLA Ops:
  2.9 17.0 %all-to-all-start = ((f32[16,8,384]{2,1,0:T(8,128)}), f32[16,8,384]{2,1,0:T(8,128)S(1)}, u32[]{:S(2)}, u32[]{:S(2)}) async-start(f32[16,8,384]{2,1,0:T(8,128)} %depth_forward.1.refs_1_), calls=%async_computation | async-start | bytes 393216 | tf_op jit(solution)/shard_map/all_to_all | solution.py:408
  18.3 6.0 %copy-start = (f32[160,512]{1,0:T(8,128)}, f32[160,512]{1,0:T(8,128)S(1)}, u32[]{:S(2)}) copy-start(f32[160,512]{1,0:T(8,128)S(1)} %get-tuple-element.53.refs_2_) | copy-start | bytes 983044
  19.8 1.4 %collective-permute-start = (f32[16,8,384]{2,1,0:T(8,128)S(1)}, f32[16,8,384]{2,1,0:T(8,128)S(1)}, u32[]{:S(2)}, u32[]{:S(2)}) collective-permute-start(f32[16,8,384]{2,1,0:T(8,128)S(1)} %all-to-all-done.refs_2_.refs_0_), channel_id=1, source_target_pairs={{0,1},{1,0},{2,3},{3,2},{4,5},{5,4},{6,7},{7,6},{8,9},{9,8},{10,11... | collective-permute-start | bytes 589832 | tf_op jit(solution)/shard_map/ppermute | solution.py:413
  22.1 35.3 %copy-start.2 = (f32[160,128]{1,0:T(8,128)}, f32[160,128]{1,0:T(8,128)S(1)}, u32[]{:S(2)}) copy-start(f32[160,128]{1,0:T(8,128)S(1)} %get-tuple-element.63.refs_0_) | copy-start | bytes 245764
  22.1 1.3 %collective-permute-start.1 = (f32[160,128]{1,0:T(8,128)S(1)}, f32[160,128]{1,0:T(8,128)S(1)}, u32[]{:S(2)}, u32[]{:S(2)}) collective-permute-start(f32[160,128]{1,0:T(8,128)S(1)} %get-tuple-element.50.refs_0_), channel_id=1, source_target_pairs={{0,1},{1,0},{2,3},{3,2},{4,5},{5,4},{6,7},{7,6},{8,9},{9,8},{10,11... | collective-permute-start | bytes 245768 | tf_op jit(solution)/shard_map/ppermute | solution.py:413
  38.6 1.0 %copy-start.1 = (f32[160,512]{1,0:T(8,128)S(1)}, f32[160,512]{1,0:T(8,128)}, u32[]{:S(2)}) copy-start(f32[160,512]{1,0:T(8,128)} %copy-done) | copy-start | bytes 983044
  52.1 1.4 %collective-permute-start.2 = (f32[16,8,384]{2,1,0:T(8,128)S(1)}, f32[16,8,384]{2,1,0:T(8,128)S(1)}, u32[]{:S(2)}, u32[]{:S(2)}) collective-permute-start(f32[16,8,384]{2,1,0:T(8,128)S(1)} %all_to_all.21.refs_0_), channel_id=1, source_target_pairs={{0,1},{1,0},{2,3},{3,2},{4,5},{5,4},{6,7},{7,6},{8,9},{9,8},{10,11... | collective-permute-start | bytes 589832 | tf_op jit(solution)/shard_map/ppermute | solution.py:413
  54.6 1.3 %collective-permute-start.3 = (f32[160,128]{1,0:T(8,128)S(1)}, f32[160,128]{1,0:T(8,128)S(1)}, u32[]{:S(2)}, u32[]{:S(2)}) collective-permute-start(f32[160,128]{1,0:T(8,128)S(1)} %get-tuple-element.57.refs_0_), channel_id=1, source_target_pairs={{0,1},{1,0},{2,3},{3,2},{4,5},{5,4},{6,7},{7,6},{8,9},{9,8},{10,11... | collective-permute-start | bytes 245768 | tf_op jit(solution)/shard_map/ppermute | solution.py:413
  57.4 12.3 %all-to-all-start.3 = ((f32[16,8,384]{2,1,0:T(8,128)}), f32[16,8,384]{2,1,0:T(8,128)S(1)}, u32[]{:S(2)}, u32[]{:S(2)}) async-start(f32[16,8,384]{2,1,0:T(8,128)} %plane_cells.3), calls=%async_computation.3 | async-start | bytes 393216 | tf_op jit(solution)/shard_map/all_to_all | solution.py:408
  61.0 0.9 %copy-start.3 = (f32[160,128]{1,0:T(8,128)S(1)}, f32[160,128]{1,0:T(8,128)}, u32[]{:S(2)}) copy-start(f32[160,128]{1,0:T(8,128)} %copy-done.2) | copy-start | bytes 245764

commit v7 on v6

--- a/solution.py
+++ b/solution.py
@@ -190,9 +190,9 @@
 
 
 def prepare(
-    sizes, source, after, tables, field, cotangent, weight, bias,
-    target, table, back, local, cot_cells,
-    here, cells, field_here, cot_here, weight_here, bias_here, semaphores, small,
+    sizes, source, after, tables, field, weight, bias,
+    target, table, back, local,
+    here, cells, field_here, weight_here, bias_here, semaphores, small,
 ):
     del after
     place = lax.axis_index("gy")
@@ -200,7 +200,6 @@
     half_rows, lanes = back.shape[0], table.shape[1]
     moves = (
         (field, field_here),
-        (cotangent, cot_here),
         (weight, weight_here),
         (bias, bias_here),
         (tables.at[place], table),
@@ -227,14 +226,12 @@
             else:
                 for s, block in enumerate(blocks):
                     target[mode, w, : sizes.channels, s * sizes.half : s * sizes.half + sizes.kept] = block.T
-        if mode == 1:
-            for copy in few:
-                copy.wait()
-            values = gather_cells(field_here, cells, sizes).astype(BF16)
-            spread = one_hot(sizes.channels * sizes.cells, sizes.channels, sizes.cells, True).astype(F32)
-            offset = jnp.sum(spread * bias_here[...].reshape(1, sizes.channels), axis=1, keepdims=True)
-            local[...] = dot(cell_mixer(weight_here[...], True, sizes), values) + offset
-            gather_cells(cot_here, cot_cells, sizes)
+    for copy in few:
+        copy.wait()
+    values = gather_cells(field_here, cells, sizes).astype(BF16)
+    spread = one_hot(sizes.channels * sizes.cells, sizes.channels, sizes.cells, True).astype(F32)
+    offset = jnp.sum(spread * bias_here[...].reshape(1, sizes.channels), axis=1, keepdims=True)
+    local[...] = dot(cell_mixer(weight_here[...], True, sizes), values) + offset
 
 
 def plane_spectra(sizes, own, other, table, target):
@@ -340,10 +337,14 @@
     return value, derivative
 
 
-def activate(sizes, received, local, cotangent, inverse, forward, pre_out, signal_out, out, spectrum):
+def activate(sizes, received, local, cotangent, inverse, forward, pre_out, signal_out, out, spectrum, cells, cot_here, semaphore):
+    copy = pltpu.make_async_copy(cotangent, cot_here, semaphore.at[0])
+    copy.start()
     pre = dot(receive_modes(received, spectrum, sizes), inverse[...], precision=EXACT) + local[...]
     pre_out[...] = pre
-    signal = (cotangent[...] * gelu_parts(pre)[1]).astype(BF16)
+    derivative = gelu_parts(pre)[1]
+    copy.wait()
+    signal = (gather_cells(cot_here, cells, sizes) * derivative).astype(BF16)
     signal_out[...] = signal
     send_modes(dot(signal, forward[...]), out, sizes)
 
@@ -435,25 +436,22 @@
     )
     own = exchange(sent)
     weight_here = pltpu.VMEM(pointwise_weight.shape, BF16)
-    turned, plane, plane_back, local, cot_cells = whole_call(
+    turned, plane, plane_back, local = whole_call(
         prepare, z, 5000,
         (
             shape_of((z.modes, z.channels, z.rows, 2 * z.half)),
             shape_of((2 * half_rows, 4 * z.half)),
             shape_of((half_rows, 8 * z.half)),
             shape_of(cells_shape),
-            shape_of(cells_shape),
         ),
         [
-            weight_scratch[0], cells_scratch, field_scratch, field_scratch, weight_here,
-            pltpu.VMEM(channel_bias.shape, F32), weight_scratch[1], pltpu.SemaphoreType.DMA((7,)),
+            weight_scratch[0], cells_scratch, field_scratch, weight_here,
+            pltpu.VMEM(channel_bias.shape, F32), weight_scratch[1], pltpu.SemaphoreType.DMA((6,)),
         ],
-        native.reshape(weight_shape), sent, jnp.asarray(plane_tables(z)), field, cotangent, pointwise_weight, channel_bias,
-        specs=[HBM, ANYWHERE] + [HBM] * 5, room=24,
-    )
-    own, turned, plane, plane_back, local, cot_cells = lax.optimization_barrier(
-        (own, turned, plane, plane_back, local, cot_cells)
-    )
+        native.reshape(weight_shape), sent, jnp.asarray(plane_tables(z)), field, pointwise_weight, channel_bias,
+        specs=[HBM, ANYWHERE] + [HBM] * 4, room=16,
+    )
+    own, turned, plane, plane_back, local = lax.optimization_barrier((own, turned, plane, plane_back, local))
     other = other_core(own)
     inverse_here, forward_here = whole_call(
         fetch_tables, z, 1000, (shape_of(inverse_first.shape), shape_of(forward_back.shape, BF16)),
@@ -467,8 +465,9 @@
     sent = whole_call(plane_cells, z, 1000, payload, [spread_scratch], mixed, other_core(mixed), plane_back)
     pre, signal, sent = whole_call(
         activate, z, 2000,
-        (shape_of(cells_shape), shape_of(cells_shape, BF16), payload), [spectrum_scratch],
-        exchange(sent), local, cot_cells, inverse_here, forward_here,
+        (shape_of(cells_shape), shape_of(cells_shape, BF16), payload),
+        [spectrum_scratch, cells_scratch, field_scratch, pltpu.SemaphoreType.DMA((1,))],
+        exchange(sent), local, cotangent, inverse_here, forward_here, specs=[VMEM, VMEM, HBM, VMEM, VMEM],
     )
     own = exchange(sent)
     back, mixed = whole_call(

time: 71.6 us -> 68.8 us (0.961)
  waiting for transfers between devices: 7.14 us -> 9.16 us
  blocking collectives: 25.5 us -> 23.5 us
  Pallas kernels: 23.6 us -> 21.8 us
  local copies, waits for them, and re-layouts: 1.87 us -> 0.89 us
    all_to_all x2, blocking collectives: 25.5 us -> 23.5 us  [exchange(): lax.all_to_all(payload, ('gx', 'gy'), split_axis=0, concat_axis=0, tiled=...]
    all_to_all x2, waiting for transfers between devices: 2.99 us -> 5.01 us  [exchange(): lax.all_to_all(payload, ('gx', 'gy'), split_axis=0, concat_axis=0, tiled=...]
    pallas_call x11, Pallas kernels: 23.6 us -> 21.8 us  [whole_call(): pl.pallas_call(kernel, out_shape=out_shape, in_specs=specs or [VMEM] * le...]
    unnamed x8 -> x4, local copies, waits for them, and re-layouts: 1.87 us -> 0.89 us
  transfers between devices with their start and end apart: 6 -> 6, of which waited for: 6 -> 6; matrix products, arithmetic and copies ran while one was open for 0% -> 0% of each run, Pallas kernels for 20% -> 18%
where the time goes in v7:
time: 68.8 us; the launch traced here: 68.3 us
  blocking collectives  23.5 us (34%)
  Pallas kernels  21.8 us (32%)
  starting transfers between devices  12.3 us (18%)
  waiting for transfers between devices  9.16 us (13%)
  local copies, waits for them, and re-layouts  0.89 us (1%)
  between operations  0.74 us (1%)
    all_to_all x2, blocking collectives, exchange(): lax.all_to_all(payload, ('gx', 'gy'), split_axis=0, concat_axis=0, tiled=...  23.5 us
    pallas_call x11, Pallas kernels, whole_call(): pl.pallas_call(kernel, out_shape=out_shape, in_specs=specs or [VMEM] * le...  21.8 us
    all_to_all x2, starting transfers between devices, exchange(): lax.all_to_all(payload, ('gx', 'gy'), split_axis=0, concat_axis=0, tiled=...  11.9 us
    all_to_all x2, waiting for transfers between devices, exchange(): lax.all_to_all(payload, ('gx', 'gy'), split_axis=0, concat_axis=0, tiled=...  5.01 us
    ppermute x4, waiting for transfers between devices, other_core(): return lax.ppermute(payload, 'gy', pairs)  4.15 us
  transfers between devices with their start and end apart: 6, of which 6 were waited for; matrix products, arithmetic and copies ran while one was open for 0% of the time, Pallas kernels for 18%

profile of v7, /device:TPU:0, one launch (start us, length us, event | category | flops | bytes accessed | tf_op | source)
XLA Modules:
  0.0 68.3 jit_solution(11446697037182350973)
XLA Ops:
  0.6 2.2 %depth_forward.1.refs_1_ = f32[16,8,384]{2,1,0:T(8,128)} custom-call(bf16[20,2,4,512]{3,2,1,0:T(4,128)(2,1)} %refs_3_.2, bf16[512,128]{1,0:T(8,128)(2,1)} %constant.10.clone.refs_1_), custom_call_target="tpu_custom_call" | custom-call | bytes 4500000 | tf_op jit(solution)/shard_map/depth_forward/pallas_call | solution.py:382
  2.9 8.3 %all-to-all-start = ((f32[16,8,384]{2,1,0:T(8,128)}), f32[16,8,384]{2,1,0:T(8,128)S(1)}, u32[]{:S(2)}, u32[]{:S(2)}) async-start(f32[16,8,384]{2,1,0:T(8,128)} %depth_forward.1.refs_1_), calls=%async_computation | async-start | bytes 393216 | tf_op jit(solution)/shard_map/all_to_all | solution.py:409
  11.2 5.1 %prepare.1 = (f32[8,20,24,128]{3,2,1,0:T(8,128)S(1)}, f32[256,256]{1,0:T(8,128)S(1)}, f32[128,512]{1,0:T(8,128)S(1)}, f32[160,512]{1,0:T(8,128)S(1)}) custom-call(f32[16,20,4,16,20]{4,3,2,1,0:T(8,128)} %bitcast.6, f32[16,8,384]{2,1,0:T(8,128)} %depth_forward.1.refs_1_, f32[4,256,256]{2,1,0:T(8,128)} %constant.14.clone.refs_2_, ...), custom_call_target="tpu_custom_call" | custom-call | bytes 15000000 | tf_op jit(solution)/shard_map/prepare/pallas_call | solution.py:382
  16.3 3.5 %all-to-all-done.refs_2_.refs_0_ = f32[16,8,384]{2,1,0:T(8,128)S(1)} async-done(((f32[16,8,384]{2,1,0:T(8,128)}), f32[16,8,384]{2,1,0:T(8,128)S(1)}, u32[]{:S(2)}, u32[]{:S(2)}) %all-to-all-start) | async-done | bytes 196640 | tf_op jit(solution)/shard_map/all_to_all | solution.py:409
  19.8 0.0 collective-permute-start
  19.8 1.0 %fetch_tables.1 = (f32[128,512]{1,0:T(8,128)S(1)}, bf16[512,128]{1,0:T(8,128)(2,1)S(1)}) custom-call(f32[128,512]{1,0:T(8,128)} %constant.13.clone.refs_0_, bf16[512,128]{1,0:T(8,128)(2,1)} %constant.11.clone.refs_1_, f32[16,8,384]{2,1,0:T(8,128)S(1)} %all-to-all-done.refs_2_.refs_0_), custom_call_target="tpu_custom_call" | custom-call | bytes 3000000 | tf_op jit(solution)/shard_map/fetch_tables/pallas_call | solution.py:382
  20.8 0.4 collective-permute-done.refs_1_
  21.3 0.9 %mix_forward.1 = (f32[160,128]{1,0:T(8,128)S(1)}, f32[160,128]{1,0:T(8,128)S(1)}) custom-call(f32[16,8,384]{2,1,0:T(8,128)S(1)} %all-to-all-done.refs_2_.refs_0_, f32[16,8,384]{2,1,0:T(8,128)S(1)} %collective-permute-done.refs_1_, f32[256,256]{1,0:T(8,128)S(1)} %get-tuple-element.45.refs_2_, f32[8,20,24,128]{3,2,1,0:T(8,128)S(1)} %get-tuple-element.46.refs_3_), custom_call_target="tpu_custom_call" | custom-call | bytes 3000000 | tf_op jit(solution)/shard_map/mix_forward/pallas_call | solution.py:382
  22.1 0.0 copy-start
  22.1 0.2 collective-permute-start.1
  22.4 1.1 %collective-permute-done.1.refs_1_ = f32[160,128]{1,0:T(8,128)S(1)} collective-permute-done((f32[160,128]{1,0:T(8,128)S(1)}, f32[160,128]{1,0:T(8,128)S(1)}, u32[]{:S(2)}, u32[]{:S(2)}) %collective-permute-start.1) | collective-permute-done | bytes 81952 | tf_op jit(solution)/shard_map/ppermute | solution.py:414
  23.5 0.8 %plane_cells.2 = f32[16,8,384]{2,1,0:T(8,128)S(1)} custom-call(f32[160,128]{1,0:T(8,128)S(1)} %get-tuple-element.47.refs_0_, f32[160,128]{1,0:T(8,128)S(1)} %collective-permute-done.1.refs_1_, f32[128,512]{1,0:T(8,128)S(1)} %get-tuple-element.48.refs_2_), custom_call_target="tpu_custom_call" | custom-call | bytes 3000000 | tf_op jit(solution)/shard_map/plane_cells/pallas_call | solution.py:382
  24.3 0.0 copy-done
  24.3 12.2 %all_to_all.20.refs_0_ = f32[16,8,384]{2,1,0:T(8,128)S(1)} all-to-all(f32[16,8,384]{2,1,0:T(8,128)S(1)} %plane_cells.2), channel_id=1, replica_groups={{0,2,4,6,8,10,12,14,16,18,20,22,24,26,28,30},{1,3,5,7,9,11,13,15,17,19,..., dimensions={0} | all-to-all | bytes 393216 | tf_op jit(solution)/shard_map/all_to_all | solution.py:409
  36.6 1.5 %activate.1 = (f32[160,512]{1,0:T(8,128)S(1)}, bf16[160,512]{1,0:T(8,128)(2,1)S(1)}, f32[16,8,384]{2,1,0:T(8,128)S(1)}) custom-call(f32[16,8,384]{2,1,0:T(8,128)S(1)} %all_to_all.20.refs_0_, f32[160,512]{1,0:T(8,128)S(1)} %get-tuple-element.49.refs_1_, bf16[20,2,4,512]{3,2,1,0:T(4,128)(2,1)} %refs_2_.3, f32[128,512]{1,0:T(8,128)S(1)} %get-tuple-element.50.refs_3_, ...), custom_call_target="tpu_custom_call" | custom-call | bytes 6000000 | tf_op jit(solution)/shard_map/activate/pallas_call | solution.py:382
  38.0 11.2 %all_to_all.21.refs_0_ = f32[16,8,384]{2,1,0:T(8,128)S(1)} all-to-all(f32[16,8,384]{2,1,0:T(8,128)S(1)} %get-tuple-element.52), channel_id=1, replica_groups={{0,2,4,6,8,10,12,14,16,18,20,22,24,26,28,30},{1,3,5,7,9,11,13,15,17,19,..., dimensions={0} | all-to-all | bytes 393216 | tf_op jit(solution)/shard_map/all_to_all | solution.py:409
  49.3 0.0 collective-permute-start.2
  49.3 1.4 %collective-permute-done.2.refs_1_ = f32[16,8,384]{2,1,0:T(8,128)S(1)} collective-permute-done((f32[16,8,384]{2,1,0:T(8,128)S(1)}, f32[16,8,384]{2,1,0:T(8,128)S(1)}, u32[]{:S(2)}, u32[]{:S(2)}) %collective-permute-start.2) | collective-permute-done | bytes 196640 | tf_op jit(solution)/shard_map/ppermute | solution.py:414
  50.7 1.1 %mix_back.1 = (f32[8,24,128]{2,1,0:T(8,128)S(1)}, f32[160,128]{1,0:T(8,128)S(1)}) custom-call(f32[16,8,384]{2,1,0:T(8,128)S(1)} %all_to_all.21.refs_0_, f32[16,8,384]{2,1,0:T(8,128)S(1)} %collective-permute-done.2.refs_1_, f32[256,256]{1,0:T(8,128)S(1)} %get-tuple-element.45.refs_2_, f32[8,20,24,128]{3,2,1,0:T(8,128)S(1)} %get-tuple-element.46.refs_3_), custom_call_target="tpu_custom_call" | custom-call | bytes 3000000 | tf_op jit(solution)/shard_map/mix_back/pallas_call | solution.py:382
  51.8 0.2 collective-permute-start.3
  52.0 1.1 %collective-permute-done.3.refs_1_ = f32[160,128]{1,0:T(8,128)S(1)} collective-permute-done((f32[160,128]{1,0:T(8,128)S(1)}, f32[160,128]{1,0:T(8,128)S(1)}, u32[]{:S(2)}, u32[]{:S(2)}) %collective-permute-start.3) | collective-permute-done | bytes 81952 | tf_op jit(solution)/shard_map/ppermute | solution.py:414
  53.1 1.5 %plane_cells.3 = f32[16,8,384]{2,1,0:T(8,128)} custom-call(f32[160,128]{1,0:T(8,128)S(1)} %get-tuple-element.53.refs_0_, f32[160,128]{1,0:T(8,128)S(1)} %collective-permute-done.3.refs_1_, f32[128,512]{1,0:T(8,128)S(1)} %get-tuple-element.48.refs_2_), custom_call_target="tpu_custom_call" | custom-call | bytes 3000000 | tf_op jit(solution)/shard_map/plane_cells/pallas_call | solution.py:382
  54.6 3.6 %all-to-all-start.3 = ((f32[16,8,384]{2,1,0:T(8,128)}), f32[16,8,384]{2,1,0:T(8,128)S(1)}, u32[]{:S(2)}, u32[]{:S(2)}) async-start(f32[16,8,384]{2,1,0:T(8,128)} %plane_cells.3), calls=%async_computation.3 | async-start | bytes 393216 | tf_op jit(solution)/shard_map/all_to_all | solution.py:409
  58.2 0.0 copy-start.1
  58.2 0.9 %copy-done.1 = f32[160,128]{1,0:T(8,128)S(1)} copy-done((f32[160,128]{1,0:T(8,128)S(1)}, f32[160,128]{1,0:T(8,128)}, u32[]{:S(2)}) %copy-start.1) | copy-done | bytes 81944
  59.1 4.6 %grad_weights.1 = f32[16,20,4,16,20]{4,3,2,1,0:T(8,128)} custom-call(f32[160,128]{1,0:T(8,128)S(1)} %copy-done.1, f32[8,24,128]{2,1,0:T(8,128)S(1)} %get-tuple-element.60.refs_1_), custom_call_target="tpu_custom_call" | custom-call | bytes 15000000 | tf_op jit(solution)/shard_map/grad_weights/pallas_call | solution.py:382
  63.6 1.8 %emit.1 = (bf16[20,2,4,512]{3,2,1,0:T(4,128)(2,1)}, f32[160,512]{1,0:T(8,128)S(1)}, f32[128,512]{1,0:T(8,128)S(1)}) custom-call(f32[160,512]{1,0:T(8,128)S(1)} %get-tuple-element.61.refs_0_, bf16[160,512]{1,0:T(8,128)(2,1)S(1)} %get-tuple-element.62.refs_1_, bf16[20,20]{1,0:T(8,128)(2,1)} %refs_2_.4, f32[128,512]{1,0:T(8,128)} %constant.12.clone.refs_3_), custom_call_target="tpu_custom_call" | custom-call | bytes 4500000 | tf_op jit(solution)/shard_map/emit/pallas_call | solution.py:382
  65.4 1.5 %all-to-all-done.3.refs_0_ = f32[16,8,384]{2,1,0:T(8,128)S(1)} async-done(((f32[16,8,384]{2,1,0:T(8,128)}), f32[16,8,384]{2,1,0:T(8,128)S(1)}, u32[]{:S(2)}, u32[]{:S(2)}) %all-to-all-start.3) | async-done | bytes 196640 | tf_op jit(solution)/shard_map/all_to_all | solution.py:409
  66.9 1.4 %finish.1 = bf16[20,2,4,512]{3,2,1,0:T(4,128)(2,1)} custom-call(f32[16,8,384]{2,1,0:T(8,128)S(1)} %all-to-all-done.3.refs_0_, f32[160,512]{1,0:T(8,128)S(1)} %get-tuple-element.68.refs_1_, f32[128,512]{1,0:T(8,128)S(1)} %get-tuple-element.69.refs_2_), custom_call_target="tpu_custom_call" | custom-call | bytes 3000000 | tf_op jit(solution)/shard_map/finish/pallas_call | solution.py:382
Async XLA Ops:
  2.9 17.0 %all-to-all-start = ((f32[16,8,384]{2,1,0:T(8,128)}), f32[16,8,384]{2,1,0:T(8,128)S(1)}, u32[]{:S(2)}, u32[]{:S(2)}) async-start(f32[16,8,384]{2,1,0:T(8,128)} %depth_forward.1.refs_1_), calls=%async_computation | async-start | bytes 393216 | tf_op jit(solution)/shard_map/all_to_all | solution.py:409
  19.8 1.4 %collective-permute-start = (f32[16,8,384]{2,1,0:T(8,128)S(1)}, f32[16,8,384]{2,1,0:T(8,128)S(1)}, u32[]{:S(2)}, u32[]{:S(2)}) collective-permute-start(f32[16,8,384]{2,1,0:T(8,128)S(1)} %all-to-all-done.refs_2_.refs_0_), channel_id=1, source_target_pairs={{0,1},{1,0},{2,3},{3,2},{4,5},{5,4},{6,7},{7,6},{8,9},{9,8},{10,11... | collective-permute-start | bytes 589832 | tf_op jit(solution)/shard_map/ppermute | solution.py:414
  22.1 2.2 %copy-start = (f32[160,128]{1,0:T(8,128)}, f32[160,128]{1,0:T(8,128)S(1)}, u32[]{:S(2)}) copy-start(f32[160,128]{1,0:T(8,128)S(1)} %get-tuple-element.59.refs_0_) | copy-start | bytes 245764
  22.1 1.3 %collective-permute-start.1 = (f32[160,128]{1,0:T(8,128)S(1)}, f32[160,128]{1,0:T(8,128)S(1)}, u32[]{:S(2)}, u32[]{:S(2)}) collective-permute-start(f32[160,128]{1,0:T(8,128)S(1)} %get-tuple-element.47.refs_0_), channel_id=1, source_target_pairs={{0,1},{1,0},{2,3},{3,2},{4,5},{5,4},{6,7},{7,6},{8,9},{9,8},{10,11... | collective-permute-start | bytes 245768 | tf_op jit(solution)/shard_map/ppermute | solution.py:414
  49.3 1.4 %collective-permute-start.2 = (f32[16,8,384]{2,1,0:T(8,128)S(1)}, f32[16,8,384]{2,1,0:T(8,128)S(1)}, u32[]{:S(2)}, u32[]{:S(2)}) collective-permute-start(f32[16,8,384]{2,1,0:T(8,128)S(1)} %all_to_all.21.refs_0_), channel_id=1, source_target_pairs={{0,1},{1,0},{2,3},{3,2},{4,5},{5,4},{6,7},{7,6},{8,9},{9,8},{10,11... | collective-permute-start | bytes 589832 | tf_op jit(solution)/shard_map/ppermute | solution.py:414
  51.8 1.3 %collective-permute-start.3 = (f32[160,128]{1,0:T(8,128)S(1)}, f32[160,128]{1,0:T(8,128)S(1)}, u32[]{:S(2)}, u32[]{:S(2)}) collective-permute-start(f32[160,128]{1,0:T(8,128)S(1)} %get-tuple-element.53.refs_0_), channel_id=1, source_target_pairs={{0,1},{1,0},{2,3},{3,2},{4,5},{5,4},{6,7},{7,6},{8,9},{9,8},{10,11... | collective-permute-start | bytes 245768 | tf_op jit(solution)/shard_map/ppermute | solution.py:414
  54.6 12.3 %all-to-all-start.3 = ((f32[16,8,384]{2,1,0:T(8,128)}), f32[16,8,384]{2,1,0:T(8,128)S(1)}, u32[]{:S(2)}, u32[]{:S(2)}) async-start(f32[16,8,384]{2,1,0:T(8,128)} %plane_cells.3), calls=%async_computation.3 | async-start | bytes 393216 | tf_op jit(solution)/shard_map/all_to_all | solution.py:409
  58.2 0.9 %copy-start.1 = (f32[160,128]{1,0:T(8,128)S(1)}, f32[160,128]{1,0:T(8,128)}, u32[]{:S(2)}) copy-start(f32[160,128]{1,0:T(8,128)} %copy-done) | copy-start | bytes 245764

commit v8 on v7

--- a/solution.py
+++ b/solution.py
@@ -13,7 +13,6 @@
 KT = 4
 NT = 16
 LANES = 128
-EXACT = lax.Precision.HIGHEST
 F32 = jnp.float32
 BF16 = jnp.bfloat16
 
@@ -65,9 +64,11 @@
         self.chips = self.nx * self.ny // 2
         self.kept = self.local_x * self.kept_y
         self.half = round_up(self.kept, LANES // 2)
-        self.flat = 2 * self.channels * self.modes
-        self.width = round_up(self.flat, LANES)
         self.all_modes = 2 * self.modes * self.nx
+        self.groups = LANES // self.modes
+        self.main = self.channels // self.groups * self.groups if self.all_modes == LANES else 0
+        self.rest = self.channels - self.main
+        self.width = 2 * self.main * self.modes + round_up(2 * self.rest * self.modes, LANES)
         self.rows = round_up(self.channels, 8)
 
 
@@ -90,20 +91,39 @@
     return lax.broadcasted_iota(jnp.int32, (sizes.cells, LANES), 1) // sizes.modes
 
 
+def turn_groups(tiles, group, sizes):
+    tiles = list(tiles)
+    step = 1
+    while step < sizes.groups:
+        low = group // step % 2 == 0
+        for first in range(sizes.groups):
+            if first // step % 2 == 0:
+                one, two = tiles[first], tiles[first + step]
+                tiles[first] = jnp.where(low, one, pltpu.roll(two, step * sizes.modes, 1))
+                tiles[first + step] = jnp.where(low, pltpu.roll(one, LANES - step * sizes.modes, 1), two)
+        step *= 2
+    return tiles
+
+
+def put_group(target, source, have, want, group, sizes):
+    if have != want:
+        source = pltpu.roll(source, (want - have) % sizes.groups * sizes.modes, 1)
+    return jnp.where(group == want, source, target)
+
+
 def send_modes(values, target, sizes):
     group = lane_group(sizes)
     tiles = [values[w * sizes.cells : (w + 1) * sizes.cells, :] for w in range(sizes.channels)]
+    blocks = sizes.main // sizes.groups
+    turned = [turn_groups(tiles[k * sizes.groups : (k + 1) * sizes.groups], group, sizes) for k in range(blocks)]
     for i in range(sizes.nx):
-        out = [jnp.zeros((sizes.cells, LANES), F32) for _ in range(sizes.width // LANES)]
+        out = [turned[k][2 * i + s] for s in range(2) for k in range(blocks)]
+        rest = [jnp.zeros((sizes.cells, LANES), F32) for _ in range(sizes.width // LANES - len(out))]
         for s in range(2):
-            have = (i * 2 + s) * sizes.modes
-            for w in range(sizes.channels):
-                tile, want = divmod((s * sizes.channels + w) * sizes.modes, LANES)
-                moved = tiles[w]
-                if want != have:
-                    moved = pltpu.roll(moved, (want - have) % LANES, 1)
-                out[tile] = jnp.where(group == want // sizes.modes, moved, out[tile])
-        for t, value in enumerate(out):
+            for r in range(sizes.rest):
+                tile, want = divmod(s * sizes.rest + r, sizes.groups)
+                rest[tile] = put_group(rest[tile], tiles[sizes.main + r], 2 * i + s, want, group, sizes)
+        for t, value in enumerate(out + rest):
             for y in range(sizes.ny // 2):
                 target[i * (sizes.ny // 2) + y, :, t * LANES : (t + 1) * LANES] = value
 
@@ -120,22 +140,36 @@
                 value = part if value is None else value + part
             row.append(value)
         tiles.append(row)
-    for w in range(sizes.channels):
-        out = jnp.zeros((sizes.cells, LANES), F32)
+    blocks = sizes.main // sizes.groups
+    out = []
+    for k in range(blocks):
+        out += turn_groups([tiles[i][s * blocks + k] for i in range(sizes.nx) for s in range(2)], group, sizes)
+    for r in range(sizes.rest):
+        value = jnp.zeros((sizes.cells, LANES), F32)
         for i in range(sizes.nx):
             for s in range(2):
-                want = (i * 2 + s) * sizes.modes
-                tile, have = divmod((s * sizes.channels + w) * sizes.modes, LANES)
-                moved = tiles[i][tile]
-                if want != have:
-                    moved = pltpu.roll(moved, (want - have) % LANES, 1)
-                out = jnp.where(group == want // sizes.modes, moved, out)
-        scratch[w * sizes.cells : (w + 1) * sizes.cells, :] = out
+                tile, have = divmod(s * sizes.rest + r, sizes.groups)
+                value = put_group(value, tiles[i][2 * blocks + tile], have, 2 * i + s, group, sizes)
+        out.append(value)
+    for w, value in enumerate(out):
+        scratch[w * sizes.cells : (w + 1) * sizes.cells, :] = value
     return scratch[...]
 
 
-def dot(left, right, **kwargs):
-    return jnp.dot(left, right, preferred_element_type=F32, **kwargs)
+def dot(left, right, contract=((1,), (0,))):
+    return lax.dot_general(left, right, (contract, ((), ())), preferred_element_type=F32)
+
+
+def halves(values):
+    high = values.astype(BF16)
+    return high, (values - high.astype(F32)).astype(BF16)
+
+
+def fine_dot(left, right, contract=((1,), (0,))):
+    left_high, left_low = halves(left)
+    right_high, right_low = halves(right)
+    small = dot(left_high, right_low, contract) + dot(left_low, right_high, contract)
+    return dot(left_high, right_high, contract) + small
 
 
 def fetch(sources, targets, semaphores):
@@ -163,7 +197,7 @@
     count = sizes.channels * sizes.cells
     left = one_hot(count, sizes.channels, sizes.cells, True)
     right = one_hot(sizes.channels, count, sizes.cells, False)
-    tall = lax.dot_general(left, weights, (((1,), (1 if across else 0,)), ((), ())), preferred_element_type=F32)
+    tall = dot(left, weights, ((1,), (1 if across else 0,)))
     wide = dot(tall.astype(BF16), right)
     row = lax.broadcasted_iota(jnp.int32, (count, count), 0)
     column = lax.broadcasted_iota(jnp.int32, (count, count), 1)
@@ -197,15 +231,22 @@
     del after
     place = lax.axis_index("gy")
     pair = place + 1 - 2 * lax.rem(place, 2)
-    half_rows, lanes = back.shape[0], table.shape[1]
+    half_rows, lanes = back.shape[0] // 2, table.shape[1] // 2
     moves = (
         (field, field_here),
         (weight, weight_here),
         (bias, bias_here),
         (tables.at[place], table),
-        (tables.at[place, pl.ds(0, half_rows)], back.at[:, pl.ds(0, lanes)]),
-        (tables.at[pair, pl.ds(half_rows, half_rows)], back.at[:, pl.ds(lanes, lanes)]),
-    )
+    )
+    for s in range(2):
+        for owner, first in ((place, 0), (pair, 1)):
+            source_lanes, rows = pl.ds(s * lanes, lanes), pl.ds(first * half_rows, half_rows)
+            moves += (
+                (
+                    tables.at[owner, rows, source_lanes],
+                    back.at[pl.ds(s * half_rows, half_rows), pl.ds(first * lanes, lanes)],
+                ),
+            )
     few = [pltpu.make_async_copy(*move, small.at[at]) for at, move in enumerate(moves)]
     copies = [pltpu.make_async_copy(source.at[at], here.at[at], semaphores.at[at]) for at in range(2 * sizes.modes)]
     for copy in few + copies:
@@ -238,22 +279,29 @@
     received = jnp.concatenate(
         [ref[...].reshape(sizes.chips * sizes.cells, sizes.width) for ref in (own, other)], 0
     )
-    both = dot(received.T, table[...], precision=EXACT)
-    count = sizes.channels * sizes.modes
-    target[:count, :] = both[:count, : 2 * sizes.half] + both[count : 2 * count, 2 * sizes.half :]
-
-
-def plane_cells(sizes, own, other, table, out, spread):
-    rows, lanes = own.shape
-    spread[...] = jnp.zeros_like(spread)
-    for at, ref in enumerate((own, other)):
-        for s in range(2):
-            first = (at * 2 + s) * lanes
-            spread[s * rows : (s + 1) * rows, first : first + lanes] = ref[...]
-    cells = lax.dot_general(
-        table[...], spread[...], (((1,), (1,)), ((), ())), precision=EXACT, preferred_element_type=F32
-    )
-    out[...] = cells.reshape(out.shape)
+    both = fine_dot(received.T, table[...])
+    lanes = 2 * sizes.half
+    first, to = 0, 0
+    for count in (sizes.main * sizes.modes, sizes.rest * sizes.modes):
+        if count:
+            middle = first + count
+            target[to : to + count, :] = both[first:middle, :lanes] + both[middle : middle + count, lanes:]
+            first, to = middle + count, to + count
+
+
+def plane_cells(sizes, own, other, table, out):
+    modes = jnp.concatenate([own[...], other[...]], 1)
+    cells = fine_dot(table[...], modes, ((1,), (1,)))
+    count = sizes.chips * sizes.cells
+    parts = [cells[:count], cells[count:]]
+    main = sizes.main * sizes.modes
+    if main:
+        for s, part in enumerate(parts):
+            out[:, :, s * main : (s + 1) * main] = part[:, :main].reshape(sizes.chips, sizes.cells, main)
+    if sizes.rest:
+        filler = jnp.zeros((count, sizes.width - 2 * sizes.channels * sizes.modes), F32)
+        rest = jnp.concatenate([part[:, main:] for part in parts] + [filler], 1)
+        out[:, :, 2 * main :] = rest.reshape(sizes.chips, sizes.cells, sizes.width - 2 * main)
 
 
 def swap_parts(values, sizes):
@@ -268,17 +316,18 @@
     return lax.broadcasted_iota(jnp.int32, (rows, 2 * sizes.half), 1) < sizes.half
 
 
-def mix_forward(sizes, own, other, table, weight, spectra, mixed):
+def mix_forward(sizes, own, other, table, weight, spectra, mixed, swapped):
     plane_spectra(sizes, own, other, table, spectra)
+    swapped[...] = swap_parts(spectra[...], sizes)
     real = first_lanes(sizes.rows, sizes)
     for m in range(sizes.modes):
         straight = jnp.zeros((sizes.rows, 2 * sizes.half), F32)
         crossed = jnp.zeros((sizes.rows, 2 * sizes.half), F32)
         for w in range(sizes.channels):
-            row = spectra[w * sizes.modes + m : w * sizes.modes + m + 1, :]
+            at = slice(w * sizes.modes + m, w * sizes.modes + m + 1)
             block = weight[m, w]
-            straight = straight + row * block
-            crossed = crossed + swap_parts(row, sizes) * block
+            straight = straight + spectra[at, :] * block
+            crossed = crossed + swapped[at, :] * block
         real_part = straight - swap_parts(straight, sizes)
         imag_part = crossed + swap_parts(crossed, sizes)
         result = jnp.where(real, real_part, imag_part)
@@ -340,7 +389,7 @@
 def activate(sizes, received, local, cotangent, inverse, forward, pre_out, signal_out, out, spectrum, cells, cot_here, semaphore):
     copy = pltpu.make_async_copy(cotangent, cot_here, semaphore.at[0])
     copy.start()
-    pre = dot(receive_modes(received, spectrum, sizes), inverse[...], precision=EXACT) + local[...]
+    pre = fine_dot(receive_modes(received, spectrum, sizes), inverse[...]) + local[...]
     pre_out[...] = pre
     derivative = gelu_parts(pre)[1]
     copy.wait()
@@ -350,7 +399,7 @@
 
 
 def finish(sizes, received, local, inverse, grad_field, spectrum):
-    spatial = dot(receive_modes(received, spectrum, sizes), inverse[...], precision=EXACT)
+    spatial = fine_dot(receive_modes(received, spectrum, sizes), inverse[...])
     scatter_cells(spatial + local[...], grad_field, sizes)
 
 
@@ -420,7 +469,6 @@
     spectrum_scratch = pltpu.VMEM((cell_rows, z.all_modes), F32)
     spectra_shape = (z.channels * z.modes, 2 * z.half)
     spectra_scratch = pltpu.VMEM(spectra_shape, F32)
-    spread_scratch = pltpu.VMEM((z.width, 8 * z.half), F32)
     field_scratch = pltpu.VMEM(field.shape, BF16)
 
     native = jnp.transpose(spectral_weight, (0, 1, 2, 4, 5, 3))
@@ -441,12 +489,12 @@
         (
             shape_of((z.modes, z.channels, z.rows, 2 * z.half)),
             shape_of((2 * half_rows, 4 * z.half)),
-            shape_of((half_rows, 8 * z.half)),
+            shape_of((2 * half_rows, 4 * z.half)),
             shape_of(cells_shape),
         ),
         [
             weight_scratch[0], cells_scratch, field_scratch, weight_here,
-            pltpu.VMEM(channel_bias.shape, F32), weight_scratch[1], pltpu.SemaphoreType.DMA((6,)),
+            pltpu.VMEM(channel_bias.shape, F32), weight_scratch[1], pltpu.SemaphoreType.DMA((8,)),
         ],
         native.reshape(weight_shape), sent, jnp.asarray(plane_tables(z)), field, pointwise_weight, channel_bias,
         specs=[HBM, ANYWHERE] + [HBM] * 4, room=16,
@@ -460,9 +508,9 @@
     )
     other, inverse_here, forward_here = lax.optimization_barrier((other, inverse_here, forward_here))
     spectra, mixed = whole_call(
-        mix_forward, z, 1000, (shape_of(spectra_shape), shape_of(spectra_shape)), [], own, other, plane, turned
-    )
-    sent = whole_call(plane_cells, z, 1000, payload, [spread_scratch], mixed, other_core(mixed), plane_back)
+        mix_forward, z, 1000, (shape_of(spectra_shape), shape_of(spectra_shape)), [spectra_scratch], own, other, plane, turned
+    )
+    sent = whole_call(plane_cells, z, 1000, payload, [], mixed, other_core(mixed), plane_back)
     pre, signal, sent = whole_call(
         activate, z, 2000,
         (shape_of(cells_shape), shape_of(cells_shape, BF16), payload),
@@ -474,7 +522,7 @@
         mix_back, z, 1000, (shape_of((z.modes, z.rows, 2 * z.half)), shape_of(spectra_shape)), [spectra_scratch],
         own, other_core(own), plane, turned,
     )
-    sent = whole_call(plane_cells, z, 1000, payload, [spread_scratch], mixed, other_core(mixed), plane_back)
+    sent = whole_call(plane_cells, z, 1000, payload, [], mixed, other_core(mixed), plane_back)
     sent, back, spectra, pre, signal = lax.optimization_barrier((sent, back, spectra, pre, signal))
     returned = exchange(sent)
     gradient = whole_call(

time: 68.8 us -> 67.3 us (0.978)
  Pallas kernels: 21.8 us -> 20.3 us
    pallas_call x11, Pallas kernels: 21.8 us -> 20.3 us  [whole_call(): pl.pallas_call(kernel, out_shape=out_shape, in_specs=specs or [VMEM] * le...]
  transfers between devices with their start and end apart: 6 -> 6, of which waited for: 6 -> 6; matrix products, arithmetic and copies ran while one was open for 0% -> 0% of each run, Pallas kernels for 18% -> 19%
where the time goes in v8:
time: 67.3 us; the launch traced here: 66.8 us
  blocking collectives  23.5 us (35%)
  Pallas kernels  20.3 us (30%)
  starting transfers between devices  12.3 us (18%)
  waiting for transfers between devices  9.06 us (13%)
  local copies, waits for them, and re-layouts  0.89 us (1%)
  between operations  0.73 us (1%)
    all_to_all x2, blocking collectives, exchange(): lax.all_to_all(payload, ('gx', 'gy'), split_axis=0, concat_axis=0, tiled=...  23.5 us
    pallas_call x11, Pallas kernels, whole_call(): pl.pallas_call(kernel, out_shape=out_shape, in_specs=specs or [VMEM] * le...  20.3 us
    all_to_all x2, starting transfers between devices, exchange(): lax.all_to_all(payload, ('gx', 'gy'), split_axis=0, concat_axis=0, tiled=...  11.9 us
    all_to_all x2, waiting for transfers between devices, exchange(): lax.all_to_all(payload, ('gx', 'gy'), split_axis=0, concat_axis=0, tiled=...  4.91 us
    ppermute x4, waiting for transfers between devices, other_core(): return lax.ppermute(payload, 'gy', pairs)  4.15 us
  transfers between devices with their start and end apart: 6, of which 6 were waited for; matrix products, arithmetic and copies ran while one was open for 0% of the time, Pallas kernels for 19%

profile of v8, /device:TPU:0, one launch (start us, length us, event | category | flops | bytes accessed | tf_op | source)
XLA Modules:
  0.0 66.8 jit_solution(8532968787026488440)
XLA Ops:
  0.6 2.1 %depth_forward.1.refs_1_ = f32[16,8,384]{2,1,0:T(8,128)} custom-call(bf16[20,2,4,512]{3,2,1,0:T(4,128)(2,1)} %refs_3_.2, bf16[512,128]{1,0:T(8,128)(2,1)} %constant.10.clone.refs_1_), custom_call_target="tpu_custom_call" | custom-call | bytes 4500000 | tf_op jit(solution)/shard_map/depth_forward/pallas_call | solution.py:431
  2.8 8.3 %all-to-all-start = ((f32[16,8,384]{2,1,0:T(8,128)}), f32[16,8,384]{2,1,0:T(8,128)S(1)}, u32[]{:S(2)}, u32[]{:S(2)}) async-start(f32[16,8,384]{2,1,0:T(8,128)} %depth_forward.1.refs_1_), calls=%async_computation | async-start | bytes 393216 | tf_op jit(solution)/shard_map/all_to_all | solution.py:458
  11.1 5.2 %prepare.1 = (f32[8,20,24,128]{3,2,1,0:T(8,128)S(1)}, f32[256,256]{1,0:T(8,128)S(1)}, f32[256,256]{1,0:T(8,128)S(1)}, f32[160,512]{1,0:T(8,128)S(1)}) custom-call(f32[16,20,4,16,20]{4,3,2,1,0:T(8,128)} %bitcast.6, f32[16,8,384]{2,1,0:T(8,128)} %depth_forward.1.refs_1_, f32[4,256,256]{2,1,0:T(8,128)} %constant.14.clone.refs_2_, ...), custom_call_target="tpu_custom_call" | custom-call | bytes 15000000 | tf_op jit(solution)/shard_map/prepare/pallas_call | solution.py:431
  16.3 3.4 %all-to-all-done.refs_2_.refs_0_ = f32[16,8,384]{2,1,0:T(8,128)S(1)} async-done(((f32[16,8,384]{2,1,0:T(8,128)}), f32[16,8,384]{2,1,0:T(8,128)S(1)}, u32[]{:S(2)}, u32[]{:S(2)}) %all-to-all-start) | async-done | bytes 196640 | tf_op jit(solution)/shard_map/all_to_all | solution.py:458
  19.8 0.0 collective-permute-start
  19.8 1.0 %fetch_tables.1 = (f32[128,512]{1,0:T(8,128)S(1)}, bf16[512,128]{1,0:T(8,128)(2,1)S(1)}) custom-call(f32[128,512]{1,0:T(8,128)} %constant.13.clone.refs_0_, bf16[512,128]{1,0:T(8,128)(2,1)} %constant.11.clone.refs_1_, f32[16,8,384]{2,1,0:T(8,128)S(1)} %all-to-all-done.refs_2_.refs_0_), custom_call_target="tpu_custom_call" | custom-call | bytes 3000000 | tf_op jit(solution)/shard_map/fetch_tables/pallas_call | solution.py:431
  20.8 0.4 collective-permute-done.refs_1_
  21.2 0.7 %mix_forward.1 = (f32[160,128]{1,0:T(8,128)S(1)}, f32[160,128]{1,0:T(8,128)S(1)}) custom-call(f32[16,8,384]{2,1,0:T(8,128)S(1)} %all-to-all-done.refs_2_.refs_0_, f32[16,8,384]{2,1,0:T(8,128)S(1)} %collective-permute-done.refs_1_, f32[256,256]{1,0:T(8,128)S(1)} %get-tuple-element.45.refs_2_, f32[8,20,24,128]{3,2,1,0:T(8,128)S(1)} %get-tuple-element.46.refs_3_), custom_call_target="tpu_custom_call" | custom-call | bytes 3000000 | tf_op jit(solution)/shard_map/mix_forward/pallas_call | solution.py:431
  21.9 0.0 copy-start
  21.9 0.2 collective-permute-start.1
  22.1 1.1 %collective-permute-done.1.refs_1_ = f32[160,128]{1,0:T(8,128)S(1)} collective-permute-done((f32[160,128]{1,0:T(8,128)S(1)}, f32[160,128]{1,0:T(8,128)S(1)}, u32[]{:S(2)}, u32[]{:S(2)}) %collective-permute-start.1) | collective-permute-done | bytes 81952 | tf_op jit(solution)/shard_map/ppermute | solution.py:463
  23.2 0.3 plane_cells.2
  23.6 0.0 copy-done
  23.6 12.3 %all_to_all.20.refs_0_ = f32[16,8,384]{2,1,0:T(8,128)S(1)} all-to-all(f32[16,8,384]{2,1,0:T(8,128)S(1)} %plane_cells.2), channel_id=1, replica_groups={{0,2,4,6,8,10,12,14,16,18,20,22,24,26,28,30},{1,3,5,7,9,11,13,15,17,19,..., dimensions={0} | all-to-all | bytes 393216 | tf_op jit(solution)/shard_map/all_to_all | solution.py:458
  35.9 1.4 %activate.1 = (f32[160,512]{1,0:T(8,128)S(1)}, bf16[160,512]{1,0:T(8,128)(2,1)S(1)}, f32[16,8,384]{2,1,0:T(8,128)S(1)}) custom-call(f32[16,8,384]{2,1,0:T(8,128)S(1)} %all_to_all.20.refs_0_, f32[160,512]{1,0:T(8,128)S(1)} %get-tuple-element.49.refs_1_, bf16[20,2,4,512]{3,2,1,0:T(4,128)(2,1)} %refs_2_.3, f32[128,512]{1,0:T(8,128)S(1)} %get-tuple-element.50.refs_3_, ...), custom_call_target="tpu_custom_call" | custom-call | bytes 6000000 | tf_op jit(solution)/shard_map/activate/pallas_call | solution.py:431
  37.3 11.2 %all_to_all.21.refs_0_ = f32[16,8,384]{2,1,0:T(8,128)S(1)} all-to-all(f32[16,8,384]{2,1,0:T(8,128)S(1)} %get-tuple-element.52), channel_id=1, replica_groups={{0,2,4,6,8,10,12,14,16,18,20,22,24,26,28,30},{1,3,5,7,9,11,13,15,17,19,..., dimensions={0} | all-to-all | bytes 393216 | tf_op jit(solution)/shard_map/all_to_all | solution.py:458
  48.6 0.0 collective-permute-start.2
  48.6 1.4 %collective-permute-done.2.refs_1_ = f32[16,8,384]{2,1,0:T(8,128)S(1)} collective-permute-done((f32[16,8,384]{2,1,0:T(8,128)S(1)}, f32[16,8,384]{2,1,0:T(8,128)S(1)}, u32[]{:S(2)}, u32[]{:S(2)}) %collective-permute-start.2) | collective-permute-done | bytes 196640 | tf_op jit(solution)/shard_map/ppermute | solution.py:463
  50.0 0.9 %mix_back.1 = (f32[8,24,128]{2,1,0:T(8,128)S(1)}, f32[160,128]{1,0:T(8,128)S(1)}) custom-call(f32[16,8,384]{2,1,0:T(8,128)S(1)} %all_to_all.21.refs_0_, f32[16,8,384]{2,1,0:T(8,128)S(1)} %collective-permute-done.2.refs_1_, f32[256,256]{1,0:T(8,128)S(1)} %get-tuple-element.45.refs_2_, f32[8,20,24,128]{3,2,1,0:T(8,128)S(1)} %get-tuple-element.46.refs_3_), custom_call_target="tpu_custom_call" | custom-call | bytes 3000000 | tf_op jit(solution)/shard_map/mix_back/pallas_call | solution.py:431
  50.9 0.2 collective-permute-start.3
  51.1 1.1 %collective-permute-done.3.refs_1_ = f32[160,128]{1,0:T(8,128)S(1)} collective-permute-done((f32[160,128]{1,0:T(8,128)S(1)}, f32[160,128]{1,0:T(8,128)S(1)}, u32[]{:S(2)}, u32[]{:S(2)}) %collective-permute-start.3) | collective-permute-done | bytes 81952 | tf_op jit(solution)/shard_map/ppermute | solution.py:463
  52.3 1.0 %plane_cells.3 = f32[16,8,384]{2,1,0:T(8,128)} custom-call(f32[160,128]{1,0:T(8,128)S(1)} %get-tuple-element.53.refs_0_, f32[160,128]{1,0:T(8,128)S(1)} %collective-permute-done.3.refs_1_, f32[256,256]{1,0:T(8,128)S(1)} %get-tuple-element.48.refs_2_), custom_call_target="tpu_custom_call" | custom-call | bytes 3000000 | tf_op jit(solution)/shard_map/plane_cells/pallas_call | solution.py:431
  53.3 3.5 %all-to-all-start.3 = ((f32[16,8,384]{2,1,0:T(8,128)}), f32[16,8,384]{2,1,0:T(8,128)S(1)}, u32[]{:S(2)}, u32[]{:S(2)}) async-start(f32[16,8,384]{2,1,0:T(8,128)} %plane_cells.3), calls=%async_computation.3 | async-start | bytes 393216 | tf_op jit(solution)/shard_map/all_to_all | solution.py:458
  56.8 0.0 copy-start.1
  56.9 0.9 %copy-done.1 = f32[160,128]{1,0:T(8,128)S(1)} copy-done((f32[160,128]{1,0:T(8,128)S(1)}, f32[160,128]{1,0:T(8,128)}, u32[]{:S(2)}) %copy-start.1) | copy-done | bytes 81944
  57.7 4.6 %grad_weights.1 = f32[16,20,4,16,20]{4,3,2,1,0:T(8,128)} custom-call(f32[160,128]{1,0:T(8,128)S(1)} %copy-done.1, f32[8,24,128]{2,1,0:T(8,128)S(1)} %get-tuple-element.60.refs_1_), custom_call_target="tpu_custom_call" | custom-call | bytes 15000000 | tf_op jit(solution)/shard_map/grad_weights/pallas_call | solution.py:431
  62.3 1.8 %emit.1 = (bf16[20,2,4,512]{3,2,1,0:T(4,128)(2,1)}, f32[160,512]{1,0:T(8,128)S(1)}, f32[128,512]{1,0:T(8,128)S(1)}) custom-call(f32[160,512]{1,0:T(8,128)S(1)} %get-tuple-element.61.refs_0_, bf16[160,512]{1,0:T(8,128)(2,1)S(1)} %get-tuple-element.62.refs_1_, bf16[20,20]{1,0:T(8,128)(2,1)} %refs_2_.4, f32[128,512]{1,0:T(8,128)} %constant.12.clone.refs_3_), custom_call_target="tpu_custom_call" | custom-call | bytes 4500000 | tf_op jit(solution)/shard_map/emit/pallas_call | solution.py:431
  64.1 1.5 %all-to-all-done.3.refs_0_ = f32[16,8,384]{2,1,0:T(8,128)S(1)} async-done(((f32[16,8,384]{2,1,0:T(8,128)}), f32[16,8,384]{2,1,0:T(8,128)S(1)}, u32[]{:S(2)}, u32[]{:S(2)}) %all-to-all-start.3) | async-done | bytes 196640 | tf_op jit(solution)/shard_map/all_to_all | solution.py:458
  65.6 1.2 %finish.1 = bf16[20,2,4,512]{3,2,1,0:T(4,128)(2,1)} custom-call(f32[16,8,384]{2,1,0:T(8,128)S(1)} %all-to-all-done.3.refs_0_, f32[160,512]{1,0:T(8,128)S(1)} %get-tuple-element.68.refs_1_, f32[128,512]{1,0:T(8,128)S(1)} %get-tuple-element.69.refs_2_), custom_call_target="tpu_custom_call" | custom-call | bytes 3000000 | tf_op jit(solution)/shard_map/finish/pallas_call | solution.py:431
Async XLA Ops:
  2.8 17.0 %all-to-all-start = ((f32[16,8,384]{2,1,0:T(8,128)}), f32[16,8,384]{2,1,0:T(8,128)S(1)}, u32[]{:S(2)}, u32[]{:S(2)}) async-start(f32[16,8,384]{2,1,0:T(8,128)} %depth_forward.1.refs_1_), calls=%async_computation | async-start | bytes 393216 | tf_op jit(solution)/shard_map/all_to_all | solution.py:458
  19.8 1.4 %collective-permute-start = (f32[16,8,384]{2,1,0:T(8,128)S(1)}, f32[16,8,384]{2,1,0:T(8,128)S(1)}, u32[]{:S(2)}, u32[]{:S(2)}) collective-permute-start(f32[16,8,384]{2,1,0:T(8,128)S(1)} %all-to-all-done.refs_2_.refs_0_), channel_id=1, source_target_pairs={{0,1},{1,0},{2,3},{3,2},{4,5},{5,4},{6,7},{7,6},{8,9},{9,8},{10,11... | collective-permute-start | bytes 589832 | tf_op jit(solution)/shard_map/ppermute | solution.py:463
  21.9 1.7 %copy-start = (f32[160,128]{1,0:T(8,128)}, f32[160,128]{1,0:T(8,128)S(1)}, u32[]{:S(2)}) copy-start(f32[160,128]{1,0:T(8,128)S(1)} %get-tuple-element.59.refs_0_) | copy-start | bytes 245764
  21.9 1.3 %collective-permute-start.1 = (f32[160,128]{1,0:T(8,128)S(1)}, f32[160,128]{1,0:T(8,128)S(1)}, u32[]{:S(2)}, u32[]{:S(2)}) collective-permute-start(f32[160,128]{1,0:T(8,128)S(1)} %get-tuple-element.47.refs_0_), channel_id=1, source_target_pairs={{0,1},{1,0},{2,3},{3,2},{4,5},{5,4},{6,7},{7,6},{8,9},{9,8},{10,11... | collective-permute-start | bytes 245768 | tf_op jit(solution)/shard_map/ppermute | solution.py:463
  48.6 1.4 %collective-permute-start.2 = (f32[16,8,384]{2,1,0:T(8,128)S(1)}, f32[16,8,384]{2,1,0:T(8,128)S(1)}, u32[]{:S(2)}, u32[]{:S(2)}) collective-permute-start(f32[16,8,384]{2,1,0:T(8,128)S(1)} %all_to_all.21.refs_0_), channel_id=1, source_target_pairs={{0,1},{1,0},{2,3},{3,2},{4,5},{5,4},{6,7},{7,6},{8,9},{9,8},{10,11... | collective-permute-start | bytes 589832 | tf_op jit(solution)/shard_map/ppermute | solution.py:463
  50.9 1.3 %collective-permute-start.3 = (f32[160,128]{1,0:T(8,128)S(1)}, f32[160,128]{1,0:T(8,128)S(1)}, u32[]{:S(2)}, u32[]{:S(2)}) collective-permute-start(f32[160,128]{1,0:T(8,128)S(1)} %get-tuple-element.53.refs_0_), channel_id=1, source_target_pairs={{0,1},{1,0},{2,3},{3,2},{4,5},{5,4},{6,7},{7,6},{8,9},{9,8},{10,11... | collective-permute-start | bytes 245768 | tf_op jit(solution)/shard_map/ppermute | solution.py:463
  53.3 12.3 %all-to-all-start.3 = ((f32[16,8,384]{2,1,0:T(8,128)}), f32[16,8,384]{2,1,0:T(8,128)S(1)}, u32[]{:S(2)}, u32[]{:S(2)}) async-start(f32[16,8,384]{2,1,0:T(8,128)} %plane_cells.3), calls=%async_computation.3 | async-start | bytes 393216 | tf_op jit(solution)/shard_map/all_to_all | solution.py:458
  56.8 0.9 %copy-start.1 = (f32[160,128]{1,0:T(8,128)S(1)}, f32[160,128]{1,0:T(8,128)}, u32[]{:S(2)}) copy-start(f32[160,128]{1,0:T(8,128)} %copy-done) | copy-start | bytes 245764

commit v9 on v8

v9 whole, which is shorter than its diff:
```python
import math

import jax
import jax.numpy as jnp
import ml_dtypes
import numpy as np
from jax import lax
from jax.experimental import pallas as pl
from jax.experimental.pallas import tpu as pltpu
from jax.sharding import PartitionSpec as P

KZ = 16
KT = 4
NT = 16
LANES = 128
F32 = jnp.float32
BF16 = jnp.bfloat16


def round_up(value, step):
    return -(-value // step) * step


def frequencies(kept):
    index = np.arange(kept)
    return np.where(index < kept // 2, index, index - kept)


def depth_time_table(cells):
    depth_cells = cells // NT
    depth = np.arange(depth_cells)[:, None, None, None] * frequencies(KZ)[None, None, :, None] * NT
    time = np.arange(NT)[None, :, None, None] * np.arange(KT)[None, None, None, :] * depth_cells
    phase = np.mod(depth + time, cells).reshape(cells, KZ * KT)
    angles = phase.astype(np.float32) * np.float32(2.0 * math.pi / cells)
    factor = np.float32(1.0 / math.sqrt(cells))
    return np.stack([np.cos(angles) * factor, -np.sin(angles) * factor], axis=1).astype(np.float32)


def plane_tables(sizes):
    length_x, length_y = sizes.nx * sizes.cells_x, sizes.ny * sizes.cells_y
    phase_x = np.mod(np.arange(length_x)[:, None] * frequencies(sizes.kept_x), length_x) / length_x
    phase_y = np.mod(np.arange(length_y)[:, None] * frequencies(sizes.kept_y), length_y) / length_y
    angle = 2.0 * math.pi * (phase_x[:, None, :, None] + phase_y[None, :, None, :])
    scale = 1.0 / math.sqrt(length_x * length_y)
    cosine, sine = np.cos(angle) * scale, np.sin(angle) * scale
    parts = np.stack([np.stack([cosine, -sine]), np.stack([sine, cosine])])
    parts = parts.reshape(
        2, 2, sizes.nx, sizes.cells_x, sizes.ny, sizes.cells_y, sizes.ny, sizes.kept
    ).transpose(6, 3, 2, 4, 5, 0, 1, 7)
    padded = np.zeros(parts.shape[:-1] + (sizes.half,), np.float32)
    padded[..., : sizes.kept] = parts
    return padded.reshape(sizes.ny, sizes.devices * sizes.cells, 4 * sizes.half)


class Sizes:
    def __init__(self, field, weight):
        self.nx, self.ny = lax.axis_size("gx"), lax.axis_size("gy")
        self.channels, self.cells_x, self.cells_y, self.depth = field.shape
        self.modes = weight.shape[0]
        self.local_x, self.kept_y = weight.shape[4:]
        self.kept_x = self.local_x * self.ny
        self.cells = self.cells_x * self.cells_y
        self.devices = self.nx * self.ny
        self.share = self.modes // 2
        self.kept = self.local_x * self.kept_y
        self.half = round_up(self.kept, LANES // 2)
        self.all_modes = 2 * self.modes * self.nx
        self.groups = LANES // self.modes
        self.main = self.channels // self.groups * self.groups if self.all_modes == LANES else 0
        self.rest = self.channels - self.main
        self.main_lanes = self.main * self.modes
        self.rest_lanes = self.rest * self.modes
        self.rest_tiles = round_up(self.rest_lanes, LANES) // LANES
        self.rest_first = self.cells_x * self.main_lanes
        self.width = self.rest_first + round_up(self.cells_x * self.rest_lanes, LANES)
        self.rows = round_up(self.channels, 8)


def gather_cells(source, scratch, sizes):
    for w in range(sizes.channels):
        for x in range(sizes.cells_x):
            first = (w * sizes.cells_x + x) * sizes.cells_y
            scratch[first : first + sizes.cells_y, :] = source[w, x].astype(F32)
    return scratch[...]


def scatter_cells(values, target, sizes):
    for w in range(sizes.channels):
        for x in range(sizes.cells_x):
            first = (w * sizes.cells_x + x) * sizes.cells_y
            target[w, x] = values[first : first + sizes.cells_y, :].astype(target.dtype)


def lane_group(sizes):
    return lax.broadcasted_iota(jnp.int32, (sizes.cells, LANES), 1) // sizes.modes


def turn_groups(tiles, group, sizes):
    tiles = list(tiles)
    step = 1
    while step < sizes.groups:
        low = group // step % 2 == 0
        for first in range(sizes.groups):
            if first // step % 2 == 0:
                one, two = tiles[first], tiles[first + step]
                tiles[first] = jnp.where(low, one, pltpu.roll(two, step * sizes.modes, 1))
                tiles[first + step] = jnp.where(low, pltpu.roll(one, LANES - step * sizes.modes, 1), two)
        step *= 2
    return tiles


def put_group(target, source, have, want, group, sizes):
    if have != want:
        source = pltpu.roll(source, (want - have) % sizes.groups * sizes.modes, 1)
    return jnp.where(group == want, source, target)


def send_modes(values, target, sizes):
    group = lane_group(sizes)
    tiles = [values[w * sizes.cells : (w + 1) * sizes.cells, :] for w in range(sizes.channels)]
    turned = []
    for first in range(0, sizes.main, sizes.groups):
        turned.append(turn_groups(tiles[first : first + sizes.groups], group, sizes))
    for at in range(2 * sizes.nx):
        main = [block[at] for block in turned]
        rest = [jnp.zeros((sizes.cells, LANES), F32) for _ in range(sizes.rest_tiles)]
        for r in range(sizes.rest):
            tile, want = divmod(r, sizes.groups)
            rest[tile] = put_group(rest[tile], tiles[sizes.main + r], at, want, group, sizes)
        last = []
        for x in range(sizes.cells_x):
            rows = slice(x * sizes.cells_y, (x + 1) * sizes.cells_y)
            for k, value in enumerate(main):
                lanes = slice(x * sizes.main_lanes + k * LANES, x * sizes.main_lanes + (k + 1) * LANES)
                for y in range(sizes.ny // 2):
                    target[at // 2 * sizes.ny + 2 * y + at % 2, :, lanes] = value[rows]
            if rest:
                last.append(jnp.concatenate([value[rows] for value in rest], 1)[:, : sizes.rest_lanes])
        if rest:
            used = sizes.rest_first + sizes.cells_x * sizes.rest_lanes
            if sizes.width > used:
                last.append(jnp.zeros((sizes.cells_y, sizes.width - used), F32))
            last = jnp.concatenate(last, 1)
            for y in range(sizes.ny // 2):
                target[at // 2 * sizes.ny + 2 * y + at % 2, :, sizes.rest_first :] = last


def receive_modes(source, scratch, sizes):
    group = lane_group(sizes)
    parts = source[...].reshape(sizes.nx, sizes.ny // 2, 2, sizes.cells_y, sizes.width)
    values = parts[:, 0]
    for y in range(1, sizes.ny // 2):
        values = values + parts[:, y]
    values = values.reshape(2 * sizes.nx, sizes.cells_y, sizes.width)
    out = []
    for k in range(sizes.main // sizes.groups):
        firsts = [x * sizes.main_lanes + k * LANES for x in range(sizes.cells_x)]
        tall = jnp.concatenate([values[:, :, first : first + LANES] for first in firsts], 1)
        out += turn_groups([tall[at] for at in range(2 * sizes.nx)], group, sizes)
    if sizes.rest:
        firsts = [sizes.rest_first + x * sizes.rest_lanes for x in range(sizes.cells_x)]
        tall = jnp.concatenate([values[:, :, first : first + sizes.rest_lanes] for first in firsts], 1)
        filler = sizes.rest_tiles * LANES - sizes.rest_lanes
        if filler:
            tall = jnp.concatenate([tall, jnp.zeros(tall.shape[:2] + (filler,), F32)], 2)
        for r in range(sizes.rest):
            value = jnp.zeros((sizes.cells, LANES), F32)
            tile, have = divmod(r, sizes.groups)
            for at in range(2 * sizes.nx):
                source_tile = tall[at, :, tile * LANES : (tile + 1) * LANES]
                value = put_group(value, source_tile, have, at, group, sizes)
            out.append(value)
    for w, value in enumerate(out):
        scratch[w * sizes.cells : (w + 1) * sizes.cells, :] = value
    return scratch[...]


def dot(left, right, contract=((1,), (0,))):
    return lax.dot_general(left, right, (contract, ((), ())), preferred_element_type=F32)


def halves(values):
    high = values.astype(BF16)
    return high, (values - high.astype(F32)).astype(BF16)


def fine_dot(left, right, contract=((1,), (0,))):
    left_high, left_low = halves(left)
    right_high, right_low = halves(right)
    small = dot(left_high, right_low, contract) + dot(left_low, right_high, contract)
    return dot(left_high, right_high, contract) + small


def fetch(sources, targets, semaphores):
    copies = [pltpu.make_async_copy(*pair, semaphores.at[at]) for at, pair in enumerate(zip(sources, targets))]
    for copy in copies:
        copy.start()
    for copy in copies:
        copy.wait()


def depth_forward(sizes, field, table, out, cells, field_here, table_here, semaphores):
    fetch((field, table), (field_here, table_here), semaphores)
    values = gather_cells(field_here, cells, sizes).astype(BF16)
    send_modes(dot(values, table_here[...]), out, sizes)


def one_hot(rows, columns, step, along_rows):
    row = lax.broadcasted_iota(jnp.int32, (rows, columns), 0)
    column = lax.broadcasted_iota(jnp.int32, (rows, columns), 1)
    same = row // step == column if along_rows else row == column // step
    return jnp.where(same, 1.0, 0.0).astype(BF16)


def cell_mixer(weights, across, sizes):
    count = sizes.channels * sizes.cells
    left = one_hot(count, sizes.channels, sizes.cells, True)
    right = one_hot(sizes.channels, count, sizes.cells, False)
    tall = dot(left, weights, ((1,), (1 if across else 0,)))
    wide = dot(tall.astype(BF16), right)
    row = lax.broadcasted_iota(jnp.int32, (count, count), 0)
    column = lax.broadcasted_iota(jnp.int32, (count, count), 1)
    same = lax.rem(row, sizes.cells) == lax.rem(column, sizes.cells)
    return jnp.where(same, wide, 0.0).astype(BF16)


def emit(sizes, pre, signal, weight, inverse, layer_out, local, inverse_out, weight_here, semaphores):
    copies = [
        pltpu.make_async_copy(weight, weight_here, semaphores.at[0]),
        pltpu.make_async_copy(inverse, inverse_out, semaphores.at[1]),
    ]
    for copy in copies:
        copy.start()
    scatter_cells(gelu_parts(pre[...])[0], layer_out, sizes)
    copies[0].wait()
    local[...] = dot(cell_mixer(weight_here[...], False, sizes), signal[...])
    copies[1].wait()


def core_of():
    return lax.rem(lax.axis_index("gy"), 2)


def start_weights(sizes, source, half, here, semaphores):
    copies = []
    for at in range(2 * sizes.share):
        copies.append(pltpu.make_async_copy(source.at[2 * sizes.share * half + at], here.at[at], semaphores.at[at]))
        copies[-1].start()
    return copies


def turn_weights(sizes, copies, here, target):
    if sizes.half > sizes.kept:
        target[...] = jnp.zeros_like(target)
    elif sizes.rows > sizes.channels:
        target[:, :, sizes.channels :, :] = jnp.zeros(
            (sizes.share, sizes.channels, sizes.rows - sizes.channels, 2 * sizes.half), F32
        )
    for mode in range(sizes.share):
        for s in range(2):
            copies[2 * mode + s].wait()
        for w in range(sizes.channels):
            blocks = [here[2 * mode + s, w].reshape(sizes.kept, sizes.channels) for s in range(2)]
            if sizes.half == sizes.kept:
                target[mode, w, : sizes.channels, :] = jnp.concatenate(blocks, 0).T
            else:
                for s, block in enumerate(blocks):
                    target[mode, w, : sizes.channels, s * sizes.half : s * sizes.half + sizes.kept] = block.T


def turn_other(sizes, source, after, target, here, semaphores):
    del after
    turn_weights(sizes, start_weights(sizes, source, 1 - core_of(), here, semaphores), here, target)


def prepare(
    sizes, source, after, tables, field, weight, bias, inverse, forward,
    target, table, local, inverse_out, forward_out,
    here, cells, field_here, weight_here, bias_here, semaphores, small,
):
    del after
    place = lax.axis_index("gy")
    lanes = 2 * sizes.half
    moves = [(field, field_here), (weight, weight_here), (bias, bias_here)]
    for s in range(2):
        for at, owner in enumerate((place, place + 1 - 2 * core_of())):
            moves.append(
                (tables.at[owner, :, pl.ds(s * lanes, lanes)], table.at[:, pl.ds((2 * s + at) * lanes, lanes)])
            )
    moves += [(inverse, inverse_out), (forward, forward_out)]
    few = [pltpu.make_async_copy(*move, small.at[at]) for at, move in enumerate(moves)]
    copies = start_weights(sizes, source, core_of(), here, semaphores)
    for copy in few:
        copy.start()
    turn_weights(sizes, copies, here, target)
    for copy in few:
        copy.wait()
    values = gather_cells(field_here, cells, sizes).astype(BF16)
    spread = one_hot(sizes.channels * sizes.cells, sizes.channels, sizes.cells, True).astype(F32)
    offset = jnp.sum(spread * bias_here[...].reshape(1, sizes.channels), axis=1, keepdims=True)
    local[...] = dot(cell_mixer(weight_here[...], True, sizes), values) + offset


def plane_spectra(sizes, received, table, targets, flat):
    for at in range(sizes.devices):
        flat[at * sizes.cells_y : (at + 1) * sizes.cells_y, :] = received[at]
    turned = flat[...].T
    blocks = []
    for first, count in ((0, sizes.main_lanes), (sizes.rest_first, sizes.rest_lanes)):
        if count:
            firsts = [first + x * count for x in range(sizes.cells_x)]
            blocks.append(jnp.concatenate([turned[at : at + count] for at in firsts], 1))
    both = fine_dot(jnp.concatenate(blocks, 0), table[...])
    rows, lanes = both.shape[0], 2 * sizes.half
    total = both[:, : 2 * lanes] + pltpu.roll(both[:, 2 * lanes :], rows - sizes.share, 0)
    for at, target in enumerate(targets):
        target[...] = total[:, at * lanes : (at + 1) * lanes]


def plane_cells(sizes, spread, table, out):
    modes = jnp.concatenate([spread[at] for at in range(4)], 1)
    cells = fine_dot(table[...], modes, ((1,), (1,)))
    count = sizes.devices * sizes.cells_y
    parts = [cells[x * count : (x + 1) * count] for x in range(sizes.cells_x)]
    pieces = [part[:, : sizes.main_lanes] for part in parts] if sizes.main else []
    if sizes.rest:
        pieces += [part[:, sizes.main_lanes :] for part in parts]
    used = sizes.rest_first + sizes.cells_x * sizes.rest_lanes
    if sizes.width > used:
        pieces.append(jnp.zeros((count, sizes.width - used), F32))
    wide = jnp.concatenate(pieces, 1)
    for at in range(sizes.devices):
        out[at] = wide[at * sizes.cells_y : (at + 1) * sizes.cells_y, :]


def swap_parts(values, sizes):
    return pltpu.roll(values, sizes.half, 1)


def mode_rows(first, sizes):
    return pl.ds(first, sizes.channels, stride=sizes.modes)


def put_mixed(spread, at, mode, values, sizes):
    for s in range(2):
        spread[2 * s + at, mode_rows(s * sizes.share + mode, sizes), :] = values


def first_lanes(rows, sizes):
    return lax.broadcasted_iota(jnp.int32, (rows, 2 * sizes.half), 1) < sizes.half


def mix_forward(sizes, received, table, weight, other_weight, spectra, other_spectra, out, spread, swapped, flat):
    plane_spectra(sizes, received, table, (spectra, other_spectra), flat)
    spread[...] = jnp.zeros_like(spread)
    real = first_lanes(sizes.rows, sizes)
    for at, (rows, block) in enumerate(((spectra, weight), (other_spectra, other_weight))):
        swapped[...] = swap_parts(rows[...], sizes)
        for m in range(sizes.share):
            straight = jnp.zeros((sizes.rows, 2 * sizes.half), F32)
            crossed = jnp.zeros((sizes.rows, 2 * sizes.half), F32)
            for w in range(sizes.channels):
                row = slice(w * sizes.modes + m, w * sizes.modes + m + 1)
                straight = straight + rows[row, :] * block[m, w]
                crossed = crossed + swapped[row, :] * block[m, w]
            real_part = straight - swap_parts(straight, sizes)
            imag_part = crossed + swap_parts(crossed, sizes)
            put_mixed(spread, at, m, jnp.where(real, real_part, imag_part)[: sizes.channels], sizes)
    plane_cells(sizes, spread, table, out)


def mix_back(sizes, received, table, weight, other_weight, back, other_back, out, spread, flat):
    plane_spectra(sizes, received, table, (back, other_back), flat)
    spread[...] = jnp.zeros_like(spread)
    real = first_lanes(sizes.channels, sizes)
    for at, (source, block) in enumerate(((back, weight), (other_back, other_weight))):
        for m in range(sizes.share):
            rows = source[mode_rows(m, sizes), :]
            if sizes.rows > sizes.channels:
                rows = jnp.concatenate([rows, jnp.zeros((sizes.rows - sizes.channels, 2 * sizes.half), F32)], 0)
            turned = swap_parts(rows, sizes)
            straight, crossed = [], []
            for w in range(sizes.channels):
                straight.append(jnp.sum(block[m, w] * rows, axis=0, keepdims=True))
                crossed.append(jnp.sum(block[m, w] * turned, axis=0, keepdims=True))
            straight = jnp.concatenate(straight, 0)
            crossed = jnp.concatenate(crossed, 0)
            real_part = straight + swap_parts(straight, sizes)
            imag_part = swap_parts(crossed, sizes) - crossed
            put_mixed(spread, at, m, jnp.where(real, real_part, imag_part), sizes)
    plane_cells(sizes, spread, table, out)


def grad_weights(
    sizes, spectra, back, given_spectra, given_back, target, here, straight, crossed, semaphores
):
    copies = []
    for which, (source, backward) in enumerate(((spectra, back), (given_spectra, given_back))):
        half = core_of() if which == 0 else 1 - core_of()
        values = source[...]
        turned = swap_parts(values, sizes)
        real = first_lanes(values.shape[0], sizes)
        straight[...] = jnp.where(real, values, turned)
        crossed[...] = jnp.where(real, turned, -values)
        for mode in range(sizes.share):
            rows = backward[mode_rows(mode, sizes), :]
            if sizes.rows > sizes.channels:
                rows = jnp.concatenate([rows, jnp.zeros((sizes.rows - sizes.channels, 2 * sizes.half), F32)], 0)
            turned = swap_parts(rows, sizes)
            local = 2 * (which * sizes.share + mode)
            for w in range(sizes.channels):
                at = slice(w * sizes.modes + mode, w * sizes.modes + mode + 1)
                block = (straight[at, :] * rows + crossed[at, :] * turned).T
                for s in range(2):
                    part = block[s * sizes.half : s * sizes.half + sizes.kept, : sizes.channels]
                    here[local + s, w] = part.reshape(sizes.local_x, sizes.kept_y, sizes.channels)
            for s in range(2):
                to = 2 * (half * sizes.share + mode) + s
                copies.append(pltpu.make_async_copy(here.at[local + s], target.at[to], semaphores.at[local + s]))
                copies[-1].start()
    for copy in copies:
        copy.wait()


def gelu_parts(pre):
    slope = math.sqrt(2.0 / math.pi)
    squared = pre * pre
    bend = jnp.tanh(slope * (pre + 0.044715 * (squared * pre)))
    value = 0.5 * pre * (1.0 + bend)
    derivative = 0.5 * (1.0 + bend) + 0.5 * pre * (1.0 - bend * bend) * (slope * (1.0 + 3.0 * 0.044715 * squared))
    return value, derivative


def activate(sizes, received, local, cotangent, inverse, forward, pre_out, signal_out, out, spectrum, cells, cot_here, semaphore):
    copy = pltpu.make_async_copy(cotangent, cot_here, semaphore.at[0])
    copy.start()
    pre = fine_dot(receive_modes(received, spectrum, sizes), inverse[...]) + local[...]
    pre_out[...] = pre
    derivative = gelu_parts(pre)[1]
    copy.wait()
    signal = (gather_cells(cot_here, cells, sizes) * derivative).astype(BF16)
    signal_out[...] = signal
    send_modes(dot(signal, forward[...]), out, sizes)


def finish(sizes, received, local, inverse, grad_field, spectrum):
    spatial = fine_dot(receive_modes(received, spectrum, sizes), inverse[...])
    scatter_cells(spatial + local[...], grad_field, sizes)


def shape_of(shape, dtype=F32):
    return jax.ShapeDtypeStruct(shape, dtype)


VMEM = pl.BlockSpec(memory_space=pltpu.VMEM)
HBM = pl.BlockSpec(memory_space=pltpu.HBM)
ANYWHERE = pl.BlockSpec(memory_space=pl.ANY)


def settings(mebibytes):
    return pltpu.CompilerParams(vmem_limit_bytes=mebibytes * 1024 * 1024)


def cost(nanoseconds):
    return pl.CostEstimate(flops=0, bytes_accessed=3000 * nanoseconds, transcendentals=0)


def whole_call(body, sizes, nanoseconds, out_shape, scratch, *args, specs=None, out_specs=None, room=16):
    def kernel(*refs):
        body(sizes, *refs)

    if specs:
        args = [
            pltpu.with_memory_space_constraint(arg, pltpu.HBM) if spec is HBM else arg for arg, spec in zip(args, specs)
        ]
    return pl.pallas_call(
        kernel,
        out_shape=out_shape,
        in_specs=specs or [VMEM] * len(args),
        out_specs=out_specs or jax.tree.map(lambda _: VMEM, out_shape),
        scratch_shapes=scratch,
        name=body.__name__,
        cost_estimate=cost(nanoseconds),
        compiler_params=settings(room),
    )(*args)


def on_device(field, cotangent, spectral_weight, pointwise_weight, channel_bias):
    z = Sizes(field, spectral_weight)
    depth_table = depth_time_table(z.depth)
    modes = depth_table.shape[2]
    kappa = np.where(np.arange(modes) % KT == 0, 1.0, 2.0).astype(np.float32)
    shares = (z.nx, 2, z.share)
    ordered = depth_table.reshape((z.depth, 2) + shares).transpose(0, 2, 3, 1, 4).reshape(z.depth, z.all_modes)
    doubled = np.repeat(kappa.reshape(z.nx, 2, 1, z.share), 2, axis=2).reshape(z.all_modes)
    forward_first = jnp.asarray(ordered.astype(ml_dtypes.bfloat16))
    forward_back = jnp.asarray((ordered.astype(ml_dtypes.bfloat16).astype(np.float32) * doubled).astype(ml_dtypes.bfloat16))
    inverse_back = jnp.asarray(np.ascontiguousarray(ordered.T))
    inverse_first = jnp.asarray(np.ascontiguousarray((ordered * doubled).T))
    pairs = [(s, s ^ 1) for s in range(z.ny)]

    def exchange(payload):
        return lax.all_to_all(payload, ("gx", "gy"), split_axis=0, concat_axis=0, tiled=True)

    def other_core(values):
        return lax.ppermute(values, "gy", pairs)

    payload = shape_of((z.devices, z.cells_y, z.width))
    cell_rows = z.channels * z.cells
    cells_shape = (cell_rows, z.depth)
    cells_scratch = pltpu.VMEM(cells_shape, F32)
    spectrum_scratch = pltpu.VMEM((cell_rows, z.all_modes), F32)
    spectra_shape = (z.channels * z.modes, 2 * z.half)
    spectra_scratch = pltpu.VMEM(spectra_shape, F32)
    flat_scratch = pltpu.VMEM((z.devices * z.cells_y, z.width), F32)
    spread_scratch = pltpu.VMEM((4,) + spectra_shape, F32)
    field_scratch = pltpu.VMEM(field.shape, BF16)
    weight_here = pltpu.VMEM(pointwise_weight.shape, BF16)
    native = jnp.transpose(spectral_weight, (0, 1, 2, 4, 5, 3))
    weight_shape = (2 * z.modes,) + native.shape[2:]
    half_scratch = pltpu.VMEM((z.modes,) + native.shape[2:], F32)
    turned_shape = shape_of((z.share, z.channels, z.rows, 2 * z.half))

    def flags(count):
        return pltpu.SemaphoreType.DMA((count,))

    sent = whole_call(
        depth_forward, z, 1500, payload,
        [cells_scratch, field_scratch, pltpu.VMEM(forward_first.shape, BF16), flags(2)],
        field, forward_first, specs=[HBM] * 2,
    )
    received = exchange(sent)
    weights = native.reshape(weight_shape)
    turned_away = whole_call(
        turn_other, z, 2700, turned_shape, [half_scratch, flags(z.modes)], weights, sent, specs=[HBM, ANYWHERE]
    )
    other_turned = other_core(turned_away)
    turned, plane, local, inverse_here, forward_here = whole_call(
        prepare, z, 3500,
        (
            turned_shape,
            shape_of((z.devices * z.cells, 8 * z.half)),
            shape_of(cells_shape),
            shape_of(inverse_first.shape),
            shape_of(forward_back.shape, BF16),
        ),
        [
            half_scratch, cells_scratch, field_scratch, weight_here, pltpu.VMEM(channel_bias.shape, F32),
            flags(z.modes), flags(9),
        ],
        weights, turned_away, jnp.asarray(plane_tables(z)), field, pointwise_weight, channel_bias,
        inverse_first, forward_back, specs=[HBM, ANYWHERE] + [HBM] * 6,
    )
    received, other_turned, turned, plane, local, inverse_here, forward_here = lax.optimization_barrier(
        (received, other_turned, turned, plane, local, inverse_here, forward_here)
    )
    spectra, other_spectra, sent = whole_call(
        mix_forward, z, 1000, (shape_of(spectra_shape), shape_of(spectra_shape), payload),
        [spread_scratch, spectra_scratch, flat_scratch], received, plane, turned, other_turned,
    )
    pre, signal, sent = whole_call(
        activate, z, 2000,
        (shape_of(cells_shape), shape_of(cells_shape, BF16), payload),
        [spectrum_scratch, cells_scratch, field_scratch, flags(1)],
        exchange(sent), local, cotangent, inverse_here, forward_here, specs=[VMEM, VMEM, HBM, VMEM, VMEM],
    )
    back, other_back, sent = whole_call(
        mix_back, z, 1000, (shape_of(spectra_shape), shape_of(spectra_shape), payload),
        [spread_scratch, flat_scratch], exchange(sent), plane, turned, other_turned,
    )
    sent, spectra, other_spectra, back, other_back, pre, signal = lax.optimization_barrier(
        (sent, spectra, other_spectra, back, other_back, pre, signal)
    )
    returned = exchange(sent)
    given_spectra, given_back = other_core(other_spectra), other_core(other_back)
    layer_out, local, inverse_here = whole_call(
        emit, z, 1500,
        (shape_of(field.shape, BF16), shape_of(cells_shape), shape_of(inverse_back.shape)),
        [weight_here, flags(2)],
        pre, signal, pointwise_weight, inverse_back, specs=[VMEM, VMEM, HBM, HBM],
    )
    gradient = whole_call(
        grad_weights, z, 5000, shape_of(weight_shape),
        [pltpu.VMEM(weight_shape, F32), spectra_scratch, spectra_scratch, flags(2 * z.modes)],
        spectra, back, given_spectra, given_back, out_specs=HBM, room=28,
    )
    returned, gradient, layer_out, local, inverse_here = lax.optimization_barrier(
        (returned, gradient, layer_out, local, inverse_here)
    )
    grad_field = whole_call(
        finish, z, 1000, shape_of(field.shape, BF16), [spectrum_scratch], returned, local, inverse_here
    )
    return (layer_out, grad_field, jnp.transpose(gradient.reshape(native.shape), (0, 1, 2, 5, 3, 4)))


def solution(mesh):
    return jax.shard_map(
        on_device,
        mesh=mesh,
        in_specs=(
            P(None, "gx", "gy", None),
            P(None, "gx", "gy", None),
            P("gx", None, None, None, "gy", None),
            P(),
            P(),
        ),
        out_specs=(
            P(None, "gx", "gy", None),
            P(None, "gx", "gy", None),
            P("gx", None, None, None, "gy", None),
        ),
        check_vma=False,
    )
```

time: 67.3 us -> 67 us (level)
  waiting for transfers between devices: 9.06 us -> 4.91 us
  local copies, waits for them, and re-layouts: 0.89 us -> 4.89 us
  Pallas kernels: 20.3 us -> 22.1 us
  starting transfers between devices: 12.3 us -> 10.9 us
    ppermute x4 -> x3, waiting for transfers between devices: 4.15 us -> 0.01 us  [other_core(): return lax.ppermute(values, 'gy', pairs)]
    unnamed x4 -> x12, local copies, waits for them, and re-layouts: 0.89 us -> 4.89 us
    all_to_all x2, starting transfers between devices: 11.9 us -> 9.79 us  [exchange(): lax.all_to_all(payload, ('gx', 'gy'), split_axis=0, concat_axis=0, tiled=...]
    pallas_call x11 -> x9, Pallas kernels: 20.3 us -> 22.1 us  [whole_call(): pl.pallas_call(kernel, out_shape=out_shape, in_specs=specs or [VMEM] * le...]
    ppermute x4 -> x3, starting transfers between devices: 0.38 us -> 1.09 us  [other_core(): return lax.ppermute(values, 'gy', pairs)]
    all_to_all x2, blocking collectives: 23.5 us -> 22.9 us  [exchange(): lax.all_to_all(payload, ('gx', 'gy'), split_axis=0, concat_axis=0, tiled=...]
  transfers between devices with their start and end apart: 6 -> 5, of which waited for: 6 -> 2; matrix products, arithmetic and copies ran while one was open for 0% -> 0% of each run, Pallas kernels for 19% -> 15%
where the time goes in v9:
time: 67 us; the launch traced here: 66.4 us
  blocking collectives  22.9 us (34%)
  Pallas kernels  22.1 us (33%)
  starting transfers between devices  10.9 us (16%)
  waiting for transfers between devices  4.91 us (7%)
  local copies, waits for them, and re-layouts  4.89 us (7%)
  between operations  0.73 us (1%)
    all_to_all x2, blocking collectives, exchange(): lax.all_to_all(payload, ('gx', 'gy'), split_axis=0, concat_axis=0, tiled=...  22.9 us
    pallas_call x9, Pallas kernels, whole_call(): pl.pallas_call(kernel, out_shape=out_shape, in_specs=specs or [VMEM] * le...  22.1 us
    all_to_all x2, starting transfers between devices, exchange(): lax.all_to_all(payload, ('gx', 'gy'), split_axis=0, concat_axis=0, tiled=...  9.79 us
    all_to_all x2, waiting for transfers between devices, exchange(): lax.all_to_all(payload, ('gx', 'gy'), split_axis=0, concat_axis=0, tiled=...  4.9 us
    unnamed x12, local copies, waits for them, and re-layouts  4.89 us
  transfers between devices with their start and end apart: 5, of which 2 were waited for; matrix products, arithmetic and copies ran while one was open for 0% of the time, Pallas kernels for 15%

profile of v9, /device:TPU:0, one launch (start us, length us, event | category | flops | bytes accessed | tf_op | source)
XLA Modules:
  0.0 66.4 jit_solution(10936768136626275522)
XLA Ops:
  0.6 2.2 %depth_forward.1.refs_1_ = f32[32,4,384]{2,1,0:T(4,128)} custom-call(bf16[20,2,4,512]{3,2,1,0:T(4,128)(2,1)} %refs_3_.2, bf16[512,128]{1,0:T(8,128)(2,1)} %constant.10.clone.refs_1_), custom_call_target="tpu_custom_call" | custom-call | bytes 4500000 | tf_op jit(solution)/shard_map/depth_forward/pallas_call | solution.py:476
  2.8 2.9 %turn_other.1.refs_1_ = f32[4,20,24,128]{3,2,1,0:T(8,128)S(1)} custom-call(f32[16,20,4,16,20]{4,3,2,1,0:T(8,128)} %bitcast.6, f32[32,4,384]{2,1,0:T(4,128)} %depth_forward.1.refs_1_), custom_call_target="tpu_custom_call" | custom-call | bytes 8100000 | tf_op jit(solution)/shard_map/turn_other/pallas_call | solution.py:476
  5.7 0.5 collective-permute-start
  6.2 7.1 %all-to-all-start = ((f32[32,4,384]{2,1,0:T(4,128)}), f32[32,4,384]{2,1,0:T(4,128)}, u32[]{:S(2)}, u32[]{:S(2)}) async-start(f32[32,4,384]{2,1,0:T(4,128)} %depth_forward.1.refs_1_), calls=%async_computation | async-start | bytes 393216 | tf_op jit(solution)/shard_map/all_to_all | solution.py:503
  13.3 3.8 %prepare.1 = (f32[4,20,24,128]{3,2,1,0:T(8,128)S(1)}, f32[256,512]{1,0:T(8,128)S(1)}, f32[160,512]{1,0:T(8,128)S(1)}, f32[128,512]{1,0:T(8,128)S(1)}, bf16[512,128]{1,0:T(8,128)(2,1)S(1)}) custom-call(f32[16,20,4,16,20]{4,3,2,1,0:T(8,128)} %bitcast.7, f32[4,20,24,128]{3,2,1,0:T(8,128)S(1)} %turn_other.1.refs_1_, f32[4,256,256]{2,1,0:T(8,128)} %constant.14.clone.refs_2_, ...), custom_call_target="tpu_custom_call" | custom-call | bytes 10500000 | tf_op jit(solution)/shard_map/prepare/pallas_call | solution.py:476
  17.1 0.0 copy-start
  17.1 0.7 %copy-done = f32[160,512]{1,0:T(8,128)} copy-done((f32[160,512]{1,0:T(8,128)}, f32[160,512]{1,0:T(8,128)S(1)}, u32[]{:S(2)}) %copy-start) | copy-done | bytes 327704
  17.9 0.0 copy-start.2
  17.9 0.7 %copy-done.2 = f32[128,512]{1,0:T(8,128)} copy-done((f32[128,512]{1,0:T(8,128)}, f32[128,512]{1,0:T(8,128)S(1)}, u32[]{:S(2)}) %copy-start.2) | copy-done | bytes 262168
  18.5 0.0 copy-start.4
  18.5 0.7 copy-done.4
  19.2 3.0 %all-to-all-done.refs_0_ = f32[32,4,384]{2,1,0:T(4,128)} async-done(((f32[32,4,384]{2,1,0:T(4,128)}), f32[32,4,384]{2,1,0:T(4,128)}, u32[]{:S(2)}, u32[]{:S(2)}) %all-to-all-start) | async-done | bytes 196640 | tf_op jit(solution)/shard_map/all_to_all | solution.py:503
  22.2 0.0 collective-permute-done.refs_3_
  22.2 2.2 %mix_forward.1 = (f32[160,128]{1,0:T(8,128)S(1)}, f32[160,128]{1,0:T(8,128)S(1)}, f32[32,4,384]{2,1,0:T(4,128)S(1)}) custom-call(f32[32,4,384]{2,1,0:T(4,128)} %all-to-all-done.refs_0_, f32[256,512]{1,0:T(8,128)S(1)} %get-tuple-element.45.refs_1_, f32[4,20,24,128]{3,2,1,0:T(8,128)S(1)} %get-tuple-element.46.refs_2_, ...), custom_call_target="tpu_custom_call" | custom-call | bytes 3000000 | tf_op jit(solution)/shard_map/mix_forward/pallas_call | solution.py:476
  24.4 11.5 %all_to_all.20.refs_0_ = f32[32,4,384]{2,1,0:T(4,128)S(1)} all-to-all(f32[32,4,384]{2,1,0:T(4,128)S(1)} %get-tuple-element.48), channel_id=1, replica_groups=mesh['gx'=8,'gy'=4] {'gx','gy'}, dimensions={0} | all-to-all | bytes 393216 | tf_op jit(solution)/shard_map/all_to_all | solution.py:503
  35.8 0.0 copy-start.1
  35.8 1.0 %copy-done.1 = f32[160,512]{1,0:T(8,128)S(1)} copy-done((f32[160,512]{1,0:T(8,128)S(1)}, f32[160,512]{1,0:T(8,128)}, u32[]{:S(2)}) %copy-start.1) | copy-done | bytes 327704
  36.8 0.0 copy-start.3
  36.8 0.9 %copy-done.3 = f32[128,512]{1,0:T(8,128)S(1)} copy-done((f32[128,512]{1,0:T(8,128)S(1)}, f32[128,512]{1,0:T(8,128)}, u32[]{:S(2)}) %copy-start.3) | copy-done | bytes 262168
  37.8 0.0 copy-start.5
  37.8 0.9 %copy-done.5 = bf16[512,128]{1,0:T(8,128)(2,1)S(1)} copy-done((bf16[512,128]{1,0:T(8,128)(2,1)S(1)}, bf16[512,128]{1,0:T(8,128)(2,1)}, u32[]{:S(2)}) %copy-start.5) | copy-done | bytes 131096
  38.7 1.4 %activate.1 = (f32[160,512]{1,0:T(8,128)S(1)}, bf16[160,512]{1,0:T(8,128)(2,1)S(1)}, f32[32,4,384]{2,1,0:T(4,128)S(1)}) custom-call(f32[32,4,384]{2,1,0:T(4,128)S(1)} %all_to_all.20.refs_0_, f32[160,512]{1,0:T(8,128)S(1)} %copy-done.1, bf16[20,2,4,512]{3,2,1,0:T(4,128)(2,1)} %refs_2_.3, f32[128,512]{1,0:T(8,128)S(1)} %copy-done.3, bf16[512,128]{1,0:T(8,128)(2,1)S(1)} %copy-done.5), custom_call_target="tpu_custom_call" | custom-call | bytes 6000000 | tf_op jit(solution)/shard_map/activate/pallas_call | solution.py:476
  40.1 11.4 %all_to_all.21.refs_0_ = f32[32,4,384]{2,1,0:T(4,128)S(1)} all-to-all(f32[32,4,384]{2,1,0:T(4,128)S(1)} %get-tuple-element.52), channel_id=1, replica_groups=mesh['gx'=8,'gy'=4] {'gx','gy'}, dimensions={0} | all-to-all | bytes 393216 | tf_op jit(solution)/shard_map/all_to_all | solution.py:503
  51.5 2.1 %mix_back.1 = (f32[160,128]{1,0:T(8,128)S(1)}, f32[160,128]{1,0:T(8,128)S(1)}, f32[32,4,384]{2,1,0:T(4,128)}) custom-call(f32[32,4,384]{2,1,0:T(4,128)S(1)} %all_to_all.21.refs_0_, f32[256,512]{1,0:T(8,128)S(1)} %get-tuple-element.45.refs_1_, f32[4,20,24,128]{3,2,1,0:T(8,128)S(1)} %get-tuple-element.46.refs_2_, ...), custom_call_target="tpu_custom_call" | custom-call | bytes 3000000 | tf_op jit(solution)/shard_map/mix_back/pallas_call | solution.py:476
  53.6 2.7 %all-to-all-start.3 = ((f32[32,4,384]{2,1,0:T(4,128)}), f32[32,4,384]{2,1,0:T(4,128)S(1)}, u32[]{:S(2)}, u32[]{:S(2)}) async-start(f32[32,4,384]{2,1,0:T(4,128)} %get-tuple-element.60), calls=%async_computation.3 | async-start | bytes 393216 | tf_op jit(solution)/shard_map/all_to_all | solution.py:503
  56.3 0.3 collective-permute-start.1
  56.6 0.3 collective-permute-start.2
  56.9 1.8 %emit.1 = (bf16[20,2,4,512]{3,2,1,0:T(4,128)(2,1)}, f32[160,512]{1,0:T(8,128)S(1)}, f32[128,512]{1,0:T(8,128)S(1)}) custom-call(f32[160,512]{1,0:T(8,128)S(1)} %get-tuple-element.65.refs_0_, bf16[160,512]{1,0:T(8,128)(2,1)S(1)} %get-tuple-element.66.refs_1_, bf16[20,20]{1,0:T(8,128)(2,1)} %refs_2_.4, f32[128,512]{1,0:T(8,128)} %constant.12.clone.refs_3_), custom_call_target="tpu_custom_call" | custom-call | bytes 4500000 | tf_op jit(solution)/shard_map/emit/pallas_call | solution.py:476
  58.7 0.0 collective-permute-done.1.refs_2_
  58.7 0.0 collective-permute-done.2.refs_3_
  58.7 4.6 %grad_weights.1 = f32[16,20,4,16,20]{4,3,2,1,0:T(8,128)} custom-call(f32[160,128]{1,0:T(8,128)S(1)} %get-tuple-element.61.refs_0_, f32[160,128]{1,0:T(8,128)S(1)} %get-tuple-element.62.refs_1_, f32[160,128]{1,0:T(8,128)S(1)} %collective-permute-done.1.refs_2_, f32[160,128]{1,0:T(8,128)S(1)} %collective-permute-done.2.refs_3_), custom_call_target="tpu_custom_call" | custom-call | bytes 15000000 | tf_op jit(solution)/shard_map/grad_weights/pallas_call | solution.py:476
  63.3 1.9 %all-to-all-done.3.refs_0_ = f32[32,4,384]{2,1,0:T(4,128)S(1)} async-done(((f32[32,4,384]{2,1,0:T(4,128)}), f32[32,4,384]{2,1,0:T(4,128)S(1)}, u32[]{:S(2)}, u32[]{:S(2)}) %all-to-all-start.3) | async-done | bytes 196640 | tf_op jit(solution)/shard_map/all_to_all | solution.py:503
  65.2 1.2 %finish.1 = bf16[20,2,4,512]{3,2,1,0:T(4,128)(2,1)} custom-call(f32[32,4,384]{2,1,0:T(4,128)S(1)} %all-to-all-done.3.refs_0_, f32[160,512]{1,0:T(8,128)S(1)} %get-tuple-element.72.refs_1_, f32[128,512]{1,0:T(8,128)S(1)} %get-tuple-element.73.refs_2_), custom_call_target="tpu_custom_call" | custom-call | bytes 3000000 | tf_op jit(solution)/shard_map/finish/pallas_call | solution.py:476
Async XLA Ops:
  5.7 16.5 %collective-permute-start = (f32[4,20,24,128]{3,2,1,0:T(8,128)S(1)}, f32[4,20,24,128]{3,2,1,0:T(8,128)S(1)}, u32[]{:S(2)}, u32[]{:S(2)}) collective-permute-start(f32[4,20,24,128]{3,2,1,0:T(8,128)S(1)} %turn_other.1.refs_1_), channel_id=1, source_target_pairs={{0,1},{1,0},{2,3},{3,2},{4,5},{5,4},{6,7},{7,6},{8,9},{9,8},{10,11... | collective-permute-start | bytes 2949128 | tf_op jit(solution)/shard_map/ppermute | solution.py:506
  6.2 16.0 %all-to-all-start = ((f32[32,4,384]{2,1,0:T(4,128)}), f32[32,4,384]{2,1,0:T(4,128)}, u32[]{:S(2)}, u32[]{:S(2)}) async-start(f32[32,4,384]{2,1,0:T(4,128)} %depth_forward.1.refs_1_), calls=%async_computation | async-start | bytes 393216 | tf_op jit(solution)/shard_map/all_to_all | solution.py:503
  17.1 0.7 %copy-start = (f32[160,512]{1,0:T(8,128)}, f32[160,512]{1,0:T(8,128)S(1)}, u32[]{:S(2)}) copy-start(f32[160,512]{1,0:T(8,128)S(1)} %get-tuple-element.49.refs_1_) | copy-start | bytes 983044
  17.9 0.7 %copy-start.2 = (f32[128,512]{1,0:T(8,128)}, f32[128,512]{1,0:T(8,128)S(1)}, u32[]{:S(2)}) copy-start(f32[128,512]{1,0:T(8,128)S(1)} %get-tuple-element.50.refs_3_) | copy-start | bytes 786436
  18.5 0.7 copy-start.4
  35.8 1.0 %copy-start.1 = (f32[160,512]{1,0:T(8,128)S(1)}, f32[160,512]{1,0:T(8,128)}, u32[]{:S(2)}) copy-start(f32[160,512]{1,0:T(8,128)} %copy-done) | copy-start | bytes 983044
  36.8 0.9 %copy-start.3 = (f32[128,512]{1,0:T(8,128)S(1)}, f32[128,512]{1,0:T(8,128)}, u32[]{:S(2)}) copy-start(f32[128,512]{1,0:T(8,128)} %copy-done.2) | copy-start | bytes 786436
  37.8 0.9 %copy-start.5 = (bf16[512,128]{1,0:T(8,128)(2,1)S(1)}, bf16[512,128]{1,0:T(8,128)(2,1)}, u32[]{:S(2)}) copy-start(bf16[512,128]{1,0:T(8,128)(2,1)} %copy-done.4) | copy-start | bytes 393220
  53.6 11.6 %all-to-all-start.3 = ((f32[32,4,384]{2,1,0:T(4,128)}), f32[32,4,384]{2,1,0:T(4,128)S(1)}, u32[]{:S(2)}, u32[]{:S(2)}) async-start(f32[32,4,384]{2,1,0:T(4,128)} %get-tuple-element.60), calls=%async_computation.3 | async-start | bytes 393216 | tf_op jit(solution)/shard_map/all_to_all | solution.py:503
  56.3 2.4 %collective-permute-start.1 = (f32[160,128]{1,0:T(8,128)S(1)}, f32[160,128]{1,0:T(8,128)S(1)}, u32[]{:S(2)}, u32[]{:S(2)}) collective-permute-start(f32[160,128]{1,0:T(8,128)S(1)} %get-tuple-element.63), channel_id=1, source_target_pairs={{0,1},{1,0},{2,3},{3,2},{4,5},{5,4},{6,7},{7,6},{8,9},{9,8},{10,11... | collective-permute-start | bytes 245768 | tf_op jit(solution)/shard_map/ppermute | solution.py:506
  56.6 2.1 %collective-permute-start.2 = (f32[160,128]{1,0:T(8,128)S(1)}, f32[160,128]{1,0:T(8,128)S(1)}, u32[]{:S(2)}, u32[]{:S(2)}) collective-permute-start(f32[160,128]{1,0:T(8,128)S(1)} %get-tuple-element.64), channel_id=1, source_target_pairs={{0,1},{1,0},{2,3},{3,2},{4,5},{5,4},{6,7},{7,6},{8,9},{9,8},{10,11... | collective-permute-start | bytes 245768 | tf_op jit(solution)/shard_map/ppermute | solution.py:506

commit v10 on v9

--- a/solution.py
+++ b/solution.py
@@ -274,9 +274,9 @@
 
 
 def prepare(
-    sizes, source, after, tables, field, weight, bias, inverse, forward,
-    target, table, local, inverse_out, forward_out,
-    here, cells, field_here, weight_here, bias_here, semaphores, small,
+    sizes, source, after, tables, field, weight, bias,
+    target, table, local,
+    here, cells, field_here, weight_here, bias_here, local_here, semaphores, small,
 ):
     del after
     place = lax.axis_index("gy")
@@ -287,7 +287,6 @@
             moves.append(
                 (tables.at[owner, :, pl.ds(s * lanes, lanes)], table.at[:, pl.ds((2 * s + at) * lanes, lanes)])
             )
-    moves += [(inverse, inverse_out), (forward, forward_out)]
     few = [pltpu.make_async_copy(*move, small.at[at]) for at, move in enumerate(moves)]
     copies = start_weights(sizes, source, core_of(), here, semaphores)
     for copy in few:
@@ -298,7 +297,10 @@
     values = gather_cells(field_here, cells, sizes).astype(BF16)
     spread = one_hot(sizes.channels * sizes.cells, sizes.channels, sizes.cells, True).astype(F32)
     offset = jnp.sum(spread * bias_here[...].reshape(1, sizes.channels), axis=1, keepdims=True)
-    local[...] = dot(cell_mixer(weight_here[...], True, sizes), values) + offset
+    local_here[...] = dot(cell_mixer(weight_here[...], True, sizes), values) + offset
+    copy = pltpu.make_async_copy(local_here, local, small.at[0])
+    copy.start()
+    copy.wait()
 
 
 def plane_spectra(sizes, received, table, targets, flat):
@@ -431,16 +433,25 @@
     return value, derivative
 
 
-def activate(sizes, received, local, cotangent, inverse, forward, pre_out, signal_out, out, spectrum, cells, cot_here, semaphore):
-    copy = pltpu.make_async_copy(cotangent, cot_here, semaphore.at[0])
-    copy.start()
-    pre = fine_dot(receive_modes(received, spectrum, sizes), inverse[...]) + local[...]
+def activate(
+    sizes, received, local, cotangent, inverse, forward, pre_out, signal_out, out,
+    spectrum, cells, inverse_here, local_here, cot_here, forward_here, semaphores,
+):
+    moves = ((inverse, inverse_here), (local, local_here), (cotangent, cot_here), (forward, forward_here))
+    copies = [pltpu.make_async_copy(*move, semaphores.at[at]) for at, move in enumerate(moves)]
+    for copy in copies:
+        copy.start()
+    values = receive_modes(received, spectrum, sizes)
+    copies[0].wait()
+    copies[1].wait()
+    pre = fine_dot(values, inverse_here[...]) + local_here[...]
     pre_out[...] = pre
     derivative = gelu_parts(pre)[1]
-    copy.wait()
+    copies[2].wait()
     signal = (gather_cells(cot_here, cells, sizes) * derivative).astype(BF16)
     signal_out[...] = signal
-    send_modes(dot(signal, forward[...]), out, sizes)
+    copies[3].wait()
+    send_modes(dot(signal, forward_here[...]), out, sizes)
 
 
 def finish(sizes, received, local, inverse, grad_field, spectrum):
@@ -532,27 +543,21 @@
     received = exchange(sent)
     weights = native.reshape(weight_shape)
     turned_away = whole_call(
-        turn_other, z, 2700, turned_shape, [half_scratch, flags(z.modes)], weights, sent, specs=[HBM, ANYWHERE]
+        turn_other, z, 100, turned_shape, [half_scratch, flags(z.modes)], weights, sent, specs=[HBM, ANYWHERE]
     )
     other_turned = other_core(turned_away)
-    turned, plane, local, inverse_here, forward_here = whole_call(
-        prepare, z, 3500,
-        (
-            turned_shape,
-            shape_of((z.devices * z.cells, 8 * z.half)),
-            shape_of(cells_shape),
-            shape_of(inverse_first.shape),
-            shape_of(forward_back.shape, BF16),
-        ),
+    turned, plane, local = whole_call(
+        prepare, z, 100,
+        (turned_shape, shape_of((z.devices * z.cells, 8 * z.half)), shape_of(cells_shape)),
         [
             half_scratch, cells_scratch, field_scratch, weight_here, pltpu.VMEM(channel_bias.shape, F32),
-            flags(z.modes), flags(9),
+            cells_scratch, flags(z.modes), flags(7),
         ],
         weights, turned_away, jnp.asarray(plane_tables(z)), field, pointwise_weight, channel_bias,
-        inverse_first, forward_back, specs=[HBM, ANYWHERE] + [HBM] * 6,
-    )
-    received, other_turned, turned, plane, local, inverse_here, forward_here = lax.optimization_barrier(
-        (received, other_turned, turned, plane, local, inverse_here, forward_here)
+        specs=[HBM, ANYWHERE] + [HBM] * 4, out_specs=(VMEM, VMEM, HBM),
+    )
+    received, other_turned, turned, plane, local = lax.optimization_barrier(
+        (received, other_turned, turned, plane, local)
     )
     spectra, other_spectra, sent = whole_call(
         mix_forward, z, 1000, (shape_of(spectra_shape), shape_of(spectra_shape), payload),
@@ -561,8 +566,11 @@
     pre, signal, sent = whole_call(
         activate, z, 2000,
         (shape_of(cells_shape), shape_of(cells_shape, BF16), payload),
-        [spectrum_scratch, cells_scratch, field_scratch, flags(1)],
-        exchange(sent), local, cotangent, inverse_here, forward_here, specs=[VMEM, VMEM, HBM, VMEM, VMEM],
+        [
+            spectrum_scratch, cells_scratch, pltpu.VMEM(inverse_first.shape, F32), cells_scratch, field_scratch,
+            pltpu.VMEM(forward_back.shape, BF16), flags(4),
+        ],
+        exchange(sent), local, cotangent, inverse_first, forward_back, specs=[VMEM] + [HBM] * 4,
     )
     back, other_back, sent = whole_call(
         mix_back, z, 1000, (shape_of(spectra_shape), shape_of(spectra_shape), payload),

time: 67 us -> 64.7 us (0.966)
  local copies, waits for them, and re-layouts: 4.89 us -> 0.72 us
  waiting for transfers between devices: 4.91 us -> 6.29 us
  Pallas kernels: 22.1 us -> 22.8 us
    unnamed x12 -> x2, local copies, waits for them, and re-layouts: 4.89 us -> 0.72 us
    all_to_all x2, waiting for transfers between devices: 4.9 us -> 6.28 us  [exchange(): lax.all_to_all(payload, ('gx', 'gy'), split_axis=0, concat_axis=0, tiled=...]
  transfers between devices with their start and end apart: 5 -> 5, of which waited for: 2 -> 2; matrix products, arithmetic and copies ran while one was open for 0% -> 0% of each run, Pallas kernels for 15% -> 16%
where the time goes in v10:
time: 64.7 us; the launch traced here: 64.2 us
  Pallas kernels  22.8 us (35%)
  blocking collectives  22.8 us (35%)
  starting transfers between devices  10.9 us (17%)
  waiting for transfers between devices  6.29 us (10%)
  between operations  0.73 us (1%)
  local copies, waits for them, and re-layouts  0.72 us (1%)
    all_to_all x2, blocking collectives, exchange(): lax.all_to_all(payload, ('gx', 'gy'), split_axis=0, concat_axis=0, tiled=...  22.8 us
    pallas_call x9, Pallas kernels, whole_call(): pl.pallas_call(kernel, out_shape=out_shape, in_specs=specs or [VMEM] * le...  22.8 us
    all_to_all x2, starting transfers between devices, exchange(): lax.all_to_all(payload, ('gx', 'gy'), split_axis=0, concat_axis=0, tiled=...  9.79 us
    all_to_all x2, waiting for transfers between devices, exchange(): lax.all_to_all(payload, ('gx', 'gy'), split_axis=0, concat_axis=0, tiled=...  6.28 us
  transfers between devices with their start and end apart: 5, of which 2 were waited for; matrix products, arithmetic and copies ran while one was open for 0% of the time, Pallas kernels for 16%

profile of v10, /device:TPU:0, one launch (start us, length us, event | category | flops | bytes accessed | tf_op | source)
XLA Modules:
  0.0 64.2 jit_solution(14107553226319824016)
XLA Ops:
  0.6 2.2 %depth_forward.1.refs_1_ = f32[32,4,384]{2,1,0:T(4,128)} custom-call(bf16[20,2,4,512]{3,2,1,0:T(4,128)(2,1)} %refs_3_.3, bf16[512,128]{1,0:T(8,128)(2,1)} %constant.10.clone.refs_1_), custom_call_target="tpu_custom_call" | custom-call | bytes 4500000 | tf_op jit(solution)/shard_map/depth_forward/pallas_call | solution.py:487
  2.8 2.9 %turn_other.1.refs_1_ = f32[4,20,24,128]{3,2,1,0:T(8,128)S(1)} custom-call(f32[16,20,4,16,20]{4,3,2,1,0:T(8,128)} %bitcast.6, f32[32,4,384]{2,1,0:T(4,128)} %depth_forward.1.refs_1_), custom_call_target="tpu_custom_call" | custom-call | bytes 300000 | tf_op jit(solution)/shard_map/turn_other/pallas_call | solution.py:487
  5.7 0.5 collective-permute-start
  6.2 7.1 %all-to-all-start = ((f32[32,4,384]{2,1,0:T(4,128)}), f32[32,4,384]{2,1,0:T(4,128)}, u32[]{:S(2)}, u32[]{:S(2)}) async-start(f32[32,4,384]{2,1,0:T(4,128)} %depth_forward.1.refs_1_), calls=%async_computation | async-start | bytes 393216 | tf_op jit(solution)/shard_map/all_to_all | solution.py:514
  13.3 3.8 %prepare.1 = (f32[4,20,24,128]{3,2,1,0:T(8,128)S(1)}, f32[256,512]{1,0:T(8,128)S(1)}, f32[160,512]{1,0:T(8,128)S(1)}) custom-call(f32[16,20,4,16,20]{4,3,2,1,0:T(8,128)} %bitcast.7, f32[4,20,24,128]{3,2,1,0:T(8,128)S(1)} %turn_other.1.refs_1_, f32[4,256,256]{2,1,0:T(8,128)} %constant.14.clone.refs_2_, bf16[20,2,4,512]{3,2,1,0:T(4,128)(2,1)} %refs_3_.3, ...), custom_call_target="tpu_custom_call" | custom-call | bytes 300000 | tf_op jit(solution)/shard_map/prepare/pallas_call | solution.py:487
  17.1 0.0 copy-start
  17.1 0.7 %copy-done = f32[160,512]{1,0:T(8,128)} copy-done((f32[160,512]{1,0:T(8,128)}, f32[160,512]{1,0:T(8,128)S(1)}, u32[]{:S(2)}) %copy-start) | copy-done | bytes 327704
  17.8 4.4 %all-to-all-done.refs_0_ = f32[32,4,384]{2,1,0:T(4,128)} async-done(((f32[32,4,384]{2,1,0:T(4,128)}), f32[32,4,384]{2,1,0:T(4,128)}, u32[]{:S(2)}, u32[]{:S(2)}) %all-to-all-start) | async-done | bytes 196640 | tf_op jit(solution)/shard_map/all_to_all | solution.py:514
  22.2 0.0 collective-permute-done.refs_3_
  22.2 2.2 %mix_forward.1 = (f32[160,128]{1,0:T(8,128)S(1)}, f32[160,128]{1,0:T(8,128)S(1)}, f32[32,4,384]{2,1,0:T(4,128)S(1)}) custom-call(f32[32,4,384]{2,1,0:T(4,128)} %all-to-all-done.refs_0_, f32[256,512]{1,0:T(8,128)S(1)} %get-tuple-element.39.refs_1_, f32[4,20,24,128]{3,2,1,0:T(8,128)S(1)} %get-tuple-element.40.refs_2_, ...), custom_call_target="tpu_custom_call" | custom-call | bytes 3000000 | tf_op jit(solution)/shard_map/mix_forward/pallas_call | solution.py:487
  24.4 11.4 %all_to_all.20.refs_0_ = f32[32,4,384]{2,1,0:T(4,128)S(1)} all-to-all(f32[32,4,384]{2,1,0:T(4,128)S(1)} %get-tuple-element.42), channel_id=1, replica_groups=mesh['gx'=8,'gy'=4] {'gx','gy'}, dimensions={0} | all-to-all | bytes 393216 | tf_op jit(solution)/shard_map/all_to_all | solution.py:514
  35.8 2.1 %activate.1 = (f32[160,512]{1,0:T(8,128)S(1)}, bf16[160,512]{1,0:T(8,128)(2,1)S(1)}, f32[32,4,384]{2,1,0:T(4,128)S(1)}) custom-call(f32[32,4,384]{2,1,0:T(4,128)S(1)} %all_to_all.20.refs_0_, f32[160,512]{1,0:T(8,128)} %copy-done, bf16[20,2,4,512]{3,2,1,0:T(4,128)(2,1)} %refs_2_.3, f32[128,512]{1,0:T(8,128)} %constant.13.clone.refs_3_, ...), custom_call_target="tpu_custom_call" | custom-call | bytes 6000000 | tf_op jit(solution)/shard_map/activate/pallas_call | solution.py:487
  37.9 11.4 %all_to_all.21.refs_0_ = f32[32,4,384]{2,1,0:T(4,128)S(1)} all-to-all(f32[32,4,384]{2,1,0:T(4,128)S(1)} %get-tuple-element.44), channel_id=1, replica_groups=mesh['gx'=8,'gy'=4] {'gx','gy'}, dimensions={0} | all-to-all | bytes 393216 | tf_op jit(solution)/shard_map/all_to_all | solution.py:514
  49.3 2.1 %mix_back.1 = (f32[160,128]{1,0:T(8,128)S(1)}, f32[160,128]{1,0:T(8,128)S(1)}, f32[32,4,384]{2,1,0:T(4,128)}) custom-call(f32[32,4,384]{2,1,0:T(4,128)S(1)} %all_to_all.21.refs_0_, f32[256,512]{1,0:T(8,128)S(1)} %get-tuple-element.39.refs_1_, f32[4,20,24,128]{3,2,1,0:T(8,128)S(1)} %get-tuple-element.40.refs_2_, ...), custom_call_target="tpu_custom_call" | custom-call | bytes 3000000 | tf_op jit(solution)/shard_map/mix_back/pallas_call | solution.py:487
  51.4 2.7 %all-to-all-start.3 = ((f32[32,4,384]{2,1,0:T(4,128)}), f32[32,4,384]{2,1,0:T(4,128)S(1)}, u32[]{:S(2)}, u32[]{:S(2)}) async-start(f32[32,4,384]{2,1,0:T(4,128)} %get-tuple-element.52), calls=%async_computation.3 | async-start | bytes 393216 | tf_op jit(solution)/shard_map/all_to_all | solution.py:514
  54.1 0.3 collective-permute-start.1
  54.4 0.3 collective-permute-start.2
  54.7 1.8 %emit.1 = (bf16[20,2,4,512]{3,2,1,0:T(4,128)(2,1)}, f32[160,512]{1,0:T(8,128)S(1)}, f32[128,512]{1,0:T(8,128)S(1)}) custom-call(f32[160,512]{1,0:T(8,128)S(1)} %get-tuple-element.57.refs_0_, bf16[160,512]{1,0:T(8,128)(2,1)S(1)} %get-tuple-element.58.refs_1_, bf16[20,20]{1,0:T(8,128)(2,1)} %refs_2_.4, f32[128,512]{1,0:T(8,128)} %constant.12.clone.refs_3_), custom_call_target="tpu_custom_call" | custom-call | bytes 4500000 | tf_op jit(solution)/shard_map/emit/pallas_call | solution.py:487
  56.5 0.0 collective-permute-done.1.refs_2_
  56.5 0.0 collective-permute-done.2.refs_3_
  56.5 4.6 %grad_weights.1 = f32[16,20,4,16,20]{4,3,2,1,0:T(8,128)} custom-call(f32[160,128]{1,0:T(8,128)S(1)} %get-tuple-element.53.refs_0_, f32[160,128]{1,0:T(8,128)S(1)} %get-tuple-element.54.refs_1_, f32[160,128]{1,0:T(8,128)S(1)} %collective-permute-done.1.refs_2_, f32[160,128]{1,0:T(8,128)S(1)} %collective-permute-done.2.refs_3_), custom_call_target="tpu_custom_call" | custom-call | bytes 15000000 | tf_op jit(solution)/shard_map/grad_weights/pallas_call | solution.py:487
  61.1 1.9 %all-to-all-done.3.refs_0_ = f32[32,4,384]{2,1,0:T(4,128)S(1)} async-done(((f32[32,4,384]{2,1,0:T(4,128)}), f32[32,4,384]{2,1,0:T(4,128)S(1)}, u32[]{:S(2)}, u32[]{:S(2)}) %all-to-all-start.3) | async-done | bytes 196640 | tf_op jit(solution)/shard_map/all_to_all | solution.py:514
  63.0 1.2 %finish.1 = bf16[20,2,4,512]{3,2,1,0:T(4,128)(2,1)} custom-call(f32[32,4,384]{2,1,0:T(4,128)S(1)} %all-to-all-done.3.refs_0_, f32[160,512]{1,0:T(8,128)S(1)} %get-tuple-element.64.refs_1_, f32[128,512]{1,0:T(8,128)S(1)} %get-tuple-element.65.refs_2_), custom_call_target="tpu_custom_call" | custom-call | bytes 3000000 | tf_op jit(solution)/shard_map/finish/pallas_call | solution.py:487
Async XLA Ops:
  5.7 16.5 %collective-permute-start = (f32[4,20,24,128]{3,2,1,0:T(8,128)S(1)}, f32[4,20,24,128]{3,2,1,0:T(8,128)S(1)}, u32[]{:S(2)}, u32[]{:S(2)}) collective-permute-start(f32[4,20,24,128]{3,2,1,0:T(8,128)S(1)} %turn_other.1.refs_1_), channel_id=1, source_target_pairs={{0,1},{1,0},{2,3},{3,2},{4,5},{5,4},{6,7},{7,6},{8,9},{9,8},{10,11... | collective-permute-start | bytes 2949128 | tf_op jit(solution)/shard_map/ppermute | solution.py:517
  6.2 16.0 %all-to-all-start = ((f32[32,4,384]{2,1,0:T(4,128)}), f32[32,4,384]{2,1,0:T(4,128)}, u32[]{:S(2)}, u32[]{:S(2)}) async-start(f32[32,4,384]{2,1,0:T(4,128)} %depth_forward.1.refs_1_), calls=%async_computation | async-start | bytes 393216 | tf_op jit(solution)/shard_map/all_to_all | solution.py:514
  17.1 0.7 %copy-start = (f32[160,512]{1,0:T(8,128)}, f32[160,512]{1,0:T(8,128)S(1)}, u32[]{:S(2)}) copy-start(f32[160,512]{1,0:T(8,128)S(1)} %get-tuple-element.43.refs_1_) | copy-start | bytes 983044
  51.4 11.6 %all-to-all-start.3 = ((f32[32,4,384]{2,1,0:T(4,128)}), f32[32,4,384]{2,1,0:T(4,128)S(1)}, u32[]{:S(2)}, u32[]{:S(2)}) async-start(f32[32,4,384]{2,1,0:T(4,128)} %get-tuple-element.52), calls=%async_computation.3 | async-start | bytes 393216 | tf_op jit(solution)/shard_map/all_to_all | solution.py:514
  54.1 2.4 %collective-permute-start.1 = (f32[160,128]{1,0:T(8,128)S(1)}, f32[160,128]{1,0:T(8,128)S(1)}, u32[]{:S(2)}, u32[]{:S(2)}) collective-permute-start(f32[160,128]{1,0:T(8,128)S(1)} %get-tuple-element.55), channel_id=1, source_target_pairs={{0,1},{1,0},{2,3},{3,2},{4,5},{5,4},{6,7},{7,6},{8,9},{9,8},{10,11... | collective-permute-start | bytes 245768 | tf_op jit(solution)/shard_map/ppermute | solution.py:517
  54.4 2.1 %collective-permute-start.2 = (f32[160,128]{1,0:T(8,128)S(1)}, f32[160,128]{1,0:T(8,128)S(1)}, u32[]{:S(2)}, u32[]{:S(2)}) collective-permute-start(f32[160,128]{1,0:T(8,128)S(1)} %get-tuple-element.56), channel_id=1, source_target_pairs={{0,1},{1,0},{2,3},{3,2},{4,5},{5,4},{6,7},{7,6},{8,9},{9,8},{10,11... | collective-permute-start | bytes 245768 | tf_op jit(solution)/shard_map/ppermute | solution.py:517

commit v11 on v10

--- a/solution.py
+++ b/solution.py
@@ -199,10 +199,26 @@
         copy.wait()
 
 
-def depth_forward(sizes, field, table, out, cells, field_here, table_here, semaphores):
-    fetch((field, table), (field_here, table_here), semaphores)
+def depth_forward(
+    sizes, field, table, source, out, target,
+    cells, field_here, table_here, out_here, here, semaphores, weight_semaphores,
+):
+    few = [
+        pltpu.make_async_copy(field, field_here, semaphores.at[0]),
+        pltpu.make_async_copy(table, table_here, semaphores.at[1]),
+    ]
+    for copy in few:
+        copy.start()
+    copies = start_weights(sizes, source, 1 - core_of(), here, weight_semaphores)
+    clear_weights(sizes, target)
+    for copy in few:
+        copy.wait()
     values = gather_cells(field_here, cells, sizes).astype(BF16)
-    send_modes(dot(values, table_here[...]), out, sizes)
+    send_modes(dot(values, table_here[...]), out_here, sizes)
+    copy = pltpu.make_async_copy(out_here, out, semaphores.at[2])
+    copy.start()
+    turn_weights(sizes, copies, here, target)
+    copy.wait()
 
 
 def one_hot(rows, columns, step, along_rows):
@@ -249,13 +265,16 @@
     return copies
 
 
-def turn_weights(sizes, copies, here, target):
+def clear_weights(sizes, target):
     if sizes.half > sizes.kept:
         target[...] = jnp.zeros_like(target)
     elif sizes.rows > sizes.channels:
         target[:, :, sizes.channels :, :] = jnp.zeros(
             (sizes.share, sizes.channels, sizes.rows - sizes.channels, 2 * sizes.half), F32
         )
+
+
+def turn_weights(sizes, copies, here, target):
     for mode in range(sizes.share):
         for s in range(2):
             copies[2 * mode + s].wait()
@@ -266,11 +285,6 @@
             else:
                 for s, block in enumerate(blocks):
                     target[mode, w, : sizes.channels, s * sizes.half : s * sizes.half + sizes.kept] = block.T
-
-
-def turn_other(sizes, source, after, target, here, semaphores):
-    del after
-    turn_weights(sizes, start_weights(sizes, source, 1 - core_of(), here, semaphores), here, target)
 
 
 def prepare(
@@ -291,6 +305,7 @@
     copies = start_weights(sizes, source, core_of(), here, semaphores)
     for copy in few:
         copy.start()
+    clear_weights(sizes, target)
     turn_weights(sizes, copies, here, target)
     for copy in few:
         copy.wait()
@@ -535,16 +550,16 @@
     def flags(count):
         return pltpu.SemaphoreType.DMA((count,))
 
-    sent = whole_call(
-        depth_forward, z, 1500, payload,
-        [cells_scratch, field_scratch, pltpu.VMEM(forward_first.shape, BF16), flags(2)],
-        field, forward_first, specs=[HBM] * 2,
+    weights = native.reshape(weight_shape)
+    sent, turned_away = whole_call(
+        depth_forward, z, 1500, (payload, turned_shape),
+        [
+            cells_scratch, field_scratch, pltpu.VMEM(forward_first.shape, BF16), pltpu.VMEM(payload.shape, F32),
+            half_scratch, flags(3), flags(z.modes),
+        ],
+        field, forward_first, weights, specs=[HBM] * 3, out_specs=(HBM, VMEM),
     )
     received = exchange(sent)
-    weights = native.reshape(weight_shape)
-    turned_away = whole_call(
-        turn_other, z, 100, turned_shape, [half_scratch, flags(z.modes)], weights, sent, specs=[HBM, ANYWHERE]
-    )
     other_turned = other_core(turned_away)
     turned, plane, local = whole_call(
         prepare, z, 100,

time: 64.7 us -> 64.1 us (level)
    pallas_call x9 -> x8, Pallas kernels: 22.8 us -> 22.2 us  [whole_call(): pl.pallas_call(kernel, out_shape=out_shape, in_specs=specs or [VMEM] * le...]
where the time goes in v11:
time: 64.1 us; the launch traced here: 63.6 us
  blocking collectives  22.8 us (36%)
  Pallas kernels  22.2 us (35%)
  starting transfers between devices  10.9 us (17%)
  waiting for transfers between devices  6.29 us (10%)
  local copies, waits for them, and re-layouts  0.72 us (1%)
  between operations  0.72 us (1%)
    all_to_all x2, blocking collectives, exchange(): lax.all_to_all(payload, ('gx', 'gy'), split_axis=0, concat_axis=0, tiled=...  22.8 us
    pallas_call x8, Pallas kernels, whole_call(): pl.pallas_call(kernel, out_shape=out_shape, in_specs=specs or [VMEM] * le...  22.2 us
    all_to_all x2, starting transfers between devices, exchange(): lax.all_to_all(payload, ('gx', 'gy'), split_axis=0, concat_axis=0, tiled=...  9.78 us
    all_to_all x2, waiting for transfers between devices, exchange(): lax.all_to_all(payload, ('gx', 'gy'), split_axis=0, concat_axis=0, tiled=...  6.28 us
  transfers between devices with their start and end apart: 5, of which 2 were waited for; matrix products, arithmetic and copies ran while one was open for 0% of the time, Pallas kernels for 16%

profile of v11, /device:TPU:0, one launch (start us, length us, event | category | flops | bytes accessed | tf_op | source)
XLA Modules:
  0.0 63.6 jit_solution(4660095650555251203)
XLA Ops:
  0.6 4.5 %depth_forward.1 = (f32[32,4,384]{2,1,0:T(4,128)}, f32[4,20,24,128]{3,2,1,0:T(8,128)S(1)}) custom-call(bf16[20,2,4,512]{3,2,1,0:T(4,128)(2,1)} %refs_3_.3, bf16[512,128]{1,0:T(8,128)(2,1)} %constant.10.clone.refs_1_, f32[16,20,4,16,20]{4,3,2,1,0:T(8,128)} %bitcast.6), custom_call_target="tpu_custom_call" | custom-call | bytes 4500000 | tf_op jit(solution)/shard_map/depth_forward/pallas_call | solution.py:502
  5.1 0.5 collective-permute-start
  5.6 7.1 %all-to-all-start = ((f32[32,4,384]{2,1,0:T(4,128)}), f32[32,4,384]{2,1,0:T(4,128)}, u32[]{:S(2)}, u32[]{:S(2)}) async-start(f32[32,4,384]{2,1,0:T(4,128)} %get-tuple-element.37), calls=%async_computation | async-start | bytes 393216 | tf_op jit(solution)/shard_map/all_to_all | solution.py:529
  12.7 3.8 %prepare.1 = (f32[4,20,24,128]{3,2,1,0:T(8,128)S(1)}, f32[256,512]{1,0:T(8,128)S(1)}, f32[160,512]{1,0:T(8,128)S(1)}) custom-call(f32[16,20,4,16,20]{4,3,2,1,0:T(8,128)} %bitcast.7, f32[4,20,24,128]{3,2,1,0:T(8,128)S(1)} %get-tuple-element.38.refs_1_, f32[4,256,256]{2,1,0:T(8,128)} %constant.14.clone.refs_2_, bf16[20,2,4,512]{3,2,1,0:T(4,128)(2,1)} %refs_3_.3, ...), custom_call_target="tpu_custom_call" | custom-call | bytes 300000 | tf_op jit(solution)/shard_map/prepare/pallas_call | solution.py:502
  16.5 0.0 copy-start
  16.5 0.7 %copy-done = f32[160,512]{1,0:T(8,128)} copy-done((f32[160,512]{1,0:T(8,128)}, f32[160,512]{1,0:T(8,128)S(1)}, u32[]{:S(2)}) %copy-start) | copy-done | bytes 327704
  17.2 4.4 %all-to-all-done.refs_0_ = f32[32,4,384]{2,1,0:T(4,128)} async-done(((f32[32,4,384]{2,1,0:T(4,128)}), f32[32,4,384]{2,1,0:T(4,128)}, u32[]{:S(2)}, u32[]{:S(2)}) %all-to-all-start) | async-done | bytes 196640 | tf_op jit(solution)/shard_map/all_to_all | solution.py:529
  21.6 0.0 collective-permute-done.refs_3_
  21.6 2.2 %mix_forward.1 = (f32[160,128]{1,0:T(8,128)S(1)}, f32[160,128]{1,0:T(8,128)S(1)}, f32[32,4,384]{2,1,0:T(4,128)S(1)}) custom-call(f32[32,4,384]{2,1,0:T(4,128)} %all-to-all-done.refs_0_, f32[256,512]{1,0:T(8,128)S(1)} %get-tuple-element.43.refs_1_, f32[4,20,24,128]{3,2,1,0:T(8,128)S(1)} %get-tuple-element.44.refs_2_, ...), custom_call_target="tpu_custom_call" | custom-call | bytes 3000000 | tf_op jit(solution)/shard_map/mix_forward/pallas_call | solution.py:502
  23.7 11.4 %all_to_all.20.refs_0_ = f32[32,4,384]{2,1,0:T(4,128)S(1)} all-to-all(f32[32,4,384]{2,1,0:T(4,128)S(1)} %get-tuple-element.46), channel_id=1, replica_groups=mesh['gx'=8,'gy'=4] {'gx','gy'}, dimensions={0} | all-to-all | bytes 393216 | tf_op jit(solution)/shard_map/all_to_all | solution.py:529
  35.2 2.1 %activate.1 = (f32[160,512]{1,0:T(8,128)S(1)}, bf16[160,512]{1,0:T(8,128)(2,1)S(1)}, f32[32,4,384]{2,1,0:T(4,128)S(1)}) custom-call(f32[32,4,384]{2,1,0:T(4,128)S(1)} %all_to_all.20.refs_0_, f32[160,512]{1,0:T(8,128)} %copy-done, bf16[20,2,4,512]{3,2,1,0:T(4,128)(2,1)} %refs_2_.3, f32[128,512]{1,0:T(8,128)} %constant.13.clone.refs_3_, ...), custom_call_target="tpu_custom_call" | custom-call | bytes 6000000 | tf_op jit(solution)/shard_map/activate/pallas_call | solution.py:502
  37.2 11.4 %all_to_all.21.refs_0_ = f32[32,4,384]{2,1,0:T(4,128)S(1)} all-to-all(f32[32,4,384]{2,1,0:T(4,128)S(1)} %get-tuple-element.48), channel_id=1, replica_groups=mesh['gx'=8,'gy'=4] {'gx','gy'}, dimensions={0} | all-to-all | bytes 393216 | tf_op jit(solution)/shard_map/all_to_all | solution.py:529
  48.6 2.1 %mix_back.1 = (f32[160,128]{1,0:T(8,128)S(1)}, f32[160,128]{1,0:T(8,128)S(1)}, f32[32,4,384]{2,1,0:T(4,128)}) custom-call(f32[32,4,384]{2,1,0:T(4,128)S(1)} %all_to_all.21.refs_0_, f32[256,512]{1,0:T(8,128)S(1)} %get-tuple-element.43.refs_1_, f32[4,20,24,128]{3,2,1,0:T(8,128)S(1)} %get-tuple-element.44.refs_2_, ...), custom_call_target="tpu_custom_call" | custom-call | bytes 3000000 | tf_op jit(solution)/shard_map/mix_back/pallas_call | solution.py:502
  50.7 2.7 %all-to-all-start.3 = ((f32[32,4,384]{2,1,0:T(4,128)}), f32[32,4,384]{2,1,0:T(4,128)S(1)}, u32[]{:S(2)}, u32[]{:S(2)}) async-start(f32[32,4,384]{2,1,0:T(4,128)} %get-tuple-element.56), calls=%async_computation.3 | async-start | bytes 393216 | tf_op jit(solution)/shard_map/all_to_all | solution.py:529
  53.5 0.3 collective-permute-start.1
  53.8 0.3 collective-permute-start.2
  54.0 1.8 %emit.1 = (bf16[20,2,4,512]{3,2,1,0:T(4,128)(2,1)}, f32[160,512]{1,0:T(8,128)S(1)}, f32[128,512]{1,0:T(8,128)S(1)}) custom-call(f32[160,512]{1,0:T(8,128)S(1)} %get-tuple-element.61.refs_0_, bf16[160,512]{1,0:T(8,128)(2,1)S(1)} %get-tuple-element.62.refs_1_, bf16[20,20]{1,0:T(8,128)(2,1)} %refs_2_.4, f32[128,512]{1,0:T(8,128)} %constant.12.clone.refs_3_), custom_call_target="tpu_custom_call" | custom-call | bytes 4500000 | tf_op jit(solution)/shard_map/emit/pallas_call | solution.py:502
  55.8 0.0 collective-permute-done.1.refs_2_
  55.9 0.0 collective-permute-done.2.refs_3_
  55.9 4.6 %grad_weights.1 = f32[16,20,4,16,20]{4,3,2,1,0:T(8,128)} custom-call(f32[160,128]{1,0:T(8,128)S(1)} %get-tuple-element.57.refs_0_, f32[160,128]{1,0:T(8,128)S(1)} %get-tuple-element.58.refs_1_, f32[160,128]{1,0:T(8,128)S(1)} %collective-permute-done.1.refs_2_, f32[160,128]{1,0:T(8,128)S(1)} %collective-permute-done.2.refs_3_), custom_call_target="tpu_custom_call" | custom-call | bytes 15000000 | tf_op jit(solution)/shard_map/grad_weights/pallas_call | solution.py:502
  60.5 1.9 %all-to-all-done.3.refs_0_ = f32[32,4,384]{2,1,0:T(4,128)S(1)} async-done(((f32[32,4,384]{2,1,0:T(4,128)}), f32[32,4,384]{2,1,0:T(4,128)S(1)}, u32[]{:S(2)}, u32[]{:S(2)}) %all-to-all-start.3) | async-done | bytes 196640 | tf_op jit(solution)/shard_map/all_to_all | solution.py:529
  62.4 1.2 %finish.1 = bf16[20,2,4,512]{3,2,1,0:T(4,128)(2,1)} custom-call(f32[32,4,384]{2,1,0:T(4,128)S(1)} %all-to-all-done.3.refs_0_, f32[160,512]{1,0:T(8,128)S(1)} %get-tuple-element.68.refs_1_, f32[128,512]{1,0:T(8,128)S(1)} %get-tuple-element.69.refs_2_), custom_call_target="tpu_custom_call" | custom-call | bytes 3000000 | tf_op jit(solution)/shard_map/finish/pallas_call | solution.py:502
Async XLA Ops:
  5.1 16.5 %collective-permute-start = (f32[4,20,24,128]{3,2,1,0:T(8,128)S(1)}, f32[4,20,24,128]{3,2,1,0:T(8,128)S(1)}, u32[]{:S(2)}, u32[]{:S(2)}) collective-permute-start(f32[4,20,24,128]{3,2,1,0:T(8,128)S(1)} %get-tuple-element.38.refs_1_), channel_id=1, source_target_pairs={{0,1},{1,0},{2,3},{3,2},{4,5},{5,4},{6,7},{7,6},{8,9},{9,8},{10,11... | collective-permute-start | bytes 2949128 | tf_op jit(solution)/shard_map/ppermute | solution.py:532
  5.6 16.0 %all-to-all-start = ((f32[32,4,384]{2,1,0:T(4,128)}), f32[32,4,384]{2,1,0:T(4,128)}, u32[]{:S(2)}, u32[]{:S(2)}) async-start(f32[32,4,384]{2,1,0:T(4,128)} %get-tuple-element.37), calls=%async_computation | async-start | bytes 393216 | tf_op jit(solution)/shard_map/all_to_all | solution.py:529
  16.5 0.7 %copy-start = (f32[160,512]{1,0:T(8,128)}, f32[160,512]{1,0:T(8,128)S(1)}, u32[]{:S(2)}) copy-start(f32[160,512]{1,0:T(8,128)S(1)} %get-tuple-element.47.refs_1_) | copy-start | bytes 983044
  50.7 11.6 %all-to-all-start.3 = ((f32[32,4,384]{2,1,0:T(4,128)}), f32[32,4,384]{2,1,0:T(4,128)S(1)}, u32[]{:S(2)}, u32[]{:S(2)}) async-start(f32[32,4,384]{2,1,0:T(4,128)} %get-tuple-element.56), calls=%async_computation.3 | async-start | bytes 393216 | tf_op jit(solution)/shard_map/all_to_all | solution.py:529
  53.5 2.4 %collective-permute-start.1 = (f32[160,128]{1,0:T(8,128)S(1)}, f32[160,128]{1,0:T(8,128)S(1)}, u32[]{:S(2)}, u32[]{:S(2)}) collective-permute-start(f32[160,128]{1,0:T(8,128)S(1)} %get-tuple-element.59), channel_id=1, source_target_pairs={{0,1},{1,0},{2,3},{3,2},{4,5},{5,4},{6,7},{7,6},{8,9},{9,8},{10,11... | collective-permute-start | bytes 245768 | tf_op jit(solution)/shard_map/ppermute | solution.py:532
  53.8 2.1 %collective-permute-start.2 = (f32[160,128]{1,0:T(8,128)S(1)}, f32[160,128]{1,0:T(8,128)S(1)}, u32[]{:S(2)}, u32[]{:S(2)}) collective-permute-start(f32[160,128]{1,0:T(8,128)S(1)} %get-tuple-element.60), channel_id=1, source_target_pairs={{0,1},{1,0},{2,3},{3,2},{4,5},{5,4},{6,7},{7,6},{8,9},{9,8},{10,11... | collective-permute-start | bytes 245768 | tf_op jit(solution)/shard_map/ppermute | solution.py:532

commit v12 on v11

--- a/solution.py
+++ b/solution.py
@@ -44,9 +44,10 @@
     scale = 1.0 / math.sqrt(length_x * length_y)
     cosine, sine = np.cos(angle) * scale, np.sin(angle) * scale
     parts = np.stack([np.stack([cosine, -sine]), np.stack([sine, cosine])])
+    pairs = sizes.cells_y // sizes.pair
     parts = parts.reshape(
-        2, 2, sizes.nx, sizes.cells_x, sizes.ny, sizes.cells_y, sizes.ny, sizes.kept
-    ).transpose(6, 3, 2, 4, 5, 0, 1, 7)
+        2, 2, sizes.nx, sizes.cells_x, sizes.ny, pairs, sizes.pair, sizes.ny, sizes.kept
+    ).transpose(7, 3, 5, 2, 4, 6, 0, 1, 8)
     padded = np.zeros(parts.shape[:-1] + (sizes.half,), np.float32)
     padded[..., : sizes.kept] = parts
     return padded.reshape(sizes.ny, sizes.devices * sizes.cells, 4 * sizes.half)
@@ -71,8 +72,12 @@
         self.main_lanes = self.main * self.modes
         self.rest_lanes = self.rest * self.modes
         self.rest_tiles = round_up(self.rest_lanes, LANES) // LANES
-        self.rest_first = self.cells_x * self.main_lanes
-        self.width = self.rest_first + round_up(self.cells_x * self.rest_lanes, LANES)
+        self.pair = math.gcd(self.cells_y, 2)
+        self.pieces = self.cells // self.pair
+        self.rest_first = self.pieces * self.main_lanes
+        self.rest_width = round_up(self.pieces * self.rest_lanes, LANES)
+        self.width = self.rest_first + self.rest_width
+        self.spread_rows = self.main_lanes + self.rest_width
         self.rows = round_up(self.channels, 8)
 
 
@@ -123,53 +128,59 @@
         turned.append(turn_groups(tiles[first : first + sizes.groups], group, sizes))
     for at in range(2 * sizes.nx):
         main = [block[at] for block in turned]
-        rest = [jnp.zeros((sizes.cells, LANES), F32) for _ in range(sizes.rest_tiles)]
+        last = [jnp.zeros((sizes.cells, LANES), F32) for _ in range(sizes.rest_width // LANES)]
         for r in range(sizes.rest):
             tile, want = divmod(r, sizes.groups)
-            rest[tile] = put_group(rest[tile], tiles[sizes.main + r], at, want, group, sizes)
-        last = []
-        for x in range(sizes.cells_x):
-            rows = slice(x * sizes.cells_y, (x + 1) * sizes.cells_y)
-            for k, value in enumerate(main):
-                lanes = slice(x * sizes.main_lanes + k * LANES, x * sizes.main_lanes + (k + 1) * LANES)
-                for y in range(sizes.ny // 2):
-                    target[at // 2 * sizes.ny + 2 * y + at % 2, :, lanes] = value[rows]
-            if rest:
-                last.append(jnp.concatenate([value[rows] for value in rest], 1)[:, : sizes.rest_lanes])
-        if rest:
-            used = sizes.rest_first + sizes.cells_x * sizes.rest_lanes
-            if sizes.width > used:
-                last.append(jnp.zeros((sizes.cells_y, sizes.width - used), F32))
-            last = jnp.concatenate(last, 1)
-            for y in range(sizes.ny // 2):
-                target[at // 2 * sizes.ny + 2 * y + at % 2, :, sizes.rest_first :] = last
-
-
-def receive_modes(source, scratch, sizes):
+            last[tile] = put_group(last[tile], tiles[sizes.main + r], at, want, group, sizes)
+        if last:
+            last = side_by_side(jnp.concatenate(last, 1), sizes.pair, sizes)
+        for y in range(sizes.ny // 2):
+            device = at // 2 * sizes.ny + 2 * y + at % 2
+            for piece in range(sizes.pieces):
+                rows = slice(piece * sizes.pair, (piece + 1) * sizes.pair)
+                for k, value in enumerate(main):
+                    first = piece * sizes.main_lanes + k * LANES
+                    target[device, :, first : first + LANES] = value[rows]
+            if sizes.rest:
+                target[device, :, sizes.rest_first :] = last
+
+
+def side_by_side(values, rows, sizes):
+    total = values[:rows]
+    for piece in range(1, sizes.pieces):
+        moved = pltpu.roll(values, piece * sizes.rest_lanes, 1)
+        total = total + moved[piece * rows : (piece + 1) * rows]
+    return total
+
+
+def receive_modes(source, scratch, tall, sizes):
     group = lane_group(sizes)
-    parts = source[...].reshape(sizes.nx, sizes.ny // 2, 2, sizes.cells_y, sizes.width)
+    parts = source[...].reshape(sizes.nx, sizes.ny // 2, 2, sizes.pair, sizes.width)
     values = parts[:, 0]
     for y in range(1, sizes.ny // 2):
         values = values + parts[:, y]
-    values = values.reshape(2 * sizes.nx, sizes.cells_y, sizes.width)
+    values = values.reshape(2 * sizes.nx, sizes.pair, sizes.width)
+    for piece in range(sizes.pieces):
+        rows = slice(piece * sizes.pair, (piece + 1) * sizes.pair)
+        if sizes.main:
+            first = piece * sizes.main_lanes
+            tall[:, rows, : sizes.main_lanes] = values[:, :, first : first + sizes.main_lanes]
+        if sizes.rest:
+            last = values[:, :, sizes.rest_first :]
+            if piece:
+                last = pltpu.roll(last, sizes.rest_width - piece * sizes.rest_lanes, 2)
+            tall[:, rows, sizes.main_lanes :] = last
     out = []
-    for k in range(sizes.main // sizes.groups):
-        firsts = [x * sizes.main_lanes + k * LANES for x in range(sizes.cells_x)]
-        tall = jnp.concatenate([values[:, :, first : first + LANES] for first in firsts], 1)
-        out += turn_groups([tall[at] for at in range(2 * sizes.nx)], group, sizes)
-    if sizes.rest:
-        firsts = [sizes.rest_first + x * sizes.rest_lanes for x in range(sizes.cells_x)]
-        tall = jnp.concatenate([values[:, :, first : first + sizes.rest_lanes] for first in firsts], 1)
-        filler = sizes.rest_tiles * LANES - sizes.rest_lanes
-        if filler:
-            tall = jnp.concatenate([tall, jnp.zeros(tall.shape[:2] + (filler,), F32)], 2)
-        for r in range(sizes.rest):
-            value = jnp.zeros((sizes.cells, LANES), F32)
-            tile, have = divmod(r, sizes.groups)
-            for at in range(2 * sizes.nx):
-                source_tile = tall[at, :, tile * LANES : (tile + 1) * LANES]
-                value = put_group(value, source_tile, have, at, group, sizes)
-            out.append(value)
+    for first in range(0, sizes.main_lanes, LANES):
+        tiles = [tall[at, :, first : first + LANES] for at in range(2 * sizes.nx)]
+        out += turn_groups(tiles, group, sizes)
+    for r in range(sizes.rest):
+        value = jnp.zeros((sizes.cells, LANES), F32)
+        tile, have = divmod(r, sizes.groups)
+        first = sizes.main_lanes + tile * LANES
+        for at in range(2 * sizes.nx):
+            value = put_group(value, tall[at, :, first : first + LANES], have, at, group, sizes)
+        out.append(value)
     for w, value in enumerate(out):
         scratch[w * sizes.cells : (w + 1) * sizes.cells, :] = value
     return scratch[...]
@@ -288,14 +299,14 @@
 
 
 def prepare(
-    sizes, source, after, tables, field, weight, bias,
-    target, table, local,
-    here, cells, field_here, weight_here, bias_here, local_here, semaphores, small,
+    sizes, source, after, tables, field, cotangent, weight, bias,
+    target, table, local, cotangent_out,
+    here, cells, field_here, cot_here, cot_cells, weight_here, bias_here, local_here, semaphores, small,
 ):
     del after
     place = lax.axis_index("gy")
     lanes = 2 * sizes.half
-    moves = [(field, field_here), (weight, weight_here), (bias, bias_here)]
+    moves = [(field, field_here), (cotangent, cot_here), (weight, weight_here), (bias, bias_here)]
     for s in range(2):
         for at, owner in enumerate((place, place + 1 - 2 * core_of())):
             moves.append(
@@ -313,22 +324,34 @@
     spread = one_hot(sizes.channels * sizes.cells, sizes.channels, sizes.cells, True).astype(F32)
     offset = jnp.sum(spread * bias_here[...].reshape(1, sizes.channels), axis=1, keepdims=True)
     local_here[...] = dot(cell_mixer(weight_here[...], True, sizes), values) + offset
-    copy = pltpu.make_async_copy(local_here, local, small.at[0])
-    copy.start()
-    copy.wait()
+    gather_cells(cot_here, cot_cells, sizes)
+    results = [
+        pltpu.make_async_copy(local_here, local, small.at[0]),
+        pltpu.make_async_copy(cot_cells, cotangent_out, small.at[1]),
+    ]
+    for copy in results:
+        copy.start()
+    for copy in results:
+        copy.wait()
 
 
 def plane_spectra(sizes, received, table, targets, flat):
+    count = sizes.devices * sizes.pair
     for at in range(sizes.devices):
-        flat[at * sizes.cells_y : (at + 1) * sizes.cells_y, :] = received[at]
-    turned = flat[...].T
-    blocks = []
-    for first, count in ((0, sizes.main_lanes), (sizes.rest_first, sizes.rest_lanes)):
-        if count:
-            firsts = [first + x * count for x in range(sizes.cells_x)]
-            blocks.append(jnp.concatenate([turned[at : at + count] for at in firsts], 1))
-    both = fine_dot(jnp.concatenate(blocks, 0), table[...])
-    rows, lanes = both.shape[0], 2 * sizes.half
+        for piece in range(sizes.pieces):
+            rows = slice(piece * count + at * sizes.pair, piece * count + (at + 1) * sizes.pair)
+            if sizes.main:
+                first = piece * sizes.main_lanes
+                flat[rows, : sizes.main_lanes] = received[at, :, first : first + sizes.main_lanes]
+            if sizes.rest:
+                flat[rows, sizes.main_lanes :] = received[at, :, sizes.rest_first :]
+    if sizes.rest:
+        for piece in range(1, sizes.pieces):
+            rows = slice(piece * count, (piece + 1) * count)
+            shift = sizes.rest_width - piece * sizes.rest_lanes
+            flat[rows, sizes.main_lanes :] = pltpu.roll(flat[rows, sizes.main_lanes :], shift, 1)
+    rows, lanes = targets[0].shape
+    both = fine_dot(flat[...].T[:rows], table[...])
     total = both[:, : 2 * lanes] + pltpu.roll(both[:, 2 * lanes :], rows - sizes.share, 0)
     for at, target in enumerate(targets):
         target[...] = total[:, at * lanes : (at + 1) * lanes]
@@ -337,17 +360,19 @@
 def plane_cells(sizes, spread, table, out):
     modes = jnp.concatenate([spread[at] for at in range(4)], 1)
     cells = fine_dot(table[...], modes, ((1,), (1,)))
-    count = sizes.devices * sizes.cells_y
-    parts = [cells[x * count : (x + 1) * count] for x in range(sizes.cells_x)]
-    pieces = [part[:, : sizes.main_lanes] for part in parts] if sizes.main else []
+    count = sizes.devices * sizes.pair
     if sizes.rest:
-        pieces += [part[:, sizes.main_lanes :] for part in parts]
-    used = sizes.rest_first + sizes.cells_x * sizes.rest_lanes
-    if sizes.width > used:
-        pieces.append(jnp.zeros((count, sizes.width - used), F32))
-    wide = jnp.concatenate(pieces, 1)
+        last = side_by_side(cells[:, sizes.main_lanes :], count, sizes)
     for at in range(sizes.devices):
-        out[at] = wide[at * sizes.cells_y : (at + 1) * sizes.cells_y, :]
+        rows = slice(at * sizes.pair, (at + 1) * sizes.pair)
+        for piece in range(sizes.pieces):
+            if sizes.main:
+                first = piece * sizes.main_lanes
+                out[at, :, first : first + sizes.main_lanes] = cells[
+                    piece * count + at * sizes.pair : piece * count + (at + 1) * sizes.pair, : sizes.main_lanes
+                ]
+        if sizes.rest:
+            out[at, :, sizes.rest_first :] = last[rows]
 
 
 def swap_parts(values, sizes):
@@ -367,7 +392,15 @@
     return lax.broadcasted_iota(jnp.int32, (rows, 2 * sizes.half), 1) < sizes.half
 
 
-def mix_forward(sizes, received, table, weight, other_weight, spectra, other_spectra, out, spread, swapped, flat):
+def mix_forward(
+    sizes, received, table, weight, other_weight, local, cotangent, inverse, forward,
+    spectra, other_spectra, out, local_out, cotangent_out, inverse_out, forward_out,
+    spread, swapped, flat, semaphores,
+):
+    moves = ((local, local_out), (cotangent, cotangent_out), (inverse, inverse_out), (forward, forward_out))
+    copies = [pltpu.make_async_copy(*move, semaphores.at[at]) for at, move in enumerate(moves)]
+    for copy in copies:
+        copy.start()
     plane_spectra(sizes, received, table, (spectra, other_spectra), flat)
     spread[...] = jnp.zeros_like(spread)
     real = first_lanes(sizes.rows, sizes)
@@ -384,6 +417,8 @@
             imag_part = crossed + swap_parts(crossed, sizes)
             put_mixed(spread, at, m, jnp.where(real, real_part, imag_part)[: sizes.channels], sizes)
     plane_cells(sizes, spread, table, out)
+    for copy in copies:
+        copy.wait()
 
 
 def mix_back(sizes, received, table, weight, other_weight, back, other_back, out, spread, flat):
@@ -449,28 +484,17 @@
 
 
 def activate(
-    sizes, received, local, cotangent, inverse, forward, pre_out, signal_out, out,
-    spectrum, cells, inverse_here, local_here, cot_here, forward_here, semaphores,
+    sizes, received, local, cotangent, inverse, forward, pre_out, signal_out, out, spectrum, tall
 ):
-    moves = ((inverse, inverse_here), (local, local_here), (cotangent, cot_here), (forward, forward_here))
-    copies = [pltpu.make_async_copy(*move, semaphores.at[at]) for at, move in enumerate(moves)]
-    for copy in copies:
-        copy.start()
-    values = receive_modes(received, spectrum, sizes)
-    copies[0].wait()
-    copies[1].wait()
-    pre = fine_dot(values, inverse_here[...]) + local_here[...]
+    pre = fine_dot(receive_modes(received, spectrum, tall, sizes), inverse[...]) + local[...]
     pre_out[...] = pre
-    derivative = gelu_parts(pre)[1]
-    copies[2].wait()
-    signal = (gather_cells(cot_here, cells, sizes) * derivative).astype(BF16)
+    signal = (cotangent[...] * gelu_parts(pre)[1]).astype(BF16)
     signal_out[...] = signal
-    copies[3].wait()
-    send_modes(dot(signal, forward_here[...]), out, sizes)
-
-
-def finish(sizes, received, local, inverse, grad_field, spectrum):
-    spatial = fine_dot(receive_modes(received, spectrum, sizes), inverse[...])
+    send_modes(dot(signal, forward[...]), out, sizes)
+
+
+def finish(sizes, received, local, inverse, grad_field, spectrum, tall):
+    spatial = fine_dot(receive_modes(received, spectrum, tall, sizes), inverse[...])
     scatter_cells(spatial + local[...], grad_field, sizes)
 
 
@@ -479,6 +503,7 @@
 
 
 VMEM = pl.BlockSpec(memory_space=pltpu.VMEM)
+HELD = pl.BlockSpec(memory_space=pltpu.VMEM)
 HBM = pl.BlockSpec(memory_space=pltpu.HBM)
 ANYWHERE = pl.BlockSpec(memory_space=pl.ANY)
 
@@ -496,8 +521,9 @@
         body(sizes, *refs)
 
     if specs:
+        spaces = [pltpu.HBM if spec is HBM else pltpu.VMEM if spec is HELD else None for spec in specs]
         args = [
-            pltpu.with_memory_space_constraint(arg, pltpu.HBM) if spec is HBM else arg for arg, spec in zip(args, specs)
+            pltpu.with_memory_space_constraint(arg, space) if space else arg for arg, space in zip(args, spaces)
         ]
     return pl.pallas_call(
         kernel,
@@ -531,15 +557,16 @@
     def other_core(values):
         return lax.ppermute(values, "gy", pairs)
 
-    payload = shape_of((z.devices, z.cells_y, z.width))
+    payload = shape_of((z.devices, z.pair, z.width))
     cell_rows = z.channels * z.cells
     cells_shape = (cell_rows, z.depth)
     cells_scratch = pltpu.VMEM(cells_shape, F32)
     spectrum_scratch = pltpu.VMEM((cell_rows, z.all_modes), F32)
     spectra_shape = (z.channels * z.modes, 2 * z.half)
     spectra_scratch = pltpu.VMEM(spectra_shape, F32)
-    flat_scratch = pltpu.VMEM((z.devices * z.cells_y, z.width), F32)
-    spread_scratch = pltpu.VMEM((4,) + spectra_shape, F32)
+    flat_scratch = pltpu.VMEM((z.devices * z.cells, z.spread_rows), F32)
+    spread_scratch = pltpu.VMEM((4, z.spread_rows, 2 * z.half), F32)
+    tall_scratch = pltpu.VMEM((2 * z.nx, z.cells, z.spread_rows), F32)
     field_scratch = pltpu.VMEM(field.shape, BF16)
     weight_here = pltpu.VMEM(pointwise_weight.shape, BF16)
     native = jnp.transpose(spectral_weight, (0, 1, 2, 4, 5, 3))
@@ -561,31 +588,33 @@
     )
     received = exchange(sent)
     other_turned = other_core(turned_away)
-    turned, plane, local = whole_call(
+    turned, plane, local, cot_cells = whole_call(
         prepare, z, 100,
-        (turned_shape, shape_of((z.devices * z.cells, 8 * z.half)), shape_of(cells_shape)),
+        (turned_shape, shape_of((z.devices * z.cells, 8 * z.half)), shape_of(cells_shape), shape_of(cells_shape)),
         [
-            half_scratch, cells_scratch, field_scratch, weight_here, pltpu.VMEM(channel_bias.shape, F32),
-            cells_scratch, flags(z.modes), flags(7),
+            half_scratch, cells_scratch, field_scratch, field_scratch, cells_scratch, weight_here,
+            pltpu.VMEM(channel_bias.shape, F32), cells_scratch, flags(z.modes), flags(8),
         ],
-        weights, turned_away, jnp.asarray(plane_tables(z)), field, pointwise_weight, channel_bias,
-        specs=[HBM, ANYWHERE] + [HBM] * 4, out_specs=(VMEM, VMEM, HBM),
-    )
-    received, other_turned, turned, plane, local = lax.optimization_barrier(
-        (received, other_turned, turned, plane, local)
-    )
-    spectra, other_spectra, sent = whole_call(
-        mix_forward, z, 1000, (shape_of(spectra_shape), shape_of(spectra_shape), payload),
-        [spread_scratch, spectra_scratch, flat_scratch], received, plane, turned, other_turned,
+        weights, turned_away, jnp.asarray(plane_tables(z)), field, cotangent, pointwise_weight, channel_bias,
+        specs=[HBM, ANYWHERE] + [HBM] * 5, out_specs=(VMEM, VMEM, HBM, HBM),
+    )
+    received, other_turned, turned, plane, local, cot_cells = lax.optimization_barrier(
+        (received, other_turned, turned, plane, local, cot_cells)
+    )
+    spectra, other_spectra, sent, local, cot_cells, inverse_here, forward_here = whole_call(
+        mix_forward, z, 1000,
+        (
+            shape_of(spectra_shape), shape_of(spectra_shape), payload, shape_of(cells_shape), shape_of(cells_shape),
+            shape_of(inverse_first.shape), shape_of(forward_back.shape, BF16),
+        ),
+        [spread_scratch, spectra_scratch, flat_scratch, flags(4)],
+        received, plane, turned, other_turned, local, cot_cells, inverse_first, forward_back,
+        specs=[HELD] + [VMEM] * 3 + [HBM] * 4,
     )
     pre, signal, sent = whole_call(
         activate, z, 2000,
-        (shape_of(cells_shape), shape_of(cells_shape, BF16), payload),
-        [
-            spectrum_scratch, cells_scratch, pltpu.VMEM(inverse_first.shape, F32), cells_scratch, field_scratch,
-            pltpu.VMEM(forward_back.shape, BF16), flags(4),
-        ],
-        exchange(sent), local, cotangent, inverse_first, forward_back, specs=[VMEM] + [HBM] * 4,
+        (shape_of(cells_shape), shape_of(cells_shape, BF16), payload), [spectrum_scratch, tall_scratch],
+        exchange(sent), local, cot_cells, inverse_here, forward_here,
     )
     back, other_back, sent = whole_call(
         mix_back, z, 1000, (shape_of(spectra_shape), shape_of(spectra_shape), payload),
@@ -611,7 +640,7 @@
         (returned, gradient, layer_out, local, inverse_here)
     )
     grad_field = whole_call(
-        finish, z, 1000, shape_of(field.shape, BF16), [spectrum_scratch], returned, local, inverse_here
+        finish, z, 1000, shape_of(field.shape, BF16), [spectrum_scratch, tall_scratch], returned, local, inverse_here
     )
     return (layer_out, grad_field, jnp.transpose(gradient.reshape(native.shape), (0, 1, 2, 5, 3, 4)))
 

time: 64.1 us -> 61.9 us (0.966)
  waiting for transfers between devices: 6.29 us -> 4.71 us
  blocking collectives: 22.8 us -> 21.7 us
  local copies, waits for them, and re-layouts: 0.72 us -> 1.44 us
    all_to_all x2, waiting for transfers between devices: 6.28 us -> 4.7 us  [exchange(): lax.all_to_all(payload, ('gx', 'gy'), split_axis=0, concat_axis=0, tiled=...]
    all_to_all x2, blocking collectives: 22.8 us -> 21.7 us  [exchange(): lax.all_to_all(payload, ('gx', 'gy'), split_axis=0, concat_axis=0, tiled=...]
    unnamed x2 -> x4, local copies, waits for them, and re-layouts: 0.72 us -> 1.44 us
  transfers between devices with their start and end apart: 5 -> 5, of which waited for: 2 -> 2; matrix products, arithmetic and copies ran while one was open for 0% -> 0% of each run, Pallas kernels for 16% -> 17%
where the time goes in v12:
time: 61.9 us; the launch traced here: 61.5 us
  Pallas kernels  22.2 us (36%)
  blocking collectives  21.7 us (35%)
  starting transfers between devices  10.7 us (17%)
  waiting for transfers between devices  4.71 us (8%)
  local copies, waits for them, and re-layouts  1.44 us (2%)
  between operations  0.72 us (1%)
    pallas_call x8, Pallas kernels, whole_call(): pl.pallas_call(kernel, out_shape=out_shape, in_specs=specs or [VMEM] * le...  22.2 us
    all_to_all x2, blocking collectives, exchange(): lax.all_to_all(payload, ('gx', 'gy'), split_axis=0, concat_axis=0, tiled=...  21.7 us
    all_to_all x2, starting transfers between devices, exchange(): lax.all_to_all(payload, ('gx', 'gy'), split_axis=0, concat_axis=0, tiled=...  9.65 us
    all_to_all x2, waiting for transfers between devices, exchange(): lax.all_to_all(payload, ('gx', 'gy'), split_axis=0, concat_axis=0, tiled=...  4.7 us
    unnamed x4, local copies, waits for them, and re-layouts  1.44 us
  transfers between devices with their start and end apart: 5, of which 2 were waited for; matrix products, arithmetic and copies ran while one was open for 0% of the time, Pallas kernels for 17%

profile of v12, /device:TPU:0, one launch (start us, length us, event | category | flops | bytes accessed | tf_op | source)
XLA Modules:
  0.0 61.5 jit_solution(5636271134812410890)
XLA Ops:
  0.6 4.5 %depth_forward.1 = (f32[32,2,640]{2,1,0:T(2,128)}, f32[4,20,24,128]{3,2,1,0:T(8,128)S(1)}) custom-call(bf16[20,2,4,512]{3,2,1,0:T(4,128)(2,1)} %refs_3_.2, bf16[512,128]{1,0:T(8,128)(2,1)} %constant.10.clone.refs_1_, f32[16,20,4,16,20]{4,3,2,1,0:T(8,128)} %bitcast.6), custom_call_target="tpu_custom_call" | custom-call | bytes 4500000 | tf_op jit(solution)/shard_map/depth_forward/pallas_call | solution.py:528
  5.1 0.5 collective-permute-start
  5.7 7.1 %all-to-all-start = ((f32[32,2,640]{2,1,0:T(2,128)}), f32[32,2,640]{2,1,0:T(2,128)}, u32[]{:S(2)}, u32[]{:S(2)}) async-start(f32[32,2,640]{2,1,0:T(2,128)} %get-tuple-element.43), calls=%async_computation | async-start | bytes 327680 | tf_op jit(solution)/shard_map/all_to_all | solution.py:555
  12.7 4.0 %prepare.1 = (f32[4,20,24,128]{3,2,1,0:T(8,128)S(1)}, f32[256,512]{1,0:T(8,128)S(1)}, f32[160,512]{1,0:T(8,128)S(1)}, f32[160,512]{1,0:T(8,128)S(1)}) custom-call(f32[16,20,4,16,20]{4,3,2,1,0:T(8,128)} %bitcast.7, f32[4,20,24,128]{3,2,1,0:T(8,128)S(1)} %get-tuple-element.44.refs_1_, f32[4,256,256]{2,1,0:T(8,128)} %constant.14.clone.refs_2_, ...), custom_call_target="tpu_custom_call" | custom-call | bytes 300000 | tf_op jit(solution)/shard_map/prepare/pallas_call | solution.py:528
  16.7 0.0 copy-start
  16.8 0.7 %copy-done = f32[160,512]{1,0:T(8,128)} copy-done((f32[160,512]{1,0:T(8,128)}, f32[160,512]{1,0:T(8,128)S(1)}, u32[]{:S(2)}) %copy-start) | copy-done | bytes 327704
  17.5 0.0 copy-start.1
  17.5 0.7 %copy-done.1 = f32[160,512]{1,0:T(8,128)} copy-done((f32[160,512]{1,0:T(8,128)}, f32[160,512]{1,0:T(8,128)S(1)}, u32[]{:S(2)}) %copy-start.1) | copy-done | bytes 327704
  18.2 3.1 %all-to-all-done.refs_0_ = f32[32,2,640]{2,1,0:T(2,128)} async-done(((f32[32,2,640]{2,1,0:T(2,128)}), f32[32,2,640]{2,1,0:T(2,128)}, u32[]{:S(2)}, u32[]{:S(2)}) %all-to-all-start) | async-done | bytes 163872 | tf_op jit(solution)/shard_map/all_to_all | solution.py:555
  21.3 0.0 collective-permute-done.refs_3_
  21.3 2.7 %mix_forward.1 = (f32[160,128]{1,0:T(8,128)S(1)}, f32[160,128]{1,0:T(8,128)S(1)}, f32[32,2,640]{2,1,0:T(2,128)S(1)}, f32[160,512]{1,0:T(8,128)S(1)}, f32[160,512...) custom-call(f32[32,2,640]{2,1,0:T(2,128)} %all-to-all-done.refs_0_, ...), custom_call_target="tpu_custom_call" | custom-call | bytes 3000000 | tf_op jit(solution)/shard_map/mix_forward/pallas_call | solution.py:528
  24.0 11.0 %all_to_all.20.refs_0_ = f32[32,2,640]{2,1,0:T(2,128)S(1)} all-to-all(f32[32,2,640]{2,1,0:T(2,128)S(1)} %get-tuple-element.55), channel_id=1, replica_groups=mesh['gx'=8,'gy'=4] {'gx','gy'}, dimensions={0} | all-to-all | bytes 327680 | tf_op jit(solution)/shard_map/all_to_all | solution.py:555
  35.1 1.2 %activate.1 = (f32[160,512]{1,0:T(8,128)S(1)}, bf16[160,512]{1,0:T(8,128)(2,1)S(1)}, f32[32,2,640]{2,1,0:T(2,128)S(1)}) custom-call(f32[32,2,640]{2,1,0:T(2,128)S(1)} %all_to_all.20.refs_0_, f32[160,512]{1,0:T(8,128)S(1)} %get-tuple-element.56.refs_1_, f32[160,512]{1,0:T(8,128)S(1)} %get-tuple-element.57.refs_2_, f32[128,512]{1,0:T(8,128)S(1)} %get-tuple-element.58.refs_3_, ...), custom_call_target="tpu_custom_call" | custom-call | bytes 6000000 | tf_op jit(solution)/shard_map/activate/pallas_call | solution.py:528
  36.2 10.7 %all_to_all.21.refs_0_ = f32[32,2,640]{2,1,0:T(2,128)S(1)} all-to-all(f32[32,2,640]{2,1,0:T(2,128)S(1)} %get-tuple-element.60), channel_id=1, replica_groups=mesh['gx'=8,'gy'=4] {'gx','gy'}, dimensions={0} | all-to-all | bytes 327680 | tf_op jit(solution)/shard_map/all_to_all | solution.py:555
  47.0 2.2 %mix_back.1 = (f32[160,128]{1,0:T(8,128)S(1)}, f32[160,128]{1,0:T(8,128)S(1)}, f32[32,2,640]{2,1,0:T(2,128)}) custom-call(f32[32,2,640]{2,1,0:T(2,128)S(1)} %all_to_all.21.refs_0_, f32[256,512]{1,0:T(8,128)S(1)} %get-tuple-element.50.refs_1_, f32[4,20,24,128]{3,2,1,0:T(8,128)S(1)} %get-tuple-element.51.refs_2_, ...), custom_call_target="tpu_custom_call" | custom-call | bytes 3000000 | tf_op jit(solution)/shard_map/mix_back/pallas_call | solution.py:528
  49.1 2.6 %all-to-all-start.3 = ((f32[32,2,640]{2,1,0:T(2,128)}), f32[32,2,640]{2,1,0:T(2,128)S(1)}, u32[]{:S(2)}, u32[]{:S(2)}) async-start(f32[32,2,640]{2,1,0:T(2,128)} %get-tuple-element.68), calls=%async_computation.3 | async-start | bytes 327680 | tf_op jit(solution)/shard_map/all_to_all | solution.py:555
  51.7 0.2 collective-permute-start.1
  51.9 0.4 collective-permute-start.2
  52.3 1.8 %emit.1 = (bf16[20,2,4,512]{3,2,1,0:T(4,128)(2,1)}, f32[160,512]{1,0:T(8,128)S(1)}, f32[128,512]{1,0:T(8,128)S(1)}) custom-call(f32[160,512]{1,0:T(8,128)S(1)} %get-tuple-element.73.refs_0_, bf16[160,512]{1,0:T(8,128)(2,1)S(1)} %get-tuple-element.74.refs_1_, bf16[20,20]{1,0:T(8,128)(2,1)} %refs_2_.2, f32[128,512]{1,0:T(8,128)} %constant.12.clone.refs_3_), custom_call_target="tpu_custom_call" | custom-call | bytes 4500000 | tf_op jit(solution)/shard_map/emit/pallas_call | solution.py:528
  54.1 0.0 collective-permute-done.1.refs_2_
  54.1 0.0 collective-permute-done.2.refs_3_
  54.1 4.6 %grad_weights.1 = f32[16,20,4,16,20]{4,3,2,1,0:T(8,128)} custom-call(f32[160,128]{1,0:T(8,128)S(1)} %get-tuple-element.69.refs_0_, f32[160,128]{1,0:T(8,128)S(1)} %get-tuple-element.70.refs_1_, f32[160,128]{1,0:T(8,128)S(1)} %collective-permute-done.1.refs_2_, f32[160,128]{1,0:T(8,128)S(1)} %collective-permute-done.2.refs_3_), custom_call_target="tpu_custom_call" | custom-call | bytes 15000000 | tf_op jit(solution)/shard_map/grad_weights/pallas_call | solution.py:528
  58.7 1.6 %all-to-all-done.3.refs_0_ = f32[32,2,640]{2,1,0:T(2,128)S(1)} async-done(((f32[32,2,640]{2,1,0:T(2,128)}), f32[32,2,640]{2,1,0:T(2,128)S(1)}, u32[]{:S(2)}, u32[]{:S(2)}) %all-to-all-start.3) | async-done | bytes 163872 | tf_op jit(solution)/shard_map/all_to_all | solution.py:555
  60.3 1.2 %finish.1 = bf16[20,2,4,512]{3,2,1,0:T(4,128)(2,1)} custom-call(f32[32,2,640]{2,1,0:T(2,128)S(1)} %all-to-all-done.3.refs_0_, f32[160,512]{1,0:T(8,128)S(1)} %get-tuple-element.80.refs_1_, f32[128,512]{1,0:T(8,128)S(1)} %get-tuple-element.81.refs_2_), custom_call_target="tpu_custom_call" | custom-call | bytes 3000000 | tf_op jit(solution)/shard_map/finish/pallas_call | solution.py:528
Async XLA Ops:
  5.1 16.2 %collective-permute-start = (f32[4,20,24,128]{3,2,1,0:T(8,128)S(1)}, f32[4,20,24,128]{3,2,1,0:T(8,128)S(1)}, u32[]{:S(2)}, u32[]{:S(2)}) collective-permute-start(f32[4,20,24,128]{3,2,1,0:T(8,128)S(1)} %get-tuple-element.44.refs_1_), channel_id=1, source_target_pairs={{0,1},{1,0},{2,3},{3,2},{4,5},{5,4},{6,7},{7,6},{8,9},{9,8},{10,11... | collective-permute-start | bytes 2949128 | tf_op jit(solution)/shard_map/ppermute | solution.py:558
  5.7 15.6 %all-to-all-start = ((f32[32,2,640]{2,1,0:T(2,128)}), f32[32,2,640]{2,1,0:T(2,128)}, u32[]{:S(2)}, u32[]{:S(2)}) async-start(f32[32,2,640]{2,1,0:T(2,128)} %get-tuple-element.43), calls=%async_computation | async-start | bytes 327680 | tf_op jit(solution)/shard_map/all_to_all | solution.py:555
  16.7 0.7 %copy-start = (f32[160,512]{1,0:T(8,128)}, f32[160,512]{1,0:T(8,128)S(1)}, u32[]{:S(2)}) copy-start(f32[160,512]{1,0:T(8,128)S(1)} %get-tuple-element.53.refs_4_) | copy-start | bytes 983044
  17.5 0.7 %copy-start.1 = (f32[160,512]{1,0:T(8,128)}, f32[160,512]{1,0:T(8,128)S(1)}, u32[]{:S(2)}) copy-start(f32[160,512]{1,0:T(8,128)S(1)} %get-tuple-element.54.refs_5_) | copy-start | bytes 983044
  49.1 11.2 %all-to-all-start.3 = ((f32[32,2,640]{2,1,0:T(2,128)}), f32[32,2,640]{2,1,0:T(2,128)S(1)}, u32[]{:S(2)}, u32[]{:S(2)}) async-start(f32[32,2,640]{2,1,0:T(2,128)} %get-tuple-element.68), calls=%async_computation.3 | async-start | bytes 327680 | tf_op jit(solution)/shard_map/all_to_all | solution.py:555
  51.7 2.4 %collective-permute-start.1 = (f32[160,128]{1,0:T(8,128)S(1)}, f32[160,128]{1,0:T(8,128)S(1)}, u32[]{:S(2)}, u32[]{:S(2)}) collective-permute-start(f32[160,128]{1,0:T(8,128)S(1)} %get-tuple-element.71), channel_id=1, source_target_pairs={{0,1},{1,0},{2,3},{3,2},{4,5},{5,4},{6,7},{7,6},{8,9},{9,8},{10,11... | collective-permute-start | bytes 245768 | tf_op jit(solution)/shard_map/ppermute | solution.py:558
  51.9 2.2 %collective-permute-start.2 = (f32[160,128]{1,0:T(8,128)S(1)}, f32[160,128]{1,0:T(8,128)S(1)}, u32[]{:S(2)}, u32[]{:S(2)}) collective-permute-start(f32[160,128]{1,0:T(8,128)S(1)} %get-tuple-element.72), channel_id=1, source_target_pairs={{0,1},{1,0},{2,3},{3,2},{4,5},{5,4},{6,7},{7,6},{8,9},{9,8},{10,11... | collective-permute-start | bytes 245768 | tf_op jit(solution)/shard_map/ppermute | solution.py:558

commit v13 on v12

--- a/solution.py
+++ b/solution.py
@@ -395,16 +395,21 @@
 def mix_forward(
     sizes, received, table, weight, other_weight, local, cotangent, inverse, forward,
     spectra, other_spectra, out, local_out, cotangent_out, inverse_out, forward_out,
-    spread, swapped, flat, semaphores,
+    spread, swapped, flat, other_here, semaphores,
 ):
-    moves = ((local, local_out), (cotangent, cotangent_out), (inverse, inverse_out), (forward, forward_out))
+    moves = (
+        (other_weight, other_here), (local, local_out), (cotangent, cotangent_out), (inverse, inverse_out),
+        (forward, forward_out),
+    )
     copies = [pltpu.make_async_copy(*move, semaphores.at[at]) for at, move in enumerate(moves)]
     for copy in copies:
         copy.start()
     plane_spectra(sizes, received, table, (spectra, other_spectra), flat)
     spread[...] = jnp.zeros_like(spread)
     real = first_lanes(sizes.rows, sizes)
-    for at, (rows, block) in enumerate(((spectra, weight), (other_spectra, other_weight))):
+    for at, (rows, block) in enumerate(((spectra, weight), (other_spectra, other_here))):
+        if at:
+            copies[0].wait()
         swapped[...] = swap_parts(rows[...], sizes)
         for m in range(sizes.share):
             straight = jnp.zeros((sizes.rows, 2 * sizes.half), F32)
@@ -417,15 +422,19 @@
             imag_part = crossed + swap_parts(crossed, sizes)
             put_mixed(spread, at, m, jnp.where(real, real_part, imag_part)[: sizes.channels], sizes)
     plane_cells(sizes, spread, table, out)
-    for copy in copies:
+    for copy in copies[1:]:
         copy.wait()
 
 
-def mix_back(sizes, received, table, weight, other_weight, back, other_back, out, spread, flat):
+def mix_back(sizes, received, table, weight, other_weight, back, other_back, out, spread, flat, other_here, semaphore):
+    copy = pltpu.make_async_copy(other_weight, other_here, semaphore.at[0])
+    copy.start()
     plane_spectra(sizes, received, table, (back, other_back), flat)
     spread[...] = jnp.zeros_like(spread)
     real = first_lanes(sizes.channels, sizes)
-    for at, (source, block) in enumerate(((back, weight), (other_back, other_weight))):
+    for at, (source, block) in enumerate(((back, weight), (other_back, other_here))):
+        if at:
+            copy.wait()
         for m in range(sizes.share):
             rows = source[mode_rows(m, sizes), :]
             if sizes.rows > sizes.channels:
@@ -590,7 +599,7 @@
     other_turned = other_core(turned_away)
     turned, plane, local, cot_cells = whole_call(
         prepare, z, 100,
-        (turned_shape, shape_of((z.devices * z.cells, 8 * z.half)), shape_of(cells_shape), shape_of(cells_shape)),
+        (turned_shape, shape_of((z.devices * z.cells, 8 * z.half)), pltpu.HBM(cells_shape, F32), pltpu.HBM(cells_shape, F32)),
         [
             half_scratch, cells_scratch, field_scratch, field_scratch, cells_scratch, weight_here,
             pltpu.VMEM(channel_bias.shape, F32), cells_scratch, flags(z.modes), flags(8),
@@ -607,9 +616,9 @@
             shape_of(spectra_shape), shape_of(spectra_shape), payload, shape_of(cells_shape), shape_of(cells_shape),
             shape_of(inverse_first.shape), shape_of(forward_back.shape, BF16),
         ),
-        [spread_scratch, spectra_scratch, flat_scratch, flags(4)],
+        [spread_scratch, spectra_scratch, flat_scratch, pltpu.VMEM(turned_shape.shape, F32), flags(5)],
         received, plane, turned, other_turned, local, cot_cells, inverse_first, forward_back,
-        specs=[HELD] + [VMEM] * 3 + [HBM] * 4,
+        specs=[HELD] + [VMEM] * 2 + [HBM] * 5,
     )
     pre, signal, sent = whole_call(
         activate, z, 2000,
@@ -618,7 +627,8 @@
     )
     back, other_back, sent = whole_call(
         mix_back, z, 1000, (shape_of(spectra_shape), shape_of(spectra_shape), payload),
-        [spread_scratch, flat_scratch], exchange(sent), plane, turned, other_turned,
+        [spread_scratch, flat_scratch, pltpu.VMEM(turned_shape.shape, F32), flags(1)],
+        exchange(sent), plane, turned, other_turned, specs=[VMEM] * 3 + [HBM],
     )
     sent, spectra, other_spectra, back, other_back, pre, signal = lax.optimization_barrier(
         (sent, spectra, other_spectra, back, other_back, pre, signal)

time: 61.9 us -> 62.1 us (level)
  local copies, waits for them, and re-layouts: 1.44 us -> 0 us
  Pallas kernels: 22.2 us -> 23.4 us
  waiting for transfers between devices: 4.71 us -> 5.55 us
    unnamed x4 -> x0, local copies, waits for them, and re-layouts: 1.44 us -> none
    pallas_call x8, Pallas kernels: 22.2 us -> 23.4 us  [whole_call(): pl.pallas_call(kernel, out_shape=out_shape, in_specs=specs or [VMEM] * le...]
    all_to_all x2, waiting for transfers between devices: 4.7 us -> 5.55 us  [exchange(): lax.all_to_all(payload, ('gx', 'gy'), split_axis=0, concat_axis=0, tiled=...]
  transfers between devices with their start and end apart: 5 -> 5, of which waited for: 2 -> 2; matrix products, arithmetic and copies ran while one was open for 0% -> 0% of each run, Pallas kernels for 17% -> 18%
where the time goes in v13:
time: 62.1 us; the launch traced here: 61.7 us
  Pallas kernels  23.4 us (38%)
  blocking collectives  21.4 us (34%)
  starting transfers between devices  10.6 us (17%)
  waiting for transfers between devices  5.55 us (9%)
  between operations  0.72 us (1%)
    pallas_call x8, Pallas kernels, whole_call(): pl.pallas_call(kernel, out_shape=out_shape, in_specs=specs or [VMEM] * le...  23.4 us
    all_to_all x2, blocking collectives, exchange(): lax.all_to_all(payload, ('gx', 'gy'), split_axis=0, concat_axis=0, tiled=...  21.4 us
    all_to_all x2, starting transfers between devices, exchange(): lax.all_to_all(payload, ('gx', 'gy'), split_axis=0, concat_axis=0, tiled=...  9.55 us
    all_to_all x2, waiting for transfers between devices, exchange(): lax.all_to_all(payload, ('gx', 'gy'), split_axis=0, concat_axis=0, tiled=...  5.55 us
  transfers between devices with their start and end apart: 5, of which 2 were waited for; matrix products, arithmetic and copies ran while one was open for 0% of the time, Pallas kernels for 18%

profile of v13, /device:TPU:0, one launch (start us, length us, event | category | flops | bytes accessed | tf_op | source)
XLA Modules:
  0.0 61.7 jit_solution(16393595834898495199)
XLA Ops:
  0.6 4.5 %depth_forward.1 = (f32[32,2,640]{2,1,0:T(2,128)}, f32[4,20,24,128]{3,2,1,0:T(8,128)S(1)}) custom-call(bf16[20,2,4,512]{3,2,1,0:T(4,128)(2,1)} %refs_3_.2, bf16[512,128]{1,0:T(8,128)(2,1)} %constant.10.clone.refs_1_, f32[16,20,4,16,20]{4,3,2,1,0:T(8,128)} %bitcast.6), custom_call_target="tpu_custom_call" | custom-call | bytes 4500000 | tf_op jit(solution)/shard_map/depth_forward/pallas_call | solution.py:537
  5.1 0.5 collective-permute-start
  5.7 7.0 %all-to-all-start = ((f32[32,2,640]{2,1,0:T(2,128)}), f32[32,2,640]{2,1,0:T(2,128)S(1)}, u32[]{:S(2)}, u32[]{:S(2)}) async-start(f32[32,2,640]{2,1,0:T(2,128)} %get-tuple-element.43), calls=%async_computation | async-start | bytes 327680 | tf_op jit(solution)/shard_map/all_to_all | solution.py:564
  12.6 4.6 %prepare.1 = (f32[4,20,24,128]{3,2,1,0:T(8,128)S(1)}, f32[256,512]{1,0:T(8,128)S(1)}, f32[160,512]{1,0:T(8,128)}, f32[160,512]{1,0:T(8,128)}) custom-call(f32[16,20,4,16,20]{4,3,2,1,0:T(8,128)} %bitcast.7, f32[4,20,24,128]{3,2,1,0:T(8,128)S(1)} %get-tuple-element.44.refs_1_, f32[4,256,256]{2,1,0:T(8,128)} %constant.14.clone.refs_2_, ...), custom_call_target="tpu_custom_call" | custom-call | bytes 300000 | tf_op jit(solution)/shard_map/prepare/pallas_call | solution.py:537
  17.2 4.0 %all-to-all-done.refs_0_ = f32[32,2,640]{2,1,0:T(2,128)S(1)} async-done(((f32[32,2,640]{2,1,0:T(2,128)}), f32[32,2,640]{2,1,0:T(2,128)S(1)}, u32[]{:S(2)}, u32[]{:S(2)}) %all-to-all-start) | async-done | bytes 163872 | tf_op jit(solution)/shard_map/all_to_all | solution.py:564
  21.2 0.0 collective-permute-done.refs_3_
  21.2 2.1 %mix_forward.1 = (f32[160,128]{1,0:T(8,128)S(1)}, f32[160,128]{1,0:T(8,128)S(1)}, f32[32,2,640]{2,1,0:T(2,128)S(1)}, f32[160,512]{1,0:T(8,128)S(1)}, f32[160,512...) custom-call(f32[32,2,640]{2,1,0:T(2,128)S(1)} %all-to-all-done.refs_0_, ...), custom_call_target="tpu_custom_call" | custom-call | bytes 3000000 | tf_op jit(solution)/shard_map/mix_forward/pallas_call | solution.py:537
  23.3 10.7 %all_to_all.20.refs_0_ = f32[32,2,640]{2,1,0:T(2,128)S(1)} all-to-all(f32[32,2,640]{2,1,0:T(2,128)S(1)} %get-tuple-element.55), channel_id=1, replica_groups=mesh['gx'=8,'gy'=4] {'gx','gy'}, dimensions={0} | all-to-all | bytes 327680 | tf_op jit(solution)/shard_map/all_to_all | solution.py:564
  34.0 1.2 %activate.1 = (f32[160,512]{1,0:T(8,128)S(1)}, bf16[160,512]{1,0:T(8,128)(2,1)S(1)}, f32[32,2,640]{2,1,0:T(2,128)S(1)}) custom-call(f32[32,2,640]{2,1,0:T(2,128)S(1)} %all_to_all.20.refs_0_, f32[160,512]{1,0:T(8,128)S(1)} %get-tuple-element.56.refs_1_, f32[160,512]{1,0:T(8,128)S(1)} %get-tuple-element.57.refs_2_, f32[128,512]{1,0:T(8,128)S(1)} %get-tuple-element.58.refs_3_, ...), custom_call_target="tpu_custom_call" | custom-call | bytes 6000000 | tf_op jit(solution)/shard_map/activate/pallas_call | solution.py:537
  35.2 10.7 %all_to_all.21.refs_0_ = f32[32,2,640]{2,1,0:T(2,128)S(1)} all-to-all(f32[32,2,640]{2,1,0:T(2,128)S(1)} %get-tuple-element.60), channel_id=1, replica_groups=mesh['gx'=8,'gy'=4] {'gx','gy'}, dimensions={0} | all-to-all | bytes 327680 | tf_op jit(solution)/shard_map/all_to_all | solution.py:564
  45.9 3.4 %mix_back.1 = (f32[160,128]{1,0:T(8,128)S(1)}, f32[160,128]{1,0:T(8,128)S(1)}, f32[32,2,640]{2,1,0:T(2,128)}) custom-call(f32[32,2,640]{2,1,0:T(2,128)S(1)} %all_to_all.21.refs_0_, f32[256,512]{1,0:T(8,128)S(1)} %get-tuple-element.50.refs_1_, f32[4,20,24,128]{3,2,1,0:T(8,128)S(1)} %get-tuple-element.51.refs_2_, f32[4,20,24,128]{3,2,1,0:T(8,128)} %collective-permute-done.refs_3_), custom_call_target="tpu_custom_call" | custom-call | bytes 3000000 | tf_op jit(solution)/shard_map/mix_back/pallas_call | solution.py:537
  49.3 2.6 %all-to-all-start.3 = ((f32[32,2,640]{2,1,0:T(2,128)}), f32[32,2,640]{2,1,0:T(2,128)S(1)}, u32[]{:S(2)}, u32[]{:S(2)}) async-start(f32[32,2,640]{2,1,0:T(2,128)} %get-tuple-element.68), calls=%async_computation.3 | async-start | bytes 327680 | tf_op jit(solution)/shard_map/all_to_all | solution.py:564
  51.9 0.2 collective-permute-start.1
  52.1 0.4 collective-permute-start.2
  52.5 1.8 %emit.1 = (bf16[20,2,4,512]{3,2,1,0:T(4,128)(2,1)}, f32[160,512]{1,0:T(8,128)S(1)}, f32[128,512]{1,0:T(8,128)S(1)}) custom-call(f32[160,512]{1,0:T(8,128)S(1)} %get-tuple-element.73.refs_0_, bf16[160,512]{1,0:T(8,128)(2,1)S(1)} %get-tuple-element.74.refs_1_, bf16[20,20]{1,0:T(8,128)(2,1)} %refs_2_.2, f32[128,512]{1,0:T(8,128)} %constant.12.clone.refs_3_), custom_call_target="tpu_custom_call" | custom-call | bytes 4500000 | tf_op jit(solution)/shard_map/emit/pallas_call | solution.py:537
  54.3 0.0 collective-permute-done.1.refs_2_
  54.3 0.0 collective-permute-done.2.refs_3_
  54.3 4.6 %grad_weights.1 = f32[16,20,4,16,20]{4,3,2,1,0:T(8,128)} custom-call(f32[160,128]{1,0:T(8,128)S(1)} %get-tuple-element.69.refs_0_, f32[160,128]{1,0:T(8,128)S(1)} %get-tuple-element.70.refs_1_, f32[160,128]{1,0:T(8,128)S(1)} %collective-permute-done.1.refs_2_, f32[160,128]{1,0:T(8,128)S(1)} %collective-permute-done.2.refs_3_), custom_call_target="tpu_custom_call" | custom-call | bytes 15000000 | tf_op jit(solution)/shard_map/grad_weights/pallas_call | solution.py:537
  58.9 1.6 %all-to-all-done.3.refs_0_ = f32[32,2,640]{2,1,0:T(2,128)S(1)} async-done(((f32[32,2,640]{2,1,0:T(2,128)}), f32[32,2,640]{2,1,0:T(2,128)S(1)}, u32[]{:S(2)}, u32[]{:S(2)}) %all-to-all-start.3) | async-done | bytes 163872 | tf_op jit(solution)/shard_map/all_to_all | solution.py:564
  60.5 1.2 %finish.1 = bf16[20,2,4,512]{3,2,1,0:T(4,128)(2,1)} custom-call(f32[32,2,640]{2,1,0:T(2,128)S(1)} %all-to-all-done.3.refs_0_, f32[160,512]{1,0:T(8,128)S(1)} %get-tuple-element.80.refs_1_, f32[128,512]{1,0:T(8,128)S(1)} %get-tuple-element.81.refs_2_), custom_call_target="tpu_custom_call" | custom-call | bytes 3000000 | tf_op jit(solution)/shard_map/finish/pallas_call | solution.py:537
Async XLA Ops:
  5.1 16.1 %collective-permute-start = (f32[4,20,24,128]{3,2,1,0:T(8,128)S(1)}, f32[4,20,24,128]{3,2,1,0:T(8,128)}, u32[]{:S(2)}, u32[]{:S(2)}) collective-permute-start(f32[4,20,24,128]{3,2,1,0:T(8,128)S(1)} %get-tuple-element.44.refs_1_), channel_id=1, source_target_pairs={{0,1},{1,0},{2,3},{3,2},{4,5},{5,4},{6,7},{7,6},{8,9},{9,8},{10,11... | collective-permute-start | bytes 2949128 | tf_op jit(solution)/shard_map/ppermute | solution.py:567
  5.7 15.5 %all-to-all-start = ((f32[32,2,640]{2,1,0:T(2,128)}), f32[32,2,640]{2,1,0:T(2,128)S(1)}, u32[]{:S(2)}, u32[]{:S(2)}) async-start(f32[32,2,640]{2,1,0:T(2,128)} %get-tuple-element.43), calls=%async_computation | async-start | bytes 327680 | tf_op jit(solution)/shard_map/all_to_all | solution.py:564
  49.3 11.2 %all-to-all-start.3 = ((f32[32,2,640]{2,1,0:T(2,128)}), f32[32,2,640]{2,1,0:T(2,128)S(1)}, u32[]{:S(2)}, u32[]{:S(2)}) async-start(f32[32,2,640]{2,1,0:T(2,128)} %get-tuple-element.68), calls=%async_computation.3 | async-start | bytes 327680 | tf_op jit(solution)/shard_map/all_to_all | solution.py:564
  51.9 2.4 %collective-permute-start.1 = (f32[160,128]{1,0:T(8,128)S(1)}, f32[160,128]{1,0:T(8,128)S(1)}, u32[]{:S(2)}, u32[]{:S(2)}) collective-permute-start(f32[160,128]{1,0:T(8,128)S(1)} %get-tuple-element.71), channel_id=1, source_target_pairs={{0,1},{1,0},{2,3},{3,2},{4,5},{5,4},{6,7},{7,6},{8,9},{9,8},{10,11... | collective-permute-start | bytes 245768 | tf_op jit(solution)/shard_map/ppermute | solution.py:567
  52.1 2.2 %collective-permute-start.2 = (f32[160,128]{1,0:T(8,128)S(1)}, f32[160,128]{1,0:T(8,128)S(1)}, u32[]{:S(2)}, u32[]{:S(2)}) collective-permute-start(f32[160,128]{1,0:T(8,128)S(1)} %get-tuple-element.72), channel_id=1, source_target_pairs={{0,1},{1,0},{2,3},{3,2},{4,5},{5,4},{6,7},{7,6},{8,9},{9,8},{10,11... | collective-permute-start | bytes 245768 | tf_op jit(solution)/shard_map/ppermute | solution.py:567

commit v14 on v13

--- a/solution.py
+++ b/solution.py
@@ -394,8 +394,8 @@
 
 def mix_forward(
     sizes, received, table, weight, other_weight, local, cotangent, inverse, forward,
-    spectra, other_spectra, out, local_out, cotangent_out, inverse_out, forward_out,
-    spread, swapped, flat, other_here, semaphores,
+    spectra, other_spectra, out, local_out, cotangent_out, inverse_out, forward_out, other_here,
+    spread, swapped, flat, semaphores,
 ):
     moves = (
         (other_weight, other_here), (local, local_out), (cotangent, cotangent_out), (inverse, inverse_out),
@@ -426,15 +426,11 @@
         copy.wait()
 
 
-def mix_back(sizes, received, table, weight, other_weight, back, other_back, out, spread, flat, other_here, semaphore):
-    copy = pltpu.make_async_copy(other_weight, other_here, semaphore.at[0])
-    copy.start()
+def mix_back(sizes, received, table, weight, other_weight, back, other_back, out, spread, flat):
     plane_spectra(sizes, received, table, (back, other_back), flat)
     spread[...] = jnp.zeros_like(spread)
     real = first_lanes(sizes.channels, sizes)
-    for at, (source, block) in enumerate(((back, weight), (other_back, other_here))):
-        if at:
-            copy.wait()
+    for at, (source, block) in enumerate(((back, weight), (other_back, other_weight))):
         for m in range(sizes.share):
             rows = source[mode_rows(m, sizes), :]
             if sizes.rows > sizes.channels:
@@ -610,13 +606,13 @@
     received, other_turned, turned, plane, local, cot_cells = lax.optimization_barrier(
         (received, other_turned, turned, plane, local, cot_cells)
     )
-    spectra, other_spectra, sent, local, cot_cells, inverse_here, forward_here = whole_call(
+    spectra, other_spectra, sent, local, cot_cells, inverse_here, forward_here, other_turned = whole_call(
         mix_forward, z, 1000,
         (
             shape_of(spectra_shape), shape_of(spectra_shape), payload, shape_of(cells_shape), shape_of(cells_shape),
-            shape_of(inverse_first.shape), shape_of(forward_back.shape, BF16),
+            shape_of(inverse_first.shape), shape_of(forward_back.shape, BF16), turned_shape,
         ),
-        [spread_scratch, spectra_scratch, flat_scratch, pltpu.VMEM(turned_shape.shape, F32), flags(5)],
+        [spread_scratch, spectra_scratch, flat_scratch, flags(5)],
         received, plane, turned, other_turned, local, cot_cells, inverse_first, forward_back,
         specs=[HELD] + [VMEM] * 2 + [HBM] * 5,
     )
@@ -627,8 +623,7 @@
     )
     back, other_back, sent = whole_call(
         mix_back, z, 1000, (shape_of(spectra_shape), shape_of(spectra_shape), payload),
-        [spread_scratch, flat_scratch, pltpu.VMEM(turned_shape.shape, F32), flags(1)],
-        exchange(sent), plane, turned, other_turned, specs=[VMEM] * 3 + [HBM],
+        [spread_scratch, flat_scratch], exchange(sent), plane, turned, other_turned,
     )
     sent, spectra, other_spectra, back, other_back, pre, signal = lax.optimization_barrier(
         (sent, spectra, other_spectra, back, other_back, pre, signal)

time: 62.1 us -> 60.8 us (0.979)
  Pallas kernels: 23.4 us -> 22.2 us
    pallas_call x8, Pallas kernels: 23.4 us -> 22.2 us  [whole_call(): pl.pallas_call(kernel, out_shape=out_shape, in_specs=specs or [VMEM] * le...]
where the time goes in v14:
time: 60.8 us; the launch traced here: 60.5 us
  Pallas kernels  22.2 us (37%)
  blocking collectives  21.4 us (35%)
  starting transfers between devices  10.6 us (17%)
  waiting for transfers between devices  5.55 us (9%)
  between operations  0.71 us (1%)
    pallas_call x8, Pallas kernels, whole_call(): pl.pallas_call(kernel, out_shape=out_shape, in_specs=specs or [VMEM] * le...  22.2 us
    all_to_all x2, blocking collectives, exchange(): lax.all_to_all(payload, ('gx', 'gy'), split_axis=0, concat_axis=0, tiled=...  21.4 us
    all_to_all x2, starting transfers between devices, exchange(): lax.all_to_all(payload, ('gx', 'gy'), split_axis=0, concat_axis=0, tiled=...  9.54 us
    all_to_all x2, waiting for transfers between devices, exchange(): lax.all_to_all(payload, ('gx', 'gy'), split_axis=0, concat_axis=0, tiled=...  5.55 us
  transfers between devices with their start and end apart: 5, of which 2 were waited for; matrix products, arithmetic and copies ran while one was open for 0% of the time, Pallas kernels for 18%

profile of v14, /device:TPU:0, one launch (start us, length us, event | category | flops | bytes accessed | tf_op | source)
XLA Modules:
  0.0 60.5 jit_solution(11339216909753789367)
XLA Ops:
  0.6 4.5 %depth_forward.1 = (f32[32,2,640]{2,1,0:T(2,128)}, f32[4,20,24,128]{3,2,1,0:T(8,128)S(1)}) custom-call(bf16[20,2,4,512]{3,2,1,0:T(4,128)(2,1)} %refs_3_.2, bf16[512,128]{1,0:T(8,128)(2,1)} %constant.10.clone.refs_1_, f32[16,20,4,16,20]{4,3,2,1,0:T(8,128)} %bitcast.6), custom_call_target="tpu_custom_call" | custom-call | bytes 4500000 | tf_op jit(solution)/shard_map/depth_forward/pallas_call | solution.py:533
  5.1 0.5 collective-permute-start
  5.7 7.0 %all-to-all-start = ((f32[32,2,640]{2,1,0:T(2,128)}), f32[32,2,640]{2,1,0:T(2,128)S(1)}, u32[]{:S(2)}, u32[]{:S(2)}) async-start(f32[32,2,640]{2,1,0:T(2,128)} %get-tuple-element.44), calls=%async_computation | async-start | bytes 327680 | tf_op jit(solution)/shard_map/all_to_all | solution.py:560
  12.6 4.6 %prepare.1 = (f32[4,20,24,128]{3,2,1,0:T(8,128)S(1)}, f32[256,512]{1,0:T(8,128)S(1)}, f32[160,512]{1,0:T(8,128)}, f32[160,512]{1,0:T(8,128)}) custom-call(f32[16,20,4,16,20]{4,3,2,1,0:T(8,128)} %bitcast.7, f32[4,20,24,128]{3,2,1,0:T(8,128)S(1)} %get-tuple-element.45.refs_1_, f32[4,256,256]{2,1,0:T(8,128)} %constant.14.clone.refs_2_, ...), custom_call_target="tpu_custom_call" | custom-call | bytes 300000 | tf_op jit(solution)/shard_map/prepare/pallas_call | solution.py:533
  17.2 4.0 %all-to-all-done.refs_0_ = f32[32,2,640]{2,1,0:T(2,128)S(1)} async-done(((f32[32,2,640]{2,1,0:T(2,128)}), f32[32,2,640]{2,1,0:T(2,128)S(1)}, u32[]{:S(2)}, u32[]{:S(2)}) %all-to-all-start) | async-done | bytes 163872 | tf_op jit(solution)/shard_map/all_to_all | solution.py:560
  21.2 0.0 collective-permute-done.refs_3_
  21.2 2.1 %mix_forward.1 = (f32[160,128]{1,0:T(8,128)S(1)}, f32[160,128]{1,0:T(8,128)S(1)}, f32[32,2,640]{2,1,0:T(2,128)S(1)}, f32[160,512]{1,0:T(8,128)S(1)}, f32[160,512...) custom-call(f32[32,2,640]{2,1,0:T(2,128)S(1)} %all-to-all-done.refs_0_, ...), custom_call_target="tpu_custom_call" | custom-call | bytes 3000000 | tf_op jit(solution)/shard_map/mix_forward/pallas_call | solution.py:533
  23.3 10.7 %all_to_all.20.refs_0_ = f32[32,2,640]{2,1,0:T(2,128)S(1)} all-to-all(f32[32,2,640]{2,1,0:T(2,128)S(1)} %get-tuple-element.56), channel_id=1, replica_groups=mesh['gx'=8,'gy'=4] {'gx','gy'}, dimensions={0} | all-to-all | bytes 327680 | tf_op jit(solution)/shard_map/all_to_all | solution.py:560
  34.0 1.2 %activate.1 = (f32[160,512]{1,0:T(8,128)S(1)}, bf16[160,512]{1,0:T(8,128)(2,1)S(1)}, f32[32,2,640]{2,1,0:T(2,128)S(1)}) custom-call(f32[32,2,640]{2,1,0:T(2,128)S(1)} %all_to_all.20.refs_0_, f32[160,512]{1,0:T(8,128)S(1)} %get-tuple-element.57.refs_1_, f32[160,512]{1,0:T(8,128)S(1)} %get-tuple-element.58.refs_2_, f32[128,512]{1,0:T(8,128)S(1)} %get-tuple-element.59.refs_3_, ...), custom_call_target="tpu_custom_call" | custom-call | bytes 6000000 | tf_op jit(solution)/shard_map/activate/pallas_call | solution.py:533
  35.2 10.7 %all_to_all.21.refs_0_ = f32[32,2,640]{2,1,0:T(2,128)S(1)} all-to-all(f32[32,2,640]{2,1,0:T(2,128)S(1)} %get-tuple-element.61), channel_id=1, replica_groups=mesh['gx'=8,'gy'=4] {'gx','gy'}, dimensions={0} | all-to-all | bytes 327680 | tf_op jit(solution)/shard_map/all_to_all | solution.py:560
  45.9 2.2 %mix_back.1 = (f32[160,128]{1,0:T(8,128)S(1)}, f32[160,128]{1,0:T(8,128)S(1)}, f32[32,2,640]{2,1,0:T(2,128)}) custom-call(f32[32,2,640]{2,1,0:T(2,128)S(1)} %all_to_all.21.refs_0_, f32[256,512]{1,0:T(8,128)S(1)} %get-tuple-element.51.refs_1_, f32[4,20,24,128]{3,2,1,0:T(8,128)S(1)} %get-tuple-element.52.refs_2_, f32[4,20,24,128]{3,2,1,0:T(8,128)S(1)} %get-tuple-element.62.refs_3_), custom_call_target="tpu_custom_call" | custom-call | bytes 3000000 | tf_op jit(solution)/shard_map/mix_back/pallas_call | solution.py:533
  48.1 2.6 %all-to-all-start.3 = ((f32[32,2,640]{2,1,0:T(2,128)}), f32[32,2,640]{2,1,0:T(2,128)S(1)}, u32[]{:S(2)}, u32[]{:S(2)}) async-start(f32[32,2,640]{2,1,0:T(2,128)} %get-tuple-element.70), calls=%async_computation.3 | async-start | bytes 327680 | tf_op jit(solution)/shard_map/all_to_all | solution.py:560
  50.6 0.2 collective-permute-start.1
  50.8 0.4 collective-permute-start.2
  51.2 1.8 %emit.1 = (bf16[20,2,4,512]{3,2,1,0:T(4,128)(2,1)}, f32[160,512]{1,0:T(8,128)S(1)}, f32[128,512]{1,0:T(8,128)S(1)}) custom-call(f32[160,512]{1,0:T(8,128)S(1)} %get-tuple-element.75.refs_0_, bf16[160,512]{1,0:T(8,128)(2,1)S(1)} %get-tuple-element.76.refs_1_, bf16[20,20]{1,0:T(8,128)(2,1)} %refs_2_.2, f32[128,512]{1,0:T(8,128)} %constant.12.clone.refs_3_), custom_call_target="tpu_custom_call" | custom-call | bytes 4500000 | tf_op jit(solution)/shard_map/emit/pallas_call | solution.py:533
  53.0 0.0 collective-permute-done.1.refs_2_
  53.0 0.0 collective-permute-done.2.refs_3_
  53.0 4.6 %grad_weights.1 = f32[16,20,4,16,20]{4,3,2,1,0:T(8,128)} custom-call(f32[160,128]{1,0:T(8,128)S(1)} %get-tuple-element.71.refs_0_, f32[160,128]{1,0:T(8,128)S(1)} %get-tuple-element.72.refs_1_, f32[160,128]{1,0:T(8,128)S(1)} %collective-permute-done.1.refs_2_, f32[160,128]{1,0:T(8,128)S(1)} %collective-permute-done.2.refs_3_), custom_call_target="tpu_custom_call" | custom-call | bytes 15000000 | tf_op jit(solution)/shard_map/grad_weights/pallas_call | solution.py:533
  57.6 1.6 %all-to-all-done.3.refs_0_ = f32[32,2,640]{2,1,0:T(2,128)S(1)} async-done(((f32[32,2,640]{2,1,0:T(2,128)}), f32[32,2,640]{2,1,0:T(2,128)S(1)}, u32[]{:S(2)}, u32[]{:S(2)}) %all-to-all-start.3) | async-done | bytes 163872 | tf_op jit(solution)/shard_map/all_to_all | solution.py:560
  59.2 1.2 %finish.1 = bf16[20,2,4,512]{3,2,1,0:T(4,128)(2,1)} custom-call(f32[32,2,640]{2,1,0:T(2,128)S(1)} %all-to-all-done.3.refs_0_, f32[160,512]{1,0:T(8,128)S(1)} %get-tuple-element.82.refs_1_, f32[128,512]{1,0:T(8,128)S(1)} %get-tuple-element.83.refs_2_), custom_call_target="tpu_custom_call" | custom-call | bytes 3000000 | tf_op jit(solution)/shard_map/finish/pallas_call | solution.py:533
Async XLA Ops:
  5.1 16.1 %collective-permute-start = (f32[4,20,24,128]{3,2,1,0:T(8,128)S(1)}, f32[4,20,24,128]{3,2,1,0:T(8,128)}, u32[]{:S(2)}, u32[]{:S(2)}) collective-permute-start(f32[4,20,24,128]{3,2,1,0:T(8,128)S(1)} %get-tuple-element.45.refs_1_), channel_id=1, source_target_pairs={{0,1},{1,0},{2,3},{3,2},{4,5},{5,4},{6,7},{7,6},{8,9},{9,8},{10,11... | collective-permute-start | bytes 2949128 | tf_op jit(solution)/shard_map/ppermute | solution.py:563
  5.7 15.5 %all-to-all-start = ((f32[32,2,640]{2,1,0:T(2,128)}), f32[32,2,640]{2,1,0:T(2,128)S(1)}, u32[]{:S(2)}, u32[]{:S(2)}) async-start(f32[32,2,640]{2,1,0:T(2,128)} %get-tuple-element.44), calls=%async_computation | async-start | bytes 327680 | tf_op jit(solution)/shard_map/all_to_all | solution.py:560
  48.1 11.2 %all-to-all-start.3 = ((f32[32,2,640]{2,1,0:T(2,128)}), f32[32,2,640]{2,1,0:T(2,128)S(1)}, u32[]{:S(2)}, u32[]{:S(2)}) async-start(f32[32,2,640]{2,1,0:T(2,128)} %get-tuple-element.70), calls=%async_computation.3 | async-start | bytes 327680 | tf_op jit(solution)/shard_map/all_to_all | solution.py:560
  50.6 2.4 %collective-permute-start.1 = (f32[160,128]{1,0:T(8,128)S(1)}, f32[160,128]{1,0:T(8,128)S(1)}, u32[]{:S(2)}, u32[]{:S(2)}) collective-permute-start(f32[160,128]{1,0:T(8,128)S(1)} %get-tuple-element.73), channel_id=1, source_target_pairs={{0,1},{1,0},{2,3},{3,2},{4,5},{5,4},{6,7},{7,6},{8,9},{9,8},{10,11... | collective-permute-start | bytes 245768 | tf_op jit(solution)/shard_map/ppermute | solution.py:563
  50.8 2.2 %collective-permute-start.2 = (f32[160,128]{1,0:T(8,128)S(1)}, f32[160,128]{1,0:T(8,128)S(1)}, u32[]{:S(2)}, u32[]{:S(2)}) collective-permute-start(f32[160,128]{1,0:T(8,128)S(1)} %get-tuple-element.74), channel_id=1, source_target_pairs={{0,1},{1,0},{2,3},{3,2},{4,5},{5,4},{6,7},{7,6},{8,9},{9,8},{10,11... | collective-permute-start | bytes 245768 | tf_op jit(solution)/shard_map/ppermute | solution.py:563

commit v15 on v14

--- a/solution.py
+++ b/solution.py
@@ -220,10 +220,10 @@
     ]
     for copy in few:
         copy.start()
-    copies = start_weights(sizes, source, 1 - core_of(), here, weight_semaphores)
     clear_weights(sizes, target)
     for copy in few:
         copy.wait()
+    copies = start_weights(sizes, source, 1 - core_of(), here, weight_semaphores)
     values = gather_cells(field_here, cells, sizes).astype(BF16)
     send_modes(dot(values, table_here[...]), out_here, sizes)
     copy = pltpu.make_async_copy(out_here, out, semaphores.at[2])
@@ -305,13 +305,10 @@
 ):
     del after
     place = lax.axis_index("gy")
-    lanes = 2 * sizes.half
+    lanes = 4 * sizes.half
     moves = [(field, field_here), (cotangent, cot_here), (weight, weight_here), (bias, bias_here)]
-    for s in range(2):
-        for at, owner in enumerate((place, place + 1 - 2 * core_of())):
-            moves.append(
-                (tables.at[owner, :, pl.ds(s * lanes, lanes)], table.at[:, pl.ds((2 * s + at) * lanes, lanes)])
-            )
+    for at, owner in enumerate((place, place + 1 - 2 * core_of())):
+        moves.append((tables.at[owner], table.at[:, pl.ds(at * lanes, lanes)]))
     few = [pltpu.make_async_copy(*move, small.at[at]) for at, move in enumerate(moves)]
     copies = start_weights(sizes, source, core_of(), here, semaphores)
     for copy in few:
@@ -335,7 +332,7 @@
         copy.wait()
 
 
-def plane_spectra(sizes, received, table, targets, flat):
+def spread_received(sizes, received, flat):
     count = sizes.devices * sizes.pair
     for at in range(sizes.devices):
         for piece in range(sizes.pieces):
@@ -350,16 +347,25 @@
             rows = slice(piece * count, (piece + 1) * count)
             shift = sizes.rest_width - piece * sizes.rest_lanes
             flat[rows, sizes.main_lanes :] = pltpu.roll(flat[rows, sizes.main_lanes :], shift, 1)
-    rows, lanes = targets[0].shape
-    both = fine_dot(flat[...].T[:rows], table[...])
-    total = both[:, : 2 * lanes] + pltpu.roll(both[:, 2 * lanes :], rows - sizes.share, 0)
-    for at, target in enumerate(targets):
-        target[...] = total[:, at * lanes : (at + 1) * lanes]
-
-
-def plane_cells(sizes, spread, table, out):
-    modes = jnp.concatenate([spread[at] for at in range(4)], 1)
-    cells = fine_dot(table[...], modes, ((1,), (1,)))
+    return flat[...].T[: sizes.channels * sizes.modes]
+
+
+def owner_lanes(at, sizes):
+    return slice(at * 4 * sizes.half, (at + 1) * 4 * sizes.half)
+
+
+def plane_spectra(sizes, values, table, at, target):
+    both = fine_dot(values, table[:, owner_lanes(at, sizes)])
+    rows, lanes = target.shape
+    target[...] = both[:, :lanes] + pltpu.roll(both[:, lanes:], rows - sizes.share, 0)
+
+
+def plane_cells(sizes, spread, table, at):
+    modes = jnp.concatenate([spread[2 * at + s] for s in range(2)], 1)
+    return fine_dot(table[:, owner_lanes(at, sizes)], modes, ((1,), (1,)))
+
+
+def send_cells(sizes, cells, out):
     count = sizes.devices * sizes.pair
     if sizes.rest:
         last = side_by_side(cells[:, sizes.main_lanes :], count, sizes)
@@ -385,7 +391,7 @@
 
 def put_mixed(spread, at, mode, values, sizes):
     for s in range(2):
-        spread[2 * s + at, mode_rows(s * sizes.share + mode, sizes), :] = values
+        spread[2 * at + s, mode_rows(s * sizes.share + mode, sizes), :] = values
 
 
 def first_lanes(rows, sizes):
@@ -404,11 +410,14 @@
     copies = [pltpu.make_async_copy(*move, semaphores.at[at]) for at, move in enumerate(moves)]
     for copy in copies:
         copy.start()
-    plane_spectra(sizes, received, table, (spectra, other_spectra), flat)
     spread[...] = jnp.zeros_like(spread)
+    values = spread_received(sizes, received, flat)
     real = first_lanes(sizes.rows, sizes)
+    cells = None
     for at, (rows, block) in enumerate(((spectra, weight), (other_spectra, other_here))):
+        plane_spectra(sizes, values, table, at, rows)
         if at:
+            cells = plane_cells(sizes, spread, table, 0)
             copies[0].wait()
         swapped[...] = swap_parts(rows[...], sizes)
         for m in range(sizes.share):
@@ -421,16 +430,18 @@
             real_part = straight - swap_parts(straight, sizes)
             imag_part = crossed + swap_parts(crossed, sizes)
             put_mixed(spread, at, m, jnp.where(real, real_part, imag_part)[: sizes.channels], sizes)
-    plane_cells(sizes, spread, table, out)
+    send_cells(sizes, cells + plane_cells(sizes, spread, table, 1), out)
     for copy in copies[1:]:
         copy.wait()
 
 
 def mix_back(sizes, received, table, weight, other_weight, back, other_back, out, spread, flat):
-    plane_spectra(sizes, received, table, (back, other_back), flat)
     spread[...] = jnp.zeros_like(spread)
+    values = spread_received(sizes, received, flat)
     real = first_lanes(sizes.channels, sizes)
+    cells = 0.0
     for at, (source, block) in enumerate(((back, weight), (other_back, other_weight))):
+        plane_spectra(sizes, values, table, at, source)
         for m in range(sizes.share):
             rows = source[mode_rows(m, sizes), :]
             if sizes.rows > sizes.channels:
@@ -445,7 +456,8 @@
             real_part = straight + swap_parts(straight, sizes)
             imag_part = swap_parts(crossed, sizes) - crossed
             put_mixed(spread, at, m, jnp.where(real, real_part, imag_part), sizes)
-    plane_cells(sizes, spread, table, out)
+        cells = cells + plane_cells(sizes, spread, table, at)
+    send_cells(sizes, cells, out)
 
 
 def grad_weights(
@@ -598,7 +610,7 @@
         (turned_shape, shape_of((z.devices * z.cells, 8 * z.half)), pltpu.HBM(cells_shape, F32), pltpu.HBM(cells_shape, F32)),
         [
             half_scratch, cells_scratch, field_scratch, field_scratch, cells_scratch, weight_here,
-            pltpu.VMEM(channel_bias.shape, F32), cells_scratch, flags(z.modes), flags(8),
+            pltpu.VMEM(channel_bias.shape, F32), cells_scratch, flags(z.modes), flags(6),
         ],
         weights, turned_away, jnp.asarray(plane_tables(z)), field, cotangent, pointwise_weight, channel_bias,
         specs=[HBM, ANYWHERE] + [HBM] * 5, out_specs=(VMEM, VMEM, HBM, HBM),

time: 60.8 us -> 60.9 us (level)
  no operation moved by 1% of the time
where the time goes in v15:
time: 60.9 us; the launch traced here: 60.6 us
  Pallas kernels  22.2 us (36%)
  blocking collectives  21.4 us (35%)
  starting transfers between devices  10.6 us (17%)
  waiting for transfers between devices  5.62 us (9%)
  between operations  0.71 us (1%)
    pallas_call x8, Pallas kernels, whole_call(): pl.pallas_call(kernel, out_shape=out_shape, in_specs=specs or [VMEM] * le...  22.2 us
    all_to_all x2, blocking collectives, exchange(): lax.all_to_all(payload, ('gx', 'gy'), split_axis=0, concat_axis=0, tiled=...  21.4 us
    all_to_all x2, starting transfers between devices, exchange(): lax.all_to_all(payload, ('gx', 'gy'), split_axis=0, concat_axis=0, tiled=...  9.54 us
    all_to_all x2, waiting for transfers between devices, exchange(): lax.all_to_all(payload, ('gx', 'gy'), split_axis=0, concat_axis=0, tiled=...  5.61 us
  transfers between devices with their start and end apart: 5, of which 2 were waited for; matrix products, arithmetic and copies ran while one was open for 0% of the time, Pallas kernels for 18%

profile of v15, /device:TPU:0, one launch (start us, length us, event | category | flops | bytes accessed | tf_op | source)
XLA Modules:
  0.0 60.6 jit_solution(7188815629314726870)
XLA Ops:
  0.6 4.3 %depth_forward.1 = (f32[32,2,640]{2,1,0:T(2,128)}, f32[4,20,24,128]{3,2,1,0:T(8,128)S(1)}) custom-call(bf16[20,2,4,512]{3,2,1,0:T(4,128)(2,1)} %refs_3_.2, bf16[512,128]{1,0:T(8,128)(2,1)} %constant.10.clone.refs_1_, f32[16,20,4,16,20]{4,3,2,1,0:T(8,128)} %bitcast.6), custom_call_target="tpu_custom_call" | custom-call | bytes 4500000 | tf_op jit(solution)/shard_map/depth_forward/pallas_call | solution.py:545
  4.9 0.5 collective-permute-start
  5.4 7.0 %all-to-all-start = ((f32[32,2,640]{2,1,0:T(2,128)}), f32[32,2,640]{2,1,0:T(2,128)S(1)}, u32[]{:S(2)}, u32[]{:S(2)}) async-start(f32[32,2,640]{2,1,0:T(2,128)} %get-tuple-element.44), calls=%async_computation | async-start | bytes 327680 | tf_op jit(solution)/shard_map/all_to_all | solution.py:572
  12.4 4.5 %prepare.1 = (f32[4,20,24,128]{3,2,1,0:T(8,128)S(1)}, f32[256,512]{1,0:T(8,128)S(1)}, f32[160,512]{1,0:T(8,128)}, f32[160,512]{1,0:T(8,128)}) custom-call(f32[16,20,4,16,20]{4,3,2,1,0:T(8,128)} %bitcast.7, f32[4,20,24,128]{3,2,1,0:T(8,128)S(1)} %get-tuple-element.45.refs_1_, f32[4,256,256]{2,1,0:T(8,128)} %constant.14.clone.refs_2_, ...), custom_call_target="tpu_custom_call" | custom-call | bytes 300000 | tf_op jit(solution)/shard_map/prepare/pallas_call | solution.py:545
  17.0 4.0 %all-to-all-done.refs_0_ = f32[32,2,640]{2,1,0:T(2,128)S(1)} async-done(((f32[32,2,640]{2,1,0:T(2,128)}), f32[32,2,640]{2,1,0:T(2,128)S(1)}, u32[]{:S(2)}, u32[]{:S(2)}) %all-to-all-start) | async-done | bytes 163872 | tf_op jit(solution)/shard_map/all_to_all | solution.py:572
  21.0 0.0 collective-permute-done.refs_3_
  21.0 2.1 %mix_forward.1 = (f32[160,128]{1,0:T(8,128)S(1)}, f32[160,128]{1,0:T(8,128)S(1)}, f32[32,2,640]{2,1,0:T(2,128)S(1)}, f32[160,512]{1,0:T(8,128)S(1)}, f32[160,512...) custom-call(f32[32,2,640]{2,1,0:T(2,128)S(1)} %all-to-all-done.refs_0_, ...), custom_call_target="tpu_custom_call" | custom-call | bytes 3000000 | tf_op jit(solution)/shard_map/mix_forward/pallas_call | solution.py:545
  23.1 10.7 %all_to_all.20.refs_0_ = f32[32,2,640]{2,1,0:T(2,128)S(1)} all-to-all(f32[32,2,640]{2,1,0:T(2,128)S(1)} %get-tuple-element.56), channel_id=1, replica_groups=mesh['gx'=8,'gy'=4] {'gx','gy'}, dimensions={0} | all-to-all | bytes 327680 | tf_op jit(solution)/shard_map/all_to_all | solution.py:572
  33.8 1.2 %activate.1 = (f32[160,512]{1,0:T(8,128)S(1)}, bf16[160,512]{1,0:T(8,128)(2,1)S(1)}, f32[32,2,640]{2,1,0:T(2,128)S(1)}) custom-call(f32[32,2,640]{2,1,0:T(2,128)S(1)} %all_to_all.20.refs_0_, f32[160,512]{1,0:T(8,128)S(1)} %get-tuple-element.57.refs_1_, f32[160,512]{1,0:T(8,128)S(1)} %get-tuple-element.58.refs_2_, f32[128,512]{1,0:T(8,128)S(1)} %get-tuple-element.59.refs_3_, ...), custom_call_target="tpu_custom_call" | custom-call | bytes 6000000 | tf_op jit(solution)/shard_map/activate/pallas_call | solution.py:545
  34.9 10.7 %all_to_all.21.refs_0_ = f32[32,2,640]{2,1,0:T(2,128)S(1)} all-to-all(f32[32,2,640]{2,1,0:T(2,128)S(1)} %get-tuple-element.61), channel_id=1, replica_groups=mesh['gx'=8,'gy'=4] {'gx','gy'}, dimensions={0} | all-to-all | bytes 327680 | tf_op jit(solution)/shard_map/all_to_all | solution.py:572
  45.6 2.5 %mix_back.1 = (f32[160,128]{1,0:T(8,128)S(1)}, f32[160,128]{1,0:T(8,128)S(1)}, f32[32,2,640]{2,1,0:T(2,128)}) custom-call(f32[32,2,640]{2,1,0:T(2,128)S(1)} %all_to_all.21.refs_0_, f32[256,512]{1,0:T(8,128)S(1)} %get-tuple-element.51.refs_1_, f32[4,20,24,128]{3,2,1,0:T(8,128)S(1)} %get-tuple-element.52.refs_2_, f32[4,20,24,128]{3,2,1,0:T(8,128)S(1)} %get-tuple-element.62.refs_3_), custom_call_target="tpu_custom_call" | custom-call | bytes 3000000 | tf_op jit(solution)/shard_map/mix_back/pallas_call | solution.py:545
  48.2 2.6 %all-to-all-start.3 = ((f32[32,2,640]{2,1,0:T(2,128)}), f32[32,2,640]{2,1,0:T(2,128)S(1)}, u32[]{:S(2)}, u32[]{:S(2)}) async-start(f32[32,2,640]{2,1,0:T(2,128)} %get-tuple-element.70), calls=%async_computation.3 | async-start | bytes 327680 | tf_op jit(solution)/shard_map/all_to_all | solution.py:572
  50.8 0.2 collective-permute-start.1
  51.0 0.4 collective-permute-start.2
  51.3 1.8 %emit.1 = (bf16[20,2,4,512]{3,2,1,0:T(4,128)(2,1)}, f32[160,512]{1,0:T(8,128)S(1)}, f32[128,512]{1,0:T(8,128)S(1)}) custom-call(f32[160,512]{1,0:T(8,128)S(1)} %get-tuple-element.75.refs_0_, bf16[160,512]{1,0:T(8,128)(2,1)S(1)} %get-tuple-element.76.refs_1_, bf16[20,20]{1,0:T(8,128)(2,1)} %refs_2_.2, f32[128,512]{1,0:T(8,128)} %constant.12.clone.refs_3_), custom_call_target="tpu_custom_call" | custom-call | bytes 4500000 | tf_op jit(solution)/shard_map/emit/pallas_call | solution.py:545
  53.1 0.0 collective-permute-done.1.refs_2_
  53.2 0.0 collective-permute-done.2.refs_3_
  53.2 4.6 %grad_weights.1 = f32[16,20,4,16,20]{4,3,2,1,0:T(8,128)} custom-call(f32[160,128]{1,0:T(8,128)S(1)} %get-tuple-element.71.refs_0_, f32[160,128]{1,0:T(8,128)S(1)} %get-tuple-element.72.refs_1_, f32[160,128]{1,0:T(8,128)S(1)} %collective-permute-done.1.refs_2_, f32[160,128]{1,0:T(8,128)S(1)} %collective-permute-done.2.refs_3_), custom_call_target="tpu_custom_call" | custom-call | bytes 15000000 | tf_op jit(solution)/shard_map/grad_weights/pallas_call | solution.py:545
  57.8 1.6 %all-to-all-done.3.refs_0_ = f32[32,2,640]{2,1,0:T(2,128)S(1)} async-done(((f32[32,2,640]{2,1,0:T(2,128)}), f32[32,2,640]{2,1,0:T(2,128)S(1)}, u32[]{:S(2)}, u32[]{:S(2)}) %all-to-all-start.3) | async-done | bytes 163872 | tf_op jit(solution)/shard_map/all_to_all | solution.py:572
  59.3 1.2 %finish.1 = bf16[20,2,4,512]{3,2,1,0:T(4,128)(2,1)} custom-call(f32[32,2,640]{2,1,0:T(2,128)S(1)} %all-to-all-done.3.refs_0_, f32[160,512]{1,0:T(8,128)S(1)} %get-tuple-element.82.refs_1_, f32[128,512]{1,0:T(8,128)S(1)} %get-tuple-element.83.refs_2_), custom_call_target="tpu_custom_call" | custom-call | bytes 3000000 | tf_op jit(solution)/shard_map/finish/pallas_call | solution.py:545
Async XLA Ops:
  4.9 16.1 %collective-permute-start = (f32[4,20,24,128]{3,2,1,0:T(8,128)S(1)}, f32[4,20,24,128]{3,2,1,0:T(8,128)}, u32[]{:S(2)}, u32[]{:S(2)}) collective-permute-start(f32[4,20,24,128]{3,2,1,0:T(8,128)S(1)} %get-tuple-element.45.refs_1_), channel_id=1, source_target_pairs={{0,1},{1,0},{2,3},{3,2},{4,5},{5,4},{6,7},{7,6},{8,9},{9,8},{10,11... | collective-permute-start | bytes 2949128 | tf_op jit(solution)/shard_map/ppermute | solution.py:575
  5.4 15.5 %all-to-all-start = ((f32[32,2,640]{2,1,0:T(2,128)}), f32[32,2,640]{2,1,0:T(2,128)S(1)}, u32[]{:S(2)}, u32[]{:S(2)}) async-start(f32[32,2,640]{2,1,0:T(2,128)} %get-tuple-element.44), calls=%async_computation | async-start | bytes 327680 | tf_op jit(solution)/shard_map/all_to_all | solution.py:572
  48.2 11.2 %all-to-all-start.3 = ((f32[32,2,640]{2,1,0:T(2,128)}), f32[32,2,640]{2,1,0:T(2,128)S(1)}, u32[]{:S(2)}, u32[]{:S(2)}) async-start(f32[32,2,640]{2,1,0:T(2,128)} %get-tuple-element.70), calls=%async_computation.3 | async-start | bytes 327680 | tf_op jit(solution)/shard_map/all_to_all | solution.py:572
  50.8 2.4 %collective-permute-start.1 = (f32[160,128]{1,0:T(8,128)S(1)}, f32[160,128]{1,0:T(8,128)S(1)}, u32[]{:S(2)}, u32[]{:S(2)}) collective-permute-start(f32[160,128]{1,0:T(8,128)S(1)} %get-tuple-element.73), channel_id=1, source_target_pairs={{0,1},{1,0},{2,3},{3,2},{4,5},{5,4},{6,7},{7,6},{8,9},{9,8},{10,11... | collective-permute-start | bytes 245768 | tf_op jit(solution)/shard_map/ppermute | solution.py:575
  51.0 2.2 %collective-permute-start.2 = (f32[160,128]{1,0:T(8,128)S(1)}, f32[160,128]{1,0:T(8,128)S(1)}, u32[]{:S(2)}, u32[]{:S(2)}) collective-permute-start(f32[160,128]{1,0:T(8,128)S(1)} %get-tuple-element.74), channel_id=1, source_target_pairs={{0,1},{1,0},{2,3},{3,2},{4,5},{5,4},{6,7},{7,6},{8,9},{9,8},{10,11... | collective-permute-start | bytes 245768 | tf_op jit(solution)/shard_map/ppermute | solution.py:575

commit v16 on v12

--- a/solution.py
+++ b/solution.py
@@ -220,10 +220,10 @@
     ]
     for copy in few:
         copy.start()
-    copies = start_weights(sizes, source, 1 - core_of(), here, weight_semaphores)
     clear_weights(sizes, target)
     for copy in few:
         copy.wait()
+    copies = start_weights(sizes, source, 1 - core_of(), here, weight_semaphores)
     values = gather_cells(field_here, cells, sizes).astype(BF16)
     send_modes(dot(values, table_here[...]), out_here, sizes)
     copy = pltpu.make_async_copy(out_here, out, semaphores.at[2])
@@ -335,6 +335,13 @@
         copy.wait()
 
 
+def fetch_weights(sizes, source, after, target, semaphore):
+    del after
+    copy = pltpu.make_async_copy(source, target, semaphore.at[0])
+    copy.start()
+    copy.wait()
+
+
 def plane_spectra(sizes, received, table, targets, flat):
     count = sizes.devices * sizes.pair
     for at in range(sizes.devices):
@@ -590,13 +597,16 @@
     other_turned = other_core(turned_away)
     turned, plane, local, cot_cells = whole_call(
         prepare, z, 100,
-        (turned_shape, shape_of((z.devices * z.cells, 8 * z.half)), shape_of(cells_shape), shape_of(cells_shape)),
+        (turned_shape, shape_of((z.devices * z.cells, 8 * z.half)), pltpu.HBM(cells_shape, F32), pltpu.HBM(cells_shape, F32)),
         [
             half_scratch, cells_scratch, field_scratch, field_scratch, cells_scratch, weight_here,
             pltpu.VMEM(channel_bias.shape, F32), cells_scratch, flags(z.modes), flags(8),
         ],
         weights, turned_away, jnp.asarray(plane_tables(z)), field, cotangent, pointwise_weight, channel_bias,
         specs=[HBM, ANYWHERE] + [HBM] * 5, out_specs=(VMEM, VMEM, HBM, HBM),
+    )
+    other_turned = whole_call(
+        fetch_weights, z, 100, turned_shape, [flags(1)], other_turned, turned, specs=[HBM, ANYWHERE]
     )
     received, other_turned, turned, plane, local, cot_cells = lax.optimization_barrier(
         (received, other_turned, turned, plane, local, cot_cells)

time: 61.9 us -> 61.1 us (0.987)
  local copies, waits for them, and re-layouts: 1.44 us -> 0 us
  Pallas kernels: 22.2 us -> 22.9 us
    unnamed x4 -> x0, local copies, waits for them, and re-layouts: 1.44 us -> none
    pallas_call x8 -> x9, Pallas kernels: 22.2 us -> 22.9 us  [whole_call(): pl.pallas_call(kernel, out_shape=out_shape, in_specs=specs or [VMEM] * le...]
  transfers between devices with their start and end apart: 5 -> 5, of which waited for: 2 -> 2; matrix products, arithmetic and copies ran while one was open for 0% -> 0% of each run, Pallas kernels for 17% -> 20%
where the time goes in v16:
time: 61.1 us; the launch traced here: 60.7 us
  Pallas kernels  22.9 us (37%)
  blocking collectives  22.2 us (36%)
  starting transfers between devices  10.6 us (17%)
  waiting for transfers between devices  4.32 us (7%)
  between operations  0.73 us (1%)
    pallas_call x9, Pallas kernels, whole_call(): pl.pallas_call(kernel, out_shape=out_shape, in_specs=specs or [VMEM] * le...  22.9 us
    all_to_all x2, blocking collectives, exchange(): lax.all_to_all(payload, ('gx', 'gy'), split_axis=0, concat_axis=0, tiled=...  22.2 us
    all_to_all x2, starting transfers between devices, exchange(): lax.all_to_all(payload, ('gx', 'gy'), split_axis=0, concat_axis=0, tiled=...  9.54 us
    all_to_all x2, waiting for transfers between devices, exchange(): lax.all_to_all(payload, ('gx', 'gy'), split_axis=0, concat_axis=0, tiled=...  4.32 us
  transfers between devices with their start and end apart: 5, of which 2 were waited for; matrix products, arithmetic and copies ran while one was open for 0% of the time, Pallas kernels for 20%

profile of v16, /device:TPU:0, one launch (start us, length us, event | category | flops | bytes accessed | tf_op | source)
XLA Modules:
  0.0 60.7 jit_solution(10881089961054480209)
XLA Ops:
  0.6 4.3 %depth_forward.1 = (f32[32,2,640]{2,1,0:T(2,128)}, f32[4,20,24,128]{3,2,1,0:T(8,128)S(1)}) custom-call(bf16[20,2,4,512]{3,2,1,0:T(4,128)(2,1)} %refs_3_.2, bf16[512,128]{1,0:T(8,128)(2,1)} %constant.10.clone.refs_1_, f32[16,20,4,16,20]{4,3,2,1,0:T(8,128)} %bitcast.6), custom_call_target="tpu_custom_call" | custom-call | bytes 4500000 | tf_op jit(solution)/shard_map/depth_forward/pallas_call | solution.py:535
  4.9 0.5 collective-permute-start
  5.4 7.0 %all-to-all-start = ((f32[32,2,640]{2,1,0:T(2,128)}), f32[32,2,640]{2,1,0:T(2,128)S(1)}, u32[]{:S(2)}, u32[]{:S(2)}) async-start(f32[32,2,640]{2,1,0:T(2,128)} %get-tuple-element.43), calls=%async_computation | async-start | bytes 327680 | tf_op jit(solution)/shard_map/all_to_all | solution.py:562
  12.4 4.6 %prepare.1 = (f32[4,20,24,128]{3,2,1,0:T(8,128)S(1)}, f32[256,512]{1,0:T(8,128)S(1)}, f32[160,512]{1,0:T(8,128)}, f32[160,512]{1,0:T(8,128)}) custom-call(f32[16,20,4,16,20]{4,3,2,1,0:T(8,128)} %bitcast.7, f32[4,20,24,128]{3,2,1,0:T(8,128)S(1)} %get-tuple-element.44.refs_1_, f32[4,256,256]{2,1,0:T(8,128)} %constant.14.clone.refs_2_, ...), custom_call_target="tpu_custom_call" | custom-call | bytes 300000 | tf_op jit(solution)/shard_map/prepare/pallas_call | solution.py:535
  17.0 0.0 collective-permute-done.refs_0_
  17.0 1.2 %fetch_weights.1.refs_3_ = f32[4,20,24,128]{3,2,1,0:T(8,128)S(1)} custom-call(f32[4,20,24,128]{3,2,1,0:T(8,128)} %collective-permute-done.refs_0_, f32[4,20,24,128]{3,2,1,0:T(8,128)S(1)} %get-tuple-element.51.refs_1_.refs_2_), custom_call_target="tpu_custom_call" | custom-call | bytes 300000 | tf_op jit(solution)/shard_map/fetch_weights/pallas_call | solution.py:535
  18.3 2.7 %all-to-all-done.refs_0_ = f32[32,2,640]{2,1,0:T(2,128)S(1)} async-done(((f32[32,2,640]{2,1,0:T(2,128)}), f32[32,2,640]{2,1,0:T(2,128)S(1)}, u32[]{:S(2)}, u32[]{:S(2)}) %all-to-all-start) | async-done | bytes 163872 | tf_op jit(solution)/shard_map/all_to_all | solution.py:562
  21.0 1.8 %mix_forward.1 = (f32[160,128]{1,0:T(8,128)S(1)}, f32[160,128]{1,0:T(8,128)S(1)}, f32[32,2,640]{2,1,0:T(2,128)S(1)}, f32[160,512]{1,0:T(8,128)S(1)}, f32[160,512...) custom-call(f32[32,2,640]{2,1,0:T(2,128)S(1)} %all-to-all-done.refs_0_, ...), custom_call_target="tpu_custom_call" | custom-call | bytes 3000000 | tf_op jit(solution)/shard_map/mix_forward/pallas_call | solution.py:535
  22.8 11.5 %all_to_all.20.refs_0_ = f32[32,2,640]{2,1,0:T(2,128)S(1)} all-to-all(f32[32,2,640]{2,1,0:T(2,128)S(1)} %get-tuple-element.55), channel_id=1, replica_groups=mesh['gx'=8,'gy'=4] {'gx','gy'}, dimensions={0} | all-to-all | bytes 327680 | tf_op jit(solution)/shard_map/all_to_all | solution.py:562
  34.3 1.2 %activate.1 = (f32[160,512]{1,0:T(8,128)S(1)}, bf16[160,512]{1,0:T(8,128)(2,1)S(1)}, f32[32,2,640]{2,1,0:T(2,128)S(1)}) custom-call(f32[32,2,640]{2,1,0:T(2,128)S(1)} %all_to_all.20.refs_0_, f32[160,512]{1,0:T(8,128)S(1)} %get-tuple-element.56.refs_1_, f32[160,512]{1,0:T(8,128)S(1)} %get-tuple-element.57.refs_2_, f32[128,512]{1,0:T(8,128)S(1)} %get-tuple-element.58.refs_3_, ...), custom_call_target="tpu_custom_call" | custom-call | bytes 6000000 | tf_op jit(solution)/shard_map/activate/pallas_call | solution.py:535
  35.5 10.7 %all_to_all.21.refs_0_ = f32[32,2,640]{2,1,0:T(2,128)S(1)} all-to-all(f32[32,2,640]{2,1,0:T(2,128)S(1)} %get-tuple-element.60), channel_id=1, replica_groups=mesh['gx'=8,'gy'=4] {'gx','gy'}, dimensions={0} | all-to-all | bytes 327680 | tf_op jit(solution)/shard_map/all_to_all | solution.py:562
  46.2 2.2 %mix_back.1 = (f32[160,128]{1,0:T(8,128)S(1)}, f32[160,128]{1,0:T(8,128)S(1)}, f32[32,2,640]{2,1,0:T(2,128)}) custom-call(f32[32,2,640]{2,1,0:T(2,128)S(1)} %all_to_all.21.refs_0_, f32[256,512]{1,0:T(8,128)S(1)} %get-tuple-element.50.refs_1_, f32[4,20,24,128]{3,2,1,0:T(8,128)S(1)} %get-tuple-element.51.refs_1_.refs_2_, ...), custom_call_target="tpu_custom_call" | custom-call | bytes 3000000 | tf_op jit(solution)/shard_map/mix_back/pallas_call | solution.py:535
  48.3 2.6 %all-to-all-start.3 = ((f32[32,2,640]{2,1,0:T(2,128)}), f32[32,2,640]{2,1,0:T(2,128)S(1)}, u32[]{:S(2)}, u32[]{:S(2)}) async-start(f32[32,2,640]{2,1,0:T(2,128)} %get-tuple-element.68), calls=%async_computation.3 | async-start | bytes 327680 | tf_op jit(solution)/shard_map/all_to_all | solution.py:562
  50.9 0.2 collective-permute-start.1
  51.1 0.4 collective-permute-start.2
  51.5 1.8 %emit.1 = (bf16[20,2,4,512]{3,2,1,0:T(4,128)(2,1)}, f32[160,512]{1,0:T(8,128)S(1)}, f32[128,512]{1,0:T(8,128)S(1)}) custom-call(f32[160,512]{1,0:T(8,128)S(1)} %get-tuple-element.73.refs_0_, bf16[160,512]{1,0:T(8,128)(2,1)S(1)} %get-tuple-element.74.refs_1_, bf16[20,20]{1,0:T(8,128)(2,1)} %refs_2_.2, f32[128,512]{1,0:T(8,128)} %constant.12.clone.refs_3_), custom_call_target="tpu_custom_call" | custom-call | bytes 4500000 | tf_op jit(solution)/shard_map/emit/pallas_call | solution.py:535
  53.3 0.0 collective-permute-done.1.refs_2_
  53.3 0.0 collective-permute-done.2.refs_3_
  53.3 4.6 %grad_weights.1 = f32[16,20,4,16,20]{4,3,2,1,0:T(8,128)} custom-call(f32[160,128]{1,0:T(8,128)S(1)} %get-tuple-element.69.refs_0_, f32[160,128]{1,0:T(8,128)S(1)} %get-tuple-element.70.refs_1_, f32[160,128]{1,0:T(8,128)S(1)} %collective-permute-done.1.refs_2_, f32[160,128]{1,0:T(8,128)S(1)} %collective-permute-done.2.refs_3_), custom_call_target="tpu_custom_call" | custom-call | bytes 15000000 | tf_op jit(solution)/shard_map/grad_weights/pallas_call | solution.py:535
  57.9 1.6 %all-to-all-done.3.refs_0_ = f32[32,2,640]{2,1,0:T(2,128)S(1)} async-done(((f32[32,2,640]{2,1,0:T(2,128)}), f32[32,2,640]{2,1,0:T(2,128)S(1)}, u32[]{:S(2)}, u32[]{:S(2)}) %all-to-all-start.3) | async-done | bytes 163872 | tf_op jit(solution)/shard_map/all_to_all | solution.py:562
  59.5 1.2 %finish.1 = bf16[20,2,4,512]{3,2,1,0:T(4,128)(2,1)} custom-call(f32[32,2,640]{2,1,0:T(2,128)S(1)} %all-to-all-done.3.refs_0_, f32[160,512]{1,0:T(8,128)S(1)} %get-tuple-element.80.refs_1_, f32[128,512]{1,0:T(8,128)S(1)} %get-tuple-element.81.refs_2_), custom_call_target="tpu_custom_call" | custom-call | bytes 3000000 | tf_op jit(solution)/shard_map/finish/pallas_call | solution.py:535
Async XLA Ops:
  4.9 12.1 %collective-permute-start = (f32[4,20,24,128]{3,2,1,0:T(8,128)S(1)}, f32[4,20,24,128]{3,2,1,0:T(8,128)}, u32[]{:S(2)}, u32[]{:S(2)}) collective-permute-start(f32[4,20,24,128]{3,2,1,0:T(8,128)S(1)} %get-tuple-element.44.refs_1_), channel_id=1, source_target_pairs={{0,1},{1,0},{2,3},{3,2},{4,5},{5,4},{6,7},{7,6},{8,9},{9,8},{10,11... | collective-permute-start | bytes 2949128 | tf_op jit(solution)/shard_map/ppermute | solution.py:565
  5.4 15.5 %all-to-all-start = ((f32[32,2,640]{2,1,0:T(2,128)}), f32[32,2,640]{2,1,0:T(2,128)S(1)}, u32[]{:S(2)}, u32[]{:S(2)}) async-start(f32[32,2,640]{2,1,0:T(2,128)} %get-tuple-element.43), calls=%async_computation | async-start | bytes 327680 | tf_op jit(solution)/shard_map/all_to_all | solution.py:562
  48.3 11.2 %all-to-all-start.3 = ((f32[32,2,640]{2,1,0:T(2,128)}), f32[32,2,640]{2,1,0:T(2,128)S(1)}, u32[]{:S(2)}, u32[]{:S(2)}) async-start(f32[32,2,640]{2,1,0:T(2,128)} %get-tuple-element.68), calls=%async_computation.3 | async-start | bytes 327680 | tf_op jit(solution)/shard_map/all_to_all | solution.py:562
  50.9 2.4 %collective-permute-start.1 = (f32[160,128]{1,0:T(8,128)S(1)}, f32[160,128]{1,0:T(8,128)S(1)}, u32[]{:S(2)}, u32[]{:S(2)}) collective-permute-start(f32[160,128]{1,0:T(8,128)S(1)} %get-tuple-element.71), channel_id=1, source_target_pairs={{0,1},{1,0},{2,3},{3,2},{4,5},{5,4},{6,7},{7,6},{8,9},{9,8},{10,11... | collective-permute-start | bytes 245768 | tf_op jit(solution)/shard_map/ppermute | solution.py:565
  51.1 2.2 %collective-permute-start.2 = (f32[160,128]{1,0:T(8,128)S(1)}, f32[160,128]{1,0:T(8,128)S(1)}, u32[]{:S(2)}, u32[]{:S(2)}) collective-permute-start(f32[160,128]{1,0:T(8,128)S(1)} %get-tuple-element.72), channel_id=1, source_target_pairs={{0,1},{1,0},{2,3},{3,2},{4,5},{5,4},{6,7},{7,6},{8,9},{9,8},{10,11... | collective-permute-start | bytes 245768 | tf_op jit(solution)/shard_map/ppermute | solution.py:565

commit v17 on v16

--- a/solution.py
+++ b/solution.py
@@ -220,10 +220,11 @@
     ]
     for copy in few:
         copy.start()
+    copies = start_weights(sizes, source, 1 - core_of(), here, weight_semaphores, 0, sizes.share)
     clear_weights(sizes, target)
     for copy in few:
         copy.wait()
-    copies = start_weights(sizes, source, 1 - core_of(), here, weight_semaphores)
+    copies += start_weights(sizes, source, 1 - core_of(), here, weight_semaphores, sizes.share)
     values = gather_cells(field_here, cells, sizes).astype(BF16)
     send_modes(dot(values, table_here[...]), out_here, sizes)
     copy = pltpu.make_async_copy(out_here, out, semaphores.at[2])
@@ -268,9 +269,9 @@
     return lax.rem(lax.axis_index("gy"), 2)
 
 
-def start_weights(sizes, source, half, here, semaphores):
+def start_weights(sizes, source, half, here, semaphores, first=0, end=None):
     copies = []
-    for at in range(2 * sizes.share):
+    for at in range(2 * sizes.share)[first:end]:
         copies.append(pltpu.make_async_copy(source.at[2 * sizes.share * half + at], here.at[at], semaphores.at[at]))
         copies[-1].start()
     return copies
@@ -313,12 +314,13 @@
                 (tables.at[owner, :, pl.ds(s * lanes, lanes)], table.at[:, pl.ds((2 * s + at) * lanes, lanes)])
             )
     few = [pltpu.make_async_copy(*move, small.at[at]) for at, move in enumerate(moves)]
+    for copy in few[:4]:
+        copy.start()
     copies = start_weights(sizes, source, core_of(), here, semaphores)
-    for copy in few:
+    for copy in few[4:]:
         copy.start()
     clear_weights(sizes, target)
-    turn_weights(sizes, copies, here, target)
-    for copy in few:
+    for copy in few[:4]:
         copy.wait()
     values = gather_cells(field_here, cells, sizes).astype(BF16)
     spread = one_hot(sizes.channels * sizes.cells, sizes.channels, sizes.cells, True).astype(F32)
@@ -331,7 +333,8 @@
     ]
     for copy in results:
         copy.start()
-    for copy in results:
+    turn_weights(sizes, copies, here, target)
+    for copy in few[4:] + results:
         copy.wait()
 
 

time: 61.1 us -> 59.4 us (0.972)
  Pallas kernels: 22.9 us -> 20.9 us
  waiting for transfers between devices: 4.32 us -> 5.37 us
  blocking collectives: 22.2 us -> 21.4 us
    pallas_call x9, Pallas kernels: 22.9 us -> 20.9 us  [whole_call(): pl.pallas_call(kernel, out_shape=out_shape, in_specs=specs or [VMEM] * le...]
    all_to_all x2, waiting for transfers between devices: 4.32 us -> 5.37 us  [exchange(): lax.all_to_all(payload, ('gx', 'gy'), split_axis=0, concat_axis=0, tiled=...]
    all_to_all x2, blocking collectives: 22.2 us -> 21.4 us  [exchange(): lax.all_to_all(payload, ('gx', 'gy'), split_axis=0, concat_axis=0, tiled=...]
  transfers between devices with their start and end apart: 5 -> 5, of which waited for: 2 -> 2; matrix products, arithmetic and copies ran while one was open for 0% -> 0% of each run, Pallas kernels for 20% -> 19%
where the time goes in v17:
time: 59.4 us; the launch traced here: 59.1 us
  blocking collectives  21.4 us (36%)
  Pallas kernels  20.9 us (35%)
  starting transfers between devices  10.6 us (18%)
  waiting for transfers between devices  5.37 us (9%)
  between operations  0.73 us (1%)
    all_to_all x2, blocking collectives, exchange(): lax.all_to_all(payload, ('gx', 'gy'), split_axis=0, concat_axis=0, tiled=...  21.4 us
    pallas_call x9, Pallas kernels, whole_call(): pl.pallas_call(kernel, out_shape=out_shape, in_specs=specs or [VMEM] * le...  20.9 us
    all_to_all x2, starting transfers between devices, exchange(): lax.all_to_all(payload, ('gx', 'gy'), split_axis=0, concat_axis=0, tiled=...  9.54 us
    all_to_all x2, waiting for transfers between devices, exchange(): lax.all_to_all(payload, ('gx', 'gy'), split_axis=0, concat_axis=0, tiled=...  5.37 us
  transfers between devices with their start and end apart: 5, of which 2 were waited for; matrix products, arithmetic and copies ran while one was open for 0% of the time, Pallas kernels for 19%

profile of v17, /device:TPU:0, one launch (start us, length us, event | category | flops | bytes accessed | tf_op | source)
XLA Modules:
  0.0 59.1 jit_solution(18081039898294420588)
XLA Ops:
  0.6 3.4 %depth_forward.1 = (f32[32,2,640]{2,1,0:T(2,128)}, f32[4,20,24,128]{3,2,1,0:T(8,128)S(1)}) custom-call(bf16[20,2,4,512]{3,2,1,0:T(4,128)(2,1)} %refs_3_.2, bf16[512,128]{1,0:T(8,128)(2,1)} %constant.10.clone.refs_1_, f32[16,20,4,16,20]{4,3,2,1,0:T(8,128)} %bitcast.6), custom_call_target="tpu_custom_call" | custom-call | bytes 4500000 | tf_op jit(solution)/shard_map/depth_forward/pallas_call | solution.py:538
  4.0 0.5 collective-permute-start
  4.6 7.0 %all-to-all-start = ((f32[32,2,640]{2,1,0:T(2,128)}), f32[32,2,640]{2,1,0:T(2,128)S(1)}, u32[]{:S(2)}, u32[]{:S(2)}) async-start(f32[32,2,640]{2,1,0:T(2,128)} %get-tuple-element.43), calls=%async_computation | async-start | bytes 327680 | tf_op jit(solution)/shard_map/all_to_all | solution.py:565
  11.5 3.6 %prepare.1 = (f32[4,20,24,128]{3,2,1,0:T(8,128)S(1)}, f32[256,512]{1,0:T(8,128)S(1)}, f32[160,512]{1,0:T(8,128)}, f32[160,512]{1,0:T(8,128)}) custom-call(f32[16,20,4,16,20]{4,3,2,1,0:T(8,128)} %bitcast.7, f32[4,20,24,128]{3,2,1,0:T(8,128)S(1)} %get-tuple-element.44.refs_1_, f32[4,256,256]{2,1,0:T(8,128)} %constant.14.clone.refs_2_, ...), custom_call_target="tpu_custom_call" | custom-call | bytes 300000 | tf_op jit(solution)/shard_map/prepare/pallas_call | solution.py:538
  15.1 0.0 collective-permute-done.refs_0_
  15.1 1.2 %fetch_weights.1.refs_3_ = f32[4,20,24,128]{3,2,1,0:T(8,128)S(1)} custom-call(f32[4,20,24,128]{3,2,1,0:T(8,128)} %collective-permute-done.refs_0_, f32[4,20,24,128]{3,2,1,0:T(8,128)S(1)} %get-tuple-element.51.refs_1_.refs_2_), custom_call_target="tpu_custom_call" | custom-call | bytes 300000 | tf_op jit(solution)/shard_map/fetch_weights/pallas_call | solution.py:538
  16.3 3.8 %all-to-all-done.refs_0_ = f32[32,2,640]{2,1,0:T(2,128)S(1)} async-done(((f32[32,2,640]{2,1,0:T(2,128)}), f32[32,2,640]{2,1,0:T(2,128)S(1)}, u32[]{:S(2)}, u32[]{:S(2)}) %all-to-all-start) | async-done | bytes 163872 | tf_op jit(solution)/shard_map/all_to_all | solution.py:565
  20.1 1.8 %mix_forward.1 = (f32[160,128]{1,0:T(8,128)S(1)}, f32[160,128]{1,0:T(8,128)S(1)}, f32[32,2,640]{2,1,0:T(2,128)S(1)}, f32[160,512]{1,0:T(8,128)S(1)}, f32[160,512...) custom-call(f32[32,2,640]{2,1,0:T(2,128)S(1)} %all-to-all-done.refs_0_, ...), custom_call_target="tpu_custom_call" | custom-call | bytes 3000000 | tf_op jit(solution)/shard_map/mix_forward/pallas_call | solution.py:538
  21.9 10.7 %all_to_all.20.refs_0_ = f32[32,2,640]{2,1,0:T(2,128)S(1)} all-to-all(f32[32,2,640]{2,1,0:T(2,128)S(1)} %get-tuple-element.55), channel_id=1, replica_groups=mesh['gx'=8,'gy'=4] {'gx','gy'}, dimensions={0} | all-to-all | bytes 327680 | tf_op jit(solution)/shard_map/all_to_all | solution.py:565
  32.6 1.2 %activate.1 = (f32[160,512]{1,0:T(8,128)S(1)}, bf16[160,512]{1,0:T(8,128)(2,1)S(1)}, f32[32,2,640]{2,1,0:T(2,128)S(1)}) custom-call(f32[32,2,640]{2,1,0:T(2,128)S(1)} %all_to_all.20.refs_0_, f32[160,512]{1,0:T(8,128)S(1)} %get-tuple-element.56.refs_1_, f32[160,512]{1,0:T(8,128)S(1)} %get-tuple-element.57.refs_2_, f32[128,512]{1,0:T(8,128)S(1)} %get-tuple-element.58.refs_3_, ...), custom_call_target="tpu_custom_call" | custom-call | bytes 6000000 | tf_op jit(solution)/shard_map/activate/pallas_call | solution.py:538
  33.8 10.7 %all_to_all.21.refs_0_ = f32[32,2,640]{2,1,0:T(2,128)S(1)} all-to-all(f32[32,2,640]{2,1,0:T(2,128)S(1)} %get-tuple-element.60), channel_id=1, replica_groups=mesh['gx'=8,'gy'=4] {'gx','gy'}, dimensions={0} | all-to-all | bytes 327680 | tf_op jit(solution)/shard_map/all_to_all | solution.py:565
  44.5 2.2 %mix_back.1 = (f32[160,128]{1,0:T(8,128)S(1)}, f32[160,128]{1,0:T(8,128)S(1)}, f32[32,2,640]{2,1,0:T(2,128)}) custom-call(f32[32,2,640]{2,1,0:T(2,128)S(1)} %all_to_all.21.refs_0_, f32[256,512]{1,0:T(8,128)S(1)} %get-tuple-element.50.refs_1_, f32[4,20,24,128]{3,2,1,0:T(8,128)S(1)} %get-tuple-element.51.refs_1_.refs_2_, ...), custom_call_target="tpu_custom_call" | custom-call | bytes 3000000 | tf_op jit(solution)/shard_map/mix_back/pallas_call | solution.py:538
  46.7 2.6 %all-to-all-start.3 = ((f32[32,2,640]{2,1,0:T(2,128)}), f32[32,2,640]{2,1,0:T(2,128)S(1)}, u32[]{:S(2)}, u32[]{:S(2)}) async-start(f32[32,2,640]{2,1,0:T(2,128)} %get-tuple-element.68), calls=%async_computation.3 | async-start | bytes 327680 | tf_op jit(solution)/shard_map/all_to_all | solution.py:565
  49.2 0.2 collective-permute-start.1
  49.4 0.4 collective-permute-start.2
  49.8 1.8 %emit.1 = (bf16[20,2,4,512]{3,2,1,0:T(4,128)(2,1)}, f32[160,512]{1,0:T(8,128)S(1)}, f32[128,512]{1,0:T(8,128)S(1)}) custom-call(f32[160,512]{1,0:T(8,128)S(1)} %get-tuple-element.73.refs_0_, bf16[160,512]{1,0:T(8,128)(2,1)S(1)} %get-tuple-element.74.refs_1_, bf16[20,20]{1,0:T(8,128)(2,1)} %refs_2_.2, f32[128,512]{1,0:T(8,128)} %constant.12.clone.refs_3_), custom_call_target="tpu_custom_call" | custom-call | bytes 4500000 | tf_op jit(solution)/shard_map/emit/pallas_call | solution.py:538
  51.6 0.0 collective-permute-done.1.refs_2_
  51.6 0.0 collective-permute-done.2.refs_3_
  51.6 4.6 %grad_weights.1 = f32[16,20,4,16,20]{4,3,2,1,0:T(8,128)} custom-call(f32[160,128]{1,0:T(8,128)S(1)} %get-tuple-element.69.refs_0_, f32[160,128]{1,0:T(8,128)S(1)} %get-tuple-element.70.refs_1_, f32[160,128]{1,0:T(8,128)S(1)} %collective-permute-done.1.refs_2_, f32[160,128]{1,0:T(8,128)S(1)} %collective-permute-done.2.refs_3_), custom_call_target="tpu_custom_call" | custom-call | bytes 15000000 | tf_op jit(solution)/shard_map/grad_weights/pallas_call | solution.py:538
  56.2 1.6 %all-to-all-done.3.refs_0_ = f32[32,2,640]{2,1,0:T(2,128)S(1)} async-done(((f32[32,2,640]{2,1,0:T(2,128)}), f32[32,2,640]{2,1,0:T(2,128)S(1)}, u32[]{:S(2)}, u32[]{:S(2)}) %all-to-all-start.3) | async-done | bytes 163872 | tf_op jit(solution)/shard_map/all_to_all | solution.py:565
  57.8 1.2 %finish.1 = bf16[20,2,4,512]{3,2,1,0:T(4,128)(2,1)} custom-call(f32[32,2,640]{2,1,0:T(2,128)S(1)} %all-to-all-done.3.refs_0_, f32[160,512]{1,0:T(8,128)S(1)} %get-tuple-element.80.refs_1_, f32[128,512]{1,0:T(8,128)S(1)} %get-tuple-element.81.refs_2_), custom_call_target="tpu_custom_call" | custom-call | bytes 3000000 | tf_op jit(solution)/shard_map/finish/pallas_call | solution.py:538
Async XLA Ops:
  4.0 11.1 %collective-permute-start = (f32[4,20,24,128]{3,2,1,0:T(8,128)S(1)}, f32[4,20,24,128]{3,2,1,0:T(8,128)}, u32[]{:S(2)}, u32[]{:S(2)}) collective-permute-start(f32[4,20,24,128]{3,2,1,0:T(8,128)S(1)} %get-tuple-element.44.refs_1_), channel_id=1, source_target_pairs={{0,1},{1,0},{2,3},{3,2},{4,5},{5,4},{6,7},{7,6},{8,9},{9,8},{10,11... | collective-permute-start | bytes 2949128 | tf_op jit(solution)/shard_map/ppermute | solution.py:568
  4.6 15.5 %all-to-all-start = ((f32[32,2,640]{2,1,0:T(2,128)}), f32[32,2,640]{2,1,0:T(2,128)S(1)}, u32[]{:S(2)}, u32[]{:S(2)}) async-start(f32[32,2,640]{2,1,0:T(2,128)} %get-tuple-element.43), calls=%async_computation | async-start | bytes 327680 | tf_op jit(solution)/shard_map/all_to_all | solution.py:565
  46.7 11.2 %all-to-all-start.3 = ((f32[32,2,640]{2,1,0:T(2,128)}), f32[32,2,640]{2,1,0:T(2,128)S(1)}, u32[]{:S(2)}, u32[]{:S(2)}) async-start(f32[32,2,640]{2,1,0:T(2,128)} %get-tuple-element.68), calls=%async_computation.3 | async-start | bytes 327680 | tf_op jit(solution)/shard_map/all_to_all | solution.py:565
  49.2 2.4 %collective-permute-start.1 = (f32[160,128]{1,0:T(8,128)S(1)}, f32[160,128]{1,0:T(8,128)S(1)}, u32[]{:S(2)}, u32[]{:S(2)}) collective-permute-start(f32[160,128]{1,0:T(8,128)S(1)} %get-tuple-element.71), channel_id=1, source_target_pairs={{0,1},{1,0},{2,3},{3,2},{4,5},{5,4},{6,7},{7,6},{8,9},{9,8},{10,11... | collective-permute-start | bytes 245768 | tf_op jit(solution)/shard_map/ppermute | solution.py:568
  49.4 2.2 %collective-permute-start.2 = (f32[160,128]{1,0:T(8,128)S(1)}, f32[160,128]{1,0:T(8,128)S(1)}, u32[]{:S(2)}, u32[]{:S(2)}) collective-permute-start(f32[160,128]{1,0:T(8,128)S(1)} %get-tuple-element.72), channel_id=1, source_target_pairs={{0,1},{1,0},{2,3},{3,2},{4,5},{5,4},{6,7},{7,6},{8,9},{9,8},{10,11... | collective-permute-start | bytes 245768 | tf_op jit(solution)/shard_map/ppermute | solution.py:568

commit v18 on v17

--- a/solution.py
+++ b/solution.py
@@ -19,6 +19,12 @@
 
 def round_up(value, step):
     return -(-value // step) * step
+
+
+def split_table(table):
+    high = table.astype(ml_dtypes.bfloat16)
+    low = (table - high.astype(np.float32)).astype(ml_dtypes.bfloat16)
+    return jnp.asarray(high), jnp.asarray(low)
 
 
 def frequencies(kept):
@@ -191,6 +197,8 @@
 
 
 def halves(values):
+    if isinstance(values, tuple):
+        return values
     high = values.astype(BF16)
     return high, (values - high.astype(F32)).astype(BF16)
 
@@ -252,10 +260,13 @@
     return jnp.where(same, wide, 0.0).astype(BF16)
 
 
-def emit(sizes, pre, signal, weight, inverse, layer_out, local, inverse_out, weight_here, semaphores):
+def emit(
+    sizes, pre, signal, weight, inverse_high, inverse_low, layer_out, local, high_out, low_out, weight_here, semaphores
+):
     copies = [
         pltpu.make_async_copy(weight, weight_here, semaphores.at[0]),
-        pltpu.make_async_copy(inverse, inverse_out, semaphores.at[1]),
+        pltpu.make_async_copy(inverse_high, high_out, semaphores.at[1]),
+        pltpu.make_async_copy(inverse_low, low_out, semaphores.at[2]),
     ]
     for copy in copies:
         copy.start()
@@ -263,6 +274,7 @@
     copies[0].wait()
     local[...] = dot(cell_mixer(weight_here[...], False, sizes), signal[...])
     copies[1].wait()
+    copies[2].wait()
 
 
 def core_of():
@@ -301,8 +313,8 @@
 
 def prepare(
     sizes, source, after, tables, field, cotangent, weight, bias,
-    target, table, local, cotangent_out,
-    here, cells, field_here, cot_here, cot_cells, weight_here, bias_here, local_here, semaphores, small,
+    target, table_high, table_low, local, cotangent_out,
+    here, cells, field_here, cot_here, cot_cells, weight_here, bias_here, local_here, table, semaphores, small,
 ):
     del after
     place = lax.axis_index("gy")
@@ -336,6 +348,7 @@
     turn_weights(sizes, copies, here, target)
     for copy in few[4:] + results:
         copy.wait()
+    table_high[...], table_low[...] = halves(table[...])
 
 
 def fetch_weights(sizes, source, after, target, semaphore):
@@ -361,7 +374,7 @@
             shift = sizes.rest_width - piece * sizes.rest_lanes
             flat[rows, sizes.main_lanes :] = pltpu.roll(flat[rows, sizes.main_lanes :], shift, 1)
     rows, lanes = targets[0].shape
-    both = fine_dot(flat[...].T[:rows], table[...])
+    both = fine_dot(flat[...].T[:rows], table)
     total = both[:, : 2 * lanes] + pltpu.roll(both[:, 2 * lanes :], rows - sizes.share, 0)
     for at, target in enumerate(targets):
         target[...] = total[:, at * lanes : (at + 1) * lanes]
@@ -369,7 +382,7 @@
 
 def plane_cells(sizes, spread, table, out):
     modes = jnp.concatenate([spread[at] for at in range(4)], 1)
-    cells = fine_dot(table[...], modes, ((1,), (1,)))
+    cells = fine_dot(table, modes, ((1,), (1,)))
     count = sizes.devices * sizes.pair
     if sizes.rest:
         last = side_by_side(cells[:, sizes.main_lanes :], count, sizes)
@@ -403,11 +416,15 @@
 
 
 def mix_forward(
-    sizes, received, table, weight, other_weight, local, cotangent, inverse, forward,
-    spectra, other_spectra, out, local_out, cotangent_out, inverse_out, forward_out,
+    sizes, received, table_high, table_low, weight, other_weight, local, cotangent, inverse_high, inverse_low, forward,
+    spectra, other_spectra, out, local_out, cotangent_out, high_out, low_out, forward_out,
     spread, swapped, flat, semaphores,
 ):
-    moves = ((local, local_out), (cotangent, cotangent_out), (inverse, inverse_out), (forward, forward_out))
+    table = (table_high[...], table_low[...])
+    moves = (
+        (local, local_out), (cotangent, cotangent_out), (inverse_high, high_out), (inverse_low, low_out),
+        (forward, forward_out),
+    )
     copies = [pltpu.make_async_copy(*move, semaphores.at[at]) for at, move in enumerate(moves)]
     for copy in copies:
         copy.start()
@@ -431,7 +448,8 @@
         copy.wait()
 
 
-def mix_back(sizes, received, table, weight, other_weight, back, other_back, out, spread, flat):
+def mix_back(sizes, received, table_high, table_low, weight, other_weight, back, other_back, out, spread, flat):
+    table = (table_high[...], table_low[...])
     plane_spectra(sizes, received, table, (back, other_back), flat)
     spread[...] = jnp.zeros_like(spread)
     real = first_lanes(sizes.channels, sizes)
@@ -494,17 +512,18 @@
 
 
 def activate(
-    sizes, received, local, cotangent, inverse, forward, pre_out, signal_out, out, spectrum, tall
+    sizes, received, local, cotangent, inverse_high, inverse_low, forward, pre_out, signal_out, out, spectrum, tall
 ):
-    pre = fine_dot(receive_modes(received, spectrum, tall, sizes), inverse[...]) + local[...]
+    inverse = (inverse_high[...], inverse_low[...])
+    pre = fine_dot(receive_modes(received, spectrum, tall, sizes), inverse) + local[...]
     pre_out[...] = pre
     signal = (cotangent[...] * gelu_parts(pre)[1]).astype(BF16)
     signal_out[...] = signal
     send_modes(dot(signal, forward[...]), out, sizes)
 
 
-def finish(sizes, received, local, inverse, grad_field, spectrum, tall):
-    spatial = fine_dot(receive_modes(received, spectrum, tall, sizes), inverse[...])
+def finish(sizes, received, local, inverse_high, inverse_low, grad_field, spectrum, tall):
+    spatial = fine_dot(receive_modes(received, spectrum, tall, sizes), (inverse_high[...], inverse_low[...]))
     scatter_cells(spatial + local[...], grad_field, sizes)
 
 
@@ -557,8 +576,9 @@
     doubled = np.repeat(kappa.reshape(z.nx, 2, 1, z.share), 2, axis=2).reshape(z.all_modes)
     forward_first = jnp.asarray(ordered.astype(ml_dtypes.bfloat16))
     forward_back = jnp.asarray((ordered.astype(ml_dtypes.bfloat16).astype(np.float32) * doubled).astype(ml_dtypes.bfloat16))
-    inverse_back = jnp.asarray(np.ascontiguousarray(ordered.T))
-    inverse_first = jnp.asarray(np.ascontiguousarray((ordered * doubled).T))
+    inverse_back = split_table(np.ascontiguousarray(ordered.T))
+    inverse_first = split_table(np.ascontiguousarray((ordered * doubled).T))
+    inverse_shape = shape_of(inverse_first[0].shape, BF16)
     pairs = [(s, s ^ 1) for s in range(z.ny)]
 
     def exchange(payload):
@@ -598,62 +618,63 @@
     )
     received = exchange(sent)
     other_turned = other_core(turned_away)
-    turned, plane, local, cot_cells = whole_call(
+    table_shape = shape_of((z.devices * z.cells, 8 * z.half), BF16)
+    turned, plane_high, plane_low, local, cot_cells = whole_call(
         prepare, z, 100,
-        (turned_shape, shape_of((z.devices * z.cells, 8 * z.half)), pltpu.HBM(cells_shape, F32), pltpu.HBM(cells_shape, F32)),
+        (turned_shape, table_shape, table_shape, pltpu.HBM(cells_shape, F32), pltpu.HBM(cells_shape, F32)),
         [
             half_scratch, cells_scratch, field_scratch, field_scratch, cells_scratch, weight_here,
-            pltpu.VMEM(channel_bias.shape, F32), cells_scratch, flags(z.modes), flags(8),
+            pltpu.VMEM(channel_bias.shape, F32), cells_scratch, pltpu.VMEM(table_shape.shape, F32), flags(z.modes), flags(8),
         ],
         weights, turned_away, jnp.asarray(plane_tables(z)), field, cotangent, pointwise_weight, channel_bias,
-        specs=[HBM, ANYWHERE] + [HBM] * 5, out_specs=(VMEM, VMEM, HBM, HBM),
+        specs=[HBM, ANYWHERE] + [HBM] * 5, out_specs=(VMEM, VMEM, VMEM, HBM, HBM),
     )
     other_turned = whole_call(
         fetch_weights, z, 100, turned_shape, [flags(1)], other_turned, turned, specs=[HBM, ANYWHERE]
     )
-    received, other_turned, turned, plane, local, cot_cells = lax.optimization_barrier(
-        (received, other_turned, turned, plane, local, cot_cells)
-    )
-    spectra, other_spectra, sent, local, cot_cells, inverse_here, forward_here = whole_call(
+    received, other_turned, turned, plane_high, plane_low, local, cot_cells = lax.optimization_barrier(
+        (received, other_turned, turned, plane_high, plane_low, local, cot_cells)
+    )
+    spectra, other_spectra, sent, local, cot_cells, high_here, low_here, forward_here = whole_call(
         mix_forward, z, 1000,
         (
             shape_of(spectra_shape), shape_of(spectra_shape), payload, shape_of(cells_shape), shape_of(cells_shape),
-            shape_of(inverse_first.shape), shape_of(forward_back.shape, BF16),
+            inverse_shape, inverse_shape, shape_of(forward_back.shape, BF16),
         ),
-        [spread_scratch, spectra_scratch, flat_scratch, flags(4)],
-        received, plane, turned, other_turned, local, cot_cells, inverse_first, forward_back,
-        specs=[HELD] + [VMEM] * 3 + [HBM] * 4,
+        [spread_scratch, spectra_scratch, flat_scratch, flags(5)],
+        received, plane_high, plane_low, turned, other_turned, local, cot_cells, *inverse_first, forward_back,
+        specs=[HELD] + [VMEM] * 4 + [HBM] * 5,
     )
     pre, signal, sent = whole_call(
         activate, z, 2000,
         (shape_of(cells_shape), shape_of(cells_shape, BF16), payload), [spectrum_scratch, tall_scratch],
-        exchange(sent), local, cot_cells, inverse_here, forward_here,
+        exchange(sent), local, cot_cells, high_here, low_here, forward_here,
     )
     back, other_back, sent = whole_call(
         mix_back, z, 1000, (shape_of(spectra_shape), shape_of(spectra_shape), payload),
-        [spread_scratch, flat_scratch], exchange(sent), plane, turned, other_turned,
+        [spread_scratch, flat_scratch], exchange(sent), plane_high, plane_low, turned, other_turned,
     )
     sent, spectra, other_spectra, back, other_back, pre, signal = lax.optimization_barrier(
         (sent, spectra, other_spectra, back, other_back, pre, signal)
     )
     returned = exchange(sent)
     given_spectra, given_back = other_core(other_spectra), other_core(other_back)
-    layer_out, local, inverse_here = whole_call(
+    layer_out, local, high_here, low_here = whole_call(
         emit, z, 1500,
-        (shape_of(field.shape, BF16), shape_of(cells_shape), shape_of(inverse_back.shape)),
-        [weight_here, flags(2)],
-        pre, signal, pointwise_weight, inverse_back, specs=[VMEM, VMEM, HBM, HBM],
+        (shape_of(field.shape, BF16), shape_of(cells_shape), inverse_shape, inverse_shape),
+        [weight_here, flags(3)],
+        pre, signal, pointwise_weight, *inverse_back, specs=[VMEM, VMEM, HBM, HBM, HBM],
     )
     gradient = whole_call(
         grad_weights, z, 5000, shape_of(weight_shape),
         [pltpu.VMEM(weight_shape, F32), spectra_scratch, spectra_scratch, flags(2 * z.modes)],
         spectra, back, given_spectra, given_back, out_specs=HBM, room=28,
     )
-    returned, gradient, layer_out, local, inverse_here = lax.optimization_barrier(
-        (returned, gradient, layer_out, local, inverse_here)
+    returned, gradient, layer_out, local, high_here, low_here = lax.optimization_barrier(
+        (returned, gradient, layer_out, local, high_here, low_here)
     )
     grad_field = whole_call(
-        finish, z, 1000, shape_of(field.shape, BF16), [spectrum_scratch, tall_scratch], returned, local, inverse_here
+        finish, z, 1000, shape_of(field.shape, BF16), [spectrum_scratch, tall_scratch], returned, local, high_here, low_here
     )
     return (layer_out, grad_field, jnp.transpose(gradient.reshape(native.shape), (0, 1, 2, 5, 3, 4)))
 

time: 59.4 us -> 59.9 us (level)
  Pallas kernels: 20.9 us -> 21.5 us
where the time goes in v18:
time: 59.9 us; the launch traced here: 59.5 us
  Pallas kernels  21.5 us (36%)
  blocking collectives  21.4 us (36%)
  starting transfers between devices  10.6 us (18%)
  waiting for transfers between devices  5.27 us (9%)
  between operations  0.73 us (1%)
    pallas_call x9, Pallas kernels, whole_call(): pl.pallas_call(kernel, out_shape=out_shape, in_specs=specs or [VMEM] * le...  21.5 us
    all_to_all x2, blocking collectives, exchange(): lax.all_to_all(payload, ('gx', 'gy'), split_axis=0, concat_axis=0, tiled=...  21.4 us
    all_to_all x2, starting transfers between devices, exchange(): lax.all_to_all(payload, ('gx', 'gy'), split_axis=0, concat_axis=0, tiled=...  9.54 us
    all_to_all x2, waiting for transfers between devices, exchange(): lax.all_to_all(payload, ('gx', 'gy'), split_axis=0, concat_axis=0, tiled=...  5.26 us
  transfers between devices with their start and end apart: 5, of which 2 were waited for; matrix products, arithmetic and copies ran while one was open for 0% of the time, Pallas kernels for 19%

profile of v18, /device:TPU:0, one launch (start us, length us, event | category | flops | bytes accessed | tf_op | source)
XLA Modules:
  0.0 59.5 jit_solution(16729579693721049451)
XLA Ops:
  0.6 3.4 %depth_forward.1 = (f32[32,2,640]{2,1,0:T(2,128)}, f32[4,20,24,128]{3,2,1,0:T(8,128)S(1)}) custom-call(bf16[20,2,4,512]{3,2,1,0:T(4,128)(2,1)} %refs_3_.2, bf16[512,128]{1,0:T(8,128)(2,1)} %constant.14.clone.refs_1_, f32[16,20,4,16,20]{4,3,2,1,0:T(8,128)} %bitcast.6), custom_call_target="tpu_custom_call" | custom-call | bytes 4500000 | tf_op jit(solution)/shard_map/depth_forward/pallas_call | solution.py:557
  4.0 0.5 collective-permute-start
  4.6 7.0 %all-to-all-start = ((f32[32,2,640]{2,1,0:T(2,128)}), f32[32,2,640]{2,1,0:T(2,128)S(1)}, u32[]{:S(2)}, u32[]{:S(2)}) async-start(f32[32,2,640]{2,1,0:T(2,128)} %get-tuple-element.48), calls=%async_computation | async-start | bytes 327680 | tf_op jit(solution)/shard_map/all_to_all | solution.py:585
  11.5 3.6 %prepare.1 = (f32[4,20,24,128]{3,2,1,0:T(8,128)S(1)}, bf16[256,512]{1,0:T(8,128)(2,1)S(1)}, bf16[256,512]{1,0:T(8,128)(2,1)S(1)}, f32[160,512]{1,0:T(8,128)}, f32[160,512]{1,0:T(8,128)}) custom-call(f32[16,20,4,16,20]{4,3,2,1,0:T(8,128)} %bitcast.7, f32[4,20,24,128]{3,2,1,0:T(8,128)S(1)} %get-tuple-element.49.refs_1_, ...), custom_call_target="tpu_custom_call" | custom-call | bytes 300000 | tf_op jit(solution)/shard_map/prepare/pallas_call | solution.py:557
  15.2 0.0 collective-permute-done.refs_0_
  15.2 1.2 %fetch_weights.1.refs_4_ = f32[4,20,24,128]{3,2,1,0:T(8,128)S(1)} custom-call(f32[4,20,24,128]{3,2,1,0:T(8,128)} %collective-permute-done.refs_0_, f32[4,20,24,128]{3,2,1,0:T(8,128)S(1)} %get-tuple-element.58.refs_1_.refs_3_), custom_call_target="tpu_custom_call" | custom-call | bytes 300000 | tf_op jit(solution)/shard_map/fetch_weights/pallas_call | solution.py:557
  16.4 3.7 %all-to-all-done.refs_0_ = f32[32,2,640]{2,1,0:T(2,128)S(1)} async-done(((f32[32,2,640]{2,1,0:T(2,128)}), f32[32,2,640]{2,1,0:T(2,128)S(1)}, u32[]{:S(2)}, u32[]{:S(2)}) %all-to-all-start) | async-done | bytes 163872 | tf_op jit(solution)/shard_map/all_to_all | solution.py:585
  20.1 2.3 %mix_forward.1 = (f32[160,128]{1,0:T(8,128)S(1)}, f32[160,128]{1,0:T(8,128)S(1)}, f32[32,2,640]{2,1,0:T(2,128)S(1)}, f32[160,512]{1,0:T(8,128)S(1)}, f32[160,512...) custom-call(f32[32,2,640]{2,1,0:T(2,128)S(1)} %all-to-all-done.refs_0_,, ...), custom_call_target="tpu_custom_call" | custom-call | bytes 3000000 | tf_op jit(solution)/shard_map/mix_forward/pallas_call | solution.py:557
  22.4 10.7 %all_to_all.20.refs_0_ = f32[32,2,640]{2,1,0:T(2,128)S(1)} all-to-all(f32[32,2,640]{2,1,0:T(2,128)S(1)} %get-tuple-element.62), channel_id=1, replica_groups=mesh['gx'=8,'gy'=4] {'gx','gy'}, dimensions={0} | all-to-all | bytes 327680 | tf_op jit(solution)/shard_map/all_to_all | solution.py:585
  33.1 1.2 %activate.1 = (f32[160,512]{1,0:T(8,128)S(1)}, bf16[160,512]{1,0:T(8,128)(2,1)S(1)}, f32[32,2,640]{2,1,0:T(2,128)S(1)}) custom-call(f32[32,2,640]{2,1,0:T(2,128)S(1)} %all_to_all.20.refs_0_, f32[160,512]{1,0:T(8,128)S(1)} %get-tuple-element.63.refs_1_, f32[160,512]{1,0:T(8,128)S(1)} %get-tuple-element.64.refs_2_, ...), custom_call_target="tpu_custom_call" | custom-call | bytes 6000000 | tf_op jit(solution)/shard_map/activate/pallas_call | solution.py:557
  34.3 10.7 %all_to_all.21.refs_0_ = f32[32,2,640]{2,1,0:T(2,128)S(1)} all-to-all(f32[32,2,640]{2,1,0:T(2,128)S(1)} %get-tuple-element.68), channel_id=1, replica_groups=mesh['gx'=8,'gy'=4] {'gx','gy'}, dimensions={0} | all-to-all | bytes 327680 | tf_op jit(solution)/shard_map/all_to_all | solution.py:585
  45.0 2.1 %mix_back.1 = (f32[160,128]{1,0:T(8,128)S(1)}, f32[160,128]{1,0:T(8,128)S(1)}, f32[32,2,640]{2,1,0:T(2,128)}) custom-call(f32[32,2,640]{2,1,0:T(2,128)S(1)} %all_to_all.21.refs_0_, bf16[256,512]{1,0:T(8,128)(2,1)S(1)} %get-tuple-element.56.refs_1_, bf16[256,512]{1,0:T(8,128)(2,1)S(1)} %get-tuple-element.57.refs_2_, ...), custom_call_target="tpu_custom_call" | custom-call | bytes 3000000 | tf_op jit(solution)/shard_map/mix_back/pallas_call | solution.py:557
  47.1 2.6 %all-to-all-start.3 = ((f32[32,2,640]{2,1,0:T(2,128)}), f32[32,2,640]{2,1,0:T(2,128)S(1)}, u32[]{:S(2)}, u32[]{:S(2)}) async-start(f32[32,2,640]{2,1,0:T(2,128)} %get-tuple-element.76), calls=%async_computation.3 | async-start | bytes 327680 | tf_op jit(solution)/shard_map/all_to_all | solution.py:585
  49.7 0.2 collective-permute-start.1
  49.9 0.4 collective-permute-start.2
  50.3 1.8 %emit.1 = (bf16[20,2,4,512]{3,2,1,0:T(4,128)(2,1)}, f32[160,512]{1,0:T(8,128)S(1)}, bf16[128,512]{1,0:T(8,128)(2,1)S(1)}, bf16[128,512]{1,0:T(8,128)(2,1)S(1)}) custom-call(f32[160,512]{1,0:T(8,128)S(1)} %get-tuple-element.81.refs_0_, bf16[160,512]{1,0:T(8,128)(2,1)S(1)} %get-tuple-element.82.refs_1_, bf16[20,20]{1,0:T(8,128)(2,1)} %refs_2_.2, ...), custom_call_target="tpu_custom_call" | custom-call | bytes 4500000 | tf_op jit(solution)/shard_map/emit/pallas_call | solution.py:557
  52.1 0.0 collective-permute-done.1.refs_2_
  52.1 0.0 collective-permute-done.2.refs_3_
  52.1 4.6 %grad_weights.1 = f32[16,20,4,16,20]{4,3,2,1,0:T(8,128)} custom-call(f32[160,128]{1,0:T(8,128)S(1)} %get-tuple-element.77.refs_0_, f32[160,128]{1,0:T(8,128)S(1)} %get-tuple-element.78.refs_1_, f32[160,128]{1,0:T(8,128)S(1)} %collective-permute-done.1.refs_2_, f32[160,128]{1,0:T(8,128)S(1)} %collective-permute-done.2.refs_3_), custom_call_target="tpu_custom_call" | custom-call | bytes 15000000 | tf_op jit(solution)/shard_map/grad_weights/pallas_call | solution.py:557
  56.7 1.6 %all-to-all-done.3.refs_0_ = f32[32,2,640]{2,1,0:T(2,128)S(1)} async-done(((f32[32,2,640]{2,1,0:T(2,128)}), f32[32,2,640]{2,1,0:T(2,128)S(1)}, u32[]{:S(2)}, u32[]{:S(2)}) %all-to-all-start.3) | async-done | bytes 163872 | tf_op jit(solution)/shard_map/all_to_all | solution.py:585
  58.3 1.2 %finish.1 = bf16[20,2,4,512]{3,2,1,0:T(4,128)(2,1)} custom-call(f32[32,2,640]{2,1,0:T(2,128)S(1)} %all-to-all-done.3.refs_0_, f32[160,512]{1,0:T(8,128)S(1)} %get-tuple-element.89.refs_1_, bf16[128,512]{1,0:T(8,128)(2,1)S(1)} %get-tuple-element.90.refs_2_, bf16[128,512]{1,0:T(8,128)(2,1)S(1)} %get-tuple-element.91.refs_3_), custom_call_target="tpu_custom_call" | custom-call | bytes 3000000 | tf_op jit(solution)/shard_map/finish/pallas_call | solution.py:557
Async XLA Ops:
  4.0 11.1 %collective-permute-start = (f32[4,20,24,128]{3,2,1,0:T(8,128)S(1)}, f32[4,20,24,128]{3,2,1,0:T(8,128)}, u32[]{:S(2)}, u32[]{:S(2)}) collective-permute-start(f32[4,20,24,128]{3,2,1,0:T(8,128)S(1)} %get-tuple-element.49.refs_1_), channel_id=1, source_target_pairs={{0,1},{1,0},{2,3},{3,2},{4,5},{5,4},{6,7},{7,6},{8,9},{9,8},{10,11... | collective-permute-start | bytes 2949128 | tf_op jit(solution)/shard_map/ppermute | solution.py:588
  4.6 15.5 %all-to-all-start = ((f32[32,2,640]{2,1,0:T(2,128)}), f32[32,2,640]{2,1,0:T(2,128)S(1)}, u32[]{:S(2)}, u32[]{:S(2)}) async-start(f32[32,2,640]{2,1,0:T(2,128)} %get-tuple-element.48), calls=%async_computation | async-start | bytes 327680 | tf_op jit(solution)/shard_map/all_to_all | solution.py:585
  47.1 11.2 %all-to-all-start.3 = ((f32[32,2,640]{2,1,0:T(2,128)}), f32[32,2,640]{2,1,0:T(2,128)S(1)}, u32[]{:S(2)}, u32[]{:S(2)}) async-start(f32[32,2,640]{2,1,0:T(2,128)} %get-tuple-element.76), calls=%async_computation.3 | async-start | bytes 327680 | tf_op jit(solution)/shard_map/all_to_all | solution.py:585
  49.7 2.4 %collective-permute-start.1 = (f32[160,128]{1,0:T(8,128)S(1)}, f32[160,128]{1,0:T(8,128)S(1)}, u32[]{:S(2)}, u32[]{:S(2)}) collective-permute-start(f32[160,128]{1,0:T(8,128)S(1)} %get-tuple-element.79), channel_id=1, source_target_pairs={{0,1},{1,0},{2,3},{3,2},{4,5},{5,4},{6,7},{7,6},{8,9},{9,8},{10,11... | collective-permute-start | bytes 245768 | tf_op jit(solution)/shard_map/ppermute | solution.py:588
  49.9 2.2 %collective-permute-start.2 = (f32[160,128]{1,0:T(8,128)S(1)}, f32[160,128]{1,0:T(8,128)S(1)}, u32[]{:S(2)}, u32[]{:S(2)}) collective-permute-start(f32[160,128]{1,0:T(8,128)S(1)} %get-tuple-element.80), channel_id=1, source_target_pairs={{0,1},{1,0},{2,3},{3,2},{4,5},{5,4},{6,7},{7,6},{8,9},{9,8},{10,11... | collective-permute-start | bytes 245768 | tf_op jit(solution)/shard_map/ppermute | solution.py:588

commit v19 on v17

--- a/solution.py
+++ b/solution.py
@@ -431,6 +431,27 @@
         copy.wait()
 
 
+def sum_rows(blocks):
+    row = lax.broadcasted_iota(jnp.int32, blocks[0].shape, 0)
+    step = 4
+    while step:
+        low = row // step % 2 == 0
+        count = len(blocks) // 2
+        blocks = [
+            jnp.where(low, one, pltpu.roll(two, step, 0)) + jnp.where(low, pltpu.roll(one, 8 - step, 0), two)
+            for one, two in zip(blocks[:count], blocks[count:])
+        ]
+        step //= 2
+    return blocks[0]
+
+
+def column_sums(products, sizes):
+    short = [sum(value[first : first + 8] for first in range(8, sizes.rows, 8)) + value[:8] for value in products]
+    short += [jnp.zeros_like(short[0])] * (round_up(len(short), 8) - len(short))
+    sums = [sum_rows(short[first : first + 8]) for first in range(0, len(short), 8)]
+    return jnp.concatenate(sums, 0)[: sizes.channels]
+
+
 def mix_back(sizes, received, table, weight, other_weight, back, other_back, out, spread, flat):
     plane_spectra(sizes, received, table, (back, other_back), flat)
     spread[...] = jnp.zeros_like(spread)
@@ -443,10 +464,10 @@
             turned = swap_parts(rows, sizes)
             straight, crossed = [], []
             for w in range(sizes.channels):
-                straight.append(jnp.sum(block[m, w] * rows, axis=0, keepdims=True))
-                crossed.append(jnp.sum(block[m, w] * turned, axis=0, keepdims=True))
-            straight = jnp.concatenate(straight, 0)
-            crossed = jnp.concatenate(crossed, 0)
+                straight.append(block[m, w] * rows)
+                crossed.append(block[m, w] * turned)
+            straight = column_sums(straight, sizes)
+            crossed = column_sums(crossed, sizes)
             real_part = straight + swap_parts(straight, sizes)
             imag_part = swap_parts(crossed, sizes) - crossed
             put_mixed(spread, at, m, jnp.where(real, real_part, imag_part), sizes)

time: 59.4 us -> 59.4 us (level)
  no operation moved by 1% of the time
where the time goes in v19:
time: 59.4 us; the launch traced here: 59 us
  blocking collectives  21.4 us (36%)
  Pallas kernels  20.9 us (35%)
  starting transfers between devices  10.6 us (18%)
  waiting for transfers between devices  5.37 us (9%)
  between operations  0.73 us (1%)
    all_to_all x2, blocking collectives, exchange(): lax.all_to_all(payload, ('gx', 'gy'), split_axis=0, concat_axis=0, tiled=...  21.4 us
    pallas_call x9, Pallas kernels, whole_call(): pl.pallas_call(kernel, out_shape=out_shape, in_specs=specs or [VMEM] * le...  20.9 us
    all_to_all x2, starting transfers between devices, exchange(): lax.all_to_all(payload, ('gx', 'gy'), split_axis=0, concat_axis=0, tiled=...  9.54 us
    all_to_all x2, waiting for transfers between devices, exchange(): lax.all_to_all(payload, ('gx', 'gy'), split_axis=0, concat_axis=0, tiled=...  5.37 us
  transfers between devices with their start and end apart: 5, of which 2 were waited for; matrix products, arithmetic and copies ran while one was open for 0% of the time, Pallas kernels for 19%

profile of v19, /device:TPU:0, one launch (start us, length us, event | category | flops | bytes accessed | tf_op | source)
XLA Modules:
  0.0 59.0 jit_solution(8508607588866391997)
XLA Ops:
  0.6 3.4 %depth_forward.1 = (f32[32,2,640]{2,1,0:T(2,128)}, f32[4,20,24,128]{3,2,1,0:T(8,128)S(1)}) custom-call(bf16[20,2,4,512]{3,2,1,0:T(4,128)(2,1)} %refs_3_.2, bf16[512,128]{1,0:T(8,128)(2,1)} %constant.10.clone.refs_1_, f32[16,20,4,16,20]{4,3,2,1,0:T(8,128)} %bitcast.6), custom_call_target="tpu_custom_call" | custom-call | bytes 4500000 | tf_op jit(solution)/shard_map/depth_forward/pallas_call | solution.py:559
  4.0 0.5 collective-permute-start
  4.6 7.0 %all-to-all-start = ((f32[32,2,640]{2,1,0:T(2,128)}), f32[32,2,640]{2,1,0:T(2,128)S(1)}, u32[]{:S(2)}, u32[]{:S(2)}) async-start(f32[32,2,640]{2,1,0:T(2,128)} %get-tuple-element.43), calls=%async_computation | async-start | bytes 327680 | tf_op jit(solution)/shard_map/all_to_all | solution.py:586
  11.5 3.6 %prepare.1 = (f32[4,20,24,128]{3,2,1,0:T(8,128)S(1)}, f32[256,512]{1,0:T(8,128)S(1)}, f32[160,512]{1,0:T(8,128)}, f32[160,512]{1,0:T(8,128)}) custom-call(f32[16,20,4,16,20]{4,3,2,1,0:T(8,128)} %bitcast.7, f32[4,20,24,128]{3,2,1,0:T(8,128)S(1)} %get-tuple-element.44.refs_1_, f32[4,256,256]{2,1,0:T(8,128)} %constant.14.clone.refs_2_, ...), custom_call_target="tpu_custom_call" | custom-call | bytes 300000 | tf_op jit(solution)/shard_map/prepare/pallas_call | solution.py:559
  15.1 0.0 collective-permute-done.refs_0_
  15.1 1.2 %fetch_weights.1.refs_3_ = f32[4,20,24,128]{3,2,1,0:T(8,128)S(1)} custom-call(f32[4,20,24,128]{3,2,1,0:T(8,128)} %collective-permute-done.refs_0_, f32[4,20,24,128]{3,2,1,0:T(8,128)S(1)} %get-tuple-element.51.refs_1_.refs_2_), custom_call_target="tpu_custom_call" | custom-call | bytes 300000 | tf_op jit(solution)/shard_map/fetch_weights/pallas_call | solution.py:559
  16.3 3.8 %all-to-all-done.refs_0_ = f32[32,2,640]{2,1,0:T(2,128)S(1)} async-done(((f32[32,2,640]{2,1,0:T(2,128)}), f32[32,2,640]{2,1,0:T(2,128)S(1)}, u32[]{:S(2)}, u32[]{:S(2)}) %all-to-all-start) | async-done | bytes 163872 | tf_op jit(solution)/shard_map/all_to_all | solution.py:586
  20.1 1.8 %mix_forward.1 = (f32[160,128]{1,0:T(8,128)S(1)}, f32[160,128]{1,0:T(8,128)S(1)}, f32[32,2,640]{2,1,0:T(2,128)S(1)}, f32[160,512]{1,0:T(8,128)S(1)}, f32[160,512...) custom-call(f32[32,2,640]{2,1,0:T(2,128)S(1)} %all-to-all-done.refs_0_, ...), custom_call_target="tpu_custom_call" | custom-call | bytes 3000000 | tf_op jit(solution)/shard_map/mix_forward/pallas_call | solution.py:559
  21.9 10.7 %all_to_all.20.refs_0_ = f32[32,2,640]{2,1,0:T(2,128)S(1)} all-to-all(f32[32,2,640]{2,1,0:T(2,128)S(1)} %get-tuple-element.55), channel_id=1, replica_groups=mesh['gx'=8,'gy'=4] {'gx','gy'}, dimensions={0} | all-to-all | bytes 327680 | tf_op jit(solution)/shard_map/all_to_all | solution.py:586
  32.6 1.2 %activate.1 = (f32[160,512]{1,0:T(8,128)S(1)}, bf16[160,512]{1,0:T(8,128)(2,1)S(1)}, f32[32,2,640]{2,1,0:T(2,128)S(1)}) custom-call(f32[32,2,640]{2,1,0:T(2,128)S(1)} %all_to_all.20.refs_0_, f32[160,512]{1,0:T(8,128)S(1)} %get-tuple-element.56.refs_1_, f32[160,512]{1,0:T(8,128)S(1)} %get-tuple-element.57.refs_2_, f32[128,512]{1,0:T(8,128)S(1)} %get-tuple-element.58.refs_3_, ...), custom_call_target="tpu_custom_call" | custom-call | bytes 6000000 | tf_op jit(solution)/shard_map/activate/pallas_call | solution.py:559
  33.8 10.7 %all_to_all.21.refs_0_ = f32[32,2,640]{2,1,0:T(2,128)S(1)} all-to-all(f32[32,2,640]{2,1,0:T(2,128)S(1)} %get-tuple-element.60), channel_id=1, replica_groups=mesh['gx'=8,'gy'=4] {'gx','gy'}, dimensions={0} | all-to-all | bytes 327680 | tf_op jit(solution)/shard_map/all_to_all | solution.py:586
  44.5 2.1 %mix_back.1 = (f32[160,128]{1,0:T(8,128)S(1)}, f32[160,128]{1,0:T(8,128)S(1)}, f32[32,2,640]{2,1,0:T(2,128)}) custom-call(f32[32,2,640]{2,1,0:T(2,128)S(1)} %all_to_all.21.refs_0_, f32[256,512]{1,0:T(8,128)S(1)} %get-tuple-element.50.refs_1_, f32[4,20,24,128]{3,2,1,0:T(8,128)S(1)} %get-tuple-element.51.refs_1_.refs_2_, ...), custom_call_target="tpu_custom_call" | custom-call | bytes 3000000 | tf_op jit(solution)/shard_map/mix_back/pallas_call | solution.py:559
  46.6 2.6 %all-to-all-start.3 = ((f32[32,2,640]{2,1,0:T(2,128)}), f32[32,2,640]{2,1,0:T(2,128)S(1)}, u32[]{:S(2)}, u32[]{:S(2)}) async-start(f32[32,2,640]{2,1,0:T(2,128)} %get-tuple-element.68), calls=%async_computation.3 | async-start | bytes 327680 | tf_op jit(solution)/shard_map/all_to_all | solution.py:586
  49.2 0.2 collective-permute-start.1
  49.4 0.4 collective-permute-start.2
  49.8 1.8 %emit.1 = (bf16[20,2,4,512]{3,2,1,0:T(4,128)(2,1)}, f32[160,512]{1,0:T(8,128)S(1)}, f32[128,512]{1,0:T(8,128)S(1)}) custom-call(f32[160,512]{1,0:T(8,128)S(1)} %get-tuple-element.73.refs_0_, bf16[160,512]{1,0:T(8,128)(2,1)S(1)} %get-tuple-element.74.refs_1_, bf16[20,20]{1,0:T(8,128)(2,1)} %refs_2_.2, f32[128,512]{1,0:T(8,128)} %constant.12.clone.refs_3_), custom_call_target="tpu_custom_call" | custom-call | bytes 4500000 | tf_op jit(solution)/shard_map/emit/pallas_call | solution.py:559
  51.6 0.0 collective-permute-done.1.refs_2_
  51.6 0.0 collective-permute-done.2.refs_3_
  51.6 4.6 %grad_weights.1 = f32[16,20,4,16,20]{4,3,2,1,0:T(8,128)} custom-call(f32[160,128]{1,0:T(8,128)S(1)} %get-tuple-element.69.refs_0_, f32[160,128]{1,0:T(8,128)S(1)} %get-tuple-element.70.refs_1_, f32[160,128]{1,0:T(8,128)S(1)} %collective-permute-done.1.refs_2_, f32[160,128]{1,0:T(8,128)S(1)} %collective-permute-done.2.refs_3_), custom_call_target="tpu_custom_call" | custom-call | bytes 15000000 | tf_op jit(solution)/shard_map/grad_weights/pallas_call | solution.py:559
  56.2 1.6 %all-to-all-done.3.refs_0_ = f32[32,2,640]{2,1,0:T(2,128)S(1)} async-done(((f32[32,2,640]{2,1,0:T(2,128)}), f32[32,2,640]{2,1,0:T(2,128)S(1)}, u32[]{:S(2)}, u32[]{:S(2)}) %all-to-all-start.3) | async-done | bytes 163872 | tf_op jit(solution)/shard_map/all_to_all | solution.py:586
  57.8 1.2 %finish.1 = bf16[20,2,4,512]{3,2,1,0:T(4,128)(2,1)} custom-call(f32[32,2,640]{2,1,0:T(2,128)S(1)} %all-to-all-done.3.refs_0_, f32[160,512]{1,0:T(8,128)S(1)} %get-tuple-element.80.refs_1_, f32[128,512]{1,0:T(8,128)S(1)} %get-tuple-element.81.refs_2_), custom_call_target="tpu_custom_call" | custom-call | bytes 3000000 | tf_op jit(solution)/shard_map/finish/pallas_call | solution.py:559
Async XLA Ops:
  4.0 11.1 %collective-permute-start = (f32[4,20,24,128]{3,2,1,0:T(8,128)S(1)}, f32[4,20,24,128]{3,2,1,0:T(8,128)}, u32[]{:S(2)}, u32[]{:S(2)}) collective-permute-start(f32[4,20,24,128]{3,2,1,0:T(8,128)S(1)} %get-tuple-element.44.refs_1_), channel_id=1, source_target_pairs={{0,1},{1,0},{2,3},{3,2},{4,5},{5,4},{6,7},{7,6},{8,9},{9,8},{10,11... | collective-permute-start | bytes 2949128 | tf_op jit(solution)/shard_map/ppermute | solution.py:589
  4.6 15.5 %all-to-all-start = ((f32[32,2,640]{2,1,0:T(2,128)}), f32[32,2,640]{2,1,0:T(2,128)S(1)}, u32[]{:S(2)}, u32[]{:S(2)}) async-start(f32[32,2,640]{2,1,0:T(2,128)} %get-tuple-element.43), calls=%async_computation | async-start | bytes 327680 | tf_op jit(solution)/shard_map/all_to_all | solution.py:586
  46.6 11.2 %all-to-all-start.3 = ((f32[32,2,640]{2,1,0:T(2,128)}), f32[32,2,640]{2,1,0:T(2,128)S(1)}, u32[]{:S(2)}, u32[]{:S(2)}) async-start(f32[32,2,640]{2,1,0:T(2,128)} %get-tuple-element.68), calls=%async_computation.3 | async-start | bytes 327680 | tf_op jit(solution)/shard_map/all_to_all | solution.py:586
  49.2 2.4 %collective-permute-start.1 = (f32[160,128]{1,0:T(8,128)S(1)}, f32[160,128]{1,0:T(8,128)S(1)}, u32[]{:S(2)}, u32[]{:S(2)}) collective-permute-start(f32[160,128]{1,0:T(8,128)S(1)} %get-tuple-element.71), channel_id=1, source_target_pairs={{0,1},{1,0},{2,3},{3,2},{4,5},{5,4},{6,7},{7,6},{8,9},{9,8},{10,11... | collective-permute-start | bytes 245768 | tf_op jit(solution)/shard_map/ppermute | solution.py:589
  49.4 2.2 %collective-permute-start.2 = (f32[160,128]{1,0:T(8,128)S(1)}, f32[160,128]{1,0:T(8,128)S(1)}, u32[]{:S(2)}, u32[]{:S(2)}) collective-permute-start(f32[160,128]{1,0:T(8,128)S(1)} %get-tuple-element.72), channel_id=1, source_target_pairs={{0,1},{1,0},{2,3},{3,2},{4,5},{5,4},{6,7},{7,6},{8,9},{9,8},{10,11... | collective-permute-start | bytes 245768 | tf_op jit(solution)/shard_map/ppermute | solution.py:589

commit v20 on v19

--- a/solution.py
+++ b/solution.py
@@ -220,11 +220,11 @@
     ]
     for copy in few:
         copy.start()
-    copies = start_weights(sizes, source, 1 - core_of(), here, weight_semaphores, 0, sizes.share)
+    copies = start_weights(sizes, source, 1 - core_of(), here, weight_semaphores, 0, sizes.share + 1)
     clear_weights(sizes, target)
     for copy in few:
         copy.wait()
-    copies += start_weights(sizes, source, 1 - core_of(), here, weight_semaphores, sizes.share)
+    copies += start_weights(sizes, source, 1 - core_of(), here, weight_semaphores, sizes.share + 1)
     values = gather_cells(field_here, cells, sizes).astype(BF16)
     send_modes(dot(values, table_here[...]), out_here, sizes)
     copy = pltpu.make_async_copy(out_here, out, semaphores.at[2])

time: 59.4 us -> 59.3 us (level)
  no operation moved by 1% of the time
where the time goes in v20:
time: 59.3 us; the launch traced here: 59 us
  blocking collectives  21.4 us (36%)
  Pallas kernels  20.8 us (35%)
  starting transfers between devices  10.6 us (18%)
  waiting for transfers between devices  5.37 us (9%)
  between operations  0.73 us (1%)
    all_to_all x2, blocking collectives, exchange(): lax.all_to_all(payload, ('gx', 'gy'), split_axis=0, concat_axis=0, tiled=...  21.4 us
    pallas_call x9, Pallas kernels, whole_call(): pl.pallas_call(kernel, out_shape=out_shape, in_specs=specs or [VMEM] * le...  20.8 us
    all_to_all x2, starting transfers between devices, exchange(): lax.all_to_all(payload, ('gx', 'gy'), split_axis=0, concat_axis=0, tiled=...  9.54 us
    all_to_all x2, waiting for transfers between devices, exchange(): lax.all_to_all(payload, ('gx', 'gy'), split_axis=0, concat_axis=0, tiled=...  5.37 us
  transfers between devices with their start and end apart: 5, of which 2 were waited for; matrix products, arithmetic and copies ran while one was open for 0% of the time, Pallas kernels for 19%

profile of v20, /device:TPU:0, one launch (start us, length us, event | category | flops | bytes accessed | tf_op | source)
XLA Modules:
  0.0 59.0 jit_solution(17339154248868943947)
XLA Ops:
  0.6 3.4 %depth_forward.1 = (f32[32,2,640]{2,1,0:T(2,128)}, f32[4,20,24,128]{3,2,1,0:T(8,128)S(1)}) custom-call(bf16[20,2,4,512]{3,2,1,0:T(4,128)(2,1)} %refs_3_.2, bf16[512,128]{1,0:T(8,128)(2,1)} %constant.10.clone.refs_1_, f32[16,20,4,16,20]{4,3,2,1,0:T(8,128)} %bitcast.6), custom_call_target="tpu_custom_call" | custom-call | bytes 4500000 | tf_op jit(solution)/shard_map/depth_forward/pallas_call | solution.py:559
  4.0 0.5 collective-permute-start
  4.5 7.0 %all-to-all-start = ((f32[32,2,640]{2,1,0:T(2,128)}), f32[32,2,640]{2,1,0:T(2,128)S(1)}, u32[]{:S(2)}, u32[]{:S(2)}) async-start(f32[32,2,640]{2,1,0:T(2,128)} %get-tuple-element.43), calls=%async_computation | async-start | bytes 327680 | tf_op jit(solution)/shard_map/all_to_all | solution.py:586
  11.5 3.6 %prepare.1 = (f32[4,20,24,128]{3,2,1,0:T(8,128)S(1)}, f32[256,512]{1,0:T(8,128)S(1)}, f32[160,512]{1,0:T(8,128)}, f32[160,512]{1,0:T(8,128)}) custom-call(f32[16,20,4,16,20]{4,3,2,1,0:T(8,128)} %bitcast.7, f32[4,20,24,128]{3,2,1,0:T(8,128)S(1)} %get-tuple-element.44.refs_1_, f32[4,256,256]{2,1,0:T(8,128)} %constant.14.clone.refs_2_, ...), custom_call_target="tpu_custom_call" | custom-call | bytes 300000 | tf_op jit(solution)/shard_map/prepare/pallas_call | solution.py:559
  15.0 0.0 collective-permute-done.refs_0_
  15.1 1.2 %fetch_weights.1.refs_3_ = f32[4,20,24,128]{3,2,1,0:T(8,128)S(1)} custom-call(f32[4,20,24,128]{3,2,1,0:T(8,128)} %collective-permute-done.refs_0_, f32[4,20,24,128]{3,2,1,0:T(8,128)S(1)} %get-tuple-element.51.refs_1_.refs_2_), custom_call_target="tpu_custom_call" | custom-call | bytes 300000 | tf_op jit(solution)/shard_map/fetch_weights/pallas_call | solution.py:559
  16.3 3.8 %all-to-all-done.refs_0_ = f32[32,2,640]{2,1,0:T(2,128)S(1)} async-done(((f32[32,2,640]{2,1,0:T(2,128)}), f32[32,2,640]{2,1,0:T(2,128)S(1)}, u32[]{:S(2)}, u32[]{:S(2)}) %all-to-all-start) | async-done | bytes 163872 | tf_op jit(solution)/shard_map/all_to_all | solution.py:586
  20.1 1.8 %mix_forward.1 = (f32[160,128]{1,0:T(8,128)S(1)}, f32[160,128]{1,0:T(8,128)S(1)}, f32[32,2,640]{2,1,0:T(2,128)S(1)}, f32[160,512]{1,0:T(8,128)S(1)}, f32[160,512...) custom-call(f32[32,2,640]{2,1,0:T(2,128)S(1)} %all-to-all-done.refs_0_, ...), custom_call_target="tpu_custom_call" | custom-call | bytes 3000000 | tf_op jit(solution)/shard_map/mix_forward/pallas_call | solution.py:559
  21.8 10.7 %all_to_all.20.refs_0_ = f32[32,2,640]{2,1,0:T(2,128)S(1)} all-to-all(f32[32,2,640]{2,1,0:T(2,128)S(1)} %get-tuple-element.55), channel_id=1, replica_groups=mesh['gx'=8,'gy'=4] {'gx','gy'}, dimensions={0} | all-to-all | bytes 327680 | tf_op jit(solution)/shard_map/all_to_all | solution.py:586
  32.6 1.2 %activate.1 = (f32[160,512]{1,0:T(8,128)S(1)}, bf16[160,512]{1,0:T(8,128)(2,1)S(1)}, f32[32,2,640]{2,1,0:T(2,128)S(1)}) custom-call(f32[32,2,640]{2,1,0:T(2,128)S(1)} %all_to_all.20.refs_0_, f32[160,512]{1,0:T(8,128)S(1)} %get-tuple-element.56.refs_1_, f32[160,512]{1,0:T(8,128)S(1)} %get-tuple-element.57.refs_2_, f32[128,512]{1,0:T(8,128)S(1)} %get-tuple-element.58.refs_3_, ...), custom_call_target="tpu_custom_call" | custom-call | bytes 6000000 | tf_op jit(solution)/shard_map/activate/pallas_call | solution.py:559
  33.7 10.7 %all_to_all.21.refs_0_ = f32[32,2,640]{2,1,0:T(2,128)S(1)} all-to-all(f32[32,2,640]{2,1,0:T(2,128)S(1)} %get-tuple-element.60), channel_id=1, replica_groups=mesh['gx'=8,'gy'=4] {'gx','gy'}, dimensions={0} | all-to-all | bytes 327680 | tf_op jit(solution)/shard_map/all_to_all | solution.py:586
  44.4 2.1 %mix_back.1 = (f32[160,128]{1,0:T(8,128)S(1)}, f32[160,128]{1,0:T(8,128)S(1)}, f32[32,2,640]{2,1,0:T(2,128)}) custom-call(f32[32,2,640]{2,1,0:T(2,128)S(1)} %all_to_all.21.refs_0_, f32[256,512]{1,0:T(8,128)S(1)} %get-tuple-element.50.refs_1_, f32[4,20,24,128]{3,2,1,0:T(8,128)S(1)} %get-tuple-element.51.refs_1_.refs_2_, ...), custom_call_target="tpu_custom_call" | custom-call | bytes 3000000 | tf_op jit(solution)/shard_map/mix_back/pallas_call | solution.py:559
  46.6 2.6 %all-to-all-start.3 = ((f32[32,2,640]{2,1,0:T(2,128)}), f32[32,2,640]{2,1,0:T(2,128)S(1)}, u32[]{:S(2)}, u32[]{:S(2)}) async-start(f32[32,2,640]{2,1,0:T(2,128)} %get-tuple-element.68), calls=%async_computation.3 | async-start | bytes 327680 | tf_op jit(solution)/shard_map/all_to_all | solution.py:586
  49.2 0.2 collective-permute-start.1
  49.3 0.4 collective-permute-start.2
  49.7 1.8 %emit.1 = (bf16[20,2,4,512]{3,2,1,0:T(4,128)(2,1)}, f32[160,512]{1,0:T(8,128)S(1)}, f32[128,512]{1,0:T(8,128)S(1)}) custom-call(f32[160,512]{1,0:T(8,128)S(1)} %get-tuple-element.73.refs_0_, bf16[160,512]{1,0:T(8,128)(2,1)S(1)} %get-tuple-element.74.refs_1_, bf16[20,20]{1,0:T(8,128)(2,1)} %refs_2_.2, f32[128,512]{1,0:T(8,128)} %constant.12.clone.refs_3_), custom_call_target="tpu_custom_call" | custom-call | bytes 4500000 | tf_op jit(solution)/shard_map/emit/pallas_call | solution.py:559
  51.5 0.0 collective-permute-done.1.refs_2_
  51.5 0.0 collective-permute-done.2.refs_3_
  51.6 4.6 %grad_weights.1 = f32[16,20,4,16,20]{4,3,2,1,0:T(8,128)} custom-call(f32[160,128]{1,0:T(8,128)S(1)} %get-tuple-element.69.refs_0_, f32[160,128]{1,0:T(8,128)S(1)} %get-tuple-element.70.refs_1_, f32[160,128]{1,0:T(8,128)S(1)} %collective-permute-done.1.refs_2_, f32[160,128]{1,0:T(8,128)S(1)} %collective-permute-done.2.refs_3_), custom_call_target="tpu_custom_call" | custom-call | bytes 15000000 | tf_op jit(solution)/shard_map/grad_weights/pallas_call | solution.py:559
  56.1 1.6 %all-to-all-done.3.refs_0_ = f32[32,2,640]{2,1,0:T(2,128)S(1)} async-done(((f32[32,2,640]{2,1,0:T(2,128)}), f32[32,2,640]{2,1,0:T(2,128)S(1)}, u32[]{:S(2)}, u32[]{:S(2)}) %all-to-all-start.3) | async-done | bytes 163872 | tf_op jit(solution)/shard_map/all_to_all | solution.py:586
  57.7 1.2 %finish.1 = bf16[20,2,4,512]{3,2,1,0:T(4,128)(2,1)} custom-call(f32[32,2,640]{2,1,0:T(2,128)S(1)} %all-to-all-done.3.refs_0_, f32[160,512]{1,0:T(8,128)S(1)} %get-tuple-element.80.refs_1_, f32[128,512]{1,0:T(8,128)S(1)} %get-tuple-element.81.refs_2_), custom_call_target="tpu_custom_call" | custom-call | bytes 3000000 | tf_op jit(solution)/shard_map/finish/pallas_call | solution.py:559
Async XLA Ops:
  4.0 11.1 %collective-permute-start = (f32[4,20,24,128]{3,2,1,0:T(8,128)S(1)}, f32[4,20,24,128]{3,2,1,0:T(8,128)}, u32[]{:S(2)}, u32[]{:S(2)}) collective-permute-start(f32[4,20,24,128]{3,2,1,0:T(8,128)S(1)} %get-tuple-element.44.refs_1_), channel_id=1, source_target_pairs={{0,1},{1,0},{2,3},{3,2},{4,5},{5,4},{6,7},{7,6},{8,9},{9,8},{10,11... | collective-permute-start | bytes 2949128 | tf_op jit(solution)/shard_map/ppermute | solution.py:589
  4.5 15.5 %all-to-all-start = ((f32[32,2,640]{2,1,0:T(2,128)}), f32[32,2,640]{2,1,0:T(2,128)S(1)}, u32[]{:S(2)}, u32[]{:S(2)}) async-start(f32[32,2,640]{2,1,0:T(2,128)} %get-tuple-element.43), calls=%async_computation | async-start | bytes 327680 | tf_op jit(solution)/shard_map/all_to_all | solution.py:586
  46.6 11.2 %all-to-all-start.3 = ((f32[32,2,640]{2,1,0:T(2,128)}), f32[32,2,640]{2,1,0:T(2,128)S(1)}, u32[]{:S(2)}, u32[]{:S(2)}) async-start(f32[32,2,640]{2,1,0:T(2,128)} %get-tuple-element.68), calls=%async_computation.3 | async-start | bytes 327680 | tf_op jit(solution)/shard_map/all_to_all | solution.py:586
  49.2 2.4 %collective-permute-start.1 = (f32[160,128]{1,0:T(8,128)S(1)}, f32[160,128]{1,0:T(8,128)S(1)}, u32[]{:S(2)}, u32[]{:S(2)}) collective-permute-start(f32[160,128]{1,0:T(8,128)S(1)} %get-tuple-element.71), channel_id=1, source_target_pairs={{0,1},{1,0},{2,3},{3,2},{4,5},{5,4},{6,7},{7,6},{8,9},{9,8},{10,11... | collective-permute-start | bytes 245768 | tf_op jit(solution)/shard_map/ppermute | solution.py:589
  49.3 2.2 %collective-permute-start.2 = (f32[160,128]{1,0:T(8,128)S(1)}, f32[160,128]{1,0:T(8,128)S(1)}, u32[]{:S(2)}, u32[]{:S(2)}) collective-permute-start(f32[160,128]{1,0:T(8,128)S(1)} %get-tuple-element.72), channel_id=1, source_target_pairs={{0,1},{1,0},{2,3},{3,2},{4,5},{5,4},{6,7},{7,6},{8,9},{9,8},{10,11... | collective-permute-start | bytes 245768 | tf_op jit(solution)/shard_map/ppermute | solution.py:589
